TPU v7x, 32 devices: a whole 2x2x4 slice. The times are simulated.
32 devices in a mesh: group: 8 (over z, y), fold: 4 (over x, core).
Axes of the slice: x: 2, y: 2, z: 4, core: 2. Of those that a mesh axis runs over, the one named last changes fastest.
Arguments:
- right_side: float32 [16, 131072], P(None, ('group', 'fold')), may hold values from -6 to 6
- initial: float32 [16, 131072], P(None, ('group', 'fold')), may hold values from -6 to 6
- counts: int32 [8, 4], P('group'), may hold values from 1 to 4096, 8192 in all within a row
- columns: int32 [512, 5], P('group'), may hold values from 0 to 69, as said below
- blocks: float32 [512, 5, 128, 128], P('group')
Outputs:
- smoothed: float32 [16, 131072], P(None, ('group', 'fold'))
Inputs may be any that keep to these rules, and one draw needn't show every extreme that they name: Every row of counts sums to 8192, and its largest entry is 4096. `columns`: index j of row block g * 64 + i names block g * 64 + j - 3; the 5 indices of a row block are distinct and lie within 3 of i + 3.
All inputs are finite; a program needn't handle non-finite values.
Results may differ from a plain program's by a relative error of at most 0.0001.
Values sent between devices are 32-bit elements; how exact they have to be, the bound alone decides.
No kernel may reach another device: no remote copies, remote signals or barrier semaphores. Data moves between devices by JAX's collectives and lax.ppermute only.
A program may use at most 192 MiB of HBM per device.

v0:
```python
import jax
import jax.numpy as jnp
from jax import lax
from jax.sharding import PartitionSpec as P

HB = 3
SWEEPS = 3
DEGREE = 4


upper_bound = 4.5
lower_bound = 1.35


def padded_2(shard, sides, width):
    for axis, dim in sides:
        devices, length = (lax.axis_size(axis), shard.shape[dim])
        up = [(i, (i + 1) % devices) for i in range(devices - 1)]
        down = [(j, i) for i, j in up]
        last = lax.slice_in_dim(shard, length - width, length, axis=dim)
        initial = lax.slice_in_dim(shard, 0, width, axis=dim)
        before = lax.ppermute(last, axis, up)
        after = lax.ppermute(initial, axis, down)
        shard = jnp.concatenate([before, shard, after], axis=dim)
    return shard


def on_device(right_side, initial, counts, columns, blocks):
    folds = lax.axis_size("fold")
    vectors, capacity = right_side.shape
    own_blocks, width = (blocks.shape[0], blocks.shape[2])
    live_rows = counts[0]
    starts = jnp.cumsum(live_rows) - live_rows
    stacked = jnp.stack([right_side, initial])
    gathered = lax.all_gather(stacked, "fold", axis=2, tiled=True)
    position = lax.axis_index("fold")
    row_ids = jnp.arange(own_blocks * width, dtype=jnp.int32)
    covered = starts[None, :] <= row_ids[:, None]
    owner_slot = jnp.sum(covered.astype(jnp.int32), axis=1) - 1
    row_start = jnp.max(jnp.where(covered, starts[None, :], 0), axis=1)
    source = owner_slot * capacity + row_ids - row_start
    owned = jnp.take(gathered, source, axis=2)
    target = owned[0]
    iterate = owned[1]

    def operate(vector):
        extended = padded_2(vector, (("group", 1),), HB * width)
        extended = extended.reshape(vectors, own_blocks + 2 * HB, width)
        picked = jnp.take(extended, columns, axis=1)
        result = jnp.einsum("nikc,ikrc->nir", picked, blocks, precision=lax.Precision.HIGHEST)
        return result.reshape(vectors, own_blocks * width)

    theta = (upper_bound + lower_bound) / 2.0
    delta = (upper_bound - lower_bound) / 2.0
    for sweep in range(SWEEPS):
        resid = target - operate(iterate)
        update = resid / theta
        ratio_now = delta / theta
        for step in range(DEGREE):
            iterate = iterate + update
            if step + 1 < DEGREE:
                resid = resid - operate(update)
                ratio_next = 1.0 / (2.0 * theta / delta - ratio_now)
                update = ratio_next * ratio_now * update + 2.0 * ratio_next / delta * resid
                ratio_now = ratio_next
    fold_ids = jnp.arange(folds, dtype=jnp.int32)
    my_start = jnp.sum(jnp.where(fold_ids == position, starts, 0))
    my_count = jnp.sum(jnp.where(fold_ids == position, live_rows, 0))
    padded = jnp.concatenate([iterate, jnp.zeros((vectors, capacity), jnp.float32)], axis=1)
    piece = lax.dynamic_slice_in_dim(padded, my_start, capacity, 1)
    valid = jnp.arange(capacity, dtype=jnp.int32) < my_count
    return jnp.where(valid[None, :], piece, jnp.float32(0.0))


def solution(mesh):
    placed = (
        P(None, ("group", "fold")),
        P(None, ("group", "fold")),
        P("group", None),
        P("group", None),
        P("group", None, None, None),
    )
    return jax.shard_map(
        on_device, mesh=mesh, in_specs=placed, out_specs=P(None, ("group", "fold")), check_vma=False
    )
```

profile of v0, /device:TPU:0, one launch (start us, length us, event | category | flops | bytes accessed | tf_op | source)
XLA Modules:
  0.0 548.4 jit_solution(4250472698478903509)
XLA Ops:
  6.5 1.9 pad_maximum_fusion
  12.0 22.2 %all-gather.2.cloned.1.call-done = f32[2,16,16384]{2,1,0:T(8,128)} async-done(((f32[2,16,4096]{2,1,0:T(8,128)}), f32[2,16,16384]{2,1,0:T(8,128)}) %all-gather.2.cloned.1.call-update) | async-done | bytes 2097168 | tf_op jit(solution)/shard_map/all_gather | solution.py:35
  34.2 18.6 %copy.304 = f32[2,16,16384]{1,0,2:T(2,128)} copy(f32[2,16,16384]{2,1,0:T(8,128)} %all-gather.2.cloned.1.call-done) | data formatting | bytes 4194304 | tf_op jit(solution)/shard_map/all_gather | solution.py:35
  52.9 62.2 %gather_fusion = f32[8192,2,16]{2,1,0:T(2,128)} fusion(f32[2,16,16384]{1,0,2:T(2,128)} %copy.304, s32[8192]{0:T(1024)S(1)} %broadcast_clamp_fusion), kind=kCustom, calls=%fused_computation.12 | custom fusion | bytes 2129920 | tf_op jit(solution)/shard_map/jit(_take)/gather | solution.py:42
  115.1 9.3 %copy.305 = f32[8192,2,16]{0,2,1:T(8,128)S(1)} copy(f32[8192,2,16]{2,1,0:T(2,128)} %gather_fusion) | data formatting | bytes 2097152 | tf_op jit(solution)/shard_map/jit(_take)/gather | solution.py:42
  124.6 3.4 collective-permute-start
  129.5 4.2 collective-permute-done.1
  133.8 1.9 gather_fusion.1
  135.7 23.1 %fusion.60 = f32[64,2,8,128]{3,2,1,0:T(8,128)S(1)} fusion(f32[64,5,128,128]{3,2,1,0:T(8,128)} %param.11, f32[64,5,16,128]{3,2,1,0:T(8,128)S(1)} %bitcast.334, pred[64,5]{1,0:T(8,128)(4,1)S(1)} %copy.306), kind=kOutput, calls=%fused_computation.73 | convolution fusion | flops 1007288320 | bytes 24117568 | tf_op jit(solution)/shard_map/nikc,ikrc->nir/dot_general | solution.py:50
  159.8 4.3 collective-permute-start.2
  165.7 4.1 collective-permute-done.3
  169.9 1.9 gather_fusion.2
  171.8 23.1 %fusion.63 = f32[64,2,8,128]{3,2,1,0:T(8,128)S(1)} fusion(f32[64,5,128,128]{3,2,1,0:T(8,128)} %param.11, f32[64,5,16,128]{3,2,1,0:T(8,128)S(1)} %bitcast.335, pred[64,5]{1,0:T(8,128)(4,1)S(1)} %copy.306), kind=kOutput, calls=%fused_computation.74 | convolution fusion | flops 1007288320 | bytes 24117568 | tf_op jit(solution)/shard_map/nikc,ikrc->nir/dot_general | solution.py:50
  195.0 3.3 collective-permute-start.4
  199.8 4.2 collective-permute-done.5
  204.1 1.9 gather_fusion.3
  206.0 23.1 %fusion.66 = f32[64,2,8,128]{3,2,1,0:T(8,128)S(1)} fusion(f32[64,5,128,128]{3,2,1,0:T(8,128)} %param.11, f32[64,5,16,128]{3,2,1,0:T(8,128)S(1)} %bitcast.336, pred[64,5]{1,0:T(8,128)(4,1)S(1)} %copy.306), kind=kOutput, calls=%fused_computation.75 | convolution fusion | flops 1007288320 | bytes 24117568 | tf_op jit(solution)/shard_map/nikc,ikrc->nir/dot_general | solution.py:50
  229.3 4.4 collective-permute-start.6
  235.5 3.9 collective-permute-done.7
  239.5 1.9 gather_fusion.4
  241.4 23.2 %fusion.69 = f32[64,2,8,128]{3,2,1,0:T(8,128)S(1)} fusion(f32[64,5,128,128]{3,2,1,0:T(8,128)} %param.11, f32[64,5,16,128]{3,2,1,0:T(8,128)S(1)} %bitcast.337, pred[64,5]{1,0:T(8,128)(4,1)S(1)} %copy.306), kind=kOutput, calls=%fused_computation.76 | convolution fusion | flops 1007288320 | bytes 24117568 | tf_op jit(solution)/shard_map/nikc,ikrc->nir/dot_general | solution.py:50
  264.9 3.3 collective-permute-start.8
  269.8 4.2 collective-permute-done.9
  274.0 1.9 gather_fusion.5
  275.9 23.1 %fusion.72 = f32[64,2,8,128]{3,2,1,0:T(8,128)S(1)} fusion(f32[64,5,128,128]{3,2,1,0:T(8,128)} %param.11, f32[64,5,16,128]{3,2,1,0:T(8,128)S(1)} %bitcast.338, pred[64,5]{1,0:T(8,128)(4,1)S(1)} %copy.306), kind=kOutput, calls=%fused_computation.77 | convolution fusion | flops 1007288320 | bytes 24117568 | tf_op jit(solution)/shard_map/nikc,ikrc->nir/dot_general | solution.py:50
  300.0 4.3 collective-permute-start.10
  305.7 4.2 collective-permute-done.11
  311.9 23.1 %fusion.75 = f32[64,2,8,128]{3,2,1,0:T(8,128)S(1)} fusion(f32[64,5,128,128]{3,2,1,0:T(8,128)} %param.11, f32[64,5,16,128]{3,2,1,0:T(8,128)S(1)} %bitcast.339, pred[64,5]{1,0:T(8,128)(4,1)S(1)} %copy.306), kind=kOutput, calls=%fused_computation.78 | convolution fusion | flops 1007288320 | bytes 24117568 | tf_op jit(solution)/shard_map/nikc,ikrc->nir/dot_general | solution.py:50
  335.1 3.4 collective-permute-start.12
  340.0 4.2 collective-permute-done.13
  344.3 1.9 gather_fusion.7
  346.3 23.1 %fusion.78 = f32[64,2,8,128]{3,2,1,0:T(8,128)S(1)} fusion(f32[64,5,128,128]{3,2,1,0:T(8,128)} %param.11, f32[64,5,16,128]{3,2,1,0:T(8,128)S(1)} %bitcast.340, pred[64,5]{1,0:T(8,128)(4,1)S(1)} %copy.306), kind=kOutput, calls=%fused_computation.79 | convolution fusion | flops 1007288320 | bytes 24117568 | tf_op jit(solution)/shard_map/nikc,ikrc->nir/dot_general | solution.py:50
  369.6 2.8 collective-permute-start.14
  373.9 4.2 collective-permute-done.15
  378.2 1.9 gather_fusion.8
  380.1 23.2 %fusion.81 = f32[64,2,8,128]{3,2,1,0:T(8,128)S(1)} fusion(f32[64,5,128,128]{3,2,1,0:T(8,128)} %param.11, f32[64,5,16,128]{3,2,1,0:T(8,128)S(1)} %bitcast.341, pred[64,5]{1,0:T(8,128)(4,1)S(1)} %copy.306), kind=kOutput, calls=%fused_computation.80 | convolution fusion | flops 1007288320 | bytes 24117568 | tf_op jit(solution)/shard_map/nikc,ikrc->nir/dot_general | solution.py:50
  403.6 2.8 collective-permute-start.16
  408.0 4.2 collective-permute-done.17
  414.1 23.1 %fusion.84 = f32[64,2,8,128]{3,2,1,0:T(8,128)S(1)} fusion(f32[64,5,128,128]{3,2,1,0:T(8,128)} %param.11, f32[64,5,16,128]{3,2,1,0:T(8,128)S(1)} %bitcast.342, pred[64,5]{1,0:T(8,128)(4,1)S(1)} %copy.306), kind=kOutput, calls=%fused_computation.81 | convolution fusion | flops 1007288320 | bytes 24117568 | tf_op jit(solution)/shard_map/nikc,ikrc->nir/dot_general | solution.py:50
  438.2 2.8 collective-permute-start.18
  442.7 4.0 collective-permute-done.19
  448.7 23.1 %fusion.87 = f32[64,2,8,128]{3,2,1,0:T(8,128)S(1)} fusion(f32[64,5,128,128]{3,2,1,0:T(8,128)} %param.11, f32[64,5,16,128]{3,2,1,0:T(8,128)S(1)} %bitcast.343, pred[64,5]{1,0:T(8,128)(4,1)S(1)} %copy.306), kind=kOutput, calls=%fused_computation.82 | convolution fusion | flops 1007288320 | bytes 24117568 | tf_op jit(solution)/shard_map/nikc,ikrc->nir/dot_general | solution.py:50
  471.9 2.8 collective-permute-start.20
  476.7 3.8 collective-permute-done.21
  480.5 1.9 gather_fusion.11
  482.5 23.1 %fusion.90 = f32[64,2,8,128]{3,2,1,0:T(8,128)S(1)} fusion(f32[64,5,128,128]{3,2,1,0:T(8,128)} %param.11, f32[64,5,16,128]{3,2,1,0:T(8,128)S(1)} %bitcast.344, pred[64,5]{1,0:T(8,128)(4,1)S(1)} %copy.306), kind=kOutput, calls=%fused_computation.83 | convolution fusion | flops 1007288320 | bytes 24117568 | tf_op jit(solution)/shard_map/nikc,ikrc->nir/dot_general | solution.py:50
  506.5 2.8 collective-permute-start.22
  517.0 23.2 %fusion.93 = f32[64,2,8,128]{3,2,1,0:T(8,128)S(1)} fusion(f32[64,5,128,128]{3,2,1,0:T(8,128)} %param.11, f32[64,5,16,128]{3,2,1,0:T(8,128)S(1)} %bitcast.333, pred[64,5]{1,0:T(8,128)(4,1)S(1)} %copy.306), kind=kOutput, calls=%fused_computation.84 | convolution fusion | flops 1007288320 | bytes 24117568 | tf_op jit(solution)/shard_map/nikc,ikrc->nir/dot_general | solution.py:50
  (175 shorter events, 39.2 us)
Async XLA Ops:
  6.5 27.7 %all-gather.2.cloned.1.call-start = ((), (), s32[]{:S(2)}) async-start(), calls=%async_computation | async-start | bytes 2621440 | tf_op jit(solution)/shard_map/all_gather | solution.py:35
  124.6 4.9 collective-permute-start
  128.0 5.7 %collective-permute-start.1 = (f32[16,384]{1,0:T(8,128)S(1)}, f32[16,384]{1,0:T(8,128)S(1)}, u32[]{:S(2)}, u32[]{:S(2)}) collective-permute-start(f32[16,384]{1,0:T(8,128)S(1)} %get-tuple-element.39), channel_id=1, source_target_pairs={{4,0},{8,4},{12,8},{16,12},{20,16},{24,20},{28,24},{5,1},{9,5},{13... | collective-permute-start | bytes 73736 | tf_op jit(solution)/shard_map/ppermute | solution.py:23
  159.8 5.9 %collective-permute-start.2 = (f32[16,384]{1,0:T(8,128)S(1)}, f32[16,384]{1,0:T(8,128)S(1)}, u32[]{:S(2)}, u32[]{:S(2)}) collective-permute-start(f32[16,384]{1,0:T(8,128)S(1)} %get-tuple-element.36), channel_id=1, source_target_pairs={{0,4},{4,8},{8,12},{12,16},{16,20},{20,24},{24,28},{1,5},{5,9},{9,... | collective-permute-start | bytes 73736 | tf_op jit(solution)/shard_map/ppermute | solution.py:22
  164.1 5.7 %collective-permute-start.3 = (f32[16,384]{1,0:T(8,128)S(1)}, f32[16,384]{1,0:T(8,128)S(1)}, u32[]{:S(2)}, u32[]{:S(2)}) collective-permute-start(f32[16,384]{1,0:T(8,128)S(1)} %get-tuple-element.37), channel_id=1, source_target_pairs={{4,0},{8,4},{12,8},{16,12},{20,16},{24,20},{28,24},{5,1},{9,5},{13... | collective-permute-start | bytes 73736 | tf_op jit(solution)/shard_map/ppermute | solution.py:23
  195.0 4.8 collective-permute-start.4
  198.3 5.7 %collective-permute-start.5 = (f32[16,384]{1,0:T(8,128)S(1)}, f32[16,384]{1,0:T(8,128)S(1)}, u32[]{:S(2)}, u32[]{:S(2)}) collective-permute-start(f32[16,384]{1,0:T(8,128)S(1)} %get-tuple-element.35), channel_id=1, source_target_pairs={{4,0},{8,4},{12,8},{16,12},{20,16},{24,20},{28,24},{5,1},{9,5},{13... | collective-permute-start | bytes 73736 | tf_op jit(solution)/shard_map/ppermute | solution.py:23
  206.0 23.2 %copy-start.21 = (f32[16,8192]{1,0:T(8,128)S(1)}, f32[16,8192]{1,0:T(8,128)}, u32[]{:S(2)}) copy-start(f32[16,8192]{1,0:T(8,128)} %copy-done.20) | copy-start | bytes 1572868
  206.0 23.2 %copy-start.30 = (f32[16,8192]{1,0:T(8,128)S(1)}, f32[16,8192]{1,0:T(8,128)}, u32[]{:S(2)}) copy-start(f32[16,8192]{1,0:T(8,128)} %get-tuple-element.15) | copy-start | bytes 1572868
  229.3 6.2 %collective-permute-start.6 = (f32[16,384]{1,0:T(8,128)S(1)}, f32[16,384]{1,0:T(8,128)S(1)}, u32[]{:S(2)}, u32[]{:S(2)}) collective-permute-start(f32[16,384]{1,0:T(8,128)S(1)} %get-tuple-element.32), channel_id=1, source_target_pairs={{0,4},{4,8},{8,12},{12,16},{16,20},{20,24},{24,28},{1,5},{5,9},{9,... | collective-permute-start | bytes 73736 | tf_op jit(solution)/shard_map/ppermute | solution.py:22
  233.7 5.7 %collective-permute-start.7 = (f32[16,384]{1,0:T(8,128)S(1)}, f32[16,384]{1,0:T(8,128)S(1)}, u32[]{:S(2)}, u32[]{:S(2)}) collective-permute-start(f32[16,384]{1,0:T(8,128)S(1)} %get-tuple-element.33), channel_id=1, source_target_pairs={{4,0},{8,4},{12,8},{16,12},{20,16},{24,20},{28,24},{5,1},{9,5},{13... | collective-permute-start | bytes 73736 | tf_op jit(solution)/shard_map/ppermute | solution.py:23
  241.4 23.2 %copy-start.2 = (f32[2,16,8192]{2,1,0:T(8,128)S(1)}, f32[2,16,8192]{2,1,0:T(8,128)}, u32[]{:S(2)}) copy-start(f32[2,16,8192]{2,1,0:T(8,128)} %copy-done) | copy-start | bytes 3145732
  241.4 23.2 %copy-start.13 = (f32[64,2,8,128]{3,2,1,0:T(8,128)S(1)}, f32[64,2,8,128]{3,2,1,0:T(8,128)}, u32[]{:S(2)}) copy-start(f32[64,2,8,128]{3,2,1,0:T(8,128)} %copy-done.11) | copy-start | bytes 1572868
  241.4 23.2 %copy-start.22 = (f32[16,8192]{1,0:T(8,128)S(1)}, f32[16,8192]{1,0:T(8,128)}, u32[]{:S(2)}) copy-start(f32[16,8192]{1,0:T(8,128)} %copy-done.20) | copy-start | bytes 1572868
  241.4 23.2 %copy-start.31 = (f32[16,8192]{1,0:T(8,128)S(1)}, f32[16,8192]{1,0:T(8,128)}, u32[]{:S(2)}) copy-start(f32[16,8192]{1,0:T(8,128)} %get-tuple-element.15) | copy-start | bytes 1572868
  241.4 23.2 %copy-start.37 = (f32[64,2,8,128]{3,2,1,0:T(8,128)S(1)}, f32[64,2,8,128]{3,2,1,0:T(8,128)}, u32[]{:S(2)}) copy-start(f32[64,2,8,128]{3,2,1,0:T(8,128)} %copy-done.36) | copy-start | bytes 1572868
  264.9 4.8 collective-permute-start.8
  268.3 5.7 %collective-permute-start.9 = (f32[16,384]{1,0:T(8,128)S(1)}, f32[16,384]{1,0:T(8,128)S(1)}, u32[]{:S(2)}, u32[]{:S(2)}) collective-permute-start(f32[16,384]{1,0:T(8,128)S(1)} %get-tuple-element.31), channel_id=1, source_target_pairs={{4,0},{8,4},{12,8},{16,12},{20,16},{24,20},{28,24},{5,1},{9,5},{13... | collective-permute-start | bytes 73736 | tf_op jit(solution)/shard_map/ppermute | solution.py:23
  300.0 5.8 %collective-permute-start.10 = (f32[16,384]{1,0:T(8,128)S(1)}, f32[16,384]{1,0:T(8,128)S(1)}, u32[]{:S(2)}, u32[]{:S(2)}) collective-permute-start(f32[16,384]{1,0:T(8,128)S(1)} %get-tuple-element.28), channel_id=1, source_target_pairs={{0,4},{4,8},{8,12},{12,16},{16,20},{20,24},{24,28},{1,5},{5,9},{9,... | collective-permute-start | bytes 73736 | tf_op jit(solution)/shard_map/ppermute | solution.py:22
  304.2 5.7 %collective-permute-start.11 = (f32[16,384]{1,0:T(8,128)S(1)}, f32[16,384]{1,0:T(8,128)S(1)}, u32[]{:S(2)}, u32[]{:S(2)}) collective-permute-start(f32[16,384]{1,0:T(8,128)S(1)} %get-tuple-element.29), channel_id=1, source_target_pairs={{4,0},{8,4},{12,8},{16,12},{20,16},{24,20},{28,24},{5,1},{9,5},{13... | collective-permute-start | bytes 73736 | tf_op jit(solution)/shard_map/ppermute | solution.py:23
  335.1 4.9 collective-permute-start.12
  338.5 5.7 %collective-permute-start.13 = (f32[16,384]{1,0:T(8,128)S(1)}, f32[16,384]{1,0:T(8,128)S(1)}, u32[]{:S(2)}, u32[]{:S(2)}) collective-permute-start(f32[16,384]{1,0:T(8,128)S(1)} %get-tuple-element.27), channel_id=1, source_target_pairs={{4,0},{8,4},{12,8},{16,12},{20,16},{24,20},{28,24},{5,1},{9,5},{13... | collective-permute-start | bytes 73736 | tf_op jit(solution)/shard_map/ppermute | solution.py:23
  346.2 23.2 %copy-start.18 = (f32[16,8192]{1,0:T(8,128)S(1)}, f32[16,8192]{1,0:T(8,128)}, u32[]{:S(2)}) copy-start(f32[16,8192]{1,0:T(8,128)} %copy-done.17) | copy-start | bytes 1572868
  346.2 23.2 %copy-start.27 = (f32[16,8192]{1,0:T(8,128)S(1)}, f32[16,8192]{1,0:T(8,128)}, u32[]{:S(2)}) copy-start(f32[16,8192]{1,0:T(8,128)} %get-tuple-element.13) | copy-start | bytes 1572868
  369.6 4.3 collective-permute-start.14
  372.4 5.7 %collective-permute-start.15 = (f32[16,384]{1,0:T(8,128)S(1)}, f32[16,384]{1,0:T(8,128)S(1)}, u32[]{:S(2)}, u32[]{:S(2)}) collective-permute-start(f32[16,384]{1,0:T(8,128)S(1)} %get-tuple-element.25), channel_id=1, source_target_pairs={{4,0},{8,4},{12,8},{16,12},{20,16},{24,20},{28,24},{5,1},{9,5},{13... | collective-permute-start | bytes 73736 | tf_op jit(solution)/shard_map/ppermute | solution.py:23
  380.1 23.2 %copy-start.10 = (f32[64,2,8,128]{3,2,1,0:T(8,128)S(1)}, f32[64,2,8,128]{3,2,1,0:T(8,128)}, u32[]{:S(2)}) copy-start(f32[64,2,8,128]{3,2,1,0:T(8,128)} %copy-done.8) | copy-start | bytes 1572868
  380.1 23.2 %copy-start.19 = (f32[16,8192]{1,0:T(8,128)S(1)}, f32[16,8192]{1,0:T(8,128)}, u32[]{:S(2)}) copy-start(f32[16,8192]{1,0:T(8,128)} %copy-done.17) | copy-start | bytes 1572868
  380.1 23.2 %copy-start.28 = (f32[16,8192]{1,0:T(8,128)S(1)}, f32[16,8192]{1,0:T(8,128)}, u32[]{:S(2)}) copy-start(f32[16,8192]{1,0:T(8,128)} %get-tuple-element.13) | copy-start | bytes 1572868
  380.1 23.2 %copy-start.35 = (f32[64,2,8,128]{3,2,1,0:T(8,128)S(1)}, f32[64,2,8,128]{3,2,1,0:T(8,128)}, u32[]{:S(2)}) copy-start(f32[64,2,8,128]{3,2,1,0:T(8,128)} %copy-done.34) | copy-start | bytes 1572868
  380.1 23.2 %copy-start.41 = (f32[16,8192]{1,0:T(8,128)S(1)}, f32[16,8192]{1,0:T(8,128)}, u32[]{:S(2)}) copy-start(f32[16,8192]{1,0:T(8,128)} %copy-done.40) | copy-start | bytes 1572868
  403.6 4.3 collective-permute-start.16
  406.5 5.7 %collective-permute-start.17 = (f32[16,384]{1,0:T(8,128)S(1)}, f32[16,384]{1,0:T(8,128)S(1)}, u32[]{:S(2)}, u32[]{:S(2)}) collective-permute-start(f32[16,384]{1,0:T(8,128)S(1)} %get-tuple-element.23), channel_id=1, source_target_pairs={{4,0},{8,4},{12,8},{16,12},{20,16},{24,20},{28,24},{5,1},{9,5},{13... | collective-permute-start | bytes 73736 | tf_op jit(solution)/shard_map/ppermute | solution.py:23
  438.2 4.5 collective-permute-start.18
  441.0 5.7 %collective-permute-start.19 = (f32[16,384]{1,0:T(8,128)S(1)}, f32[16,384]{1,0:T(8,128)S(1)}, u32[]{:S(2)}, u32[]{:S(2)}) collective-permute-start(f32[16,384]{1,0:T(8,128)S(1)} %get-tuple-element.21), channel_id=1, source_target_pairs={{4,0},{8,4},{12,8},{16,12},{20,16},{24,20},{28,24},{5,1},{9,5},{13... | collective-permute-start | bytes 73736 | tf_op jit(solution)/shard_map/ppermute | solution.py:23
  448.7 27.4 %copy-start.42 = (s32[1,4]{1,0:T(1,128)S(1)}, s32[1,4]{1,0:T(1,128)}, u32[]{:S(2)}) copy-start(s32[1,4]{1,0:T(1,128)} %param.9) | copy-start | bytes 52
  448.7 27.4 %copy-start.44 = (s32[4,1]{0,1:T(1,128)S(1)}, s32[4,1]{0,1:T(1,128)}, u32[]{:S(2)}) copy-start(s32[4,1]{0,1:T(1,128)} %copy-done.43) | copy-start | bytes 52
  471.9 4.8 collective-permute-start.20
  474.8 5.7 %collective-permute-start.21 = (f32[16,384]{1,0:T(8,128)S(1)}, f32[16,384]{1,0:T(8,128)S(1)}, u32[]{:S(2)}, u32[]{:S(2)}) collective-permute-start(f32[16,384]{1,0:T(8,128)S(1)} %get-tuple-element.19), channel_id=1, source_target_pairs={{4,0},{8,4},{12,8},{16,12},{20,16},{24,20},{28,24},{5,1},{9,5},{13... | collective-permute-start | bytes 73736 | tf_op jit(solution)/shard_map/ppermute | solution.py:23
  482.5 23.2 %copy-start.15 = (f32[16,8192]{1,0:T(8,128)S(1)}, f32[16,8192]{1,0:T(8,128)}, u32[]{:S(2)}) copy-start(f32[16,8192]{1,0:T(8,128)} %copy-done.14) | copy-start | bytes 1572868
  482.5 23.2 %copy-start.24 = (f32[16,8192]{1,0:T(8,128)S(1)}, f32[16,8192]{1,0:T(8,128)}, u32[]{:S(2)}) copy-start(f32[16,8192]{1,0:T(8,128)} %get-tuple-element.11) | copy-start | bytes 1572868
  506.5 6.7 %collective-permute-start.22 = (f32[16,384]{1,0:T(8,128)S(1)}, f32[16,384]{1,0:T(8,128)S(1)}, u32[]{:S(2)}, u32[]{:S(2)}) collective-permute-start(f32[16,384]{1,0:T(8,128)S(1)} %get-tuple-element.16), channel_id=1, source_target_pairs={{0,4},{4,8},{8,12},{12,16},{16,20},{20,24},{24,28},{1,5},{5,9},{9,... | collective-permute-start | bytes 73736 | tf_op jit(solution)/shard_map/ppermute | solution.py:22
  509.3 5.7 %collective-permute-start.23 = (f32[16,384]{1,0:T(8,128)S(1)}, f32[16,384]{1,0:T(8,128)S(1)}, u32[]{:S(2)}, u32[]{:S(2)}) collective-permute-start(f32[16,384]{1,0:T(8,128)S(1)} %get-tuple-element.17), channel_id=1, source_target_pairs={{4,0},{8,4},{12,8},{16,12},{20,16},{24,20},{28,24},{5,1},{9,5},{13... | collective-permute-start | bytes 73736 | tf_op jit(solution)/shard_map/ppermute | solution.py:23
  517.0 23.2 %copy-start.7 = (f32[64,2,8,128]{3,2,1,0:T(8,128)S(1)}, f32[64,2,8,128]{3,2,1,0:T(8,128)}, u32[]{:S(2)}) copy-start(f32[64,2,8,128]{3,2,1,0:T(8,128)} %copy-done.5) | copy-start | bytes 1572868
  517.0 23.2 %copy-start.16 = (f32[16,8192]{1,0:T(8,128)S(1)}, f32[16,8192]{1,0:T(8,128)}, u32[]{:S(2)}) copy-start(f32[16,8192]{1,0:T(8,128)} %copy-done.14) | copy-start | bytes 1572868
  517.0 23.2 %copy-start.25 = (f32[16,8192]{1,0:T(8,128)S(1)}, f32[16,8192]{1,0:T(8,128)}, u32[]{:S(2)}) copy-start(f32[16,8192]{1,0:T(8,128)} %get-tuple-element.11) | copy-start | bytes 1572868
  517.0 23.2 %copy-start.33 = (f32[64,2,8,128]{3,2,1,0:T(8,128)S(1)}, f32[64,2,8,128]{3,2,1,0:T(8,128)}, u32[]{:S(2)}) copy-start(f32[64,2,8,128]{3,2,1,0:T(8,128)} %copy-done.32) | copy-start | bytes 1572868
  517.0 23.2 %copy-start.39 = (f32[16,8192]{1,0:T(8,128)S(1)}, f32[16,8192]{1,0:T(8,128)}, u32[]{:S(2)}) copy-start(f32[16,8192]{1,0:T(8,128)} %copy-done.38) | copy-start | bytes 1572868
  (22 other events, 304.7 us)
Sparse Core Ops, SparseCore 0:
  8.9 25.2 all-gather.1
where the time goes:
time: 556 us; the launch traced here: 548 us
  matrix products  277 us (50%)
  local copies, waits for them, and re-layouts  115 us (21%)
  waiting for transfers between devices  70.3 us (13%)
  starting transfers between devices  57.7 us (10%)
  between operations  16.6 us (3%)
  other arithmetic  11.9 us (2%)
    dot_general x12, matrix products, operate(): jnp.einsum('nikc,ikrc->nir', picked, blocks, precision=lax.Precision.HIGH...  277 us
    gather x2, local copies, waits for them, and re-layouts, on_device(): owned = jnp.take(gathered, source, axis=2)  71.6 us
    ppermute x12, waiting for transfers between devices, padded_2(): after = lax.ppermute(initial, axis, down)  47.1 us
    ppermute x12, starting transfers between devices, padded_2(): before = lax.ppermute(last, axis, up)  40.5 us
    gather x12, local copies, waits for them, and re-layouts, operate(): picked = jnp.take(extended, columns, axis=1)  22.7 us
    all_gather x1, waiting for transfers between devices, on_device(): gathered = lax.all_gather(stacked, 'fold', axis=2, tiled=True)  22.2 us
    all_gather x1, local copies, waits for them, and re-layouts, on_device(): gathered = lax.all_gather(stacked, 'fold', axis=2, tiled=True)  18.6 us
    ppermute x12, starting transfers between devices, padded_2(): after = lax.ppermute(initial, axis, down)  17.3 us
  transfers between devices with their start and end apart: 25, of which 18 were waited for; matrix products, arithmetic and copies ran while one was open for 1% of the time, Pallas kernels for 0%

commit v1 on v0

v1 whole, which is shorter than its diff:
```python
import functools

import jax
import jax.numpy as jnp
from jax import lax
from jax.experimental import pallas as pl
from jax.experimental.pallas import tpu as pltpu
from jax.sharding import PartitionSpec as P

HB = 3
SWEEPS = 3
DEGREE = 4
APPLIES = SWEEPS * DEGREE

upper_bound = 4.5
lower_bound = 1.35

AXES = ("group", "fold")
F32 = jnp.float32
BF16 = jnp.bfloat16
VMEM = pl.BlockSpec(memory_space=pltpu.VMEM)
SMEM = pl.BlockSpec(memory_space=pltpu.SMEM)
ANY = pl.BlockSpec(memory_space=pl.ANY)


def coefficients():
    theta = (upper_bound + lower_bound) / 2.0
    delta = (upper_bound - lower_bound) / 2.0
    pairs = []
    for sweep in range(SWEEPS):
        pairs.append((0.0, 1.0 / theta))
        ratio = delta / theta
        for step in range(1, DEGREE):
            ratio_next = 1.0 / (2.0 * theta / delta - ratio)
            pairs.append((ratio_next * ratio, 2.0 * ratio_next / delta))
            ratio = ratio_next
    return pairs


def params(limit=40):
    return pltpu.CompilerParams(vmem_limit_bytes=limit * 2**20)


def split(value):
    high = value.astype(BF16)
    return high, (value - high.astype(F32)).astype(BF16)


def pick_lanes(window, low, shift):
    lane = lax.broadcasted_iota(jnp.int32, (16, 128), 1)
    turn = (128 - shift) % 128
    first = pltpu.roll(window(low), turn, 1)
    second = pltpu.roll(window(low + 1), turn, 1)
    return jnp.where(lane < 128 - shift, first, second)


def align_kernel(folds, ob, begin, extent, facts, *refs):
    sources, (x_out, u_out, r_out) = refs[:-3], refs[-3:]
    capacity = sources[0].shape[-1]
    lane = lax.broadcasted_iota(jnp.int32, (16, 128), 1)
    base = facts[0] * (ob * 128)
    x_out[...] = jnp.zeros_like(x_out)

    def block(e, carry):
        row = base + e * 128
        totals = [jnp.zeros((16, 128), F32), jnp.zeros((16, 128), F32)]
        for j in range(folds):
            start, count = facts[1 + j], facts[1 + folds + j]
            at = row - start
            low = at >> 7
            shift = at & 127
            index = at + lane
            valid = (index >= 0) & (index < count)
            for a, out in enumerate((1, 0)):

                def window(b, a=a, j=j):
                    b = jnp.clip(b, 0, capacity // 128 - 1)
                    return sources[j][a, :, pl.ds(pl.multiple_of(b * 128, 128), 128)]

                totals[out] = jnp.where(valid, pick_lanes(window, low, shift), totals[out])
        u_out[e] = totals[0]
        r_out[e] = totals[1]
        return carry

    lax.fori_loop(0, ob, block, 0, unroll=2)


def prepare_kernel(rows, halo, facts, blocks, out, raw, sem):
    own = blocks.shape[0]
    first = facts[0] * (rows - 2 * halo) - halo
    depth = raw.shape[0]

    def copy(a, slot):
        i = jnp.clip(first + a, 0, own - 1)
        return pltpu.make_async_copy(blocks.at[i], raw.at[slot], sem.at[slot])

    for a in range(depth - 1):
        copy(a, a).start()

    def row(a, carry):
        slot = a % depth
        copy(a, slot).wait()

        @pl.when(a + depth - 1 < rows)
        def _():
            copy(a + depth - 1, (a + depth - 1) % depth).start()

        for k in range(raw.shape[1]):
            high, low = split(raw[slot, k].T)
            out[a, k * 128 : (k + 1) * 128, :128] = high
            out[a, k * 128 : (k + 1) * 128, 128:] = low
        return carry

    lax.fori_loop(0, rows, row, 0)


def border_kernel(folds, rows, halo, facts, prepared, raw, out):
    del prepared
    fold = facts[0]

    @pl.when((fold == 0) | (fold == folds - 1))
    def _():
        first = jnp.where(fold == 0, 0, rows - halo)

        def row(a, carry):
            for k in range(raw.shape[1]):
                high, low = split(raw[a, k].T)
                out[first + a, k * 128 : (k + 1) * 128, :128] = high
                out[first + a, k * 128 : (k + 1) * 128, 128:] = low
            return carry

        lax.fori_loop(0, halo, row, 0)


def phase_kernel(ob, steps, pairs, last, facts, offsets, operator, x_in, u_in, r_in, got_a, got_b, *refs):
    h = HB * steps
    inner = h - HB
    extent = ob + 2 * h
    rows = ob + 2 * inner
    width = offsets.shape[0] // rows
    if last:
        x_out, u, r, pieces = refs
    else:
        x_out, u_out, r_out, pay_a, pay_b, u, r, pieces = refs
    even = facts[1] == 0
    for got, right in ((got_a, even), (got_b, jnp.logical_not(even))):
        u[pl.ds(jnp.where(right, h + ob, 0), h)] = got[:h]
        if inner:
            r[pl.ds(jnp.where(right, h + ob, HB), inner)] = got[h:]
    u[h : h + ob] = u_in[...]
    r[h : h + ob] = r_in[...]
    high, low = split(u[...])
    pieces[0, :, :16] = high
    pieces[0, :, 16:] = low
    x = x_in[...]
    for t in range(steps):
        x = x + u[h : h + ob]
        now, later = t % 2, (t + 1) % 2
        old, new = pairs[t]
        done = t == steps - 1

        def row(e, carry):
            a = e - HB
            left = jnp.concatenate([pieces[now, e + offsets[a * width + k]] for k in range(width)], axis=1)
            product = jnp.dot(left, operator[a], preferred_element_type=F32)
            product = product[:16] + product[16:]
            resid = r[e] - (product[:, :128] + product[:, 128:])
            r[e] = resid
            update = new * resid if old == 0.0 else old * u[e] + new * resid
            u[e] = update
            if not done:
                first, second = split(update)
                pieces[later, e, :16] = first
                pieces[later, e, 16:] = second
            return carry

        lower, upper = HB * (t + 1), extent - HB * (t + 1)
        lax.fori_loop(lower, upper, row, 0, unroll=True)
    if last:
        x_out[...] = x + u[h : h + ob]
        return
    x_out[...] = x
    u_out[...] = u[h : h + ob]
    r_out[...] = r[h : h + ob]
    for pay, right in ((pay_a, even), (pay_b, jnp.logical_not(even))):
        pay[:h] = u[pl.ds(jnp.where(right, h + ob - h, h), h)]
        if inner:
            pay[h:] = r[pl.ds(jnp.where(right, h + ob - inner, h), inner)]


def finish_kernel(ob, facts, *refs):
    parts, (out, whole) = refs[:-2], refs[-2:]
    total = whole.shape[0]
    for j, part in enumerate(parts):
        whole[pl.ds(facts[2 + j] * ob, ob)] = part[...]
    start, count = facts[0], facts[1]
    lane = lax.broadcasted_iota(jnp.int32, (16, 128), 1)
    low, shift = start >> 7, start & 127

    def block(b, carry):
        piece = pick_lanes(lambda i: whole[jnp.minimum(i, total - 1)], low + b, shift)
        piece = jnp.where(b * 128 + lane < count, piece, 0.0)
        out[:, pl.ds(pl.multiple_of(b * 128, 128), 128)] = piece
        return carry

    lax.fori_loop(0, out.shape[1] // 128, block, 0, unroll=4)


def collect(array, folds):
    held = {(0, 0): array}
    for d in range(1, folds // 2):
        held[d, 0] = lax.ppermute(array, "fold", [((i + 2 * d) % folds, i) for i in range(folds)])
    swap = [(i, i ^ 1) for i in range(folds)]
    for d in range(folds // 2):
        held[d, 1] = lax.ppermute(held[d, 0], "fold", swap)
    return held


def on_device(right_side, initial, counts, columns, blocks):
    groups, folds = lax.axis_size("group"), lax.axis_size("fold")
    vectors, capacity = right_side.shape
    own, width, side = blocks.shape[0], blocks.shape[1], blocks.shape[2]
    ob = own // folds
    steps = 3 if ob >= 9 else 2
    h = HB * steps
    inner = h - HB
    rows = ob + 2 * inner
    pairs = coefficients()
    fold = lax.axis_index("fold")
    me = lax.axis_index("group") * folds + fold
    devices = groups * folds

    last_fold = folds - 1
    border_perm = [(g * folds, (g + 1) * folds) for g in range(groups - 1)]
    border_perm += [((g + 1) * folds + last_fold, g * folds + last_fold) for g in range(groups - 1)]
    to_right = fold == 0
    outward = lax.dynamic_slice_in_dim(blocks, jnp.where(to_right, own - inner, 0), inner, 0)
    relative = columns - (jnp.arange(own, dtype=jnp.int32)[:, None] + HB)
    outward_relative = lax.dynamic_slice_in_dim(relative, jnp.where(to_right, own - inner, 0), inner, 0)
    border = lax.ppermute(outward, AXES, border_perm)
    border_relative = lax.ppermute(outward_relative, AXES, border_perm)

    around = jnp.concatenate([border_relative, relative, border_relative], axis=0)
    offsets = lax.dynamic_slice_in_dim(around, fold * ob, rows, 0).reshape(-1)

    facts = jnp.stack([fold, me % 2]).astype(jnp.int32)
    prepared = pl.pallas_call(
        functools.partial(prepare_kernel, rows, inner),
        out_shape=pltpu.VMEM((rows, width * side, 2 * side), BF16),
        in_specs=[SMEM, ANY],
        out_specs=VMEM,
        scratch_shapes=[pltpu.VMEM((4, width, side, side), F32), pltpu.SemaphoreType.DMA((4,))],
        compiler_params=params(),
        cost_estimate=pl.CostEstimate(flops=10**7, bytes_accessed=rows * width * side * side * 4, transcendentals=0),
    )(facts, blocks)
    operator = pl.pallas_call(
        functools.partial(border_kernel, folds, rows, inner),
        out_shape=pltpu.VMEM((rows, width * side, 2 * side), BF16),
        in_specs=[SMEM, VMEM, VMEM],
        out_specs=VMEM,
        input_output_aliases={1: 0},
        compiler_params=params(),
    )(facts, prepared, border)

    live = counts[0]
    starts = jnp.cumsum(live) - live
    stacked = jnp.stack([right_side, initial])
    held = collect(stacked, folds)
    keys = list(held)
    order = jnp.stack([((fold // 2 + d) % (folds // 2)) * 2 + ((fold % 2) ^ c) for d, c in keys]).astype(jnp.int32)
    align_facts = jnp.concatenate([fold[None].astype(jnp.int32), starts[order], live[order]])
    shape = jax.ShapeDtypeStruct((ob, vectors, side), F32)
    x, u, r = pl.pallas_call(
        functools.partial(align_kernel, folds, ob, 0, ob),
        out_shape=(shape, shape, shape),
        in_specs=[SMEM] + [VMEM] * folds,
        out_specs=(VMEM, VMEM, VMEM),
        compiler_params=params(),
    )(align_facts, *[held[k] for k in keys])

    even = me % 2 == 0

    def payload(right):
        at_u = jnp.where(right, ob - h, 0)
        at_r = jnp.where(right, ob - inner, 0)
        return jnp.concatenate([lax.dynamic_slice_in_dim(u, at_u, h, 0), lax.dynamic_slice_in_dim(r, at_r, inner, 0)])

    pay_a, pay_b = payload(even), payload(jnp.logical_not(even))
    swap_a = [(i, i ^ 1) for i in range(devices)]
    swap_b = [(i, i + 1) for i in range(1, devices - 1, 2)]
    swap_b += [(j, i) for i, j in swap_b]
    pay_shape = jax.ShapeDtypeStruct((2 * h - HB, vectors, side), F32)
    for phase in range(APPLIES // steps):
        got_b = lax.ppermute(pay_b, AXES, swap_b)
        got_a = lax.ppermute(pay_a, AXES, swap_a)
        last = (phase + 1) * steps == APPLIES
        outs = pl.pallas_call(
            functools.partial(phase_kernel, ob, steps, pairs[phase * steps : (phase + 1) * steps], last),
            out_shape=shape if last else (shape, shape, shape, pay_shape, pay_shape),
            in_specs=[SMEM, SMEM] + [VMEM] * 6,
            out_specs=VMEM if last else (VMEM,) * 5,
            scratch_shapes=[
                pltpu.VMEM((ob + 2 * h, vectors, side), F32),
                pltpu.VMEM((ob + 2 * h, vectors, side), F32),
                pltpu.VMEM((2, ob + 2 * h, 2 * vectors, side), BF16),
            ],
            compiler_params=params(),
        )(facts, offsets, pltpu.with_memory_space_constraint(operator, pltpu.VMEM), x, u, r, got_a, got_b)
        if last:
            x = outs
        else:
            x, u, r, pay_a, pay_b = outs

    held = collect(x, folds)
    start = jnp.sum(jnp.where(jnp.arange(folds) == fold, starts, 0))
    count = jnp.sum(jnp.where(jnp.arange(folds) == fold, live, 0))
    finish_facts = jnp.concatenate([jnp.stack([start, count]).astype(jnp.int32), order])
    return pl.pallas_call(
        functools.partial(finish_kernel, ob),
        out_shape=jax.ShapeDtypeStruct((vectors, capacity), F32),
        in_specs=[SMEM] + [VMEM] * folds,
        out_specs=VMEM,
        scratch_shapes=[pltpu.VMEM((own, vectors, side), F32)],
        compiler_params=params(),
    )(finish_facts, *[held[k] for k in keys])


def solution(mesh):
    placed = (
        P(None, AXES),
        P(None, AXES),
        P("group", None),
        P("group", None),
        P("group", None, None, None),
    )
    return jax.shard_map(on_device, mesh=mesh, in_specs=placed, out_specs=P(None, AXES), check_vma=False)
```

time: 556 us -> 128 us (0.23)
  the two profiles are of different devices: /device:TPU:0 before, /device:TPU:9 now
where the time goes in v1:
time: 128 us; the launch traced here: 127 us
  Pallas kernels  59 us (46%)
  waiting for transfers between devices  25.4 us (20%)
  starting transfers between devices  24.7 us (19%)
  local copies, waits for them, and re-layouts  13.8 us (11%)
  other arithmetic  4.3 us (3%)
    pallas_call x4, Pallas kernels, on_device(): pl.pallas_call(functools.partial(phase_kernel, ob, steps, pairs[phase * s...  43.2 us
    ppermute x2, waiting for transfers between devices, collect(): lax.ppermute(array, 'fold', [((i + 2 * d) % folds, i) for i in range(fold...  13.3 us
    ppermute x4, waiting for transfers between devices, on_device(): got_b = lax.ppermute(pay_b, AXES, swap_b)  12.1 us
    pallas_call x1, Pallas kernels, on_device(): pl.pallas_call(functools.partial(prepare_kernel, rows, inner), out_shape=...  10.9 us
    ppermute x4, starting transfers between devices, on_device(): got_b = lax.ppermute(pay_b, AXES, swap_b)  10.4 us
    unnamed x4, local copies, waits for them, and re-layouts  7.13 us
    ppermute x4, starting transfers between devices, on_device(): got_a = lax.ppermute(pay_a, AXES, swap_a)  6.23 us
    ppermute x2, starting transfers between devices, collect(): lax.ppermute(array, 'fold', [((i + 2 * d) % folds, i) for i in range(fold...  3.53 us
  transfers between devices with their start and end apart: 16, of which 5 were waited for; matrix products, arithmetic and copies ran while one was open for 6% of the time, Pallas kernels for 11%

profile of v1, /device:TPU:9, one launch (start us, length us, event | category | flops | bytes accessed | tf_op | source)
XLA Modules:
  0.0 127.5 jit_solution(349632404646416493)
XLA Ops:
  0.0 3.0 %constant_dynamic-slice_fusion.4 = f32[6,5,128,128]{3,2,1,0:T(8,128)} fusion(f32[64,5,128,128]{3,2,1,0:T(8,128)} %blocks.1, s32[]{:T(128)S(6)} %select_n.89), kind=kLoop, calls=%fused_computation.13 | loop fusion | bytes 3932164 | tf_op jit(solution)/shard_map/dynamic_slice | solution.py:237
  3.0 0.8 collective-permute-start.1
  3.8 1.1 pad_maximum_fusion.refs_0_
  4.9 3.5 %collective-permute-start.2 = (f32[2,16,4096]{2,1,0:T(8,128)S(1)}, f32[2,16,4096]{2,1,0:T(8,128)S(1)}, u32[]{:S(2)}, u32[]{:S(2)}) collective-permute-start(f32[2,16,4096]{2,1,0:T(8,128)S(1)} %pad_maximum_fusion.refs_0_), channel_id=1, source_target_pairs={{2,0},{3,1},{0,2},{1,3},{6,4},{7,5},{4,6},{5,7},{10,8},{11,9},{8,1... | collective-permute-start | bytes 1572872 | tf_op jit(solution)/shard_map/ppermute | solution.py:212
  8.4 0.0 collective-permute-start.3
  8.4 0.7 broadcast_subtract_fusion
  9.1 0.1 constant_dynamic-slice_fusion.6
  9.2 0.6 collective-permute-start
  9.9 0.8 reduce-window.9
  10.7 0.1 fusion.2
  10.8 9.3 %collective-permute-done.2.refs_1_ = f32[2,16,4096]{2,1,0:T(8,128)S(1)} collective-permute-done((f32[2,16,4096]{2,1,0:T(8,128)S(1)}, f32[2,16,4096]{2,1,0:T(8,128)S(1)}, u32[]{:S(2)}, u32[]{:S(2)}) %collective-permute-start.2) | collective-permute-done | bytes 524320 | tf_op jit(solution)/shard_map/ppermute | solution.py:212
  20.1 1.2 collective-permute-start.4
  21.3 1.4 %fusion = (s32[]{:T(128)}, s32[4]{0:T(128)S(1)}, s32[]{:T(128)}) fusion(s32[]{:T(128)} %axis_index.22, s32[1,4]{1,0:T(1,128)} %param.7, s32[4,1]{0,1:T(1,128)S(1)} %reduce-window.9), kind=kLoop, calls=%fused_computation.18 | loop fusion | flops 22 | bytes 60 | tf_op jit(solution)/shard_map/reduce_sum | solution.py:315
  22.7 0.6 gather_fusion
  23.3 1.3 %gather_fusion.1 = s32[4]{0:T(128)S(1)} fusion(s32[4]{0:T(128)} %bitcast.25, s32[1024]{0:T(1024)S(1)} %pad_clamp_fusion), kind=kCustom, calls=%fused_computation.1 | custom fusion | bytes 48 | tf_op jit(solution)/shard_map/gather | solution.py:271
  24.6 0.1 pad_add_fusion.1.facts
  24.7 10.9 %shard_map.55.prepared = bf16[28,640,256]{2,1,0:T(8,128)(2,1)S(1)} custom-call(s32[2]{0:T(128)S(1)} %pad_add_fusion.1.facts, f32[64,5,128,128]{3,2,1,0:T(8,128)} %blocks.1), custom_call_target="tpu_custom_call" | custom-call | flops 10000000 | bytes 9175040 | tf_op jit(solution)/shard_map/pallas_call | solution.py:247
  35.6 3.5 %copy-done = bf16[28,640,256]{2,1,0:T(8,128)(2,1)} copy-done((bf16[28,640,256]{2,1,0:T(8,128)(2,1)}, bf16[28,640,256]{2,1,0:T(8,128)(2,1)S(1)}, u32[]{:S(2)}) %copy-start) | copy-done | bytes 9175064
  39.1 0.1 pad_add_fusion.2.facts
  39.2 0.0 collective-permute-done.4.refs_3_
  39.2 2.4 %shard_map.57 = (f32[16,16,128]{2,1,0:T(8,128)S(1)}, f32[16,16,128]{2,1,0:T(8,128)S(1)}, f32[16,16,128]{2,1,0:T(8,128)S(1)}) custom-call(s32[9]{0:T(128)S(1)} %pad_add_fusion.2.facts, f32[2,16,4096]{2,1,0:T(8,128)S(1)} %pad_maximum_fusion.refs_0_, f32[2,16,4096]{2,1,0:T(8,128)S(1)} %collective-permute-done.2.refs_1_, ...), custom_call_target="tpu_custom_call" | custom-call | tf_op jit(solution)/shard_map/pallas_call | solution.py:273
  41.7 0.1 collective-permute-start.5
  41.8 3.7 %collective-permute-start.6 = (f32[15,16,128]{2,1,0:T(8,128)S(1)}, f32[15,16,128]{2,1,0:T(8,128)S(1)}, u32[]{:S(2)}, u32[]{:S(2)}) collective-permute-start(f32[15,16,128]{2,1,0:T(8,128)S(1)} %pad_maximum_fusion.2), channel_id=1, source_target_pairs={{1,2},{3,4},{5,6},{7,8},{9,10},{11,12},{13,14},{15,16},{17,18},{19... | collective-permute-start | bytes 368648 | tf_op jit(solution)/shard_map/ppermute | solution.py:294
  45.5 0.1 pad_add_fusion
  45.6 0.1 constant_dynamic-slice_fusion.5
  45.7 0.1 copy.7
  45.8 0.1 reshape.198.offsets
  45.9 3.6 %copy-done.1 = bf16[28,640,256]{2,1,0:T(8,128)(2,1)S(1)} copy-done((bf16[28,640,256]{2,1,0:T(8,128)(2,1)S(1)}, bf16[28,640,256]{2,1,0:T(8,128)(2,1)}, u32[]{:S(2)}) %copy-start.1) | copy-done | bytes 9175064
  49.5 0.5 shard_map.56.operator
  50.1 10.8 %shard_map.58 = (f32[16,16,128]{2,1,0:T(8,128)S(1)}, f32[16,16,128]{2,1,0:T(8,128)S(1)}, f32[16,16,128]{2,1,0:T(8,128)S(1)}, f32[15,16,128]{2,1,0:T(8,128)S(1)}, f32[15,16,128]{2,1,0:T(8,128)S(1)}) custom-call(s32[2]{0:T(128)S(1)} %pad_add_fusion.1.facts, s32[140]{0:T(256)S(1)} %reshape.198.offsets, bf16[28,640,256]{2,1,0:T(8,128)(2,1)S(1)} %shard_map.56.operator, ...), custom_call_target="tpu_custom_call" | custom-call | tf_op jit(solution)/shard_map/pallas_call | solution.py:297
  60.9 1.1 collective-permute-start.7
  61.9 2.4 %collective-permute-start.8 = (f32[15,16,128]{2,1,0:T(8,128)S(1)}, f32[15,16,128]{2,1,0:T(8,128)S(1)}, u32[]{:S(2)}, u32[]{:S(2)}) collective-permute-start(f32[15,16,128]{2,1,0:T(8,128)S(1)} %get-tuple-element.30), channel_id=1, source_target_pairs={{1,2},{3,4},{5,6},{7,8},{9,10},{11,12},{13,14},{15,16},{17,18},{19... | collective-permute-start | bytes 368648 | tf_op jit(solution)/shard_map/ppermute | solution.py:294
  64.3 5.0 %collective-permute-done.8.got_b = f32[15,16,128]{2,1,0:T(8,128)S(1)} collective-permute-done((f32[15,16,128]{2,1,0:T(8,128)S(1)}, f32[15,16,128]{2,1,0:T(8,128)S(1)}, u32[]{:S(2)}, u32[]{:S(2)}) %collective-permute-start.8) | collective-permute-done | bytes 122912 | tf_op jit(solution)/shard_map/ppermute | solution.py:294
  69.4 10.8 %shard_map.59 = (f32[16,16,128]{2,1,0:T(8,128)S(1)}, f32[16,16,128]{2,1,0:T(8,128)S(1)}, f32[16,16,128]{2,1,0:T(8,128)S(1)}, f32[15,16,128]{2,1,0:T(8,128)S(1)}, f32[15,16,128]{2,1,0:T(8,128)S(1)}) custom-call(s32[2]{0:T(128)S(1)} %pad_add_fusion.1.facts, s32[140]{0:T(256)S(1)} %reshape.198.offsets, bf16[28,640,256]{2,1,0:T(8,128)(2,1)S(1)} %shard_map.56.operator, ...), custom_call_target="tpu_custom_call" | custom-call | tf_op jit(solution)/shard_map/pallas_call | solution.py:297
  80.1 2.1 %collective-permute-start.10 = (f32[15,16,128]{2,1,0:T(8,128)S(1)}, f32[15,16,128]{2,1,0:T(8,128)S(1)}, u32[]{:S(2)}, u32[]{:S(2)}) collective-permute-start(f32[15,16,128]{2,1,0:T(8,128)S(1)} %get-tuple-element.35), channel_id=1, source_target_pairs={{1,2},{3,4},{5,6},{7,8},{9,10},{11,12},{13,14},{15,16},{17,18},{19... | collective-permute-start | bytes 368648 | tf_op jit(solution)/shard_map/ppermute | solution.py:294
  82.3 2.8 %collective-permute-start.9 = (f32[15,16,128]{2,1,0:T(8,128)S(1)}, f32[15,16,128]{2,1,0:T(8,128)S(1)}, u32[]{:S(2)}, u32[]{:S(2)}) collective-permute-start(f32[15,16,128]{2,1,0:T(8,128)S(1)} %get-tuple-element.34), channel_id=1, source_target_pairs={{0,1},{1,0},{2,3},{3,2},{4,5},{5,4},{6,7},{7,6},{8,9},{9,8},{10,11... | collective-permute-start | bytes 368648 | tf_op jit(solution)/shard_map/ppermute | solution.py:295
  85.1 1.6 %collective-permute-done.10.got_b = f32[15,16,128]{2,1,0:T(8,128)S(1)} collective-permute-done((f32[15,16,128]{2,1,0:T(8,128)S(1)}, f32[15,16,128]{2,1,0:T(8,128)S(1)}, u32[]{:S(2)}, u32[]{:S(2)}) %collective-permute-start.10) | collective-permute-done | bytes 122912 | tf_op jit(solution)/shard_map/ppermute | solution.py:294
  86.7 10.8 %shard_map.60 = (f32[16,16,128]{2,1,0:T(8,128)S(1)}, f32[16,16,128]{2,1,0:T(8,128)S(1)}, f32[16,16,128]{2,1,0:T(8,128)S(1)}, f32[15,16,128]{2,1,0:T(8,128)S(1)}, f32[15,16,128]{2,1,0:T(8,128)S(1)}) custom-call(s32[2]{0:T(128)S(1)} %pad_add_fusion.1.facts, s32[140]{0:T(256)S(1)} %reshape.198.offsets, bf16[28,640,256]{2,1,0:T(8,128)(2,1)S(1)} %shard_map.56.operator, ...), custom_call_target="tpu_custom_call" | custom-call | tf_op jit(solution)/shard_map/pallas_call | solution.py:297
  97.5 2.3 %collective-permute-start.11 = (f32[15,16,128]{2,1,0:T(8,128)S(1)}, f32[15,16,128]{2,1,0:T(8,128)S(1)}, u32[]{:S(2)}, u32[]{:S(2)}) collective-permute-start(f32[15,16,128]{2,1,0:T(8,128)S(1)} %get-tuple-element.39), channel_id=1, source_target_pairs={{0,1},{1,0},{2,3},{3,2},{4,5},{5,4},{6,7},{7,6},{8,9},{9,8},{10,11... | collective-permute-start | bytes 368648 | tf_op jit(solution)/shard_map/ppermute | solution.py:295
  99.8 2.2 %collective-permute-start.12 = (f32[15,16,128]{2,1,0:T(8,128)S(1)}, f32[15,16,128]{2,1,0:T(8,128)S(1)}, u32[]{:S(2)}, u32[]{:S(2)}) collective-permute-start(f32[15,16,128]{2,1,0:T(8,128)S(1)} %get-tuple-element.40), channel_id=1, source_target_pairs={{1,2},{3,4},{5,6},{7,8},{9,10},{11,12},{13,14},{15,16},{17,18},{19... | collective-permute-start | bytes 368648 | tf_op jit(solution)/shard_map/ppermute | solution.py:294
  102.0 5.4 %collective-permute-done.12.got_b = f32[15,16,128]{2,1,0:T(8,128)S(1)} collective-permute-done((f32[15,16,128]{2,1,0:T(8,128)S(1)}, f32[15,16,128]{2,1,0:T(8,128)S(1)}, u32[]{:S(2)}, u32[]{:S(2)}) %collective-permute-start.12) | collective-permute-done | bytes 122912 | tf_op jit(solution)/shard_map/ppermute | solution.py:294
  107.4 10.8 %shard_map.61.refs_0_ = f32[16,16,128]{2,1,0:T(8,128)S(1)} custom-call(s32[2]{0:T(128)S(1)} %pad_add_fusion.1.facts, s32[140]{0:T(256)S(1)} %reshape.198.offsets, bf16[28,640,256]{2,1,0:T(8,128)(2,1)S(1)} %shard_map.56.operator, f32[16,16,128]{2,1,0:T(8,128)S(1)} %get-tuple-element.36.x_in, f32[16,16,128]{2,1,0:T(8,128)S(1)} %get-tuple-element.37.u_in, ...), custom_call_target="tpu_custom_call" | custom-call | tf_op jit(solution)/shard_map/pallas_call | solution.py:297
  118.2 0.0 collective-permute-start.13
  118.2 0.6 collective-permute-start.14
  118.8 4.0 %collective-permute-done.13.refs_1_ = f32[16,16,128]{2,1,0:T(8,128)S(1)} collective-permute-done((f32[16,16,128]{2,1,0:T(8,128)S(1)}, f32[16,16,128]{2,1,0:T(8,128)S(1)}, u32[]{:S(2)}, u32[]{:S(2)}) %collective-permute-start.13) | collective-permute-done | bytes 131104 | tf_op jit(solution)/shard_map/ppermute | solution.py:212
  122.8 1.3 %collective-permute-start.15 = (f32[16,16,128]{2,1,0:T(8,128)S(1)}, f32[16,16,128]{2,1,0:T(8,128)S(1)}, u32[]{:S(2)}, u32[]{:S(2)}) collective-permute-start(f32[16,16,128]{2,1,0:T(8,128)S(1)} %collective-permute-done.13.refs_1_), channel_id=1, source_target_pairs={{0,1},{1,0},{2,3},{3,2},{4,5},{5,4},{6,7},{7,6},{8,9},{9,8},{10,11... | collective-permute-start | bytes 393224 | tf_op jit(solution)/shard_map/ppermute | solution.py:215
  124.1 1.3 %concatenate.35.facts = s32[6]{0:T(128)S(1)} concatenate(s32[1]{0:T(128)} %bitcast.3, s32[1]{0:T(128)} %bitcast.4, s32[1]{0:T(128)} %bitcast.5, s32[1]{0:T(128)} %bitcast.6, s32[1]{0:T(128)} %bitcast.7, s32[1]{0:T(128)} %bitcast.8), dimensions={0} | concatenate | bytes 48 | tf_op jit(solution)/shard_map/concatenate | solution.py:317
  125.5 2.0 %shard_map.62 = f32[16,4096]{1,0:T(8,128)} custom-call(s32[6]{0:T(128)S(1)} %concatenate.35.facts, f32[16,16,128]{2,1,0:T(8,128)S(1)} %shard_map.61.refs_0_, f32[16,16,128]{2,1,0:T(8,128)S(1)} %collective-permute-done.13.refs_1_, f32[16,16,128]{2,1,0:T(8,128)S(1)} %collective-permute-done.14.refs_2_, f32[16,16,128]{2,1,0:T(8,128)S(1)} %collective-permute-done.15.refs_3_), custom_call_target="tpu_custom_call" | custom-call | tf_op jit(solution)/shard_map/pallas_call | solution.py:318
  (18 shorter events, 0.1 us)
Async XLA Ops:
  3.0 42.9 %collective-permute-start.1 = (f32[6,5,128,128]{3,2,1,0:T(8,128)}, f32[6,5,128,128]{3,2,1,0:T(8,128)S(1)}, u32[]{:S(2)}, u32[]{:S(2)}) collective-permute-start(f32[6,5,128,128]{3,2,1,0:T(8,128)} %constant_dynamic-slice_fusion.4), channel_id=1, source_target_pairs={{0,4},{4,8},{8,12},{12,16},{16,20},{20,24},{24,28},{7,3},{11,7},{1... | collective-permute-start | bytes 5898248 | tf_op jit(solution)/shard_map/ppermute | solution.py:240
  4.9 15.2 %collective-permute-start.2 = (f32[2,16,4096]{2,1,0:T(8,128)S(1)}, f32[2,16,4096]{2,1,0:T(8,128)S(1)}, u32[]{:S(2)}, u32[]{:S(2)}) collective-permute-start(f32[2,16,4096]{2,1,0:T(8,128)S(1)} %pad_maximum_fusion.refs_0_), channel_id=1, source_target_pairs={{2,0},{3,1},{0,2},{1,3},{6,4},{7,5},{4,6},{5,7},{10,8},{11,9},{8,1... | collective-permute-start | bytes 1572872 | tf_op jit(solution)/shard_map/ppermute | solution.py:212
  8.4 30.8 %collective-permute-start.3 = (f32[2,16,4096]{2,1,0:T(8,128)S(1)}, f32[2,16,4096]{2,1,0:T(8,128)}, u32[]{:S(2)}, u32[]{:S(2)}) collective-permute-start(f32[2,16,4096]{2,1,0:T(8,128)S(1)} %pad_maximum_fusion.refs_0_), channel_id=1, source_target_pairs={{0,1},{1,0},{2,3},{3,2},{4,5},{5,4},{6,7},{7,6},{8,9},{9,8},{10,11... | collective-permute-start | bytes 1572872 | tf_op jit(solution)/shard_map/ppermute | solution.py:215
  9.2 36.4 %collective-permute-start = (s32[6,5]{0,1:T(8,128)S(1)}, s32[6,5]{0,1:T(8,128)S(1)}, u32[]{:S(2)}, u32[]{:S(2)}) collective-permute-start(s32[6,5]{0,1:T(8,128)S(1)} %constant_dynamic-slice_fusion.6), channel_id=1, source_target_pairs={{0,4},{4,8},{8,12},{12,16},{16,20},{20,24},{24,28},{7,3},{11,7},{1... | collective-permute-start | bytes 368 | tf_op jit(solution)/shard_map/ppermute | solution.py:241
  20.1 19.1 %collective-permute-start.4 = (f32[2,16,4096]{2,1,0:T(8,128)S(1)}, f32[2,16,4096]{2,1,0:T(8,128)}, u32[]{:S(2)}, u32[]{:S(2)}) collective-permute-start(f32[2,16,4096]{2,1,0:T(8,128)S(1)} %collective-permute-done.2.refs_1_), channel_id=1, source_target_pairs={{0,1},{1,0},{2,3},{3,2},{4,5},{5,4},{6,7},{7,6},{8,9},{9,8},{10,11... | collective-permute-start | bytes 1572872 | tf_op jit(solution)/shard_map/ppermute | solution.py:215
  35.6 3.5 %copy-start = (bf16[28,640,256]{2,1,0:T(8,128)(2,1)}, bf16[28,640,256]{2,1,0:T(8,128)(2,1)S(1)}, u32[]{:S(2)}) copy-start(bf16[28,640,256]{2,1,0:T(8,128)(2,1)S(1)} %shard_map.55.prepared) | copy-start | bytes 27525124
  41.7 8.4 %collective-permute-start.5 = (f32[15,16,128]{2,1,0:T(8,128)S(1)}, f32[15,16,128]{2,1,0:T(8,128)S(1)}, u32[]{:S(2)}, u32[]{:S(2)}) collective-permute-start(f32[15,16,128]{2,1,0:T(8,128)S(1)} %pad_maximum_fusion.1), channel_id=1, source_target_pairs={{0,1},{1,0},{2,3},{3,2},{4,5},{5,4},{6,7},{7,6},{8,9},{9,8},{10,11... | collective-permute-start | bytes 368648 | tf_op jit(solution)/shard_map/ppermute | solution.py:295
  41.8 8.3 %collective-permute-start.6 = (f32[15,16,128]{2,1,0:T(8,128)S(1)}, f32[15,16,128]{2,1,0:T(8,128)S(1)}, u32[]{:S(2)}, u32[]{:S(2)}) collective-permute-start(f32[15,16,128]{2,1,0:T(8,128)S(1)} %pad_maximum_fusion.2), channel_id=1, source_target_pairs={{1,2},{3,4},{5,6},{7,8},{9,10},{11,12},{13,14},{15,16},{17,18},{19... | collective-permute-start | bytes 368648 | tf_op jit(solution)/shard_map/ppermute | solution.py:294
  45.9 3.6 %copy-start.1 = (bf16[28,640,256]{2,1,0:T(8,128)(2,1)S(1)}, bf16[28,640,256]{2,1,0:T(8,128)(2,1)}, u32[]{:S(2)}) copy-start(bf16[28,640,256]{2,1,0:T(8,128)(2,1)} %copy-done) | copy-start | bytes 27525124
  60.9 3.5 %collective-permute-start.7 = (f32[15,16,128]{2,1,0:T(8,128)S(1)}, f32[15,16,128]{2,1,0:T(8,128)S(1)}, u32[]{:S(2)}, u32[]{:S(2)}) collective-permute-start(f32[15,16,128]{2,1,0:T(8,128)S(1)} %get-tuple-element.29), channel_id=1, source_target_pairs={{0,1},{1,0},{2,3},{3,2},{4,5},{5,4},{6,7},{7,6},{8,9},{9,8},{10,11... | collective-permute-start | bytes 368648 | tf_op jit(solution)/shard_map/ppermute | solution.py:295
  61.9 7.5 %collective-permute-start.8 = (f32[15,16,128]{2,1,0:T(8,128)S(1)}, f32[15,16,128]{2,1,0:T(8,128)S(1)}, u32[]{:S(2)}, u32[]{:S(2)}) collective-permute-start(f32[15,16,128]{2,1,0:T(8,128)S(1)} %get-tuple-element.30), channel_id=1, source_target_pairs={{1,2},{3,4},{5,6},{7,8},{9,10},{11,12},{13,14},{15,16},{17,18},{19... | collective-permute-start | bytes 368648 | tf_op jit(solution)/shard_map/ppermute | solution.py:294
  80.1 6.6 %collective-permute-start.10 = (f32[15,16,128]{2,1,0:T(8,128)S(1)}, f32[15,16,128]{2,1,0:T(8,128)S(1)}, u32[]{:S(2)}, u32[]{:S(2)}) collective-permute-start(f32[15,16,128]{2,1,0:T(8,128)S(1)} %get-tuple-element.35), channel_id=1, source_target_pairs={{1,2},{3,4},{5,6},{7,8},{9,10},{11,12},{13,14},{15,16},{17,18},{19... | collective-permute-start | bytes 368648 | tf_op jit(solution)/shard_map/ppermute | solution.py:294
  82.3 4.5 %collective-permute-start.9 = (f32[15,16,128]{2,1,0:T(8,128)S(1)}, f32[15,16,128]{2,1,0:T(8,128)S(1)}, u32[]{:S(2)}, u32[]{:S(2)}) collective-permute-start(f32[15,16,128]{2,1,0:T(8,128)S(1)} %get-tuple-element.34), channel_id=1, source_target_pairs={{0,1},{1,0},{2,3},{3,2},{4,5},{5,4},{6,7},{7,6},{8,9},{9,8},{10,11... | collective-permute-start | bytes 368648 | tf_op jit(solution)/shard_map/ppermute | solution.py:295
  97.5 4.4 %collective-permute-start.11 = (f32[15,16,128]{2,1,0:T(8,128)S(1)}, f32[15,16,128]{2,1,0:T(8,128)S(1)}, u32[]{:S(2)}, u32[]{:S(2)}) collective-permute-start(f32[15,16,128]{2,1,0:T(8,128)S(1)} %get-tuple-element.39), channel_id=1, source_target_pairs={{0,1},{1,0},{2,3},{3,2},{4,5},{5,4},{6,7},{7,6},{8,9},{9,8},{10,11... | collective-permute-start | bytes 368648 | tf_op jit(solution)/shard_map/ppermute | solution.py:295
  99.8 7.6 %collective-permute-start.12 = (f32[15,16,128]{2,1,0:T(8,128)S(1)}, f32[15,16,128]{2,1,0:T(8,128)S(1)}, u32[]{:S(2)}, u32[]{:S(2)}) collective-permute-start(f32[15,16,128]{2,1,0:T(8,128)S(1)} %get-tuple-element.40), channel_id=1, source_target_pairs={{1,2},{3,4},{5,6},{7,8},{9,10},{11,12},{13,14},{15,16},{17,18},{19... | collective-permute-start | bytes 368648 | tf_op jit(solution)/shard_map/ppermute | solution.py:294
  118.2 4.6 %collective-permute-start.13 = (f32[16,16,128]{2,1,0:T(8,128)S(1)}, f32[16,16,128]{2,1,0:T(8,128)S(1)}, u32[]{:S(2)}, u32[]{:S(2)}) collective-permute-start(f32[16,16,128]{2,1,0:T(8,128)S(1)} %shard_map.61.refs_0_), channel_id=1, source_target_pairs={{2,0},{3,1},{0,2},{1,3},{6,4},{7,5},{4,6},{5,7},{10,8},{11,9},{8,1... | collective-permute-start | bytes 393224 | tf_op jit(solution)/shard_map/ppermute | solution.py:212
  118.2 7.2 %collective-permute-start.14 = (f32[16,16,128]{2,1,0:T(8,128)S(1)}, f32[16,16,128]{2,1,0:T(8,128)S(1)}, u32[]{:S(2)}, u32[]{:S(2)}) collective-permute-start(f32[16,16,128]{2,1,0:T(8,128)S(1)} %shard_map.61.refs_0_), channel_id=1, source_target_pairs={{0,1},{1,0},{2,3},{3,2},{4,5},{5,4},{6,7},{7,6},{8,9},{9,8},{10,11... | collective-permute-start | bytes 393224 | tf_op jit(solution)/shard_map/ppermute | solution.py:215
  122.8 2.7 %collective-permute-start.15 = (f32[16,16,128]{2,1,0:T(8,128)S(1)}, f32[16,16,128]{2,1,0:T(8,128)S(1)}, u32[]{:S(2)}, u32[]{:S(2)}) collective-permute-start(f32[16,16,128]{2,1,0:T(8,128)S(1)} %collective-permute-done.13.refs_1_), channel_id=1, source_target_pairs={{0,1},{1,0},{2,3},{3,2},{4,5},{5,4},{6,7},{7,6},{8,9},{9,8},{10,11... | collective-permute-start | bytes 393224 | tf_op jit(solution)/shard_map/ppermute | solution.py:215

commit v2 on v1

v2 whole, which is shorter than its diff:
```python
import functools

import jax
import jax.numpy as jnp
from jax import lax
from jax.experimental import pallas as pl
from jax.experimental.pallas import tpu as pltpu
from jax.sharding import PartitionSpec as P

HB = 3
SWEEPS = 3
DEGREE = 4
APPLIES = SWEEPS * DEGREE

upper_bound = 4.5
lower_bound = 1.35

AXES = ("group", "fold")
F32 = jnp.float32
BF16 = jnp.bfloat16
VMEM = pl.BlockSpec(memory_space=pltpu.VMEM)
SMEM = pl.BlockSpec(memory_space=pltpu.SMEM)
ANY = pl.BlockSpec(memory_space=pl.ANY)


def coefficients():
    theta = (upper_bound + lower_bound) / 2.0
    delta = (upper_bound - lower_bound) / 2.0
    pairs = []
    for sweep in range(SWEEPS):
        pairs.append((0.0, 1.0 / theta))
        ratio = delta / theta
        for step in range(1, DEGREE):
            ratio_next = 1.0 / (2.0 * theta / delta - ratio)
            pairs.append((ratio_next * ratio, 2.0 * ratio_next / delta))
            ratio = ratio_next
    return pairs


def params(limit=40):
    return pltpu.CompilerParams(vmem_limit_bytes=limit * 2**20)


def split(value):
    high = value.astype(BF16)
    return high, (value - high.astype(F32)).astype(BF16)


def pick_lanes(window, low, shift):
    lane = lax.broadcasted_iota(jnp.int32, (16, 128), 1)
    turn = (128 - shift) % 128
    first = pltpu.roll(window(low), turn, 1)
    second = pltpu.roll(window(low + 1), turn, 1)
    return jnp.where(lane < 128 - shift, first, second)


def put_payloads(ob, steps, even, u, at, r, pay_a, pay_b):
    h = HB * steps
    inner = h - HB
    for pay, right in ((pay_a, even), (pay_b, jnp.logical_not(even))):
        pay[:h] = u[pl.ds(at + jnp.where(right, ob - h, 0), h)]
        if inner:
            pay[h:] = r[pl.ds(at + jnp.where(right, ob - inner, 0), inner)]


def begin_of(counts, j):
    total = 0
    for i in range(counts.shape[1]):
        total = total + jnp.where(i < j, counts[0, i], 0)
    return total


def holder(fold, folds, d, c):
    return jax.lax.rem(fold // 2 + d, folds // 2) * 2 + jnp.where(c, 1 - fold % 2, fold % 2)


def align_kernel(ob, steps, keys, facts, counts, *refs):
    sources, (x_out, u_out, r_out, pay_a, pay_b) = refs[:-5], refs[-5:]
    capacity = sources[0].shape[-1]
    folds = len(keys)
    lane = lax.broadcasted_iota(jnp.int32, (16, 128), 1)
    base = facts[0] * (ob * 128)
    x_out[...] = jnp.zeros_like(x_out)
    spans = []
    for d, c in keys:
        j = holder(facts[0], folds, d, c)
        spans.append((begin_of(counts, j), counts[0, j]))

    def block(e, carry):
        row = base + e * 128
        totals = [jnp.zeros((16, 128), F32), jnp.zeros((16, 128), F32)]
        for j, (start, count) in enumerate(spans):
            at = row - start
            low = at >> 7
            shift = at & 127
            index = at + lane
            valid = (index >= 0) & (index < count)
            for a in range(2):

                def window(b, source=sources[2 * j + a]):
                    b = jnp.clip(b, 0, capacity // 128 - 1)
                    return source[:, pl.ds(pl.multiple_of(b * 128, 128), 128)]

                totals[a] = jnp.where(valid, pick_lanes(window, low, shift), totals[a])
        u_out[e] = totals[0]
        r_out[e] = totals[1]
        return carry

    lax.fori_loop(0, ob, block, 0, unroll=2)
    put_payloads(ob, steps, facts[1] == 0, u_out, 0, r_out, pay_a, pay_b)


def prepare_kernel(ob, halo, facts, blocks, out, token, raw, sem):
    own, width, side = blocks.shape[0], blocks.shape[1], blocks.shape[2]
    rows = ob + 2 * halo
    first = facts[0] * ob - halo

    def copy(a):
        return pltpu.make_async_copy(blocks.at[jnp.clip(first + a, 0, own - 1)], raw.at[a], sem.at[a])

    for a in range(rows):
        copy(a).start()
    group = 4 if rows % 4 == 0 else 2

    def several(g, carry):
        for s in range(group):
            a = g * group + s
            copy(a).wait()
            for k in range(width):
                high, low = split(raw[a, k])
                out[a, k * side : (k + 1) * side, :side] = high.T
                out[a, k * side : (k + 1) * side, side:] = low.T
        return carry

    lax.fori_loop(0, rows // group, several, 0)
    token[...] = jnp.zeros_like(token)


def border_kernel(ob, folds, halo, piece, facts, prepared, raw, out):
    del prepared
    fold = facts[0]
    count, width, side = raw.shape[0], raw.shape[1], raw.shape[2]

    @pl.when((fold == 0) | (fold == folds - 1))
    def _():
        first = jnp.where(fold == 0, halo - count * (piece + 1), halo + ob + count * piece)
        for a in range(count):
            for k in range(width):
                high, low = split(raw[a, k])
                out[first + a, k * side : (k + 1) * side, :side] = high.T
                out[first + a, k * side : (k + 1) * side, side:] = low.T


def phase_kernel(ob, halo, steps, after, pairs, facts, offsets, operator, x_in, u_in, r_in, got_a, got_b, *refs):
    h = HB * steps
    inner = h - HB
    extent = ob + 2 * h
    width = offsets.shape[0] // (ob + 2 * halo)
    if after:
        x_out, u_out, r_out, pay_a, pay_b, u, r, *pieces = refs
    else:
        x_out, u, r, *pieces = refs
    even = facts[1] == 0
    for got, right in ((got_a, even), (got_b, jnp.logical_not(even))):
        u[pl.ds(jnp.where(right, h + ob, 0), h)] = got[:h]
        if inner:
            r[pl.ds(jnp.where(right, h + ob, HB), inner)] = got[h:]
    u[h : h + ob] = u_in[...]
    r[h : h + ob] = r_in[...]
    high, low = split(u[...])
    pieces[0][:, :16] = high
    pieces[0][:, 16:] = low
    x = x_in[...]
    for t in range(steps):
        x = x + u[h : h + ob]
        now, later = pieces[t % 2], pieces[(t + 1) % 2]
        old, new = pairs[t]
        done = t == steps - 1

        def row(e, carry):
            a = e - h + halo
            left = jnp.concatenate([now[e + offsets[a * width + k]] for k in range(width)], axis=1)
            product = jnp.dot(left, operator[a], preferred_element_type=F32)
            product = product[:16] + product[16:]
            resid = r[e] - (product[:, :128] + product[:, 128:])
            r[e] = resid
            update = new * resid if old == 0.0 else old * u[e] + new * resid
            u[e] = update
            if not done:
                first, second = split(update)
                later[e, :16] = first
                later[e, 16:] = second
            return carry

        lower, upper = HB * (t + 1), extent - HB * (t + 1)
        lax.fori_loop(lower, upper, row, 0, unroll=True)
    if not after:
        x_out[...] = x + u[h : h + ob]
        return
    x_out[...] = x
    u_out[...] = u[h : h + ob]
    r_out[...] = r[h : h + ob]
    put_payloads(ob, after, even, u, h, r, pay_a, pay_b)


def finish_kernel(ob, keys, facts, counts, *refs):
    parts, (out, whole) = refs[:-2], refs[-2:]
    total = whole.shape[0]
    for (d, c), part in zip(keys, parts):
        whole[pl.ds(holder(facts[0], len(keys), d, c) * ob, ob)] = part[...]
    start, count = begin_of(counts, facts[0]), counts[0, facts[0]]
    lane = lax.broadcasted_iota(jnp.int32, (16, 128), 1)
    low, shift = start >> 7, start & 127

    def block(b, carry):
        piece = pick_lanes(lambda i: whole[jnp.minimum(i, total - 1)], low + b, shift)
        piece = jnp.where(b * 128 + lane < count, piece, 0.0)
        out[:, pl.ds(pl.multiple_of(b * 128, 128), 128)] = piece
        return carry

    lax.fori_loop(0, out.shape[1] // 128, block, 0, unroll=8)


def over_chips(array, d, folds):
    return lax.ppermute(array, "fold", [((i + 2 * d) % folds, i) for i in range(folds)])


def other_core(array, folds):
    return lax.ppermute(array, "fold", [(i, i ^ 1) for i in range(folds)])


def on_device(right_side, initial, counts, columns, blocks):
    groups, folds = lax.axis_size("group"), lax.axis_size("fold")
    vectors, capacity = right_side.shape
    own, width, side = blocks.shape[0], blocks.shape[1], blocks.shape[2]
    ob = own // folds
    plan = [2, 3, 3, 4] if ob >= 12 else [2] * 6
    halo = HB * (max(plan) - 1)
    rows = ob + 2 * halo
    pairs = coefficients()
    fold = lax.axis_index("fold")
    me = lax.axis_index("group") * folds + fold
    devices = groups * folds
    facts = jnp.stack([fold, me % 2]).astype(jnp.int32)
    state = jax.ShapeDtypeStruct((ob, vectors, side), F32)

    def payload(steps):
        return jax.ShapeDtypeStruct((2 * HB * steps - HB, vectors, side), F32)

    near = (initial, right_side)
    far = [tuple(over_chips(array, d, folds) for array in near) for d in range(1, folds // 2)]

    last_fold = folds - 1
    border_perm = [(g * folds, (g + 1) * folds) for g in range(groups - 1)]
    border_perm += [((g + 1) * folds + last_fold, g * folds + last_fold) for g in range(groups - 1)]
    to_right = fold == 0
    borders = []
    for piece in range(halo // HB):
        at = jnp.where(to_right, own - HB * (piece + 1), HB * piece)
        borders.append(lax.ppermute(lax.dynamic_slice_in_dim(blocks, at, HB, 0), AXES, border_perm))
    relative = columns - (jnp.arange(own, dtype=jnp.int32)[:, None] + HB)
    outward = lax.dynamic_slice_in_dim(relative, jnp.where(to_right, own - halo, 0), halo, 0)
    outward = lax.ppermute(outward, AXES, border_perm)
    around = jnp.concatenate([outward, relative, outward], axis=0)
    offsets = lax.dynamic_slice_in_dim(around, fold * ob, rows, 0).reshape(-1)

    operator, token = pl.pallas_call(
        functools.partial(prepare_kernel, ob, halo),
        out_shape=(pltpu.VMEM((rows, width * side, 2 * side), BF16), jax.ShapeDtypeStruct((8, 128), F32)),
        in_specs=[SMEM, ANY],
        out_specs=(VMEM, VMEM),
        scratch_shapes=[pltpu.VMEM((rows, width, side, side), F32), pltpu.SemaphoreType.DMA((rows,))],
        compiler_params=params(),
        cost_estimate=pl.CostEstimate(flops=10**7, bytes_accessed=2 * rows * width * side * side * 4, transcendentals=0),
    )(facts, blocks)
    far, _ = lax.optimization_barrier((far, token))

    keys, arrays = [], []
    for d, pair in enumerate([near, *far]):
        keys += [(d, False), (d, True)]
        arrays += [*pair, *(other_core(array, folds) for array in pair)]
    x, u, r, pay_a, pay_b = pl.pallas_call(
        functools.partial(align_kernel, ob, plan[0], keys),
        out_shape=(state, state, state, payload(plan[0]), payload(plan[0])),
        in_specs=[SMEM, SMEM] + [VMEM] * (2 * folds),
        out_specs=(VMEM,) * 5,
        compiler_params=params(),
    )(facts, counts, *arrays)

    def with_border(operator, piece):
        return pl.pallas_call(
            functools.partial(border_kernel, ob, folds, halo, piece),
            out_shape=pltpu.VMEM((rows, width * side, 2 * side), BF16),
            in_specs=[SMEM, VMEM, VMEM],
            out_specs=VMEM,
            input_output_aliases={1: 0},
            compiler_params=params(),
        )(facts, pltpu.with_memory_space_constraint(operator, pltpu.VMEM), borders[piece])

    swap_a = [(i, i ^ 1) for i in range(devices)]
    swap_b = [(i, i + 1) for i in range(1, devices - 1, 2)]
    swap_b += [(j, i) for i, j in swap_b]
    there, done = 0, 0
    for phase, steps in enumerate(plan):
        got_b = lax.ppermute(pay_b, AXES, swap_b)
        got_a = lax.ppermute(pay_a, AXES, swap_a)
        while there < steps - 1:
            operator = with_border(operator, there)
            there += 1
        after = plan[phase + 1] if phase + 1 < len(plan) else 0
        outs = pl.pallas_call(
            functools.partial(phase_kernel, ob, halo, steps, after, pairs[done : done + steps]),
            out_shape=(state, state, state, payload(after), payload(after)) if after else state,
            in_specs=[SMEM, SMEM] + [VMEM] * 6,
            out_specs=(VMEM,) * 5 if after else VMEM,
            scratch_shapes=[
                pltpu.VMEM((ob + 2 * HB * steps, vectors, side), F32),
                pltpu.VMEM((ob + 2 * HB * steps, vectors, side), F32),
                pltpu.VMEM((ob + 2 * HB * steps, 2 * vectors, side), BF16),
                pltpu.VMEM((ob + 2 * HB * steps, 2 * vectors, side), BF16),
            ],
            compiler_params=params(),
        )(facts, offsets, pltpu.with_memory_space_constraint(operator, pltpu.VMEM), x, u, r, got_a, got_b)
        done += steps
        if after:
            x, u, r, pay_a, pay_b = outs
        else:
            x = outs

    parts = []
    for d in range(folds // 2):
        part = over_chips(x, d, folds) if d else x
        parts += [part, other_core(part, folds)]
    return pl.pallas_call(
        functools.partial(finish_kernel, ob, keys),
        out_shape=jax.ShapeDtypeStruct((vectors, capacity), F32),
        in_specs=[SMEM, SMEM] + [VMEM] * folds,
        out_specs=VMEM,
        scratch_shapes=[pltpu.VMEM((own, vectors, side), F32)],
        compiler_params=params(),
    )(facts, counts, *parts)


def solution(mesh):
    placed = (
        P(None, AXES),
        P(None, AXES),
        P("group", None),
        P("group", None),
        P("group", None, None, None),
    )
    return jax.shard_map(on_device, mesh=mesh, in_specs=placed, out_specs=P(None, AXES), check_vma=False)
```

time: 128 us -> 118 us (0.922)
  Pallas kernels: 59 us -> 31.7 us
  starting transfers between devices: 24.7 us -> 52 us
  waiting for transfers between devices: 25.4 us -> 15.6 us
  local copies, waits for them, and re-layouts: 13.8 us -> 17.5 us
  other arithmetic: 4.3 us -> 0.85 us
    pallas_call x8 -> x10, Pallas kernels: 59 us -> 31.7 us  [the longest x4 18 us: on_device(): pl.pallas_call(functools.partial(phase_kernel, ob, halo, steps, after, pa...]
    ppermute x8 -> x13, starting transfers between devices: 8.06 us -> 32.8 us  [the longest x6 24.3 us: other_core(): return lax.ppermute(array, 'fold', [(i, i ^ 1) for i in range(folds)])]
    ppermute x8 -> x13, waiting for transfers between devices: 13.3 us -> 4.79 us  [the longest x3 3.79 us: over_chips(): lax.ppermute(array, 'fold', [((i + 2 * d) % folds, i) for i in range(fold...]
    unnamed x4 -> x38, local copies, waits for them, and re-layouts: 7.13 us -> 13.5 us
    ppermute x4, starting transfers between devices: 10.4 us -> 14.5 us  [on_device(): got_b = lax.ppermute(pay_b, AXES, swap_b)]
    gather x2 -> x0, local copies, waits for them, and re-layouts: 1.93 us -> none  [the longest x1 1.29 us: on_device(): live[order]]
    another operation x2 -> x0, other arithmetic: 1.9 us -> none  [the longest x1 1.07 us: on_device(): stacked = jnp.stack([right_side, initial])]
    ppermute x4, starting transfers between devices: 6.23 us -> 4.75 us  [on_device(): got_a = lax.ppermute(pay_a, AXES, swap_a)]
  transfers between devices with their start and end apart: 16 -> 21, of which waited for: 5 -> 5; matrix products, arithmetic and copies ran while one was open for 6% -> 1% of each run, Pallas kernels for 11% -> 20%
where the time goes in v2:
time: 118 us
  starting transfers between devices  52 us (44%)
  Pallas kernels  31.7 us (27%)
  local copies, waits for them, and re-layouts  17.5 us (15%)
  waiting for transfers between devices  15.6 us (13%)
    ppermute x6, starting transfers between devices, other_core(): return lax.ppermute(array, 'fold', [(i, i ^ 1) for i in range(folds)])  24.3 us
    pallas_call x4, Pallas kernels, on_device(): pl.pallas_call(functools.partial(phase_kernel, ob, halo, steps, after, pa...  18 us
    ppermute x4, starting transfers between devices, on_device(): got_b = lax.ppermute(pay_b, AXES, swap_b)  14.5 us
    unnamed x38, local copies, waits for them, and re-layouts  13.5 us
    ppermute x4, waiting for transfers between devices, on_device(): got_b = lax.ppermute(pay_b, AXES, swap_b)  10.8 us
    pallas_call x1, Pallas kernels, on_device(): pl.pallas_call(functools.partial(prepare_kernel, ob, halo), out_shape=(pl...  7.27 us
    ppermute x3, starting transfers between devices, over_chips(): lax.ppermute(array, 'fold', [((i + 2 * d) % folds, i) for i in range(fold...  5.55 us
    ppermute x4, starting transfers between devices, on_device(): got_a = lax.ppermute(pay_a, AXES, swap_a)  4.75 us
  transfers between devices with their start and end apart: 21, of which 5 were waited for; matrix products, arithmetic and copies ran while one was open for 1% of the time, Pallas kernels for 20%

profile of v2, /device:TPU:9, one launch (start us, length us, event | category | flops | bytes accessed | tf_op | source)
XLA Modules:
  0.0 118.0 jit_solution(4368723989105269564)
XLA Ops:
  0.0 3.6 %constant_dynamic-slice_fusion = (f32[3,5,128,128]{3,2,1,0:T(8,128)}, f32[3,5,128,128]{3,2,1,0:T(8,128)}, f32[3,5,128,128]{3,2,1,0:T(8,128)}) fusion(f32[64,5,128,128]{3,2,1,0:T(8,128)} %blocks.1, s32[]{:T(128)S(6)} %select_n.32, s32[]{:T(128)S(6)} %select_n.30, s32[]{:T(128)S(6)} %select_n.31), kind=kLoop, calls=%fused_computation.2 | loop fusion | bytes 5898252 | tf_op jit(solution)/shard_map/dynamic_slice | solution.py:260
  3.6 0.9 collective-permute-start.1
  4.5 3.6 %collective-permute-start.6 = (f32[16,4096]{1,0:T(8,128)}, f32[16,4096]{1,0:T(8,128)S(1)}, u32[]{:S(2)}, u32[]{:S(2)}) collective-permute-start(f32[16,4096]{1,0:T(8,128)} %refs_0_.1), channel_id=1, source_target_pairs={{2,0},{3,1},{0,2},{1,3},{6,4},{7,5},{4,6},{5,7},{10,8},{11,9},{8,1... | collective-permute-start | bytes 786440 | tf_op jit(solution)/shard_map/ppermute | solution.py:225
  8.0 0.1 collective-permute-start.7
  8.1 0.7 collective-permute-start.2
  8.8 0.7 broadcast_subtract_fusion
  9.6 0.6 collective-permute-start
  10.3 21.8 %collective-permute-start.4 = (f32[16,4096]{1,0:T(8,128)}, f32[16,4096]{1,0:T(8,128)S(1)}, u32[]{:S(2)}, u32[]{:S(2)}) collective-permute-start(f32[16,4096]{1,0:T(8,128)} %refs_0_.1), channel_id=1, source_target_pairs={{0,1},{1,0},{2,3},{3,2},{4,5},{5,4},{6,7},{7,6},{8,9},{9,8},{10,11... | collective-permute-start | bytes 786440 | tf_op jit(solution)/shard_map/ppermute | solution.py:229
  32.2 0.6 copy-done.4
  32.8 0.7 copy-done.6
  33.5 0.7 collective-permute-start.3
  34.2 0.7 copy-done.8
  34.9 1.8 %collective-permute-start.8 = (f32[16,4096]{1,0:T(8,128)}, f32[16,4096]{1,0:T(8,128)}, u32[]{:S(2)}, u32[]{:S(2)}) collective-permute-start(f32[16,4096]{1,0:T(8,128)} %copy-done.4), channel_id=1, source_target_pairs={{0,1},{1,0},{2,3},{3,2},{4,5},{5,4},{6,7},{7,6},{8,9},{9,8},{10,11... | collective-permute-start | bytes 786440 | tf_op jit(solution)/shard_map/ppermute | solution.py:229
  36.7 0.7 copy-done.10
  37.5 0.1 pad_add_fusion.1.facts
  37.5 7.3 %shard_map.55 = (bf16[34,640,256]{2,1,0:T(8,128)(2,1)S(1)}, f32[8,128]{1,0:T(8,128)}) custom-call(s32[2]{0:T(128)S(1)} %pad_add_fusion.1.facts, f32[64,5,128,128]{3,2,1,0:T(8,128)} %blocks.1), custom_call_target="tpu_custom_call" | custom-call | flops 10000000 | bytes 22282240 | tf_op jit(solution)/shard_map/pallas_call | solution.py:267
  44.8 4.2 %copy-done = bf16[34,640,256]{2,1,0:T(8,128)(2,1)} copy-done((bf16[34,640,256]{2,1,0:T(8,128)(2,1)}, bf16[34,640,256]{2,1,0:T(8,128)(2,1)S(1)}, u32[]{:S(2)}) %copy-start) | copy-done | bytes 11141144
  49.2 2.9 %shard_map.59 = (f32[16,16,128]{2,1,0:T(8,128)S(1)}, f32[16,16,128]{2,1,0:T(8,128)S(1)}, f32[16,16,128]{2,1,0:T(8,128)S(1)}, f32[9,16,128]{2,1,0:T(8,128)}, f32[9,16,128]{2,1,0:T(8,128)S(1)}) custom-call(s32[2]{0:T(128)S(1)} %pad_add_fusion.1.facts, s32[1,4]{1,0:T(1,128)S(1)} %copy-done.18, f32[16,4096]{1,0:T(8,128)S(1)} %copy-done.2, ...), custom_call_target="tpu_custom_call" | custom-call | tf_op jit(solution)/shard_map/pallas_call | solution.py:282
  52.1 0.7 copy-done.12
  52.7 0.7 copy-done.14
  53.4 0.6 copy-done.16
  54.0 3.1 %collective-permute-start.10 = (f32[9,16,128]{2,1,0:T(8,128)}, f32[9,16,128]{2,1,0:T(8,128)S(1)}, u32[]{:S(2)}, u32[]{:S(2)}) collective-permute-start(f32[9,16,128]{2,1,0:T(8,128)} %get-tuple-element.34), channel_id=1, source_target_pairs={{0,1},{1,0},{2,3},{3,2},{4,5},{5,4},{6,7},{7,6},{8,9},{9,8},{10,11... | collective-permute-start | bytes 221192 | tf_op jit(solution)/shard_map/ppermute | solution.py:306
  57.1 1.9 %collective-permute-start.11 = (f32[9,16,128]{2,1,0:T(8,128)S(1)}, f32[9,16,128]{2,1,0:T(8,128)S(1)}, u32[]{:S(2)}, u32[]{:S(2)}) collective-permute-start(f32[9,16,128]{2,1,0:T(8,128)S(1)} %get-tuple-element.35), channel_id=1, source_target_pairs={{1,2},{3,4},{5,6},{7,8},{9,10},{11,12},{13,14},{15,16},{17,18},{19... | collective-permute-start | bytes 221192 | tf_op jit(solution)/shard_map/ppermute | solution.py:305
  59.0 0.1 constant_dynamic-slice_fusion.3
  59.1 0.1 copy.9
  59.2 0.1 reshape.8.offsets
  59.3 4.2 %copy-done.1 = bf16[34,640,256]{2,1,0:T(8,128)(2,1)S(1)} copy-done((bf16[34,640,256]{2,1,0:T(8,128)(2,1)S(1)}, bf16[34,640,256]{2,1,0:T(8,128)(2,1)}, u32[]{:S(2)}) %copy-start.1) | copy-done | bytes 11141144
  63.5 0.5 shard_map.56.prepared.operator
  64.1 0.3 copy-done.13
  64.5 2.8 %shard_map.60 = (f32[16,16,128]{2,1,0:T(8,128)S(1)}, f32[16,16,128]{2,1,0:T(8,128)S(1)}, f32[16,16,128]{2,1,0:T(8,128)S(1)}, f32[15,16,128]{2,1,0:T(8,128)S(1)}, f32[15,16,128]{2,1,0:T(8,128)S(1)}) custom-call(s32[2]{0:T(128)S(1)} %pad_add_fusion.1.facts, s32[170]{0:T(256)S(1)} %reshape.8.offsets, bf16[34,640,256]{2,1,0:T(8,128)(2,1)S(1)} %shard_map.56.prepared.operator, ...), custom_call_target="tpu_custom_call" | custom-call | tf_op jit(solution)/shard_map/pallas_call | solution.py:311
  67.3 0.1 collective-permute-start.12
  67.5 5.4 %collective-permute-start.13 = (f32[15,16,128]{2,1,0:T(8,128)S(1)}, f32[15,16,128]{2,1,0:T(8,128)S(1)}, u32[]{:S(2)}, u32[]{:S(2)}) collective-permute-start(f32[15,16,128]{2,1,0:T(8,128)S(1)} %get-tuple-element.40), channel_id=1, source_target_pairs={{1,2},{3,4},{5,6},{7,8},{9,10},{11,12},{13,14},{15,16},{17,18},{19... | collective-permute-start | bytes 368648 | tf_op jit(solution)/shard_map/ppermute | solution.py:305
  72.9 0.6 shard_map.57.prepared.operator
  73.5 3.1 %collective-permute-done.13.got_b = f32[15,16,128]{2,1,0:T(8,128)S(1)} collective-permute-done((f32[15,16,128]{2,1,0:T(8,128)S(1)}, f32[15,16,128]{2,1,0:T(8,128)S(1)}, u32[]{:S(2)}, u32[]{:S(2)}) %collective-permute-start.13) | collective-permute-done | bytes 122912 | tf_op jit(solution)/shard_map/ppermute | solution.py:305
  76.6 4.4 %shard_map.61 = (f32[16,16,128]{2,1,0:T(8,128)S(1)}, f32[16,16,128]{2,1,0:T(8,128)S(1)}, f32[16,16,128]{2,1,0:T(8,128)S(1)}, f32[15,16,128]{2,1,0:T(8,128)S(1)}, f32[15,16,128]{2,1,0:T(8,128)S(1)}) custom-call(s32[2]{0:T(128)S(1)} %pad_add_fusion.1.facts, s32[170]{0:T(256)S(1)} %reshape.8.offsets, bf16[34,640,256]{2,1,0:T(8,128)(2,1)S(1)} %shard_map.57.prepared.operator, ...), custom_call_target="tpu_custom_call" | custom-call | tf_op jit(solution)/shard_map/pallas_call | solution.py:311
  81.1 3.7 %collective-permute-start.15 = (f32[15,16,128]{2,1,0:T(8,128)S(1)}, f32[15,16,128]{2,1,0:T(8,128)S(1)}, u32[]{:S(2)}, u32[]{:S(2)}) collective-permute-start(f32[15,16,128]{2,1,0:T(8,128)S(1)} %get-tuple-element.45), channel_id=1, source_target_pairs={{1,2},{3,4},{5,6},{7,8},{9,10},{11,12},{13,14},{15,16},{17,18},{19... | collective-permute-start | bytes 368648 | tf_op jit(solution)/shard_map/ppermute | solution.py:305
  84.8 3.5 %collective-permute-done.15.got_b = f32[15,16,128]{2,1,0:T(8,128)S(1)} collective-permute-done((f32[15,16,128]{2,1,0:T(8,128)S(1)}, f32[15,16,128]{2,1,0:T(8,128)S(1)}, u32[]{:S(2)}, u32[]{:S(2)}) %collective-permute-start.15) | collective-permute-done | bytes 122912 | tf_op jit(solution)/shard_map/ppermute | solution.py:305
  88.3 4.4 %shard_map.62 = (f32[16,16,128]{2,1,0:T(8,128)S(1)}, f32[16,16,128]{2,1,0:T(8,128)S(1)}, f32[16,16,128]{2,1,0:T(8,128)S(1)}, f32[21,16,128]{2,1,0:T(8,128)S(1)}, f32[21,16,128]{2,1,0:T(8,128)S(1)}) custom-call(s32[2]{0:T(128)S(1)} %pad_add_fusion.1.facts, s32[170]{0:T(256)S(1)} %reshape.8.offsets, bf16[34,640,256]{2,1,0:T(8,128)(2,1)S(1)} %shard_map.57.prepared.operator, ...), custom_call_target="tpu_custom_call" | custom-call | tf_op jit(solution)/shard_map/pallas_call | solution.py:311
  92.7 1.5 %collective-permute-start.16 = (f32[21,16,128]{2,1,0:T(8,128)S(1)}, f32[21,16,128]{2,1,0:T(8,128)S(1)}, u32[]{:S(2)}, u32[]{:S(2)}) collective-permute-start(f32[21,16,128]{2,1,0:T(8,128)S(1)} %get-tuple-element.49), channel_id=1, source_target_pairs={{0,1},{1,0},{2,3},{3,2},{4,5},{5,4},{6,7},{7,6},{8,9},{9,8},{10,11... | collective-permute-start | bytes 516104 | tf_op jit(solution)/shard_map/ppermute | solution.py:306
  94.2 3.5 %collective-permute-start.17 = (f32[21,16,128]{2,1,0:T(8,128)S(1)}, f32[21,16,128]{2,1,0:T(8,128)S(1)}, u32[]{:S(2)}, u32[]{:S(2)}) collective-permute-start(f32[21,16,128]{2,1,0:T(8,128)S(1)} %get-tuple-element.50), channel_id=1, source_target_pairs={{1,2},{3,4},{5,6},{7,8},{9,10},{11,12},{13,14},{15,16},{17,18},{19... | collective-permute-start | bytes 516104 | tf_op jit(solution)/shard_map/ppermute | solution.py:305
  97.7 0.7 shard_map.58.operator
  98.4 4.2 %collective-permute-done.17.got_b = f32[21,16,128]{2,1,0:T(8,128)S(1)} collective-permute-done((f32[21,16,128]{2,1,0:T(8,128)S(1)}, f32[21,16,128]{2,1,0:T(8,128)S(1)}, u32[]{:S(2)}, u32[]{:S(2)}) %collective-permute-start.17) | collective-permute-done | bytes 172064 | tf_op jit(solution)/shard_map/ppermute | solution.py:305
  102.6 6.3 %shard_map.63.refs_0_ = f32[16,16,128]{2,1,0:T(8,128)S(1)} custom-call(s32[2]{0:T(128)S(1)} %pad_add_fusion.1.facts, s32[170]{0:T(256)S(1)} %reshape.8.offsets, bf16[34,640,256]{2,1,0:T(8,128)(2,1)S(1)} %shard_map.58.operator, f32[16,16,128]{2,1,0:T(8,128)S(1)} %get-tuple-element.46.x_in, f32[16,16,128]{2,1,0:T(8,128)S(1)} %get-tuple-element.47.u_in, ...), custom_call_target="tpu_custom_call" | custom-call | tf_op jit(solution)/shard_map/pallas_call | solution.py:311
  108.9 1.9 %collective-permute-start.19 = (f32[16,16,128]{2,1,0:T(8,128)S(1)}, f32[16,16,128]{2,1,0:T(8,128)S(1)}, u32[]{:S(2)}, u32[]{:S(2)}) collective-permute-start(f32[16,16,128]{2,1,0:T(8,128)S(1)} %shard_map.63.refs_0_), channel_id=1, source_target_pairs={{2,0},{3,1},{0,2},{1,3},{6,4},{7,5},{4,6},{5,7},{10,8},{11,9},{8,1... | collective-permute-start | bytes 393224 | tf_op jit(solution)/shard_map/ppermute | solution.py:225
  110.8 3.8 %collective-permute-done.19.refs_2_ = f32[16,16,128]{2,1,0:T(8,128)S(1)} collective-permute-done((f32[16,16,128]{2,1,0:T(8,128)S(1)}, f32[16,16,128]{2,1,0:T(8,128)S(1)}, u32[]{:S(2)}, u32[]{:S(2)}) %collective-permute-start.19) | collective-permute-done | bytes 131104 | tf_op jit(solution)/shard_map/ppermute | solution.py:225
  114.6 0.7 collective-permute-start.20
  115.3 1.0 collective-permute-done.20.refs_3_
  116.3 1.7 %shard_map.64 = f32[16,4096]{1,0:T(8,128)} custom-call(s32[2]{0:T(128)S(1)} %pad_add_fusion.1.facts, s32[1,4]{1,0:T(1,128)S(1)} %copy-done.18, f32[16,16,128]{2,1,0:T(8,128)S(1)} %shard_map.63.refs_0_, f32[16,16,128]{2,1,0:T(8,128)S(1)} %collective-permute-done.18.refs_1_, f32[16,16,128]{2,1,0:T(8,128)S(1)} %collective-permute-done.19.refs_2_, ...), custom_call_target="tpu_custom_call" | custom-call | tf_op jit(solution)/shard_map/pallas_call | solution.py:334
  (51 shorter events, 0.5 us)
Async XLA Ops:
  3.6 45.5 %copy-start.2 = (f32[16,4096]{1,0:T(8,128)S(1)}, f32[16,4096]{1,0:T(8,128)}, u32[]{:S(2)}) copy-start(f32[16,4096]{1,0:T(8,128)} %refs_0_.1) | copy-start | bytes 786436
  3.6 45.5 %copy-start.3 = (f32[16,4096]{1,0:T(8,128)S(1)}, f32[16,4096]{1,0:T(8,128)}, u32[]{:S(2)}) copy-start(f32[16,4096]{1,0:T(8,128)} %refs_1_.1) | copy-start | bytes 786436
  3.6 45.5 %copy-start.18 = (s32[1,4]{1,0:T(1,128)S(1)}, s32[1,4]{1,0:T(1,128)}, u32[]{:S(2)}) copy-start(s32[1,4]{1,0:T(1,128)} %counts.3) | copy-start | bytes 52
  3.6 55.7 %collective-permute-start.1 = (f32[3,5,128,128]{3,2,1,0:T(8,128)}, f32[3,5,128,128]{3,2,1,0:T(8,128)S(1)}, u32[]{:S(2)}, u32[]{:S(2)}) collective-permute-start(f32[3,5,128,128]{3,2,1,0:T(8,128)} %get-tuple-element.52), channel_id=1, source_target_pairs={{0,4},{4,8},{8,12},{12,16},{16,20},{20,24},{24,28},{7,3},{11,7},{1... | collective-permute-start | bytes 2949128 | tf_op jit(solution)/shard_map/ppermute | solution.py:260
  4.5 27.6 %collective-permute-start.6 = (f32[16,4096]{1,0:T(8,128)}, f32[16,4096]{1,0:T(8,128)S(1)}, u32[]{:S(2)}, u32[]{:S(2)}) collective-permute-start(f32[16,4096]{1,0:T(8,128)} %refs_0_.1), channel_id=1, source_target_pairs={{2,0},{3,1},{0,2},{1,3},{6,4},{7,5},{4,6},{5,7},{10,8},{11,9},{8,1... | collective-permute-start | bytes 786440 | tf_op jit(solution)/shard_map/ppermute | solution.py:225
  8.0 24.1 %collective-permute-start.7 = (f32[16,4096]{1,0:T(8,128)}, f32[16,4096]{1,0:T(8,128)S(1)}, u32[]{:S(2)}, u32[]{:S(2)}) collective-permute-start(f32[16,4096]{1,0:T(8,128)} %refs_1_.1), channel_id=1, source_target_pairs={{2,0},{3,1},{0,2},{1,3},{6,4},{7,5},{4,6},{5,7},{10,8},{11,9},{8,1... | collective-permute-start | bytes 786440 | tf_op jit(solution)/shard_map/ppermute | solution.py:225
  8.1 64.8 %collective-permute-start.2 = (f32[3,5,128,128]{3,2,1,0:T(8,128)}, f32[3,5,128,128]{3,2,1,0:T(8,128)S(1)}, u32[]{:S(2)}, u32[]{:S(2)}) collective-permute-start(f32[3,5,128,128]{3,2,1,0:T(8,128)} %get-tuple-element.53), channel_id=1, source_target_pairs={{0,4},{4,8},{8,12},{12,16},{16,20},{20,24},{24,28},{7,3},{11,7},{1... | collective-permute-start | bytes 2949128 | tf_op jit(solution)/shard_map/ppermute | solution.py:260
  9.6 0.7 collective-permute-start
  10.3 23.9 %collective-permute-start.4 = (f32[16,4096]{1,0:T(8,128)}, f32[16,4096]{1,0:T(8,128)S(1)}, u32[]{:S(2)}, u32[]{:S(2)}) collective-permute-start(f32[16,4096]{1,0:T(8,128)} %refs_0_.1), channel_id=1, source_target_pairs={{0,1},{1,0},{2,3},{3,2},{4,5},{5,4},{6,7},{7,6},{8,9},{9,8},{10,11... | collective-permute-start | bytes 786440 | tf_op jit(solution)/shard_map/ppermute | solution.py:229
  32.1 0.7 copy-start.4
  32.1 4.7 %collective-permute-start.5 = (f32[16,4096]{1,0:T(8,128)}, f32[16,4096]{1,0:T(8,128)S(1)}, u32[]{:S(2)}, u32[]{:S(2)}) collective-permute-start(f32[16,4096]{1,0:T(8,128)} %refs_1_.1), channel_id=1, source_target_pairs={{0,1},{1,0},{2,3},{3,2},{4,5},{5,4},{6,7},{7,6},{8,9},{9,8},{10,11... | collective-permute-start | bytes 786440 | tf_op jit(solution)/shard_map/ppermute | solution.py:229
  32.8 0.7 copy-start.6
  33.5 64.2 %collective-permute-start.3 = (f32[3,5,128,128]{3,2,1,0:T(8,128)}, f32[3,5,128,128]{3,2,1,0:T(8,128)S(1)}, u32[]{:S(2)}, u32[]{:S(2)}) collective-permute-start(f32[3,5,128,128]{3,2,1,0:T(8,128)} %get-tuple-element.51), channel_id=1, source_target_pairs={{0,4},{4,8},{8,12},{12,16},{16,20},{20,24},{24,28},{7,3},{11,7},{1... | collective-permute-start | bytes 2949128 | tf_op jit(solution)/shard_map/ppermute | solution.py:260
  34.2 0.7 copy-start.8
  34.9 14.2 %collective-permute-start.8 = (f32[16,4096]{1,0:T(8,128)}, f32[16,4096]{1,0:T(8,128)}, u32[]{:S(2)}, u32[]{:S(2)}) collective-permute-start(f32[16,4096]{1,0:T(8,128)} %copy-done.4), channel_id=1, source_target_pairs={{0,1},{1,0},{2,3},{3,2},{4,5},{5,4},{6,7},{7,6},{8,9},{9,8},{10,11... | collective-permute-start | bytes 786440 | tf_op jit(solution)/shard_map/ppermute | solution.py:229
  36.7 0.7 copy-start.10
  37.4 11.7 %collective-permute-start.9 = (f32[16,4096]{1,0:T(8,128)}, f32[16,4096]{1,0:T(8,128)}, u32[]{:S(2)}, u32[]{:S(2)}) collective-permute-start(f32[16,4096]{1,0:T(8,128)} %copy-done.6), channel_id=1, source_target_pairs={{0,1},{1,0},{2,3},{3,2},{4,5},{5,4},{6,7},{7,6},{8,9},{9,8},{10,11... | collective-permute-start | bytes 786440 | tf_op jit(solution)/shard_map/ppermute | solution.py:229
  37.4 11.7 %copy-start.5 = (f32[16,4096]{1,0:T(8,128)S(1)}, f32[16,4096]{1,0:T(8,128)}, u32[]{:S(2)}) copy-start(f32[16,4096]{1,0:T(8,128)} %copy-done.4) | copy-start | bytes 786436
  37.4 11.7 %copy-start.7 = (f32[16,4096]{1,0:T(8,128)S(1)}, f32[16,4096]{1,0:T(8,128)}, u32[]{:S(2)}) copy-start(f32[16,4096]{1,0:T(8,128)} %copy-done.6) | copy-start | bytes 786436
  37.4 11.7 %copy-start.9 = (f32[16,4096]{1,0:T(8,128)S(1)}, f32[16,4096]{1,0:T(8,128)}, u32[]{:S(2)}) copy-start(f32[16,4096]{1,0:T(8,128)} %copy-done.8) | copy-start | bytes 786436
  37.5 11.7 %copy-start.11 = (f32[16,4096]{1,0:T(8,128)S(1)}, f32[16,4096]{1,0:T(8,128)}, u32[]{:S(2)}) copy-start(f32[16,4096]{1,0:T(8,128)} %copy-done.10) | copy-start | bytes 786436
  44.8 4.2 %copy-start = (bf16[34,640,256]{2,1,0:T(8,128)(2,1)}, bf16[34,640,256]{2,1,0:T(8,128)(2,1)S(1)}, u32[]{:S(2)}) copy-start(bf16[34,640,256]{2,1,0:T(8,128)(2,1)S(1)} %get-tuple-element.28.prepared) | copy-start | bytes 33423364
  52.1 0.7 copy-start.12
  52.7 0.7 copy-start.14
  53.4 0.6 copy-start.16
  54.0 10.0 %collective-permute-start.10 = (f32[9,16,128]{2,1,0:T(8,128)}, f32[9,16,128]{2,1,0:T(8,128)S(1)}, u32[]{:S(2)}, u32[]{:S(2)}) collective-permute-start(f32[9,16,128]{2,1,0:T(8,128)} %get-tuple-element.34), channel_id=1, source_target_pairs={{0,1},{1,0},{2,3},{3,2},{4,5},{5,4},{6,7},{7,6},{8,9},{9,8},{10,11... | collective-permute-start | bytes 221192 | tf_op jit(solution)/shard_map/ppermute | solution.py:306
  57.1 7.0 %collective-permute-start.11 = (f32[9,16,128]{2,1,0:T(8,128)S(1)}, f32[9,16,128]{2,1,0:T(8,128)S(1)}, u32[]{:S(2)}, u32[]{:S(2)}) collective-permute-start(f32[9,16,128]{2,1,0:T(8,128)S(1)} %get-tuple-element.35), channel_id=1, source_target_pairs={{1,2},{3,4},{5,6},{7,8},{9,10},{11,12},{13,14},{15,16},{17,18},{19... | collective-permute-start | bytes 221192 | tf_op jit(solution)/shard_map/ppermute | solution.py:305
  59.3 4.2 %copy-start.1 = (bf16[34,640,256]{2,1,0:T(8,128)(2,1)S(1)}, bf16[34,640,256]{2,1,0:T(8,128)(2,1)}, u32[]{:S(2)}) copy-start(bf16[34,640,256]{2,1,0:T(8,128)(2,1)} %copy-done) | copy-start | bytes 33423364
  63.5 0.9 copy-start.13
  63.5 1.0 copy-start.15
  63.5 1.0 copy-start.17
  67.3 6.1 %collective-permute-start.12 = (f32[15,16,128]{2,1,0:T(8,128)S(1)}, f32[15,16,128]{2,1,0:T(8,128)S(1)}, u32[]{:S(2)}, u32[]{:S(2)}) collective-permute-start(f32[15,16,128]{2,1,0:T(8,128)S(1)} %get-tuple-element.39), channel_id=1, source_target_pairs={{0,1},{1,0},{2,3},{3,2},{4,5},{5,4},{6,7},{7,6},{8,9},{9,8},{10,11... | collective-permute-start | bytes 368648 | tf_op jit(solution)/shard_map/ppermute | solution.py:306
  67.5 9.1 %collective-permute-start.13 = (f32[15,16,128]{2,1,0:T(8,128)S(1)}, f32[15,16,128]{2,1,0:T(8,128)S(1)}, u32[]{:S(2)}, u32[]{:S(2)}) collective-permute-start(f32[15,16,128]{2,1,0:T(8,128)S(1)} %get-tuple-element.40), channel_id=1, source_target_pairs={{1,2},{3,4},{5,6},{7,8},{9,10},{11,12},{13,14},{15,16},{17,18},{19... | collective-permute-start | bytes 368648 | tf_op jit(solution)/shard_map/ppermute | solution.py:305
  81.0 3.7 %collective-permute-start.14 = (f32[15,16,128]{2,1,0:T(8,128)S(1)}, f32[15,16,128]{2,1,0:T(8,128)S(1)}, u32[]{:S(2)}, u32[]{:S(2)}) collective-permute-start(f32[15,16,128]{2,1,0:T(8,128)S(1)} %get-tuple-element.44), channel_id=1, source_target_pairs={{0,1},{1,0},{2,3},{3,2},{4,5},{5,4},{6,7},{7,6},{8,9},{9,8},{10,11... | collective-permute-start | bytes 368648 | tf_op jit(solution)/shard_map/ppermute | solution.py:306
  81.1 7.2 %collective-permute-start.15 = (f32[15,16,128]{2,1,0:T(8,128)S(1)}, f32[15,16,128]{2,1,0:T(8,128)S(1)}, u32[]{:S(2)}, u32[]{:S(2)}) collective-permute-start(f32[15,16,128]{2,1,0:T(8,128)S(1)} %get-tuple-element.45), channel_id=1, source_target_pairs={{1,2},{3,4},{5,6},{7,8},{9,10},{11,12},{13,14},{15,16},{17,18},{19... | collective-permute-start | bytes 368648 | tf_op jit(solution)/shard_map/ppermute | solution.py:305
  92.7 5.7 %collective-permute-start.16 = (f32[21,16,128]{2,1,0:T(8,128)S(1)}, f32[21,16,128]{2,1,0:T(8,128)S(1)}, u32[]{:S(2)}, u32[]{:S(2)}) collective-permute-start(f32[21,16,128]{2,1,0:T(8,128)S(1)} %get-tuple-element.49), channel_id=1, source_target_pairs={{0,1},{1,0},{2,3},{3,2},{4,5},{5,4},{6,7},{7,6},{8,9},{9,8},{10,11... | collective-permute-start | bytes 516104 | tf_op jit(solution)/shard_map/ppermute | solution.py:306
  94.2 8.4 %collective-permute-start.17 = (f32[21,16,128]{2,1,0:T(8,128)S(1)}, f32[21,16,128]{2,1,0:T(8,128)S(1)}, u32[]{:S(2)}, u32[]{:S(2)}) collective-permute-start(f32[21,16,128]{2,1,0:T(8,128)S(1)} %get-tuple-element.50), channel_id=1, source_target_pairs={{1,2},{3,4},{5,6},{7,8},{9,10},{11,12},{13,14},{15,16},{17,18},{19... | collective-permute-start | bytes 516104 | tf_op jit(solution)/shard_map/ppermute | solution.py:305
  108.9 5.7 %collective-permute-start.19 = (f32[16,16,128]{2,1,0:T(8,128)S(1)}, f32[16,16,128]{2,1,0:T(8,128)S(1)}, u32[]{:S(2)}, u32[]{:S(2)}) collective-permute-start(f32[16,16,128]{2,1,0:T(8,128)S(1)} %shard_map.63.refs_0_), channel_id=1, source_target_pairs={{2,0},{3,1},{0,2},{1,3},{6,4},{7,5},{4,6},{5,7},{10,8},{11,9},{8,1... | collective-permute-start | bytes 393224 | tf_op jit(solution)/shard_map/ppermute | solution.py:225
  110.8 4.5 %collective-permute-start.18 = (f32[16,16,128]{2,1,0:T(8,128)S(1)}, f32[16,16,128]{2,1,0:T(8,128)S(1)}, u32[]{:S(2)}, u32[]{:S(2)}) collective-permute-start(f32[16,16,128]{2,1,0:T(8,128)S(1)} %shard_map.63.refs_0_), channel_id=1, source_target_pairs={{0,1},{1,0},{2,3},{3,2},{4,5},{5,4},{6,7},{7,6},{8,9},{9,8},{10,11... | collective-permute-start | bytes 393224 | tf_op jit(solution)/shard_map/ppermute | solution.py:229
  114.6 1.6 %collective-permute-start.20 = (f32[16,16,128]{2,1,0:T(8,128)S(1)}, f32[16,16,128]{2,1,0:T(8,128)S(1)}, u32[]{:S(2)}, u32[]{:S(2)}) collective-permute-start(f32[16,16,128]{2,1,0:T(8,128)S(1)} %collective-permute-done.19.refs_2_), channel_id=1, source_target_pairs={{0,1},{1,0},{2,3},{3,2},{4,5},{5,4},{6,7},{7,6},{8,9},{9,8},{10,11... | collective-permute-start | bytes 393224 | tf_op jit(solution)/shard_map/ppermute | solution.py:229

commit v3 on v2

--- a/solution.py
+++ b/solution.py
@@ -20,7 +20,7 @@
 BF16 = jnp.bfloat16
 VMEM = pl.BlockSpec(memory_space=pltpu.VMEM)
 SMEM = pl.BlockSpec(memory_space=pltpu.SMEM)
-ANY = pl.BlockSpec(memory_space=pl.ANY)
+HBM = pl.BlockSpec(memory_space=pltpu.HBM)
 
 
 def coefficients():
@@ -37,7 +37,7 @@
     return pairs
 
 
-def params(limit=40):
+def params(limit=16):
     return pltpu.CompilerParams(vmem_limit_bytes=limit * 2**20)
 
 
@@ -75,42 +75,85 @@
 
 
 def align_kernel(ob, steps, keys, facts, counts, *refs):
-    sources, (x_out, u_out, r_out, pay_a, pay_b) = refs[:-5], refs[-5:]
+    n = 2 * len(keys)
+    sources, (u_out, r_out, pay_a, pay_b), windows, sem = refs[:n], refs[n : n + 4], refs[n + 4 : 2 * n + 4], refs[-1]
     capacity = sources[0].shape[-1]
+    length = windows[0].shape[-1]
     folds = len(keys)
     lane = lax.broadcasted_iota(jnp.int32, (16, 128), 1)
     base = facts[0] * (ob * 128)
-    x_out[...] = jnp.zeros_like(x_out)
-    spans = []
-    for d, c in keys:
-        j = holder(facts[0], folds, d, c)
-        spans.append((begin_of(counts, j), counts[0, j]))
+    spans, copies = [], []
+    for j, (d, c) in enumerate(keys):
+        owner = holder(facts[0], folds, d, c)
+        start = begin_of(counts, owner)
+        first = jnp.clip((base - start) >> 7, 0, (capacity - length) // 128)
+        spans.append((start, counts[0, owner], first))
+        for i in (2 * j, 2 * j + 1):
+            source = sources[i].at[:, pl.ds(pl.multiple_of(first * 128, 128), length)]
+            copies.append(pltpu.make_async_copy(source, windows[i], sem.at[i]))
+    for copy in copies:
+        copy.start()
+    for copy in copies:
+        copy.wait()
 
     def block(e, carry):
         row = base + e * 128
         totals = [jnp.zeros((16, 128), F32), jnp.zeros((16, 128), F32)]
-        for j, (start, count) in enumerate(spans):
+        for j, (start, count, first) in enumerate(spans):
             at = row - start
-            low = at >> 7
+            low = (at >> 7) - first
             shift = at & 127
             index = at + lane
             valid = (index >= 0) & (index < count)
             for a in range(2):
 
-                def window(b, source=sources[2 * j + a]):
-                    b = jnp.clip(b, 0, capacity // 128 - 1)
-                    return source[:, pl.ds(pl.multiple_of(b * 128, 128), 128)]
+                def window(b, held=windows[2 * j + a]):
+                    b = jnp.clip(b, 0, length // 128 - 1)
+                    return held[:, pl.ds(pl.multiple_of(b * 128, 128), 128)]
 
                 totals[a] = jnp.where(valid, pick_lanes(window, low, shift), totals[a])
         u_out[e] = totals[0]
         r_out[e] = totals[1]
         return carry
 
-    lax.fori_loop(0, ob, block, 0, unroll=2)
+    lax.fori_loop(0, ob, block, 0, unroll=4)
     put_payloads(ob, steps, facts[1] == 0, u_out, 0, r_out, pay_a, pay_b)
 
 
-def prepare_kernel(ob, halo, facts, blocks, out, token, raw, sem):
+def outward_kernel(folds, halo, facts, columns, blocks, *refs):
+    *pieces, indices, sem = refs
+    own, width = columns.shape
+    fold = facts[0]
+
+    def copies():
+        for piece, out in enumerate(pieces):
+            at = jnp.where(fold == 0, own - HB * (piece + 1), HB * piece)
+            yield pltpu.make_async_copy(blocks.at[pl.ds(at, HB)], out, sem.at[piece])
+
+    edge = (fold == 0) | (fold == folds - 1)
+
+    @pl.when(edge)
+    def _():
+        for copy in copies():
+            copy.start()
+
+    for i in range(halo):
+        at = jnp.where(fold < folds // 2, own - halo + i, i)
+        for k in range(width):
+            indices[i * width + k] = columns[at, k]
+
+    @pl.when(edge)
+    def _():
+        for copy in copies():
+            copy.wait()
+
+
+def gate_kernel(n, *refs):
+    del n, refs
+
+
+def prepare_kernel(ob, halo, facts, columns, blocks, out, token, raw, sem):
+    del columns
     own, width, side = blocks.shape[0], blocks.shape[1], blocks.shape[2]
     rows = ob + 2 * halo
     first = facts[0] * ob - halo
@@ -136,7 +179,11 @@
     token[...] = jnp.zeros_like(token)
 
 
-def border_kernel(ob, folds, halo, piece, facts, prepared, raw, out):
+def border_kernel(ob, folds, halo, piece, facts, *refs):
+    if piece:
+        prepared, raw, out = refs
+    else:
+        columns, indices, prepared, raw, out, offsets = refs
     del prepared
     fold = facts[0]
     count, width, side = raw.shape[0], raw.shape[1], raw.shape[2]
@@ -150,12 +197,33 @@
                 out[first + a, k * side : (k + 1) * side, :side] = high.T
                 out[first + a, k * side : (k + 1) * side, side:] = low.T
 
-
-def phase_kernel(ob, halo, steps, after, pairs, facts, offsets, operator, x_in, u_in, r_in, got_a, got_b, *refs):
+    if piece:
+        return
+    own = columns.shape[0]
+
+    def row(a, carry):
+        i = fold * ob - halo + a
+        inside = (i >= 0) & (i < own)
+        outside = jnp.where(i < 0, i + halo, jnp.clip(i - own, 0, halo - 1))
+        local = jnp.where(i < 0, i + own, jnp.where(inside, i, i - own))
+        for k in range(width):
+            theirs = indices[jnp.clip(outside, 0, halo - 1) * width + k]
+            mine = columns[jnp.clip(i, 0, own - 1), k]
+            offset = jnp.where(inside, mine, theirs) - HB - local
+            offsets[a * width + k] = jnp.clip(offset, -HB, HB)
+        return carry
+
+    lax.fori_loop(0, ob + 2 * halo, row, 0, unroll=2)
+
+
+def phase_kernel(ob, halo, steps, first, after, pairs, facts, offsets, operator, *refs):
     h = HB * steps
     inner = h - HB
     extent = ob + 2 * h
     width = offsets.shape[0] // (ob + 2 * halo)
+    if not first:
+        x_in, *refs = refs
+    u_in, r_in, got_a, got_b, *refs = refs
     if after:
         x_out, u_out, r_out, pay_a, pay_b, u, r, *pieces = refs
     else:
@@ -170,9 +238,9 @@
     high, low = split(u[...])
     pieces[0][:, :16] = high
     pieces[0][:, 16:] = low
-    x = x_in[...]
+    x = None if first else x_in[...]
     for t in range(steps):
-        x = x + u[h : h + ob]
+        x = u[h : h + ob] if x is None else x + u[h : h + ob]
         now, later = pieces[t % 2], pieces[(t + 1) % 2]
         old, new = pairs[t]
         done = t == steps - 1
@@ -187,9 +255,9 @@
             update = new * resid if old == 0.0 else old * u[e] + new * resid
             u[e] = update
             if not done:
-                first, second = split(update)
-                later[e, :16] = first
-                later[e, 16:] = second
+                big, small = split(update)
+                later[e, :16] = big
+                later[e, 16:] = small
             return carry
 
         lower, upper = HB * (t + 1), extent - HB * (t + 1)
@@ -253,49 +321,65 @@
     last_fold = folds - 1
     border_perm = [(g * folds, (g + 1) * folds) for g in range(groups - 1)]
     border_perm += [((g + 1) * folds + last_fold, g * folds + last_fold) for g in range(groups - 1)]
-    to_right = fold == 0
-    borders = []
-    for piece in range(halo // HB):
-        at = jnp.where(to_right, own - HB * (piece + 1), HB * piece)
-        borders.append(lax.ppermute(lax.dynamic_slice_in_dim(blocks, at, HB, 0), AXES, border_perm))
-    relative = columns - (jnp.arange(own, dtype=jnp.int32)[:, None] + HB)
-    outward = lax.dynamic_slice_in_dim(relative, jnp.where(to_right, own - halo, 0), halo, 0)
-    outward = lax.ppermute(outward, AXES, border_perm)
-    around = jnp.concatenate([outward, relative, outward], axis=0)
-    offsets = lax.dynamic_slice_in_dim(around, fold * ob, rows, 0).reshape(-1)
+    count = halo // HB
+    fixed = pltpu.with_memory_space_constraint(blocks, pltpu.HBM)
+    *borders, indices = pl.pallas_call(
+        functools.partial(outward_kernel, folds, halo),
+        out_shape=(pltpu.VMEM((HB, width, side, side), F32),) * count + (jax.ShapeDtypeStruct((halo * width,), jnp.int32),),
+        in_specs=[SMEM, SMEM, HBM],
+        out_specs=(VMEM,) * count + (SMEM,),
+        scratch_shapes=[pltpu.SemaphoreType.DMA((count,))],
+        compiler_params=params(),
+    )(facts, columns, fixed)
+    borders = [lax.ppermute(piece, AXES, border_perm) for piece in borders]
+    index_perm = [(g * folds + 1, (g + 1) * folds) for g in range(groups - 1)]
+    index_perm += [((g + 1) * folds + last_fold - 1, g * folds + last_fold) for g in range(groups - 1)]
+    indices = lax.ppermute(indices, AXES, index_perm)
 
     operator, token = pl.pallas_call(
         functools.partial(prepare_kernel, ob, halo),
         out_shape=(pltpu.VMEM((rows, width * side, 2 * side), BF16), jax.ShapeDtypeStruct((8, 128), F32)),
-        in_specs=[SMEM, ANY],
+        in_specs=[SMEM, SMEM, HBM],
         out_specs=(VMEM, VMEM),
         scratch_shapes=[pltpu.VMEM((rows, width, side, side), F32), pltpu.SemaphoreType.DMA((rows,))],
+        compiler_params=params(32),
+        cost_estimate=pl.CostEstimate(flops=10**7, bytes_accessed=2 * rows * width * side * side * 4, transcendentals=0),
+    )(facts, columns, fixed)
+    flat = [array for pair in far for array in pair]
+    flat = pl.pallas_call(
+        functools.partial(gate_kernel, len(flat)),
+        out_shape=tuple(pltpu.HBM(array.shape, F32) for array in flat),
+        in_specs=[HBM] * (len(flat) + 1),
+        out_specs=(HBM,) * len(flat),
+        input_output_aliases={i: i for i in range(len(flat))},
         compiler_params=params(),
-        cost_estimate=pl.CostEstimate(flops=10**7, bytes_accessed=2 * rows * width * side * side * 4, transcendentals=0),
-    )(facts, blocks)
-    far, _ = lax.optimization_barrier((far, token))
+    )(*[pltpu.with_memory_space_constraint(array, pltpu.HBM) for array in flat], token)
+    far = [flat[2 * d : 2 * d + 2] for d in range(len(far))]
 
     keys, arrays = [], []
     for d, pair in enumerate([near, *far]):
         keys += [(d, False), (d, True)]
         arrays += [*pair, *(other_core(array, folds) for array in pair)]
-    x, u, r, pay_a, pay_b = pl.pallas_call(
+    u, r, pay_a, pay_b = pl.pallas_call(
         functools.partial(align_kernel, ob, plan[0], keys),
-        out_shape=(state, state, state, payload(plan[0]), payload(plan[0])),
-        in_specs=[SMEM, SMEM] + [VMEM] * (2 * folds),
-        out_specs=(VMEM,) * 5,
+        out_shape=(state, state, payload(plan[0]), payload(plan[0])),
+        in_specs=[SMEM, SMEM] + [HBM] * (2 * folds),
+        out_specs=(VMEM,) * 4,
+        scratch_shapes=[pltpu.VMEM((vectors, (ob + 1) * side), F32)] * (2 * folds) + [pltpu.SemaphoreType.DMA((2 * folds,))],
         compiler_params=params(),
-    )(facts, counts, *arrays)
+    )(facts, counts, *[pltpu.with_memory_space_constraint(array, pltpu.HBM) for array in arrays])
 
     def with_border(operator, piece):
+        whole = pltpu.VMEM((rows, width * side, 2 * side), BF16)
+        held = pltpu.with_memory_space_constraint(operator, pltpu.VMEM)
         return pl.pallas_call(
             functools.partial(border_kernel, ob, folds, halo, piece),
-            out_shape=pltpu.VMEM((rows, width * side, 2 * side), BF16),
-            in_specs=[SMEM, VMEM, VMEM],
-            out_specs=VMEM,
-            input_output_aliases={1: 0},
+            out_shape=whole if piece else (whole, jax.ShapeDtypeStruct((rows * width,), jnp.int32)),
+            in_specs=[SMEM, VMEM, VMEM] if piece else [SMEM, SMEM, SMEM, VMEM, VMEM],
+            out_specs=VMEM if piece else (VMEM, SMEM),
+            input_output_aliases={1: 0} if piece else {3: 0},
             compiler_params=params(),
-        )(facts, pltpu.with_memory_space_constraint(operator, pltpu.VMEM), borders[piece])
+        )(facts, *([] if piece else [columns, indices]), held, borders[piece])
 
     swap_a = [(i, i ^ 1) for i in range(devices)]
     swap_b = [(i, i + 1) for i in range(1, devices - 1, 2)]
@@ -305,13 +389,16 @@
         got_b = lax.ppermute(pay_b, AXES, swap_b)
         got_a = lax.ppermute(pay_a, AXES, swap_a)
         while there < steps - 1:
-            operator = with_border(operator, there)
+            if there:
+                operator = with_border(operator, there)
+            else:
+                operator, offsets = with_border(operator, 0)
             there += 1
         after = plan[phase + 1] if phase + 1 < len(plan) else 0
         outs = pl.pallas_call(
-            functools.partial(phase_kernel, ob, halo, steps, after, pairs[done : done + steps]),
+            functools.partial(phase_kernel, ob, halo, steps, phase == 0, after, pairs[done : done + steps]),
             out_shape=(state, state, state, payload(after), payload(after)) if after else state,
-            in_specs=[SMEM, SMEM] + [VMEM] * 6,
+            in_specs=[SMEM, SMEM] + [VMEM] * (6 if phase else 5),
             out_specs=(VMEM,) * 5 if after else VMEM,
             scratch_shapes=[
                 pltpu.VMEM((ob + 2 * HB * steps, vectors, side), F32),
@@ -320,7 +407,7 @@
                 pltpu.VMEM((ob + 2 * HB * steps, 2 * vectors, side), BF16),
             ],
             compiler_params=params(),
-        )(facts, offsets, pltpu.with_memory_space_constraint(operator, pltpu.VMEM), x, u, r, got_a, got_b)
+        )(facts, offsets, pltpu.with_memory_space_constraint(operator, pltpu.VMEM), *([x] if phase else []), u, r, got_a, got_b)
         done += steps
         if after:
             x, u, r, pay_a, pay_b = outs

time: 118 us -> 102 us (0.86)
  local copies, waits for them, and re-layouts: 17.5 us -> 1.55 us
  starting transfers between devices: 52 us -> 39.7 us
  waiting for transfers between devices: 15.6 us -> 24.8 us
  Pallas kernels: 31.7 us -> 35.4 us
    unnamed x38 -> x19, local copies, waits for them, and re-layouts: 13.5 us -> 1.55 us
    ppermute x6, starting transfers between devices: 24.3 us -> 14.3 us  [other_core(): return lax.ppermute(array, 'fold', [(i, i ^ 1) for i in range(folds)])]
    ppermute x4, starting transfers between devices: 14.5 us -> 7.65 us  [on_device(): got_b = lax.ppermute(pay_b, AXES, swap_b)]
    ppermute x4, waiting for transfers between devices: 10.8 us -> 15.1 us  [on_device(): got_b = lax.ppermute(pay_b, AXES, swap_b)]
    dynamic_slice x4 -> x0, local copies, waits for them, and re-layouts: 3.84 us -> none  [the longest x1 3.59 us: on_device(): lax.dynamic_slice_in_dim(blocks, at, HB, 0)]
    ppermute x3, waiting for transfers between devices: 3.79 us -> 7.41 us  [over_chips(): lax.ppermute(array, 'fold', [((i + 2 * d) % folds, i) for i in range(fold...]
    ppermute x4, starting transfers between devices: 2.92 us -> 6.44 us  [the longest x1 4.29 us: on_device(): indices = lax.ppermute(indices, AXES, index_perm)]
    pallas_call x3, Pallas kernels: 1.83 us -> 3.87 us  [with_border(): pl.pallas_call(functools.partial(border_kernel, ob, folds, halo, piece),...]
  transfers between devices with their start and end apart: 21 -> 21, of which waited for: 5 -> 9; matrix products, arithmetic and copies ran while one was open for 1% -> 0% of each run, Pallas kernels for 20% -> 25%
where the time goes in v3:
time: 102 us
  starting transfers between devices  39.7 us (39%)
  Pallas kernels  35.4 us (35%)
  waiting for transfers between devices  24.8 us (24%)
  local copies, waits for them, and re-layouts  1.55 us (2%)
    pallas_call x4, Pallas kernels, on_device(): pl.pallas_call(functools.partial(phase_kernel, ob, halo, steps, phase ==...  17.9 us
    ppermute x4, waiting for transfers between devices, on_device(): got_b = lax.ppermute(pay_b, AXES, swap_b)  15.1 us
    ppermute x6, starting transfers between devices, other_core(): return lax.ppermute(array, 'fold', [(i, i ^ 1) for i in range(folds)])  14.3 us
    ppermute x4, starting transfers between devices, on_device(): got_b = lax.ppermute(pay_b, AXES, swap_b)  7.65 us
    ppermute x3, waiting for transfers between devices, over_chips(): lax.ppermute(array, 'fold', [((i + 2 * d) % folds, i) for i in range(fold...  7.41 us
    pallas_call x1, Pallas kernels, on_device(): pl.pallas_call(functools.partial(prepare_kernel, ob, halo), out_shape=(pl...  7.25 us
    ppermute x3, starting transfers between devices, over_chips(): lax.ppermute(array, 'fold', [((i + 2 * d) % folds, i) for i in range(fold...  6.84 us
    ppermute x4, starting transfers between devices, on_device(): got_a = lax.ppermute(pay_a, AXES, swap_a)  4.53 us
  transfers between devices with their start and end apart: 21, of which 9 were waited for; matrix products, arithmetic and copies ran while one was open for 0% of the time, Pallas kernels for 25%

profile of v3, /device:TPU:9, one launch (start us, length us, event | category | flops | bytes accessed | tf_op | source)
XLA Modules:
  0.0 101.9 jit_solution(16742278768929457126)
XLA Ops:
  0.0 0.8 copy.13.columns.refs_0_
  0.8 0.1 pad_add_fusion.facts
  0.9 1.8 %shard_map.55 = (f32[3,5,128,128]{3,2,1,0:T(8,128)S(1)}, f32[3,5,128,128]{3,2,1,0:T(8,128)S(1)}, f32[3,5,128,128]{3,2,1,0:T(8,128)S(1)}, s32[45]{0:T(128)S(1)}) custom-call(s32[2]{0:T(128)S(1)} %pad_add_fusion.facts, s32[64,5]{1,0:T(8,128)S(1)} %copy.13.columns.refs_0_, f32[64,5,128,128]{3,2,1,0:T(8,128)} %blocks.3), custom_call_target="tpu_custom_call" | custom-call | tf_op jit(solution)/shard_map/pallas_call | solution.py:326
  2.7 0.0 copy-start
  2.7 0.7 collective-permute-start.1
  3.4 5.3 %collective-permute-start.6 = (f32[16,4096]{1,0:T(8,128)S(1)}, f32[16,4096]{1,0:T(8,128)S(1)}, u32[]{:S(2)}, u32[]{:S(2)}) collective-permute-start(f32[16,4096]{1,0:T(8,128)S(1)} %copy-done.3), channel_id=1, source_target_pairs={{2,0},{3,1},{0,2},{1,3},{6,4},{7,5},{4,6},{5,7},{10,8},{11,9},{8,1... | collective-permute-start | bytes 786440 | tf_op jit(solution)/shard_map/ppermute | solution.py:293
  8.8 0.7 collective-permute-start.2
  9.5 1.5 %collective-permute-start.7 = (f32[16,4096]{1,0:T(8,128)S(1)}, f32[16,4096]{1,0:T(8,128)S(1)}, u32[]{:S(2)}, u32[]{:S(2)}) collective-permute-start(f32[16,4096]{1,0:T(8,128)S(1)} %copy-done.4), channel_id=1, source_target_pairs={{2,0},{3,1},{0,2},{1,3},{6,4},{7,5},{4,6},{5,7},{10,8},{11,9},{8,1... | collective-permute-start | bytes 786440 | tf_op jit(solution)/shard_map/ppermute | solution.py:293
  11.0 1.2 %collective-permute-start.4 = (f32[16,4096]{1,0:T(8,128)S(1)}, f32[16,4096]{1,0:T(8,128)S(1)}, u32[]{:S(2)}, u32[]{:S(2)}) collective-permute-start(f32[16,4096]{1,0:T(8,128)S(1)} %copy-done.3), channel_id=1, source_target_pairs={{0,1},{1,0},{2,3},{3,2},{4,5},{5,4},{6,7},{7,6},{8,9},{9,8},{10,11... | collective-permute-start | bytes 786440 | tf_op jit(solution)/shard_map/ppermute | solution.py:297
  12.2 2.6 %collective-permute-done.6.refs_0_ = f32[16,4096]{1,0:T(8,128)S(1)} collective-permute-done((f32[16,4096]{1,0:T(8,128)S(1)}, f32[16,4096]{1,0:T(8,128)S(1)}, u32[]{:S(2)}, u32[]{:S(2)}) %collective-permute-start.6) | collective-permute-done | bytes 262176 | tf_op jit(solution)/shard_map/ppermute | solution.py:293
  14.8 3.0 %collective-permute-start.5 = (f32[16,4096]{1,0:T(8,128)S(1)}, f32[16,4096]{1,0:T(8,128)S(1)}, u32[]{:S(2)}, u32[]{:S(2)}) collective-permute-start(f32[16,4096]{1,0:T(8,128)S(1)} %copy-done.4), channel_id=1, source_target_pairs={{0,1},{1,0},{2,3},{3,2},{4,5},{5,4},{6,7},{7,6},{8,9},{9,8},{10,11... | collective-permute-start | bytes 786440 | tf_op jit(solution)/shard_map/ppermute | solution.py:297
  17.9 2.6 %collective-permute-done.7.refs_1_ = f32[16,4096]{1,0:T(8,128)S(1)} collective-permute-done((f32[16,4096]{1,0:T(8,128)S(1)}, f32[16,4096]{1,0:T(8,128)S(1)}, u32[]{:S(2)}, u32[]{:S(2)}) %collective-permute-start.7) | collective-permute-done | bytes 262176 | tf_op jit(solution)/shard_map/ppermute | solution.py:293
  20.5 0.7 collective-permute-start.3
  21.2 7.3 %shard_map.56 = (bf16[34,640,256]{2,1,0:T(8,128)(2,1)S(1)}, f32[8,128]{1,0:T(8,128)S(1)}) custom-call(s32[2]{0:T(128)S(1)} %pad_add_fusion.facts, s32[64,5]{1,0:T(8,128)S(1)} %copy.13.columns.refs_0_, f32[64,5,128,128]{3,2,1,0:T(8,128)} %blocks.3), custom_call_target="tpu_custom_call" | custom-call | flops 10000000 | bytes 22282240 | tf_op jit(solution)/shard_map/pallas_call | solution.py:339
  28.5 0.0 copy-start.5
  28.5 5.6 %collective-permute-start.8 = (f32[16,4096]{1,0:T(8,128)}, f32[16,4096]{1,0:T(8,128)S(1)}, u32[]{:S(2)}, u32[]{:S(2)}) collective-permute-start(f32[16,4096]{1,0:T(8,128)} %get-tuple-element.42.refs_4_), channel_id=1, source_target_pairs={{0,1},{1,0},{2,3},{3,2},{4,5},{5,4},{6,7},{7,6},{8,9},{9,8},{10,11... | collective-permute-start | bytes 786440 | tf_op jit(solution)/shard_map/ppermute | solution.py:297
  34.1 0.0 collective-permute-done.5.refs_3_
  34.1 0.1 collective-permute-start.9
  34.2 1.3 %collective-permute-done.8.refs_6_ = f32[16,4096]{1,0:T(8,128)S(1)} collective-permute-done((f32[16,4096]{1,0:T(8,128)}, f32[16,4096]{1,0:T(8,128)S(1)}, u32[]{:S(2)}, u32[]{:S(2)}) %collective-permute-start.8) | collective-permute-done | bytes 262176 | tf_op jit(solution)/shard_map/ppermute | solution.py:297
  35.5 4.3 %collective-permute-start = (s32[45]{0:T(128)S(1)}, s32[45]{0:T(128)S(1)}, u32[]{:S(2)}, u32[]{:S(2)}) collective-permute-start(s32[45]{0:T(128)S(1)} %get-tuple-element.34), channel_id=1, source_target_pairs={{1,4},{5,8},{9,12},{13,16},{17,20},{21,24},{25,28},{6,3},{10,7},{1... | collective-permute-start | bytes 548 | tf_op jit(solution)/shard_map/ppermute | solution.py:337
  39.9 0.7 copy-done.8
  40.5 2.9 %shard_map.61 = (f32[16,16,128]{2,1,0:T(8,128)S(1)}, f32[16,16,128]{2,1,0:T(8,128)S(1)}, f32[9,16,128]{2,1,0:T(8,128)S(1)}, f32[9,16,128]{2,1,0:T(8,128)S(1)}) custom-call(s32[2]{0:T(128)S(1)} %pad_add_fusion.facts, s32[1,4]{1,0:T(1,128)S(1)} %copy-done, f32[16,4096]{1,0:T(8,128)} %refs_0_.2, f32[16,4096]{1,0:T(8,128)} %refs_1_.1, f32[16,4096]{1,0:T(8,128)} %copy-done.5, ...), custom_call_target="tpu_custom_call" | custom-call | tf_op jit(solution)/shard_map/pallas_call | solution.py:363
  43.4 0.1 collective-permute-start.10
  43.5 0.0 collective-permute-done.refs_1_
  43.5 1.9 %collective-permute-start.11 = (f32[9,16,128]{2,1,0:T(8,128)S(1)}, f32[9,16,128]{2,1,0:T(8,128)S(1)}, u32[]{:S(2)}, u32[]{:S(2)}) collective-permute-start(f32[9,16,128]{2,1,0:T(8,128)S(1)} %get-tuple-element.47), channel_id=1, source_target_pairs={{1,2},{3,4},{5,6},{7,8},{9,10},{11,12},{13,14},{15,16},{17,18},{19... | collective-permute-start | bytes 221192 | tf_op jit(solution)/shard_map/ppermute | solution.py:389
  45.4 2.6 %shard_map.57 = (bf16[34,640,256]{2,1,0:T(8,128)(2,1)S(1)}, s32[170]{0:T(256)S(1)}) custom-call(s32[2]{0:T(128)S(1)} %pad_add_fusion.facts, s32[64,5]{1,0:T(8,128)S(1)} %copy.13.columns.refs_0_, s32[45]{0:T(128)S(1)} %collective-permute-done.refs_1_, bf16[34,640,256]{2,1,0:T(8,128)(2,1)S(1)} %get-tuple-element.35.refs_2_, ...), custom_call_target="tpu_custom_call", output_to_operand_aliasing={{0}: (3, {})} | custom-call | tf_op jit(solution)/shard_map/pallas_call | solution.py:375
  48.1 1.8 %collective-permute-done.11.refs_3_ = f32[9,16,128]{2,1,0:T(8,128)S(1)} collective-permute-done((f32[9,16,128]{2,1,0:T(8,128)S(1)}, f32[9,16,128]{2,1,0:T(8,128)S(1)}, u32[]{:S(2)}, u32[]{:S(2)}) %collective-permute-start.11) | collective-permute-done | bytes 73760 | tf_op jit(solution)/shard_map/ppermute | solution.py:389
  49.8 2.8 %shard_map.62 = (f32[16,16,128]{2,1,0:T(8,128)S(1)}, f32[16,16,128]{2,1,0:T(8,128)S(1)}, f32[16,16,128]{2,1,0:T(8,128)S(1)}, f32[15,16,128]{2,1,0:T(8,128)S(1)}, f32[15,16,128]{2,1,0:T(8,128)S(1)}) custom-call(s32[2]{0:T(128)S(1)} %pad_add_fusion.facts, s32[170]{0:T(256)S(1)} %get-tuple-element.37.offsets, ...), custom_call_target="tpu_custom_call" | custom-call | tf_op jit(solution)/shard_map/pallas_call | solution.py:398
  52.6 1.7 %collective-permute-start.12 = (f32[15,16,128]{2,1,0:T(8,128)S(1)}, f32[15,16,128]{2,1,0:T(8,128)S(1)}, u32[]{:S(2)}, u32[]{:S(2)}) collective-permute-start(f32[15,16,128]{2,1,0:T(8,128)S(1)} %get-tuple-element.51), channel_id=1, source_target_pairs={{0,1},{1,0},{2,3},{3,2},{4,5},{5,4},{6,7},{7,6},{8,9},{9,8},{10,11... | collective-permute-start | bytes 368648 | tf_op jit(solution)/shard_map/ppermute | solution.py:390
  54.3 1.9 %collective-permute-start.13 = (f32[15,16,128]{2,1,0:T(8,128)S(1)}, f32[15,16,128]{2,1,0:T(8,128)S(1)}, u32[]{:S(2)}, u32[]{:S(2)}) collective-permute-start(f32[15,16,128]{2,1,0:T(8,128)S(1)} %get-tuple-element.52), channel_id=1, source_target_pairs={{1,2},{3,4},{5,6},{7,8},{9,10},{11,12},{13,14},{15,16},{17,18},{19... | collective-permute-start | bytes 368648 | tf_op jit(solution)/shard_map/ppermute | solution.py:389
  56.3 0.6 shard_map.58.refs_0_.operator
  56.8 4.4 %collective-permute-done.13.refs_4_ = f32[15,16,128]{2,1,0:T(8,128)S(1)} collective-permute-done((f32[15,16,128]{2,1,0:T(8,128)S(1)}, f32[15,16,128]{2,1,0:T(8,128)S(1)}, u32[]{:S(2)}, u32[]{:S(2)}) %collective-permute-start.13) | collective-permute-done | bytes 122912 | tf_op jit(solution)/shard_map/ppermute | solution.py:389
  61.3 4.4 %shard_map.63 = (f32[16,16,128]{2,1,0:T(8,128)S(1)}, f32[16,16,128]{2,1,0:T(8,128)S(1)}, f32[16,16,128]{2,1,0:T(8,128)S(1)}, f32[15,16,128]{2,1,0:T(8,128)S(1)}, f32[15,16,128]{2,1,0:T(8,128)S(1)}) custom-call(s32[2]{0:T(128)S(1)} %pad_add_fusion.facts, s32[170]{0:T(256)S(1)} %get-tuple-element.37.offsets, ...), custom_call_target="tpu_custom_call" | custom-call | tf_op jit(solution)/shard_map/pallas_call | solution.py:398
  65.7 1.2 %collective-permute-start.14 = (f32[15,16,128]{2,1,0:T(8,128)S(1)}, f32[15,16,128]{2,1,0:T(8,128)S(1)}, u32[]{:S(2)}, u32[]{:S(2)}) collective-permute-start(f32[15,16,128]{2,1,0:T(8,128)S(1)} %get-tuple-element.56), channel_id=1, source_target_pairs={{0,1},{1,0},{2,3},{3,2},{4,5},{5,4},{6,7},{7,6},{8,9},{9,8},{10,11... | collective-permute-start | bytes 368648 | tf_op jit(solution)/shard_map/ppermute | solution.py:390
  66.8 1.9 %collective-permute-start.15 = (f32[15,16,128]{2,1,0:T(8,128)S(1)}, f32[15,16,128]{2,1,0:T(8,128)S(1)}, u32[]{:S(2)}, u32[]{:S(2)}) collective-permute-start(f32[15,16,128]{2,1,0:T(8,128)S(1)} %get-tuple-element.57), channel_id=1, source_target_pairs={{1,2},{3,4},{5,6},{7,8},{9,10},{11,12},{13,14},{15,16},{17,18},{19... | collective-permute-start | bytes 368648 | tf_op jit(solution)/shard_map/ppermute | solution.py:389
  68.8 4.6 %collective-permute-done.15.refs_4_ = f32[15,16,128]{2,1,0:T(8,128)S(1)} collective-permute-done((f32[15,16,128]{2,1,0:T(8,128)S(1)}, f32[15,16,128]{2,1,0:T(8,128)S(1)}, u32[]{:S(2)}, u32[]{:S(2)}) %collective-permute-start.15) | collective-permute-done | bytes 122912 | tf_op jit(solution)/shard_map/ppermute | solution.py:389
  73.3 4.4 %shard_map.64 = (f32[16,16,128]{2,1,0:T(8,128)S(1)}, f32[16,16,128]{2,1,0:T(8,128)S(1)}, f32[16,16,128]{2,1,0:T(8,128)S(1)}, f32[21,16,128]{2,1,0:T(8,128)S(1)}, f32[21,16,128]{2,1,0:T(8,128)S(1)}) custom-call(s32[2]{0:T(128)S(1)} %pad_add_fusion.facts, s32[170]{0:T(256)S(1)} %get-tuple-element.37.offsets, ...), custom_call_target="tpu_custom_call" | custom-call | tf_op jit(solution)/shard_map/pallas_call | solution.py:398
  77.8 1.6 %collective-permute-start.16 = (f32[21,16,128]{2,1,0:T(8,128)S(1)}, f32[21,16,128]{2,1,0:T(8,128)S(1)}, u32[]{:S(2)}, u32[]{:S(2)}) collective-permute-start(f32[21,16,128]{2,1,0:T(8,128)S(1)} %get-tuple-element.61), channel_id=1, source_target_pairs={{0,1},{1,0},{2,3},{3,2},{4,5},{5,4},{6,7},{7,6},{8,9},{9,8},{10,11... | collective-permute-start | bytes 516104 | tf_op jit(solution)/shard_map/ppermute | solution.py:390
  79.3 1.9 %collective-permute-start.17 = (f32[21,16,128]{2,1,0:T(8,128)S(1)}, f32[21,16,128]{2,1,0:T(8,128)S(1)}, u32[]{:S(2)}, u32[]{:S(2)}) collective-permute-start(f32[21,16,128]{2,1,0:T(8,128)S(1)} %get-tuple-element.62), channel_id=1, source_target_pairs={{1,2},{3,4},{5,6},{7,8},{9,10},{11,12},{13,14},{15,16},{17,18},{19... | collective-permute-start | bytes 516104 | tf_op jit(solution)/shard_map/ppermute | solution.py:389
  81.3 0.7 shard_map.59.operator
  82.0 4.3 %collective-permute-done.17.refs_4_ = f32[21,16,128]{2,1,0:T(8,128)S(1)} collective-permute-done((f32[21,16,128]{2,1,0:T(8,128)S(1)}, f32[21,16,128]{2,1,0:T(8,128)S(1)}, u32[]{:S(2)}, u32[]{:S(2)}) %collective-permute-start.17) | collective-permute-done | bytes 172064 | tf_op jit(solution)/shard_map/ppermute | solution.py:389
  86.3 6.3 %shard_map.65.refs_0_ = f32[16,16,128]{2,1,0:T(8,128)S(1)} custom-call(s32[2]{0:T(128)S(1)} %pad_add_fusion.facts, s32[170]{0:T(256)S(1)} %get-tuple-element.37.offsets, bf16[34,640,256]{2,1,0:T(8,128)(2,1)S(1)} %shard_map.59.operator, f32[16,16,128]{2,1,0:T(8,128)S(1)} %get-tuple-element.58.refs_0_, f32[16,16,128]{2,1,0:T(8,128)S(1)} %get-tuple-element.59.refs_1_, ...), custom_call_target="tpu_custom_call" | custom-call | tf_op jit(solution)/shard_map/pallas_call | solution.py:398
  92.6 0.0 collective-permute-start.19
  92.7 1.6 %collective-permute-start.18 = (f32[16,16,128]{2,1,0:T(8,128)S(1)}, f32[16,16,128]{2,1,0:T(8,128)S(1)}, u32[]{:S(2)}, u32[]{:S(2)}) collective-permute-start(f32[16,16,128]{2,1,0:T(8,128)S(1)} %shard_map.65.refs_0_), channel_id=1, source_target_pairs={{0,1},{1,0},{2,3},{3,2},{4,5},{5,4},{6,7},{7,6},{8,9},{9,8},{10,11... | collective-permute-start | bytes 393224 | tf_op jit(solution)/shard_map/ppermute | solution.py:297
  94.3 2.2 %collective-permute-done.19.refs_2_ = f32[16,16,128]{2,1,0:T(8,128)S(1)} collective-permute-done((f32[16,16,128]{2,1,0:T(8,128)S(1)}, f32[16,16,128]{2,1,0:T(8,128)S(1)}, u32[]{:S(2)}, u32[]{:S(2)}) %collective-permute-start.19) | collective-permute-done | bytes 131104 | tf_op jit(solution)/shard_map/ppermute | solution.py:293
  96.5 2.7 %collective-permute-start.20 = (f32[16,16,128]{2,1,0:T(8,128)S(1)}, f32[16,16,128]{2,1,0:T(8,128)S(1)}, u32[]{:S(2)}, u32[]{:S(2)}) collective-permute-start(f32[16,16,128]{2,1,0:T(8,128)S(1)} %collective-permute-done.19.refs_2_), channel_id=1, source_target_pairs={{0,1},{1,0},{2,3},{3,2},{4,5},{5,4},{6,7},{7,6},{8,9},{9,8},{10,11... | collective-permute-start | bytes 393224 | tf_op jit(solution)/shard_map/ppermute | solution.py:297
  99.2 1.0 collective-permute-done.20.refs_3_
  100.1 1.7 %shard_map.66 = f32[16,4096]{1,0:T(8,128)} custom-call(s32[2]{0:T(128)S(1)} %pad_add_fusion.facts, s32[1,4]{1,0:T(1,128)S(1)} %copy-done, f32[16,16,128]{2,1,0:T(8,128)S(1)} %shard_map.65.refs_0_, f32[16,16,128]{2,1,0:T(8,128)S(1)} %collective-permute-done.18.refs_1_, f32[16,16,128]{2,1,0:T(8,128)S(1)} %collective-permute-done.19.refs_2_, ...), custom_call_target="tpu_custom_call" | custom-call | tf_op jit(solution)/shard_map/pallas_call | solution.py:421
  (26 shorter events, 0.1 us)
Async XLA Ops:
  0.0 3.4 %copy-start.3 = (f32[16,4096]{1,0:T(8,128)S(1)}, f32[16,4096]{1,0:T(8,128)}, u32[]{:S(2)}) copy-start(f32[16,4096]{1,0:T(8,128)} %refs_0_.2) | copy-start | bytes 786436
  0.0 9.5 %copy-start.4 = (f32[16,4096]{1,0:T(8,128)S(1)}, f32[16,4096]{1,0:T(8,128)}, u32[]{:S(2)}) copy-start(f32[16,4096]{1,0:T(8,128)} %refs_1_.1) | copy-start | bytes 786436
  2.7 37.9 %copy-start = (s32[1,4]{1,0:T(1,128)S(1)}, s32[1,4]{1,0:T(1,128)}, u32[]{:S(2)}) copy-start(s32[1,4]{1,0:T(1,128)} %counts.3) | copy-start | bytes 52
  2.7 42.7 %collective-permute-start.1 = (f32[3,5,128,128]{3,2,1,0:T(8,128)S(1)}, f32[3,5,128,128]{3,2,1,0:T(8,128)S(1)}, u32[]{:S(2)}, u32[]{:S(2)}) collective-permute-start(f32[3,5,128,128]{3,2,1,0:T(8,128)S(1)} %get-tuple-element.36), channel_id=1, source_target_pairs={{0,4},{4,8},{8,12},{12,16},{16,20},{20,24},{24,28},{7,3},{11,7},{1... | collective-permute-start | bytes 2949128 | tf_op jit(solution)/shard_map/ppermute | solution.py:334
  3.4 11.4 %collective-permute-start.6 = (f32[16,4096]{1,0:T(8,128)S(1)}, f32[16,4096]{1,0:T(8,128)S(1)}, u32[]{:S(2)}, u32[]{:S(2)}) collective-permute-start(f32[16,4096]{1,0:T(8,128)S(1)} %copy-done.3), channel_id=1, source_target_pairs={{2,0},{3,1},{0,2},{1,3},{6,4},{7,5},{4,6},{5,7},{10,8},{11,9},{8,1... | collective-permute-start | bytes 786440 | tf_op jit(solution)/shard_map/ppermute | solution.py:293
  8.8 47.5 %collective-permute-start.2 = (f32[3,5,128,128]{3,2,1,0:T(8,128)S(1)}, f32[3,5,128,128]{3,2,1,0:T(8,128)S(1)}, u32[]{:S(2)}, u32[]{:S(2)}) collective-permute-start(f32[3,5,128,128]{3,2,1,0:T(8,128)S(1)} %get-tuple-element.39), channel_id=1, source_target_pairs={{0,4},{4,8},{8,12},{12,16},{16,20},{20,24},{24,28},{7,3},{11,7},{1... | collective-permute-start | bytes 2949128 | tf_op jit(solution)/shard_map/ppermute | solution.py:334
  9.5 11.0 %collective-permute-start.7 = (f32[16,4096]{1,0:T(8,128)S(1)}, f32[16,4096]{1,0:T(8,128)S(1)}, u32[]{:S(2)}, u32[]{:S(2)}) collective-permute-start(f32[16,4096]{1,0:T(8,128)S(1)} %copy-done.4), channel_id=1, source_target_pairs={{2,0},{3,1},{0,2},{1,3},{6,4},{7,5},{4,6},{5,7},{10,8},{11,9},{8,1... | collective-permute-start | bytes 786440 | tf_op jit(solution)/shard_map/ppermute | solution.py:293
  11.0 17.5 %collective-permute-start.4 = (f32[16,4096]{1,0:T(8,128)S(1)}, f32[16,4096]{1,0:T(8,128)S(1)}, u32[]{:S(2)}, u32[]{:S(2)}) collective-permute-start(f32[16,4096]{1,0:T(8,128)S(1)} %copy-done.3), channel_id=1, source_target_pairs={{0,1},{1,0},{2,3},{3,2},{4,5},{5,4},{6,7},{7,6},{8,9},{9,8},{10,11... | collective-permute-start | bytes 786440 | tf_op jit(solution)/shard_map/ppermute | solution.py:297
  14.8 13.6 %copy-start.1 = (f32[16,4096]{1,0:T(8,128)}, f32[16,4096]{1,0:T(8,128)S(1)}, u32[]{:S(2)}) copy-start(f32[16,4096]{1,0:T(8,128)S(1)} %collective-permute-done.6.refs_0_) | copy-start | bytes 786436
  14.8 19.3 %collective-permute-start.5 = (f32[16,4096]{1,0:T(8,128)S(1)}, f32[16,4096]{1,0:T(8,128)S(1)}, u32[]{:S(2)}, u32[]{:S(2)}) collective-permute-start(f32[16,4096]{1,0:T(8,128)S(1)} %copy-done.4), channel_id=1, source_target_pairs={{0,1},{1,0},{2,3},{3,2},{4,5},{5,4},{6,7},{7,6},{8,9},{9,8},{10,11... | collective-permute-start | bytes 786440 | tf_op jit(solution)/shard_map/ppermute | solution.py:297
  20.5 8.0 %copy-start.2 = (f32[16,4096]{1,0:T(8,128)}, f32[16,4096]{1,0:T(8,128)S(1)}, u32[]{:S(2)}) copy-start(f32[16,4096]{1,0:T(8,128)S(1)} %collective-permute-done.7.refs_1_) | copy-start | bytes 786436
  20.5 60.8 %collective-permute-start.3 = (f32[3,5,128,128]{3,2,1,0:T(8,128)S(1)}, f32[3,5,128,128]{3,2,1,0:T(8,128)S(1)}, u32[]{:S(2)}, u32[]{:S(2)}) collective-permute-start(f32[3,5,128,128]{3,2,1,0:T(8,128)S(1)} %get-tuple-element.40), channel_id=1, source_target_pairs={{0,4},{4,8},{8,12},{12,16},{16,20},{20,24},{24,28},{7,3},{11,7},{1... | collective-permute-start | bytes 2949128 | tf_op jit(solution)/shard_map/ppermute | solution.py:334
  28.5 11.3 %copy-start.5 = (f32[16,4096]{1,0:T(8,128)}, f32[16,4096]{1,0:T(8,128)S(1)}, u32[]{:S(2)}) copy-start(f32[16,4096]{1,0:T(8,128)S(1)} %collective-permute-done.4.refs_2_) | copy-start | bytes 786436
  28.5 7.0 %collective-permute-start.8 = (f32[16,4096]{1,0:T(8,128)}, f32[16,4096]{1,0:T(8,128)S(1)}, u32[]{:S(2)}, u32[]{:S(2)}) collective-permute-start(f32[16,4096]{1,0:T(8,128)} %get-tuple-element.42.refs_4_), channel_id=1, source_target_pairs={{0,1},{1,0},{2,3},{3,2},{4,5},{5,4},{6,7},{7,6},{8,9},{9,8},{10,11... | collective-permute-start | bytes 786440 | tf_op jit(solution)/shard_map/ppermute | solution.py:297
  34.1 5.7 %copy-start.6 = (f32[16,4096]{1,0:T(8,128)}, f32[16,4096]{1,0:T(8,128)S(1)}, u32[]{:S(2)}) copy-start(f32[16,4096]{1,0:T(8,128)S(1)} %collective-permute-done.5.refs_3_) | copy-start | bytes 786436
  34.1 5.7 %collective-permute-start.9 = (f32[16,4096]{1,0:T(8,128)}, f32[16,4096]{1,0:T(8,128)S(1)}, u32[]{:S(2)}, u32[]{:S(2)}) collective-permute-start(f32[16,4096]{1,0:T(8,128)} %get-tuple-element.43.refs_5_), channel_id=1, source_target_pairs={{0,1},{1,0},{2,3},{3,2},{4,5},{5,4},{6,7},{7,6},{8,9},{9,8},{10,11... | collective-permute-start | bytes 786440 | tf_op jit(solution)/shard_map/ppermute | solution.py:297
  35.5 4.3 %copy-start.7 = (f32[16,4096]{1,0:T(8,128)}, f32[16,4096]{1,0:T(8,128)S(1)}, u32[]{:S(2)}) copy-start(f32[16,4096]{1,0:T(8,128)S(1)} %collective-permute-done.8.refs_6_) | copy-start | bytes 786436
  35.5 8.0 %collective-permute-start = (s32[45]{0:T(128)S(1)}, s32[45]{0:T(128)S(1)}, u32[]{:S(2)}, u32[]{:S(2)}) collective-permute-start(s32[45]{0:T(128)S(1)} %get-tuple-element.34), channel_id=1, source_target_pairs={{1,4},{5,8},{9,12},{13,16},{17,20},{21,24},{25,28},{6,3},{10,7},{1... | collective-permute-start | bytes 548 | tf_op jit(solution)/shard_map/ppermute | solution.py:337
  39.8 0.7 copy-start.8
  43.4 4.6 %collective-permute-start.10 = (f32[9,16,128]{2,1,0:T(8,128)S(1)}, f32[9,16,128]{2,1,0:T(8,128)S(1)}, u32[]{:S(2)}, u32[]{:S(2)}) collective-permute-start(f32[9,16,128]{2,1,0:T(8,128)S(1)} %get-tuple-element.46), channel_id=1, source_target_pairs={{0,1},{1,0},{2,3},{3,2},{4,5},{5,4},{6,7},{7,6},{8,9},{9,8},{10,11... | collective-permute-start | bytes 221192 | tf_op jit(solution)/shard_map/ppermute | solution.py:390
  43.5 6.3 %collective-permute-start.11 = (f32[9,16,128]{2,1,0:T(8,128)S(1)}, f32[9,16,128]{2,1,0:T(8,128)S(1)}, u32[]{:S(2)}, u32[]{:S(2)}) collective-permute-start(f32[9,16,128]{2,1,0:T(8,128)S(1)} %get-tuple-element.47), channel_id=1, source_target_pairs={{1,2},{3,4},{5,6},{7,8},{9,10},{11,12},{13,14},{15,16},{17,18},{19... | collective-permute-start | bytes 221192 | tf_op jit(solution)/shard_map/ppermute | solution.py:389
  52.6 4.2 %collective-permute-start.12 = (f32[15,16,128]{2,1,0:T(8,128)S(1)}, f32[15,16,128]{2,1,0:T(8,128)S(1)}, u32[]{:S(2)}, u32[]{:S(2)}) collective-permute-start(f32[15,16,128]{2,1,0:T(8,128)S(1)} %get-tuple-element.51), channel_id=1, source_target_pairs={{0,1},{1,0},{2,3},{3,2},{4,5},{5,4},{6,7},{7,6},{8,9},{9,8},{10,11... | collective-permute-start | bytes 368648 | tf_op jit(solution)/shard_map/ppermute | solution.py:390
  54.3 6.9 %collective-permute-start.13 = (f32[15,16,128]{2,1,0:T(8,128)S(1)}, f32[15,16,128]{2,1,0:T(8,128)S(1)}, u32[]{:S(2)}, u32[]{:S(2)}) collective-permute-start(f32[15,16,128]{2,1,0:T(8,128)S(1)} %get-tuple-element.52), channel_id=1, source_target_pairs={{1,2},{3,4},{5,6},{7,8},{9,10},{11,12},{13,14},{15,16},{17,18},{19... | collective-permute-start | bytes 368648 | tf_op jit(solution)/shard_map/ppermute | solution.py:389
  65.7 3.1 %collective-permute-start.14 = (f32[15,16,128]{2,1,0:T(8,128)S(1)}, f32[15,16,128]{2,1,0:T(8,128)S(1)}, u32[]{:S(2)}, u32[]{:S(2)}) collective-permute-start(f32[15,16,128]{2,1,0:T(8,128)S(1)} %get-tuple-element.56), channel_id=1, source_target_pairs={{0,1},{1,0},{2,3},{3,2},{4,5},{5,4},{6,7},{7,6},{8,9},{9,8},{10,11... | collective-permute-start | bytes 368648 | tf_op jit(solution)/shard_map/ppermute | solution.py:390
  66.8 6.5 %collective-permute-start.15 = (f32[15,16,128]{2,1,0:T(8,128)S(1)}, f32[15,16,128]{2,1,0:T(8,128)S(1)}, u32[]{:S(2)}, u32[]{:S(2)}) collective-permute-start(f32[15,16,128]{2,1,0:T(8,128)S(1)} %get-tuple-element.57), channel_id=1, source_target_pairs={{1,2},{3,4},{5,6},{7,8},{9,10},{11,12},{13,14},{15,16},{17,18},{19... | collective-permute-start | bytes 368648 | tf_op jit(solution)/shard_map/ppermute | solution.py:389
  77.8 4.2 %collective-permute-start.16 = (f32[21,16,128]{2,1,0:T(8,128)S(1)}, f32[21,16,128]{2,1,0:T(8,128)S(1)}, u32[]{:S(2)}, u32[]{:S(2)}) collective-permute-start(f32[21,16,128]{2,1,0:T(8,128)S(1)} %get-tuple-element.61), channel_id=1, source_target_pairs={{0,1},{1,0},{2,3},{3,2},{4,5},{5,4},{6,7},{7,6},{8,9},{9,8},{10,11... | collective-permute-start | bytes 516104 | tf_op jit(solution)/shard_map/ppermute | solution.py:390
  79.3 7.0 %collective-permute-start.17 = (f32[21,16,128]{2,1,0:T(8,128)S(1)}, f32[21,16,128]{2,1,0:T(8,128)S(1)}, u32[]{:S(2)}, u32[]{:S(2)}) collective-permute-start(f32[21,16,128]{2,1,0:T(8,128)S(1)} %get-tuple-element.62), channel_id=1, source_target_pairs={{1,2},{3,4},{5,6},{7,8},{9,10},{11,12},{13,14},{15,16},{17,18},{19... | collective-permute-start | bytes 516104 | tf_op jit(solution)/shard_map/ppermute | solution.py:389
  92.6 3.8 %collective-permute-start.19 = (f32[16,16,128]{2,1,0:T(8,128)S(1)}, f32[16,16,128]{2,1,0:T(8,128)S(1)}, u32[]{:S(2)}, u32[]{:S(2)}) collective-permute-start(f32[16,16,128]{2,1,0:T(8,128)S(1)} %shard_map.65.refs_0_), channel_id=1, source_target_pairs={{2,0},{3,1},{0,2},{1,3},{6,4},{7,5},{4,6},{5,7},{10,8},{11,9},{8,1... | collective-permute-start | bytes 393224 | tf_op jit(solution)/shard_map/ppermute | solution.py:293
  92.7 6.5 %collective-permute-start.18 = (f32[16,16,128]{2,1,0:T(8,128)S(1)}, f32[16,16,128]{2,1,0:T(8,128)S(1)}, u32[]{:S(2)}, u32[]{:S(2)}) collective-permute-start(f32[16,16,128]{2,1,0:T(8,128)S(1)} %shard_map.65.refs_0_), channel_id=1, source_target_pairs={{0,1},{1,0},{2,3},{3,2},{4,5},{5,4},{6,7},{7,6},{8,9},{9,8},{10,11... | collective-permute-start | bytes 393224 | tf_op jit(solution)/shard_map/ppermute | solution.py:297
  96.5 3.7 %collective-permute-start.20 = (f32[16,16,128]{2,1,0:T(8,128)S(1)}, f32[16,16,128]{2,1,0:T(8,128)S(1)}, u32[]{:S(2)}, u32[]{:S(2)}) collective-permute-start(f32[16,16,128]{2,1,0:T(8,128)S(1)} %collective-permute-done.19.refs_2_), channel_id=1, source_target_pairs={{0,1},{1,0},{2,3},{3,2},{4,5},{5,4},{6,7},{7,6},{8,9},{9,8},{10,11... | collective-permute-start | bytes 393224 | tf_op jit(solution)/shard_map/ppermute | solution.py:297

commit v4 on v2

v4 whole, which is shorter than its diff:
```python
import functools

import jax
import jax.numpy as jnp
from jax import lax
from jax.experimental import pallas as pl
from jax.experimental.pallas import tpu as pltpu
from jax.sharding import PartitionSpec as P

HB = 3
SWEEPS = 3
DEGREE = 4
APPLIES = SWEEPS * DEGREE

upper_bound = 4.5
lower_bound = 1.35

AXES = ("group", "fold")
F32 = jnp.float32
BF16 = jnp.bfloat16
VMEM = pl.BlockSpec(memory_space=pltpu.VMEM)
SMEM = pl.BlockSpec(memory_space=pltpu.SMEM)
HBM = pl.BlockSpec(memory_space=pltpu.HBM)


def coefficients():
    theta = (upper_bound + lower_bound) / 2.0
    delta = (upper_bound - lower_bound) / 2.0
    pairs = []
    for sweep in range(SWEEPS):
        pairs.append((0.0, 1.0 / theta))
        ratio = delta / theta
        for step in range(1, DEGREE):
            ratio_next = 1.0 / (2.0 * theta / delta - ratio)
            pairs.append((ratio_next * ratio, 2.0 * ratio_next / delta))
            ratio = ratio_next
    return pairs


def params(limit=16):
    return pltpu.CompilerParams(vmem_limit_bytes=limit * 2**20)


def split(value):
    high = value.astype(BF16)
    return high, (value - high.astype(F32)).astype(BF16)


def pick_lanes(window, low, shift):
    lane = lax.broadcasted_iota(jnp.int32, (16, 128), 1)
    turn = (128 - shift) % 128
    first = pltpu.roll(window(low), turn, 1)
    second = pltpu.roll(window(low + 1), turn, 1)
    return jnp.where(lane < 128 - shift, first, second)


def put_payloads(ob, steps, even, u, at, r, pay_a, pay_b):
    h = HB * steps
    inner = h - HB
    for pay, right in ((pay_a, even), (pay_b, jnp.logical_not(even))):
        pay[:h] = u[pl.ds(at + jnp.where(right, ob - h, 0), h)]
        if inner:
            pay[h:] = r[pl.ds(at + jnp.where(right, ob - inner, 0), inner)]


def begin_of(counts, j):
    total = 0
    for i in range(counts.shape[1]):
        total = total + jnp.where(i < j, counts[0, i], 0)
    return total


def holder(fold, folds, d, c):
    return lax.rem(fold // 2 + d, folds // 2) * 2 + jnp.where(c, 1 - fold % 2, fold % 2)


def part_of(fold, folds, backwards):
    return jnp.where(backwards == 1, folds - 1 - fold, fold)


def align_kernel(ob, steps, keys, facts, counts, *refs):
    folds = len(keys)
    sources, (u_out, r_out, pay_a, pay_b), windows, sem = refs[: folds + 1], refs[folds + 1 : folds + 5], refs[-2], refs[-1]
    capacity = sources[0].shape[-1]
    length = windows.shape[-1]
    lane = lax.broadcasted_iota(jnp.int32, (16, 128), 1)
    base = facts[0] * (ob * 128)
    spans, copies = [], []
    for j, (d, c) in enumerate(keys):
        owner = holder(facts[2], folds, d, c)
        start = begin_of(counts, owner)
        first = jnp.clip((base - start) >> 7, 0, (capacity - length) // 128)
        spans.append((start, counts[0, owner], first))
        for i in range(2):
            source = sources[i] if j == 0 else sources[j + 1].at[i]
            source = source.at[:, pl.ds(pl.multiple_of(first * 128, 128), length)]
            copies.append(pltpu.make_async_copy(source, windows.at[2 * j + i], sem.at[2 * j + i]))
    for copy in copies:
        copy.start()
    for copy in copies:
        copy.wait()

    def block(e, carry):
        row = base + e * 128
        totals = [jnp.zeros((16, 128), F32), jnp.zeros((16, 128), F32)]
        for j, (start, count, first) in enumerate(spans):
            at = row - start
            low = (at >> 7) - first
            shift = at & 127
            index = at + lane
            valid = (index >= 0) & (index < count)
            for a in range(2):

                def window(b, held=windows.at[2 * j + a]):
                    b = jnp.clip(b, 0, length // 128 - 1)
                    return held[:, pl.ds(pl.multiple_of(b * 128, 128), 128)]

                totals[a] = jnp.where(valid, pick_lanes(window, low, shift), totals[a])
        u_out[e] = totals[0]
        r_out[e] = totals[1]
        return carry

    lax.fori_loop(0, ob, block, 0, unroll=4)
    put_payloads(ob, steps, facts[1] == 0, u_out, 0, r_out, pay_a, pay_b)


def outward_kernel(folds, halo, width, facts, columns, initial, right_side, blocks, stacked, border, sem):
    own = columns.shape[1]
    size = blocks.shape[0] // own
    part = facts[0]
    pair = [pltpu.make_async_copy(array, stacked.at[i], sem.at[i]) for i, array in enumerate((initial, right_side))]
    for copy in pair:
        copy.start()
    first = jnp.where(part == 0, 0, own - halo)

    @pl.when((part == 0) | (part == folds - 1))
    def _():
        rows = blocks.at[pl.ds(pl.multiple_of(first * size, size), halo * size)]
        copy = pltpu.make_async_copy(rows, border.at[: halo * size], sem.at[2])
        copy.start()
        lane = lax.broadcasted_iota(jnp.int32, (8, 128), 1)
        indices = jnp.zeros((8, 128), jnp.int32)
        for i in range(halo):
            for k in range(width):
                indices = jnp.where(lane == i * width + k, columns[k, first + i], indices)
        border[halo * size :] = indices.astype(F32)
        copy.wait()

    for copy in pair:
        copy.wait()


def gate_kernel(n, *refs):
    del n, refs


def put_row(out, a, raw):
    side = raw.shape[-1]
    for k in range(out.shape[1] // side):
        high, low = split(raw[k * side : (k + 1) * side])
        out[a, k * side : (k + 1) * side, :side] = high.T
        out[a, k * side : (k + 1) * side, side:] = low.T


def prepare_kernel(ob, halo, width, facts, columns, blocks, out, token, offsets, raw, sem):
    rows, size = raw.shape[0], raw.shape[1]
    own = blocks.shape[0] // size
    first = facts[0] * ob - halo

    def copy(a):
        i = pl.multiple_of(jnp.clip(first + a, 0, own - 1) * size, size)
        return pltpu.make_async_copy(blocks.at[pl.ds(i, size)], raw.at[a], sem.at[a])

    for a in range(rows):
        copy(a).start()

    def indices(a, carry):
        i = first + a
        for k in range(width):
            offsets[a * width + k] = columns[k, jnp.clip(i, 0, own - 1)] - HB - i
        return carry

    lax.fori_loop(0, rows, indices, 0)
    token[...] = jnp.zeros_like(token)
    group = 4 if rows % 4 == 0 else 2

    def several(g, carry):
        for s in range(group):
            a = g * group + s
            copy(a).wait()
            put_row(out, a, raw.at[a])
        return carry

    lax.fori_loop(0, rows // group, several, 0)


def border_kernel(ob, folds, halo, width, facts, known, prepared, raw, out, offsets, vector, scalars, sem):
    del prepared
    part = facts[0]
    size = out.shape[1]

    def keep(n, carry):
        offsets[n] = known[n]
        return carry

    lax.fori_loop(0, known.shape[0], keep, 0, unroll=10)

    @pl.when((part == 0) | (part == folds - 1))
    def _():
        vector[...] = raw[halo * size :].astype(jnp.int32)
        copy = pltpu.make_async_copy(vector, scalars, sem)
        copy.start()
        first = jnp.where(part == 0, 0, halo + ob)
        for a in range(halo):
            put_row(out, first + a, raw.at[a * size : (a + 1) * size])
        copy.wait()
        own = ob * folds
        for i in range(halo):
            local = jnp.where(part == 0, own - halo + i, i)
            for k in range(width):
                offset = jnp.clip(scalars[0, i * width + k] - HB - local, -HB, HB)
                offsets[(first + i) * width + k] = offset


def phase_kernel(ob, halo, steps, first, after, pairs, facts, offsets, operator, *refs):
    h = HB * steps
    inner = h - HB
    extent = ob + 2 * h
    width = offsets.shape[0] // (ob + 2 * halo)
    if not first:
        x_in, *refs = refs
    u_in, r_in, got_a, got_b, *refs = refs
    if after:
        x_out, u_out, r_out, pay_a, pay_b, u, r, *pieces = refs
    else:
        x_out, u, r, *pieces = refs
    even = facts[1] == 0
    for got, right in ((got_a, even), (got_b, jnp.logical_not(even))):
        u[pl.ds(jnp.where(right, h + ob, 0), h)] = got[:h]
        if inner:
            r[pl.ds(jnp.where(right, h + ob, HB), inner)] = got[h:]
    u[h : h + ob] = u_in[...]
    r[h : h + ob] = r_in[...]
    high, low = split(u[...])
    pieces[0][:, :16] = high
    pieces[0][:, 16:] = low
    x = None if first else x_in[...]
    for t in range(steps):
        x = u[h : h + ob] if x is None else x + u[h : h + ob]
        now, later = pieces[t % 2], pieces[(t + 1) % 2]
        old, new = pairs[t]
        done = t == steps - 1

        def row(e, carry):
            a = e - h + halo
            left = jnp.concatenate([now[e + offsets[a * width + k]] for k in range(width)], axis=1)
            product = jnp.dot(left, operator[a], preferred_element_type=F32)
            product = product[:16] + product[16:]
            resid = r[e] - (product[:, :128] + product[:, 128:])
            r[e] = resid
            update = new * resid if old == 0.0 else old * u[e] + new * resid
            u[e] = update
            if not done:
                big, small = split(update)
                later[e, :16] = big
                later[e, 16:] = small
            return carry

        lower, upper = HB * (t + 1), extent - HB * (t + 1)
        lax.fori_loop(lower, upper, row, 0, unroll=True)
    if not after:
        x_out[...] = x + u[h : h + ob]
        return
    x_out[...] = x
    u_out[...] = u[h : h + ob]
    r_out[...] = r[h : h + ob]
    put_payloads(ob, after, even, u, h, r, pay_a, pay_b)


def finish_kernel(ob, keys, facts, counts, *refs):
    parts, (out, whole) = refs[:-2], refs[-2:]
    total = whole.shape[0]
    for (d, c), part in zip(keys, parts):
        theirs = part_of(holder(facts[2], len(keys), d, c), len(keys), facts[3])
        whole[pl.ds(theirs * ob, ob)] = part[...]
    start, count = begin_of(counts, facts[2]), counts[0, facts[2]]
    lane = lax.broadcasted_iota(jnp.int32, (16, 128), 1)
    low, shift = start >> 7, start & 127

    def block(b, carry):
        piece = pick_lanes(lambda i: whole[jnp.minimum(i, total - 1)], low + b, shift)
        piece = jnp.where(b * 128 + lane < count, piece, 0.0)
        out[:, pl.ds(pl.multiple_of(b * 128, 128), 128)] = piece
        return carry

    lax.fori_loop(0, out.shape[1] // 128, block, 0, unroll=8)


def over_chips(array, d, folds):
    return lax.ppermute(array, "fold", [((i + 2 * d) % folds, i) for i in range(folds)])


def other_core(array, folds):
    return lax.ppermute(array, "fold", [(i, i ^ 1) for i in range(folds)])


def on_device(right_side, initial, counts, columns, blocks):
    groups, folds = lax.axis_size("group"), lax.axis_size("fold")
    vectors, capacity = right_side.shape
    own, width, side = blocks.shape[0], blocks.shape[1], blocks.shape[2]
    size = width * side
    ob = own // folds
    steps = 3 if ob >= 9 else 2
    halo = HB * (steps - 1)
    rows = ob + 2 * halo
    pairs = coefficients()
    fold = lax.axis_index("fold")
    backwards = lax.axis_index("group") % 2
    part = part_of(fold, folds, backwards)
    devices = groups * folds
    facts = jnp.stack([part, part % 2, fold, backwards]).astype(jnp.int32)
    state = jax.ShapeDtypeStruct((ob, vectors, side), F32)
    operator_shape = pltpu.VMEM((rows, size, 2 * side), BF16)

    payload = jax.ShapeDtypeStruct((2 * HB * steps - HB, vectors, side), F32)

    line = [g * folds + (folds - 1 - p if g % 2 else p) for g in range(groups) for p in range(folds)]

    def swap(first, distance):
        ends = [(line[i], line[i + 1]) for i in range(first, devices - 1, distance)]
        return ends + [(j, i) for i, j in ends]

    swap_a, swap_b, swap_border = swap(0, 2), swap(1, 2), swap(folds - 1, folds)

    turned = columns.T
    flat = pltpu.with_memory_space_constraint(blocks.reshape(own * size, side), pltpu.HBM)
    near = [pltpu.with_memory_space_constraint(array, pltpu.HBM) for array in (initial, right_side)]
    stacked, border = pl.pallas_call(
        functools.partial(outward_kernel, folds, halo, width),
        out_shape=(pltpu.VMEM((2, vectors, capacity), F32), pltpu.VMEM((halo * size + 8, side), F32)),
        in_specs=[SMEM, SMEM, HBM, HBM, HBM],
        out_specs=(VMEM, VMEM),
        scratch_shapes=[pltpu.SemaphoreType.DMA((3,))],
        compiler_params=params(),
    )(facts, turned, *near, flat)
    far = [over_chips(stacked, d, folds) for d in range(1, folds // 2)]
    border = lax.ppermute(border, AXES, swap_border)

    operator, token, offsets = pl.pallas_call(
        functools.partial(prepare_kernel, ob, halo, width),
        out_shape=(operator_shape, jax.ShapeDtypeStruct((8, 128), F32), jax.ShapeDtypeStruct((rows * width,), jnp.int32)),
        in_specs=[SMEM, SMEM, HBM],
        out_specs=(VMEM, VMEM, SMEM),
        scratch_shapes=[
            pltpu.VMEM((rows, size, side), F32),
            pltpu.SemaphoreType.DMA((rows,)),
        ],
        compiler_params=params(),
        cost_estimate=pl.CostEstimate(flops=10**7, bytes_accessed=2 * rows * size * side * 4, transcendentals=0),
    )(facts, turned, flat)

    def gate(arrays, spaces, token):
        return pl.pallas_call(
            functools.partial(gate_kernel, len(arrays)),
            out_shape=tuple(space(array.shape, F32) for array, space in zip(arrays, spaces)),
            in_specs=[pl.BlockSpec(memory_space=space) for space in spaces] + [pl.BlockSpec(memory_space=pl.ANY)],
            out_specs=tuple(pl.BlockSpec(memory_space=space) for space in spaces),
            input_output_aliases={i: i for i in range(len(arrays))},
            compiler_params=params(),
        )(*[pltpu.with_memory_space_constraint(array, space) for array, space in zip(arrays, spaces)], token)

    far = gate(far, [pltpu.HBM] * len(far), token)

    keys, arrays = [], []
    for d, array in enumerate([stacked, *far]):
        keys += [(d, False), (d, True)]
        arrays += ([array] if d else []) + [other_core(array, folds)]
    u, r, pay_a, pay_b = pl.pallas_call(
        functools.partial(align_kernel, ob, steps, keys),
        out_shape=(state, state, payload, payload),
        in_specs=[SMEM, SMEM] + [HBM] * (folds + 1),
        out_specs=(VMEM,) * 4,
        scratch_shapes=[
            pltpu.VMEM((2 * folds, vectors, (ob + 1) * side), F32),
            pltpu.SemaphoreType.DMA((2 * folds,)),
        ],
        compiler_params=params(),
    )(facts, counts, *near, *[pltpu.with_memory_space_constraint(array, pltpu.HBM) for array in arrays])

    operator, offsets = pl.pallas_call(
        functools.partial(border_kernel, ob, folds, halo, width),
        out_shape=(operator_shape, jax.ShapeDtypeStruct((rows * width,), jnp.int32)),
        in_specs=[SMEM, SMEM, VMEM, VMEM],
        out_specs=(VMEM, SMEM),
        input_output_aliases={2: 0},
        scratch_shapes=[
            pltpu.VMEM((8, 128), jnp.int32),
            pltpu.SMEM((8, 128), jnp.int32),
            pltpu.SemaphoreType.DMA(()),
        ],
        compiler_params=params(),
    )(facts, offsets, pltpu.with_memory_space_constraint(operator, pltpu.VMEM), border)
    operator = pltpu.with_memory_space_constraint(operator, pltpu.VMEM)

    x = None
    extent = ob + 2 * HB * steps
    for done in range(0, APPLIES, steps):
        got_a = lax.ppermute(pay_a, AXES, swap_a)
        got_b = lax.ppermute(pay_b, AXES, swap_b)
        first, last = done == 0, done + steps == APPLIES
        outs = pl.pallas_call(
            functools.partial(phase_kernel, ob, halo, steps, first, 0 if last else steps, pairs[done : done + steps]),
            out_shape=state if last else (state, state, state, payload, payload),
            in_specs=[SMEM, SMEM] + [VMEM] * (5 if first else 6),
            out_specs=VMEM if last else (VMEM,) * 5,
            scratch_shapes=[pltpu.VMEM((extent, vectors, side), F32)] * 2
            + [pltpu.VMEM((extent, 2 * vectors, side), BF16)] * 2,
            compiler_params=params(),
        )(facts, offsets, operator, *([] if first else [x]), u, r, got_a, got_b)
        if last:
            x = outs
        else:
            x, u, r, pay_a, pay_b = outs

    parts = []
    for d in range(folds // 2):
        piece = over_chips(x, d, folds) if d else x
        parts += [piece, other_core(piece, folds)]
    return pl.pallas_call(
        functools.partial(finish_kernel, ob, keys),
        out_shape=jax.ShapeDtypeStruct((vectors, capacity), F32),
        in_specs=[SMEM, SMEM] + [VMEM] * folds,
        out_specs=VMEM,
        scratch_shapes=[pltpu.VMEM((own, vectors, side), F32)],
        compiler_params=params(),
    )(facts, counts, *parts)


def solution(mesh):
    placed = (
        P(None, AXES),
        P(None, AXES),
        P("group", None),
        P("group", None),
        P("group", None, None, None),
    )
    return jax.shard_map(on_device, mesh=mesh, in_specs=placed, out_specs=P(None, AXES), check_vma=False)
```

time: 118 us -> 83.8 us (0.71)
  starting transfers between devices: 52 us -> 23.3 us
  local copies, waits for them, and re-layouts: 17.5 us -> 2.32 us
  waiting for transfers between devices: 15.6 us -> 26.1 us
    ppermute x6 -> x4, starting transfers between devices: 24.3 us -> 4.89 us  [other_core(): return lax.ppermute(array, 'fold', [(i, i ^ 1) for i in range(folds)])]
    unnamed x38 -> x10, local copies, waits for them, and re-layouts: 13.5 us -> 2.32 us
    ppermute x4, starting transfers between devices: 14.5 us -> 8.91 us  [on_device(): got_b = lax.ppermute(pay_b, AXES, swap_b)]
    ppermute x4, waiting for transfers between devices: 10.8 us -> 15.5 us  [on_device(): got_b = lax.ppermute(pay_b, AXES, swap_b)]
    ppermute x3 -> x2, waiting for transfers between devices: 3.79 us -> 7.83 us  [over_chips(): lax.ppermute(array, 'fold', [((i + 2 * d) % folds, i) for i in range(fold...]
    dynamic_slice x4 -> x0, local copies, waits for them, and re-layouts: 3.84 us -> none  [the longest x1 3.59 us: on_device(): lax.dynamic_slice_in_dim(blocks, at, HB, 0)]
    ppermute x4 -> x1, starting transfers between devices: 2.92 us -> 0.79 us  [on_device(): border = lax.ppermute(border, AXES, swap_border)]
    ppermute x6 -> x4, waiting for transfers between devices: 1 us -> 2.73 us  [other_core(): return lax.ppermute(array, 'fold', [(i, i ^ 1) for i in range(folds)])]
  transfers between devices with their start and end apart: 21 -> 15, of which waited for: 5 -> 8; matrix products, arithmetic and copies ran while one was open for 1% -> 0% of each run, Pallas kernels for 20% -> 13%
where the time goes in v4:
time: 83.8 us; the launch traced here: 83.5 us
  Pallas kernels  31.5 us (38%)
  waiting for transfers between devices  26.1 us (31%)
  starting transfers between devices  23.3 us (28%)
  local copies, waits for them, and re-layouts  2.32 us (3%)
    pallas_call x4, Pallas kernels, on_device(): pl.pallas_call(functools.partial(phase_kernel, ob, halo, steps, first, 0...  17.6 us
    ppermute x4, waiting for transfers between devices, on_device(): got_b = lax.ppermute(pay_b, AXES, swap_b)  15.5 us
    ppermute x4, starting transfers between devices, on_device(): got_b = lax.ppermute(pay_b, AXES, swap_b)  8.91 us
    ppermute x2, waiting for transfers between devices, over_chips(): lax.ppermute(array, 'fold', [((i + 2 * d) % folds, i) for i in range(fold...  7.83 us
    pallas_call x1, Pallas kernels, on_device(): pl.pallas_call(functools.partial(prepare_kernel, ob, halo, width), out_sh...  6.31 us
    ppermute x4, starting transfers between devices, other_core(): return lax.ppermute(array, 'fold', [(i, i ^ 1) for i in range(folds)])  4.89 us
    ppermute x4, starting transfers between devices, on_device(): got_a = lax.ppermute(pay_a, AXES, swap_a)  4.39 us
    ppermute x2, starting transfers between devices, over_chips(): lax.ppermute(array, 'fold', [((i + 2 * d) % folds, i) for i in range(fold...  4.35 us
  transfers between devices with their start and end apart: 15, of which 8 were waited for; matrix products, arithmetic and copies ran while one was open for 0% of the time, Pallas kernels for 13%

profile of v4, /device:TPU:9, one launch (start us, length us, event | category | flops | bytes accessed | tf_op | source)
XLA Modules:
  0.0 83.5 jit_solution(37729376085084903)
XLA Ops:
  0.0 0.1 pad_add_fusion.facts
  0.1 0.0 copy-start
  0.1 0.7 copy-done
  0.8 1.7 %shard_map.56 = (f32[2,16,4096]{2,1,0:T(8,128)S(1)}, f32[3848,128]{1,0:T(8,128)S(1)}) custom-call(s32[4]{0:T(128)S(1)} %pad_add_fusion.facts, s32[5,64]{1,0:T(8,128)S(1)} %bitcast.6, f32[16,4096]{1,0:T(8,128)} %refs_0_.1, f32[16,4096]{1,0:T(8,128)} %refs_1_.1, f32[40960,128]{1,0:T(8,128)} %bitcast.8), custom_call_target="tpu_custom_call" | custom-call | tf_op jit(solution)/shard_map/pallas_call | solution.py:338
  2.4 0.8 collective-permute-start
  3.2 0.0 copy-start.1
  3.2 4.3 %collective-permute-start.2 = (f32[2,16,4096]{2,1,0:T(8,128)S(1)}, f32[2,16,4096]{2,1,0:T(8,128)S(1)}, u32[]{:S(2)}, u32[]{:S(2)}) collective-permute-start(f32[2,16,4096]{2,1,0:T(8,128)S(1)} %get-tuple-element.36), channel_id=1, source_target_pairs={{2,0},{3,1},{0,2},{1,3},{6,4},{7,5},{4,6},{5,7},{10,8},{11,9},{8,1... | collective-permute-start | bytes 1572872 | tf_op jit(solution)/shard_map/ppermute | solution.py:300
  7.6 0.0 collective-permute-start.1
  7.6 6.3 %shard_map.55 = (bf16[28,640,256]{2,1,0:T(8,128)(2,1)S(1)}, f32[8,128]{1,0:T(8,128)S(1)}, s32[140]{0:T(256)S(1)}) custom-call(s32[4]{0:T(128)S(1)} %pad_add_fusion.facts, s32[5,64]{1,0:T(8,128)S(1)} %bitcast.7, f32[40960,128]{1,0:T(8,128)} %bitcast.9), custom_call_target="tpu_custom_call" | custom-call | flops 10000000 | bytes 18350080 | tf_op jit(solution)/shard_map/pallas_call | solution.py:349
  13.9 5.3 %collective-permute-done.2.refs_0_ = f32[2,16,4096]{2,1,0:T(8,128)S(1)} collective-permute-done((f32[2,16,4096]{2,1,0:T(8,128)S(1)}, f32[2,16,4096]{2,1,0:T(8,128)S(1)}, u32[]{:S(2)}, u32[]{:S(2)}) %collective-permute-start.2) | collective-permute-done | bytes 524320 | tf_op jit(solution)/shard_map/ppermute | solution.py:300
  19.2 0.0 copy-start.2
  19.2 0.8 copy-done.2
  20.0 1.3 %collective-permute-start.3 = (f32[2,16,4096]{2,1,0:T(8,128)}, f32[2,16,4096]{2,1,0:T(8,128)S(1)}, u32[]{:S(2)}, u32[]{:S(2)}) collective-permute-start(f32[2,16,4096]{2,1,0:T(8,128)} %shard_map.58.refs_3_), channel_id=1, source_target_pairs={{0,1},{1,0},{2,3},{3,2},{4,5},{5,4},{6,7},{7,6},{8,9},{9,8},{10,11... | collective-permute-start | bytes 1572872 | tf_op jit(solution)/shard_map/ppermute | solution.py:304
  21.3 0.0 collective-permute-done.1.refs_2_
  21.3 1.7 %collective-permute-done.3.refs_4_ = f32[2,16,4096]{2,1,0:T(8,128)S(1)} collective-permute-done((f32[2,16,4096]{2,1,0:T(8,128)}, f32[2,16,4096]{2,1,0:T(8,128)S(1)}, u32[]{:S(2)}, u32[]{:S(2)}) %collective-permute-start.3) | collective-permute-done | bytes 524320 | tf_op jit(solution)/shard_map/ppermute | solution.py:304
  23.0 0.0 copy-done.3
  23.0 0.8 copy-done.4
  23.8 0.0 copy-done.1
  23.8 2.8 %shard_map.59 = (f32[16,16,128]{2,1,0:T(8,128)S(1)}, f32[16,16,128]{2,1,0:T(8,128)S(1)}, f32[15,16,128]{2,1,0:T(8,128)S(1)}, f32[15,16,128]{2,1,0:T(8,128)S(1)}) custom-call(s32[4]{0:T(128)S(1)} %pad_add_fusion.facts, s32[1,4]{1,0:T(1,128)S(1)} %copy-done.1, f32[16,4096]{1,0:T(8,128)} %refs_0_.1, f32[16,4096]{1,0:T(8,128)} %refs_1_.1, ...), custom_call_target="tpu_custom_call" | custom-call | tf_op jit(solution)/shard_map/pallas_call | solution.py:378
  26.7 0.4 collective-permute-start.4
  27.1 3.0 %collective-permute-start.5 = (f32[15,16,128]{2,1,0:T(8,128)S(1)}, f32[15,16,128]{2,1,0:T(8,128)S(1)}, u32[]{:S(2)}, u32[]{:S(2)}) collective-permute-start(f32[15,16,128]{2,1,0:T(8,128)S(1)} %get-tuple-element.41), channel_id=1, source_target_pairs={{1,2},{3,7},{6,5},{4,8},{9,10},{11,15},{14,13},{12,16},{17,18},{19... | collective-permute-start | bytes 368648 | tf_op jit(solution)/shard_map/ppermute | solution.py:409
  30.1 0.0 collective-permute-done.raw
  30.1 1.4 %shard_map.57 = (bf16[28,640,256]{2,1,0:T(8,128)(2,1)S(1)}, s32[140]{0:T(256)S(1)}) custom-call(s32[4]{0:T(128)S(1)} %pad_add_fusion.facts, s32[140]{0:T(256)S(1)} %get-tuple-element.31.known, bf16[28,640,256]{2,1,0:T(8,128)(2,1)S(1)} %get-tuple-element.32.prepared, f32[3848,128]{1,0:T(8,128)S(1)} %collective-permute-done.raw), custom_call_target="tpu_custom_call", output_to_operand_aliasing={{0}: (2, {})} | custom-call | tf_op jit(solution)/shard_map/pallas_call | solution.py:390
  31.5 0.0 collective-permute-done.4.refs_2_
  31.5 2.1 %collective-permute-done.5.refs_3_ = f32[15,16,128]{2,1,0:T(8,128)S(1)} collective-permute-done((f32[15,16,128]{2,1,0:T(8,128)S(1)}, f32[15,16,128]{2,1,0:T(8,128)S(1)}, u32[]{:S(2)}, u32[]{:S(2)}) %collective-permute-start.5) | collective-permute-done | bytes 122912 | tf_op jit(solution)/shard_map/ppermute | solution.py:409
  33.6 4.4 %shard_map.60 = (f32[16,16,128]{2,1,0:T(8,128)S(1)}, f32[16,16,128]{2,1,0:T(8,128)S(1)}, f32[16,16,128]{2,1,0:T(8,128)S(1)}, f32[15,16,128]{2,1,0:T(8,128)S(1)}, f32[15,16,128]{2,1,0:T(8,128)S(1)}) custom-call(s32[4]{0:T(128)S(1)} %pad_add_fusion.facts, s32[140]{0:T(256)S(1)} %get-tuple-element.34.offsets, ...), custom_call_target="tpu_custom_call" | custom-call | tf_op jit(solution)/shard_map/pallas_call | solution.py:411
  38.0 1.4 %collective-permute-start.6 = (f32[15,16,128]{2,1,0:T(8,128)S(1)}, f32[15,16,128]{2,1,0:T(8,128)S(1)}, u32[]{:S(2)}, u32[]{:S(2)}) collective-permute-start(f32[15,16,128]{2,1,0:T(8,128)S(1)} %get-tuple-element.45), channel_id=1, source_target_pairs={{0,1},{2,3},{7,6},{5,4},{8,9},{10,11},{15,14},{13,12},{16,17},{18,... | collective-permute-start | bytes 368648 | tf_op jit(solution)/shard_map/ppermute | solution.py:408
  39.4 1.9 %collective-permute-start.7 = (f32[15,16,128]{2,1,0:T(8,128)S(1)}, f32[15,16,128]{2,1,0:T(8,128)S(1)}, u32[]{:S(2)}, u32[]{:S(2)}) collective-permute-start(f32[15,16,128]{2,1,0:T(8,128)S(1)} %get-tuple-element.46), channel_id=1, source_target_pairs={{1,2},{3,7},{6,5},{4,8},{9,10},{11,15},{14,13},{12,16},{17,18},{19... | collective-permute-start | bytes 368648 | tf_op jit(solution)/shard_map/ppermute | solution.py:409
  41.3 0.0 collective-permute-done.6.refs_3_
  41.3 4.6 %collective-permute-done.7.refs_4_ = f32[15,16,128]{2,1,0:T(8,128)S(1)} collective-permute-done((f32[15,16,128]{2,1,0:T(8,128)S(1)}, f32[15,16,128]{2,1,0:T(8,128)S(1)}, u32[]{:S(2)}, u32[]{:S(2)}) %collective-permute-start.7) | collective-permute-done | bytes 122912 | tf_op jit(solution)/shard_map/ppermute | solution.py:409
  45.9 4.4 %shard_map.61 = (f32[16,16,128]{2,1,0:T(8,128)S(1)}, f32[16,16,128]{2,1,0:T(8,128)S(1)}, f32[16,16,128]{2,1,0:T(8,128)S(1)}, f32[15,16,128]{2,1,0:T(8,128)S(1)}, f32[15,16,128]{2,1,0:T(8,128)S(1)}) custom-call(s32[4]{0:T(128)S(1)} %pad_add_fusion.facts, s32[140]{0:T(256)S(1)} %get-tuple-element.34.offsets, ...), custom_call_target="tpu_custom_call" | custom-call | tf_op jit(solution)/shard_map/pallas_call | solution.py:411
  50.3 1.3 %collective-permute-start.8 = (f32[15,16,128]{2,1,0:T(8,128)S(1)}, f32[15,16,128]{2,1,0:T(8,128)S(1)}, u32[]{:S(2)}, u32[]{:S(2)}) collective-permute-start(f32[15,16,128]{2,1,0:T(8,128)S(1)} %get-tuple-element.50), channel_id=1, source_target_pairs={{0,1},{2,3},{7,6},{5,4},{8,9},{10,11},{15,14},{13,12},{16,17},{18,... | collective-permute-start | bytes 368648 | tf_op jit(solution)/shard_map/ppermute | solution.py:408
  51.5 1.9 %collective-permute-start.9 = (f32[15,16,128]{2,1,0:T(8,128)S(1)}, f32[15,16,128]{2,1,0:T(8,128)S(1)}, u32[]{:S(2)}, u32[]{:S(2)}) collective-permute-start(f32[15,16,128]{2,1,0:T(8,128)S(1)} %get-tuple-element.51), channel_id=1, source_target_pairs={{1,2},{3,7},{6,5},{4,8},{9,10},{11,15},{14,13},{12,16},{17,18},{19... | collective-permute-start | bytes 368648 | tf_op jit(solution)/shard_map/ppermute | solution.py:409
  53.5 0.0 collective-permute-done.8.refs_3_
  53.5 4.6 %collective-permute-done.9.refs_4_ = f32[15,16,128]{2,1,0:T(8,128)S(1)} collective-permute-done((f32[15,16,128]{2,1,0:T(8,128)S(1)}, f32[15,16,128]{2,1,0:T(8,128)S(1)}, u32[]{:S(2)}, u32[]{:S(2)}) %collective-permute-start.9) | collective-permute-done | bytes 122912 | tf_op jit(solution)/shard_map/ppermute | solution.py:409
  58.0 4.4 %shard_map.62 = (f32[16,16,128]{2,1,0:T(8,128)S(1)}, f32[16,16,128]{2,1,0:T(8,128)S(1)}, f32[16,16,128]{2,1,0:T(8,128)S(1)}, f32[15,16,128]{2,1,0:T(8,128)S(1)}, f32[15,16,128]{2,1,0:T(8,128)S(1)}) custom-call(s32[4]{0:T(128)S(1)} %pad_add_fusion.facts, s32[140]{0:T(256)S(1)} %get-tuple-element.34.offsets, ...), custom_call_target="tpu_custom_call" | custom-call | tf_op jit(solution)/shard_map/pallas_call | solution.py:411
  62.4 1.3 %collective-permute-start.10 = (f32[15,16,128]{2,1,0:T(8,128)S(1)}, f32[15,16,128]{2,1,0:T(8,128)S(1)}, u32[]{:S(2)}, u32[]{:S(2)}) collective-permute-start(f32[15,16,128]{2,1,0:T(8,128)S(1)} %get-tuple-element.55), channel_id=1, source_target_pairs={{0,1},{2,3},{7,6},{5,4},{8,9},{10,11},{15,14},{13,12},{16,17},{18,... | collective-permute-start | bytes 368648 | tf_op jit(solution)/shard_map/ppermute | solution.py:408
  63.7 2.1 %collective-permute-start.11 = (f32[15,16,128]{2,1,0:T(8,128)S(1)}, f32[15,16,128]{2,1,0:T(8,128)S(1)}, u32[]{:S(2)}, u32[]{:S(2)}) collective-permute-start(f32[15,16,128]{2,1,0:T(8,128)S(1)} %get-tuple-element.56), channel_id=1, source_target_pairs={{1,2},{3,7},{6,5},{4,8},{9,10},{11,15},{14,13},{12,16},{17,18},{19... | collective-permute-start | bytes 368648 | tf_op jit(solution)/shard_map/ppermute | solution.py:409
  65.8 0.0 collective-permute-done.10.refs_3_
  65.8 4.4 %collective-permute-done.11.refs_4_ = f32[15,16,128]{2,1,0:T(8,128)S(1)} collective-permute-done((f32[15,16,128]{2,1,0:T(8,128)S(1)}, f32[15,16,128]{2,1,0:T(8,128)S(1)}, u32[]{:S(2)}, u32[]{:S(2)}) %collective-permute-start.11) | collective-permute-done | bytes 122912 | tf_op jit(solution)/shard_map/ppermute | solution.py:409
  70.2 4.4 %shard_map.63.refs_0_ = f32[16,16,128]{2,1,0:T(8,128)S(1)} custom-call(s32[4]{0:T(128)S(1)} %pad_add_fusion.facts, s32[140]{0:T(256)S(1)} %get-tuple-element.34.offsets, bf16[28,640,256]{2,1,0:T(8,128)(2,1)S(1)} %get-tuple-element.35.operator, f32[16,16,128]{2,1,0:T(8,128)S(1)} %get-tuple-element.52.refs_0_, f32[16,16,128]{2,1,0:T(8,128)S(1)} %get-tuple-element.53.refs_1_, ...), custom_call_target="tpu_custom_call" | custom-call | tf_op jit(solution)/shard_map/pallas_call | solution.py:411
  74.6 0.0 collective-permute-start.13
  74.6 1.3 %collective-permute-start.12 = (f32[16,16,128]{2,1,0:T(8,128)S(1)}, f32[16,16,128]{2,1,0:T(8,128)S(1)}, u32[]{:S(2)}, u32[]{:S(2)}) collective-permute-start(f32[16,16,128]{2,1,0:T(8,128)S(1)} %shard_map.63.refs_0_), channel_id=1, source_target_pairs={{0,1},{1,0},{2,3},{3,2},{4,5},{5,4},{6,7},{7,6},{8,9},{9,8},{10,11... | collective-permute-start | bytes 393224 | tf_op jit(solution)/shard_map/ppermute | solution.py:304
  75.9 2.5 %collective-permute-done.13.refs_2_ = f32[16,16,128]{2,1,0:T(8,128)S(1)} collective-permute-done((f32[16,16,128]{2,1,0:T(8,128)S(1)}, f32[16,16,128]{2,1,0:T(8,128)S(1)}, u32[]{:S(2)}, u32[]{:S(2)}) %collective-permute-start.13) | collective-permute-done | bytes 131104 | tf_op jit(solution)/shard_map/ppermute | solution.py:300
  78.4 2.3 %collective-permute-start.14 = (f32[16,16,128]{2,1,0:T(8,128)S(1)}, f32[16,16,128]{2,1,0:T(8,128)S(1)}, u32[]{:S(2)}, u32[]{:S(2)}) collective-permute-start(f32[16,16,128]{2,1,0:T(8,128)S(1)} %collective-permute-done.13.refs_2_), channel_id=1, source_target_pairs={{0,1},{1,0},{2,3},{3,2},{4,5},{5,4},{6,7},{7,6},{8,9},{9,8},{10,11... | collective-permute-start | bytes 393224 | tf_op jit(solution)/shard_map/ppermute | solution.py:304
  80.8 0.0 collective-permute-done.12.refs_1_
  80.8 1.0 %collective-permute-done.14.refs_3_ = f32[16,16,128]{2,1,0:T(8,128)S(1)} collective-permute-done((f32[16,16,128]{2,1,0:T(8,128)S(1)}, f32[16,16,128]{2,1,0:T(8,128)S(1)}, u32[]{:S(2)}, u32[]{:S(2)}) %collective-permute-start.14) | collective-permute-done | bytes 131104 | tf_op jit(solution)/shard_map/ppermute | solution.py:304
  81.8 1.7 %shard_map.64 = f32[16,4096]{1,0:T(8,128)} custom-call(s32[4]{0:T(128)S(1)} %pad_add_fusion.facts, s32[1,4]{1,0:T(1,128)S(1)} %copy-done.1, f32[16,16,128]{2,1,0:T(8,128)S(1)} %shard_map.63.refs_0_, f32[16,16,128]{2,1,0:T(8,128)S(1)} %collective-permute-done.12.refs_1_, f32[16,16,128]{2,1,0:T(8,128)S(1)} %collective-permute-done.13.refs_2_, ...), custom_call_target="tpu_custom_call" | custom-call | tf_op jit(solution)/shard_map/pallas_call | solution.py:429
  (3 shorter events, 0.0 us)
Async XLA Ops:
  0.1 0.7 copy-start
  2.4 27.7 %collective-permute-start = (f32[3848,128]{1,0:T(8,128)S(1)}, f32[3848,128]{1,0:T(8,128)S(1)}, u32[]{:S(2)}, u32[]{:S(2)}) collective-permute-start(f32[3848,128]{1,0:T(8,128)S(1)} %get-tuple-element.33), channel_id=1, source_target_pairs={{3,7},{4,8},{11,15},{12,16},{19,23},{20,24},{27,31},{7,3},{8,4},{1... | collective-permute-start | bytes 5910536 | tf_op jit(solution)/shard_map/ppermute | solution.py:347
  3.2 20.6 %copy-start.1 = (s32[1,4]{1,0:T(1,128)S(1)}, s32[1,4]{1,0:T(1,128)}, u32[]{:S(2)}) copy-start(s32[1,4]{1,0:T(1,128)} %counts.3) | copy-start | bytes 52
  3.2 15.9 %collective-permute-start.2 = (f32[2,16,4096]{2,1,0:T(8,128)S(1)}, f32[2,16,4096]{2,1,0:T(8,128)S(1)}, u32[]{:S(2)}, u32[]{:S(2)}) collective-permute-start(f32[2,16,4096]{2,1,0:T(8,128)S(1)} %get-tuple-element.36), channel_id=1, source_target_pairs={{2,0},{3,1},{0,2},{1,3},{6,4},{7,5},{4,6},{5,7},{10,8},{11,9},{8,1... | collective-permute-start | bytes 1572872 | tf_op jit(solution)/shard_map/ppermute | solution.py:300
  7.6 13.7 %collective-permute-start.1 = (f32[2,16,4096]{2,1,0:T(8,128)S(1)}, f32[2,16,4096]{2,1,0:T(8,128)S(1)}, u32[]{:S(2)}, u32[]{:S(2)}) collective-permute-start(f32[2,16,4096]{2,1,0:T(8,128)S(1)} %get-tuple-element.36), channel_id=1, source_target_pairs={{0,1},{1,0},{2,3},{3,2},{4,5},{5,4},{6,7},{7,6},{8,9},{9,8},{10,11... | collective-permute-start | bytes 1572872 | tf_op jit(solution)/shard_map/ppermute | solution.py:304
  19.2 0.8 copy-start.2
  20.0 3.0 %collective-permute-start.3 = (f32[2,16,4096]{2,1,0:T(8,128)}, f32[2,16,4096]{2,1,0:T(8,128)S(1)}, u32[]{:S(2)}, u32[]{:S(2)}) collective-permute-start(f32[2,16,4096]{2,1,0:T(8,128)} %shard_map.58.refs_3_), channel_id=1, source_target_pairs={{0,1},{1,0},{2,3},{3,2},{4,5},{5,4},{6,7},{7,6},{8,9},{9,8},{10,11... | collective-permute-start | bytes 1572872 | tf_op jit(solution)/shard_map/ppermute | solution.py:304
  21.3 1.7 %copy-start.3 = (f32[2,16,4096]{2,1,0:T(8,128)}, f32[2,16,4096]{2,1,0:T(8,128)S(1)}, u32[]{:S(2)}) copy-start(f32[2,16,4096]{2,1,0:T(8,128)S(1)} %collective-permute-done.1.refs_2_) | copy-start | bytes 1572868
  23.0 0.8 copy-start.4
  26.7 4.8 %collective-permute-start.4 = (f32[15,16,128]{2,1,0:T(8,128)S(1)}, f32[15,16,128]{2,1,0:T(8,128)S(1)}, u32[]{:S(2)}, u32[]{:S(2)}) collective-permute-start(f32[15,16,128]{2,1,0:T(8,128)S(1)} %get-tuple-element.40), channel_id=1, source_target_pairs={{0,1},{2,3},{7,6},{5,4},{8,9},{10,11},{15,14},{13,12},{16,17},{18,... | collective-permute-start | bytes 368648 | tf_op jit(solution)/shard_map/ppermute | solution.py:408
  27.1 6.5 %collective-permute-start.5 = (f32[15,16,128]{2,1,0:T(8,128)S(1)}, f32[15,16,128]{2,1,0:T(8,128)S(1)}, u32[]{:S(2)}, u32[]{:S(2)}) collective-permute-start(f32[15,16,128]{2,1,0:T(8,128)S(1)} %get-tuple-element.41), channel_id=1, source_target_pairs={{1,2},{3,7},{6,5},{4,8},{9,10},{11,15},{14,13},{12,16},{17,18},{19... | collective-permute-start | bytes 368648 | tf_op jit(solution)/shard_map/ppermute | solution.py:409
  38.0 3.3 %collective-permute-start.6 = (f32[15,16,128]{2,1,0:T(8,128)S(1)}, f32[15,16,128]{2,1,0:T(8,128)S(1)}, u32[]{:S(2)}, u32[]{:S(2)}) collective-permute-start(f32[15,16,128]{2,1,0:T(8,128)S(1)} %get-tuple-element.45), channel_id=1, source_target_pairs={{0,1},{2,3},{7,6},{5,4},{8,9},{10,11},{15,14},{13,12},{16,17},{18,... | collective-permute-start | bytes 368648 | tf_op jit(solution)/shard_map/ppermute | solution.py:408
  39.4 6.5 %collective-permute-start.7 = (f32[15,16,128]{2,1,0:T(8,128)S(1)}, f32[15,16,128]{2,1,0:T(8,128)S(1)}, u32[]{:S(2)}, u32[]{:S(2)}) collective-permute-start(f32[15,16,128]{2,1,0:T(8,128)S(1)} %get-tuple-element.46), channel_id=1, source_target_pairs={{1,2},{3,7},{6,5},{4,8},{9,10},{11,15},{14,13},{12,16},{17,18},{19... | collective-permute-start | bytes 368648 | tf_op jit(solution)/shard_map/ppermute | solution.py:409
  50.3 3.2 %collective-permute-start.8 = (f32[15,16,128]{2,1,0:T(8,128)S(1)}, f32[15,16,128]{2,1,0:T(8,128)S(1)}, u32[]{:S(2)}, u32[]{:S(2)}) collective-permute-start(f32[15,16,128]{2,1,0:T(8,128)S(1)} %get-tuple-element.50), channel_id=1, source_target_pairs={{0,1},{2,3},{7,6},{5,4},{8,9},{10,11},{15,14},{13,12},{16,17},{18,... | collective-permute-start | bytes 368648 | tf_op jit(solution)/shard_map/ppermute | solution.py:408
  51.5 6.5 %collective-permute-start.9 = (f32[15,16,128]{2,1,0:T(8,128)S(1)}, f32[15,16,128]{2,1,0:T(8,128)S(1)}, u32[]{:S(2)}, u32[]{:S(2)}) collective-permute-start(f32[15,16,128]{2,1,0:T(8,128)S(1)} %get-tuple-element.51), channel_id=1, source_target_pairs={{1,2},{3,7},{6,5},{4,8},{9,10},{11,15},{14,13},{12,16},{17,18},{19... | collective-permute-start | bytes 368648 | tf_op jit(solution)/shard_map/ppermute | solution.py:409
  62.4 3.4 %collective-permute-start.10 = (f32[15,16,128]{2,1,0:T(8,128)S(1)}, f32[15,16,128]{2,1,0:T(8,128)S(1)}, u32[]{:S(2)}, u32[]{:S(2)}) collective-permute-start(f32[15,16,128]{2,1,0:T(8,128)S(1)} %get-tuple-element.55), channel_id=1, source_target_pairs={{0,1},{2,3},{7,6},{5,4},{8,9},{10,11},{15,14},{13,12},{16,17},{18,... | collective-permute-start | bytes 368648 | tf_op jit(solution)/shard_map/ppermute | solution.py:408
  63.7 6.5 %collective-permute-start.11 = (f32[15,16,128]{2,1,0:T(8,128)S(1)}, f32[15,16,128]{2,1,0:T(8,128)S(1)}, u32[]{:S(2)}, u32[]{:S(2)}) collective-permute-start(f32[15,16,128]{2,1,0:T(8,128)S(1)} %get-tuple-element.56), channel_id=1, source_target_pairs={{1,2},{3,7},{6,5},{4,8},{9,10},{11,15},{14,13},{12,16},{17,18},{19... | collective-permute-start | bytes 368648 | tf_op jit(solution)/shard_map/ppermute | solution.py:409
  74.6 3.8 %collective-permute-start.13 = (f32[16,16,128]{2,1,0:T(8,128)S(1)}, f32[16,16,128]{2,1,0:T(8,128)S(1)}, u32[]{:S(2)}, u32[]{:S(2)}) collective-permute-start(f32[16,16,128]{2,1,0:T(8,128)S(1)} %shard_map.63.refs_0_), channel_id=1, source_target_pairs={{2,0},{3,1},{0,2},{1,3},{6,4},{7,5},{4,6},{5,7},{10,8},{11,9},{8,1... | collective-permute-start | bytes 393224 | tf_op jit(solution)/shard_map/ppermute | solution.py:300
  74.6 6.2 %collective-permute-start.12 = (f32[16,16,128]{2,1,0:T(8,128)S(1)}, f32[16,16,128]{2,1,0:T(8,128)S(1)}, u32[]{:S(2)}, u32[]{:S(2)}) collective-permute-start(f32[16,16,128]{2,1,0:T(8,128)S(1)} %shard_map.63.refs_0_), channel_id=1, source_target_pairs={{0,1},{1,0},{2,3},{3,2},{4,5},{5,4},{6,7},{7,6},{8,9},{9,8},{10,11... | collective-permute-start | bytes 393224 | tf_op jit(solution)/shard_map/ppermute | solution.py:304
  78.4 3.3 %collective-permute-start.14 = (f32[16,16,128]{2,1,0:T(8,128)S(1)}, f32[16,16,128]{2,1,0:T(8,128)S(1)}, u32[]{:S(2)}, u32[]{:S(2)}) collective-permute-start(f32[16,16,128]{2,1,0:T(8,128)S(1)} %collective-permute-done.13.refs_2_), channel_id=1, source_target_pairs={{0,1},{1,0},{2,3},{3,2},{4,5},{5,4},{6,7},{7,6},{8,9},{9,8},{10,11... | collective-permute-start | bytes 393224 | tf_op jit(solution)/shard_map/ppermute | solution.py:304

commit v5 on v4

v5 whole, which is shorter than its diff:
```python
import functools

import jax
import jax.numpy as jnp
from jax import lax
from jax.experimental import pallas as pl
from jax.experimental.pallas import tpu as pltpu
from jax.sharding import PartitionSpec as P

HB = 3
SWEEPS = 3
DEGREE = 4
APPLIES = SWEEPS * DEGREE

upper_bound = 4.5
lower_bound = 1.35

AXES = ("group", "fold")
F32 = jnp.float32
BF16 = jnp.bfloat16
VMEM = pl.BlockSpec(memory_space=pltpu.VMEM)
SMEM = pl.BlockSpec(memory_space=pltpu.SMEM)
HBM = pl.BlockSpec(memory_space=pltpu.HBM)


def coefficients():
    theta = (upper_bound + lower_bound) / 2.0
    delta = (upper_bound - lower_bound) / 2.0
    pairs = []
    for sweep in range(SWEEPS):
        pairs.append((0.0, 1.0 / theta))
        ratio = delta / theta
        for step in range(1, DEGREE):
            ratio_next = 1.0 / (2.0 * theta / delta - ratio)
            pairs.append((ratio_next * ratio, 2.0 * ratio_next / delta))
            ratio = ratio_next
    return pairs


def params(limit=16):
    return pltpu.CompilerParams(vmem_limit_bytes=limit * 2**20)


def split(value):
    high = value.astype(BF16)
    return high, (value - high.astype(F32)).astype(BF16)


def pick_lanes(window, low, shift):
    lane = lax.broadcasted_iota(jnp.int32, (16, 128), 1)
    turn = (128 - shift) % 128
    first = pltpu.roll(window(low), turn, 1)
    second = pltpu.roll(window(low + 1), turn, 1)
    return jnp.where(lane < 128 - shift, first, second)


def sides(even, right_is_a):
    return even if right_is_a else jnp.logical_not(even)


def put_payload(ob, steps, right, u, r, pay):
    h = HB * steps
    inner = h - HB
    pay[:h] = u[pl.ds(h + jnp.where(right, ob - h, 0), h)]
    if inner:
        pay[h:] = r[pl.ds(h + jnp.where(right, ob - inner, 0), inner)]


def take_payload(ob, steps, right, got, u, r, now):
    h = HB * steps
    inner = h - HB
    at = jnp.where(right, h + ob, 0)
    u[pl.ds(at, h)] = got[:h]
    if inner:
        r[pl.ds(jnp.where(right, h + ob, HB), inner)] = got[h:]
    high, low = split(got[:h])
    now[pl.ds(at, h), :16] = high
    now[pl.ds(at, h), 16:] = low


def begin_of(counts, j):
    total = 0
    for i in range(counts.shape[1]):
        total = total + jnp.where(i < j, counts[0, i], 0)
    return total


def holder(fold, folds, d, c):
    return lax.rem(fold // 2 + d, folds // 2) * 2 + jnp.where(c, 1 - fold % 2, fold % 2)


def part_of(fold, folds, backwards):
    return jnp.where(backwards == 1, folds - 1 - fold, fold)


def align_kernel(ob, steps, keys, facts, counts, *refs):
    folds = len(keys)
    sources, (x, u, r, now, later, pay_a, pay_b) = refs[:folds], refs[folds:]
    del x, later
    h = HB * steps
    capacity = sources[0].shape[-1]
    lane = lax.broadcasted_iota(jnp.int32, (16, 128), 1)
    base = facts[0] * (ob * 128)
    spans = []
    for d, c in keys:
        owner = holder(facts[2], folds, d, c)
        spans.append((begin_of(counts, owner), counts[0, owner]))

    def block(e, carry):
        row = base + e * 128
        totals = [jnp.zeros((16, 128), F32), jnp.zeros((16, 128), F32)]
        for source, (start, count) in zip(sources, spans):
            at = row - start
            low = at >> 7
            shift = at & 127
            index = at + lane
            valid = (index >= 0) & (index < count)
            for a in range(2):

                def window(b, a=a, source=source):
                    b = jnp.clip(b, 0, capacity // 128 - 1)
                    return source[a, :, pl.ds(pl.multiple_of(b * 128, 128), 128)]

                totals[a] = jnp.where(valid, pick_lanes(window, low, shift), totals[a])
        u[h + e] = totals[0]
        r[h + e] = totals[1]
        high, low = split(totals[0])
        now[h + e, :16] = high
        now[h + e, 16:] = low
        return carry

    lax.fori_loop(0, ob, block, 0, unroll=4)
    even = facts[1] == 0
    put_payload(ob, steps, sides(even, True), u, r, pay_a)
    put_payload(ob, steps, sides(even, False), u, r, pay_b)


def stack_kernel(initial, right_side, stacked, sem):
    pair = [pltpu.make_async_copy(array, stacked.at[i], sem.at[i]) for i, array in enumerate((initial, right_side))]
    for copy in pair:
        copy.start()
    for copy in pair:
        copy.wait()


def outward_kernel(folds, halo, width, facts, columns, blocks, border, sem):
    own = columns.shape[1]
    size = blocks.shape[0] // own
    part = facts[0]
    first = jnp.where(part == 0, 0, own - halo)

    @pl.when((part == 0) | (part == folds - 1))
    def _():
        rows = blocks.at[pl.ds(pl.multiple_of(first * size, size), halo * size)]
        copy = pltpu.make_async_copy(rows, border.at[: halo * size], sem)
        copy.start()
        lane = lax.broadcasted_iota(jnp.int32, (8, 128), 1)
        indices = jnp.zeros((8, 128), jnp.int32)
        for i in range(halo):
            for k in range(width):
                indices = jnp.where(lane == i * width + k, columns[k, first + i], indices)
        border[halo * size :] = indices.astype(F32)
        copy.wait()


def gate_kernel(n, *refs):
    del n, refs


def put_row(out, a, raw):
    side = raw.shape[-1]
    for k in range(out.shape[1] // side):
        high, low = split(raw[k * side : (k + 1) * side])
        out[a, k * side : (k + 1) * side, :side] = high.T
        out[a, k * side : (k + 1) * side, side:] = low.T


def prepare_kernel(ob, halo, width, facts, columns, blocks, out, token, offsets, raw, sem):
    rows, size = raw.shape[0], raw.shape[1]
    own = blocks.shape[0] // size
    first = facts[0] * ob - halo

    def copy(a):
        i = pl.multiple_of(jnp.clip(first + a, 0, own - 1) * size, size)
        return pltpu.make_async_copy(blocks.at[pl.ds(i, size)], raw.at[a], sem.at[a])

    for a in range(rows):
        copy(a).start()

    def indices(a, carry):
        i = first + a
        for k in range(width):
            offsets[a * width + k] = columns[k, jnp.clip(i, 0, own - 1)] - HB - i
        return carry

    lax.fori_loop(0, rows, indices, 0)
    token[...] = jnp.zeros_like(token)
    group = 4 if rows % 4 == 0 else 2

    def several(g, carry):
        for s in range(group):
            a = g * group + s
            copy(a).wait()
            put_row(out, a, raw.at[a])
        return carry

    lax.fori_loop(0, rows // group, several, 0)


def border_kernel(ob, folds, halo, width, facts, prepared, raw, before, out, offsets, vector, scalars, sem):
    del prepared, before
    part = facts[0]
    size = out.shape[1]

    @pl.when((part == 0) | (part == folds - 1))
    def _():
        vector[...] = raw[halo * size :].astype(jnp.int32)
        copy = pltpu.make_async_copy(vector, scalars, sem)
        copy.start()
        first = jnp.where(part == 0, 0, halo + ob)
        for a in range(halo):
            put_row(out, first + a, raw.at[a * size : (a + 1) * size])
        copy.wait()
        for i in range(halo):
            local = jnp.where(part == 0, ob * folds - halo + i, i)
            for k in range(width):
                offsets[i * width + k] = jnp.clip(scalars[0, i * width + k] - HB - local, -HB, HB)


def apply_rows(t, steps, starts, count, first, last, pair, offset, operator, x, u, r, pieces):
    now, later = pieces[t % 2], pieces[(t + 1) % 2]
    width = operator.shape[1] // 128
    old, new = pair
    final = last and t == steps - 1

    def row(n, carry):
        e = starts + n
        a = e - HB
        left = jnp.concatenate([now[e + offset(a, k)] for k in range(width)], axis=1)
        product = jnp.dot(left, operator[a], preferred_element_type=F32)
        product = product[:16] + product[16:]
        resid = r[e] - (product[:, :128] + product[:, 128:])
        before = u[e]
        update = new * resid if old == 0.0 else old * before + new * resid
        total = before if first and t == 0 else x[e] + before
        x[e] = total + update if final else total
        if not final:
            r[e] = resid
            u[e] = update
            high, low = split(update)
            later[e, :16] = high
            later[e, 16:] = low
        return carry

    lax.fori_loop(0, count, row, 0, unroll=True)


def inner_kernel(ob, folds, steps, first, last, pairs, facts, offsets, operator, *refs):
    got_a, (x, u, r, *pieces) = refs[5], refs[6:]
    h = HB * steps
    width = operator.shape[1] // 128
    even = facts[1] == 0
    take_payload(ob, steps, sides(even, True), got_a, u, r, pieces[0])

    def offset(a, k):
        return offsets[a * width + k]

    for t in range(steps):
        starts = jnp.where(even, h + HB + HB * t, HB + HB * t)
        count = ob + h - 2 * HB - 2 * HB * t
        apply_rows(t, steps, starts, count, first, last, pairs[t], offset, operator, x, u, r, pieces)


def outer_kernel(ob, folds, steps, first, last, pairs, facts, offsets, lent, operator, *refs):
    got_b, (x, u, r, *pieces), outs = refs[5], refs[6:11], refs[11:]
    h = HB * steps
    inner = h - HB
    width = operator.shape[1] // 128
    even = facts[1] == 0
    edge = (facts[0] == 0) | (facts[0] == folds - 1)
    take_payload(ob, steps, sides(even, False), got_b, u, r, pieces[0])

    def offset(a, k):
        i = jnp.where(even, a, a - inner - ob)
        outside = edge & (i >= 0) & (i < inner)
        return jnp.where(outside, lent[jnp.clip(i, 0, inner - 1) * width + k], offsets[a * width + k])

    for t in range(steps):
        starts = jnp.where(even, HB + HB * t, h + ob - HB - HB * t)
        apply_rows(t, steps, starts, h, first, last, pairs[t], offset, operator, x, u, r, pieces)
    if last:
        outs[0][...] = x[h : h + ob]
    else:
        put_payload(ob, steps, sides(even, True), u, r, outs[0])
        put_payload(ob, steps, sides(even, False), u, r, outs[1])


def finish_kernel(ob, keys, facts, counts, *refs):
    parts, (out, whole) = refs[:-2], refs[-2:]
    total = whole.shape[0]
    for (d, c), part in zip(keys, parts):
        theirs = part_of(holder(facts[2], len(keys), d, c), len(keys), facts[3])
        whole[pl.ds(theirs * ob, ob)] = part[...]
    start, count = begin_of(counts, facts[2]), counts[0, facts[2]]
    lane = lax.broadcasted_iota(jnp.int32, (16, 128), 1)
    low, shift = start >> 7, start & 127

    def block(b, carry):
        piece = pick_lanes(lambda i: whole[jnp.minimum(i, total - 1)], low + b, shift)
        piece = jnp.where(b * 128 + lane < count, piece, 0.0)
        out[:, pl.ds(pl.multiple_of(b * 128, 128), 128)] = piece
        return carry

    lax.fori_loop(0, out.shape[1] // 128, block, 0, unroll=8)


def over_chips(array, d, folds):
    return lax.ppermute(array, "fold", [((i + 2 * d) % folds, i) for i in range(folds)])


def other_core(array, folds):
    return lax.ppermute(array, "fold", [(i, i ^ 1) for i in range(folds)])


def on_device(right_side, initial, counts, columns, blocks):
    groups, folds = lax.axis_size("group"), lax.axis_size("fold")
    vectors, capacity = right_side.shape
    own, width, side = blocks.shape[0], blocks.shape[1], blocks.shape[2]
    size = width * side
    ob = own // folds
    steps = 3 if ob >= 9 else 2
    halo = HB * (steps - 1)
    rows = ob + 2 * halo
    pairs = coefficients()
    fold = lax.axis_index("fold")
    backwards = lax.axis_index("group") % 2
    part = part_of(fold, folds, backwards)
    devices = groups * folds
    facts = jnp.stack([part, part % 2, fold, backwards]).astype(jnp.int32)
    operator_shape = pltpu.VMEM((rows, size, 2 * side), BF16)

    payload = jax.ShapeDtypeStruct((2 * HB * steps - HB, vectors, side), F32)

    line = [g * folds + (folds - 1 - p if g % 2 else p) for g in range(groups) for p in range(folds)]

    def swap(first, distance):
        ends = [(line[i], line[i + 1]) for i in range(first, devices - 1, distance)]
        return ends + [(j, i) for i, j in ends]

    swap_a, swap_b, swap_border = swap(0, 2), swap(1, 2), swap(folds - 1, folds)

    near = [pltpu.with_memory_space_constraint(array, pltpu.HBM) for array in (initial, right_side)]
    stacked = pl.pallas_call(
        stack_kernel,
        out_shape=pltpu.VMEM((2, vectors, capacity), F32),
        in_specs=[HBM, HBM],
        out_specs=VMEM,
        scratch_shapes=[pltpu.SemaphoreType.DMA((2,))],
        compiler_params=params(),
    )(*near)
    far = [over_chips(stacked, d, folds) for d in range(1, folds // 2)]
    turned = columns.T
    flat = pltpu.with_memory_space_constraint(blocks.reshape(own * size, side), pltpu.HBM)
    border = pl.pallas_call(
        functools.partial(outward_kernel, folds, halo, width),
        out_shape=pltpu.VMEM((halo * size + 8, side), F32),
        in_specs=[SMEM, SMEM, HBM],
        out_specs=VMEM,
        scratch_shapes=[pltpu.SemaphoreType.DMA(())],
        compiler_params=params(),
    )(facts, turned, flat)
    border = lax.ppermute(border, AXES, swap_border)

    operator, token, offsets = pl.pallas_call(
        functools.partial(prepare_kernel, ob, halo, width),
        out_shape=(operator_shape, jax.ShapeDtypeStruct((8, 128), F32), jax.ShapeDtypeStruct((rows * width,), jnp.int32)),
        in_specs=[SMEM, SMEM, HBM],
        out_specs=(VMEM, VMEM, SMEM),
        scratch_shapes=[
            pltpu.VMEM((rows, size, side), F32),
            pltpu.SemaphoreType.DMA((rows,)),
        ],
        compiler_params=params(),
        cost_estimate=pl.CostEstimate(flops=10**7, bytes_accessed=2 * rows * size * side * 4, transcendentals=0),
    )(facts, turned, flat)

    def gate(arrays, spaces, token):
        return pl.pallas_call(
            functools.partial(gate_kernel, len(arrays)),
            out_shape=tuple(space(array.shape, F32) for array, space in zip(arrays, spaces)),
            in_specs=[pl.BlockSpec(memory_space=space) for space in spaces] + [pl.BlockSpec(memory_space=pl.ANY)],
            out_specs=tuple(pl.BlockSpec(memory_space=space) for space in spaces),
            input_output_aliases={i: i for i in range(len(arrays))},
            compiler_params=params(),
        )(*[pltpu.with_memory_space_constraint(array, space) for array, space in zip(arrays, spaces)], token)

    far = gate(far, [pltpu.VMEM] * len(far), token)

    keys, arrays = [], []
    for d, array in enumerate([stacked, *far]):
        keys += [(d, False), (d, True)]
        arrays += [array, other_core(array, folds)]
    extent = ob + 2 * HB * steps
    state = (pltpu.VMEM((extent, vectors, side), F32),) * 3 + (pltpu.VMEM((extent, 2 * vectors, side), BF16),) * 2
    *held, pay_a, pay_b = pl.pallas_call(
        functools.partial(align_kernel, ob, steps, keys),
        out_shape=(*state, payload, payload),
        in_specs=[SMEM, SMEM] + [VMEM] * folds,
        out_specs=(VMEM,) * 7,
        compiler_params=params(),
    )(facts, counts, *[pltpu.with_memory_space_constraint(array, pltpu.VMEM) for array in arrays])

    def part_of_phase(kernel, operator, indices, held, got, outs):
        held = [pltpu.with_memory_space_constraint(array, pltpu.VMEM) for array in held]
        n = len(indices)
        results = pl.pallas_call(
            functools.partial(kernel, ob, folds, steps, done == 0, done + steps == APPLIES, pairs[done : done + steps]),
            out_shape=(*state, *outs),
            in_specs=[SMEM] * (1 + n) + [VMEM] * 7,
            out_specs=(VMEM,) * (5 + len(outs)),
            input_output_aliases={2 + n + i: i for i in range(5)},
            compiler_params=params(),
        )(facts, *indices, pltpu.with_memory_space_constraint(operator, pltpu.VMEM), *held, got)
        return results[:5], results[5:]

    for done in range(0, APPLIES, steps):
        got_b = lax.ppermute(pay_b, AXES, swap_b)
        got_a = lax.ppermute(pay_a, AXES, swap_a)
        held, _ = part_of_phase(inner_kernel, operator, [offsets], held, got_a, ())
        if done == 0:
            operator, lent = pl.pallas_call(
                functools.partial(border_kernel, ob, folds, halo, width),
                out_shape=(operator_shape, jax.ShapeDtypeStruct((halo * width,), jnp.int32)),
                in_specs=[SMEM, VMEM, VMEM, pl.BlockSpec(memory_space=pl.ANY)],
                out_specs=(VMEM, SMEM),
                input_output_aliases={1: 0},
                scratch_shapes=[
                    pltpu.VMEM((8, 128), jnp.int32),
                    pltpu.SMEM((8, 128), jnp.int32),
                    pltpu.SemaphoreType.DMA(()),
                ],
                compiler_params=params(),
            )(facts, pltpu.with_memory_space_constraint(operator, pltpu.VMEM), border, held[0])
        if done + steps < APPLIES:
            held, (pay_a, pay_b) = part_of_phase(
                outer_kernel, operator, [offsets, lent], held, got_b, (payload, payload)
            )
        else:
            result = jax.ShapeDtypeStruct((ob, vectors, side), F32)
            held, (x,) = part_of_phase(outer_kernel, operator, [offsets, lent], held, got_b, (result,))
        if steps % 2:
            held = [*held[:3], held[4], held[3]]

    parts = []
    for d in range(folds // 2):
        piece = over_chips(x, d, folds) if d else x
        parts += [piece, other_core(piece, folds)]
    return pl.pallas_call(
        functools.partial(finish_kernel, ob, keys),
        out_shape=jax.ShapeDtypeStruct((vectors, capacity), F32),
        in_specs=[SMEM, SMEM] + [VMEM] * folds,
        out_specs=VMEM,
        scratch_shapes=[pltpu.VMEM((own, vectors, side), F32)],
        compiler_params=params(),
    )(facts, counts, *parts)


def solution(mesh):
    placed = (
        P(None, AXES),
        P(None, AXES),
        P("group", None),
        P("group", None),
        P("group", None, None, None),
    )
    return jax.shard_map(on_device, mesh=mesh, in_specs=placed, out_specs=P(None, AXES), check_vma=False)
```

time: 83.8 us -> 74.3 us (0.89)
  waiting for transfers between devices: 26.1 us -> 14.6 us
  Pallas kernels: 31.5 us -> 33.3 us
  starting transfers between devices: 23.3 us -> 25 us
  local copies, waits for them, and re-layouts: 2.32 us -> 0.69 us
    ppermute x4, waiting for transfers between devices: 15.5 us -> 4.23 us  [on_device(): got_b = lax.ppermute(pay_b, AXES, swap_b)]
    pallas_call x4 -> x9, Pallas kernels: 17.6 us -> 22 us  [the longest x8 20.9 us: part_of_phase(): pl.pallas_call(functools.partial(kernel, ob, folds, steps, done == 0, don...]
    unnamed x10 -> x4, local copies, waits for them, and re-layouts: 2.32 us -> 0.69 us
    pallas_call x1, Pallas kernels: 2.84 us -> 1.53 us  [on_device(): pl.pallas_call(functools.partial(align_kernel, ob, steps, keys), out_shap...]
    pallas_call x1, Pallas kernels: 1.66 us -> 0.62 us  [on_device(): pl.pallas_call(functools.partial(outward_kernel, folds, halo, width), out...]
    ppermute x2, starting transfers between devices: 4.35 us -> 5.22 us  [over_chips(): lax.ppermute(array, 'fold', [((i + 2 * d) % folds, i) for i in range(fold...]
  transfers between devices with their start and end apart: 15 -> 15, of which waited for: 8 -> 7; matrix products, arithmetic and copies ran while one was open for 0% -> 0% of each run, Pallas kernels for 13% -> 29%
where the time goes in v5:
time: 74.3 us; the launch traced here: 73.8 us
  Pallas kernels  33.3 us (45%)
  starting transfers between devices  25 us (34%)
  waiting for transfers between devices  14.6 us (20%)
    pallas_call x8, Pallas kernels, part_of_phase(): pl.pallas_call(functools.partial(kernel, ob, folds, steps, done == 0, don...  20.9 us
    ppermute x4, starting transfers between devices, on_device(): got_b = lax.ppermute(pay_b, AXES, swap_b)  9.54 us
    ppermute x2, waiting for transfers between devices, over_chips(): lax.ppermute(array, 'fold', [((i + 2 * d) % folds, i) for i in range(fold...  7.8 us
    pallas_call x1, Pallas kernels, on_device(): pl.pallas_call(functools.partial(prepare_kernel, ob, halo, width), out_sh...  6.31 us
    ppermute x2, starting transfers between devices, over_chips(): lax.ppermute(array, 'fold', [((i + 2 * d) % folds, i) for i in range(fold...  5.22 us
    ppermute x4, starting transfers between devices, other_core(): return lax.ppermute(array, 'fold', [(i, i ^ 1) for i in range(folds)])  4.93 us
    ppermute x4, starting transfers between devices, on_device(): got_a = lax.ppermute(pay_a, AXES, swap_a)  4.53 us
    ppermute x4, waiting for transfers between devices, on_device(): got_b = lax.ppermute(pay_b, AXES, swap_b)  4.23 us
  transfers between devices with their start and end apart: 15, of which 7 were waited for; matrix products, arithmetic and copies ran while one was open for 0% of the time, Pallas kernels for 29%

profile of v5, /device:TPU:9, one launch (start us, length us, event | category | flops | bytes accessed | tf_op | source)
XLA Modules:
  0.0 73.8 jit_solution(13595453762024362680)
XLA Ops:
  0.0 0.1 pad_add_fusion.facts
  0.1 0.7 copy-done
  0.8 0.6 shard_map.56
  1.4 0.8 %collective-permute-start = (f32[3848,128]{1,0:T(8,128)S(1)}, f32[3848,128]{1,0:T(8,128)S(1)}, u32[]{:S(2)}, u32[]{:S(2)}) collective-permute-start(f32[3848,128]{1,0:T(8,128)S(1)} %shard_map.56), channel_id=1, source_target_pairs={{3,7},{4,8},{11,15},{12,16},{19,23},{20,24},{27,31},{7,3},{8,4},{1... | collective-permute-start | bytes 5910536 | tf_op jit(solution)/shard_map/ppermute | solution.py:372
  2.2 1.0 %shard_map.57.refs_0_ = f32[2,16,4096]{2,1,0:T(8,128)S(1)} custom-call(f32[16,4096]{1,0:T(8,128)} %initial.1, f32[16,4096]{1,0:T(8,128)} %right_side.1), custom_call_target="tpu_custom_call" | custom-call | tf_op jit(solution)/shard_map/pallas_call | solution.py:353
  3.2 0.0 copy-start.1
  3.3 5.2 %collective-permute-start.2 = (f32[2,16,4096]{2,1,0:T(8,128)S(1)}, f32[2,16,4096]{2,1,0:T(8,128)S(1)}, u32[]{:S(2)}, u32[]{:S(2)}) collective-permute-start(f32[2,16,4096]{2,1,0:T(8,128)S(1)} %shard_map.57.refs_0_), channel_id=1, source_target_pairs={{2,0},{3,1},{0,2},{1,3},{6,4},{7,5},{4,6},{5,7},{10,8},{11,9},{8,1... | collective-permute-start | bytes 1572872 | tf_op jit(solution)/shard_map/ppermute | solution.py:318
  8.4 0.0 collective-permute-start.1
  8.4 6.3 %shard_map.55 = (bf16[28,640,256]{2,1,0:T(8,128)(2,1)S(1)}, f32[8,128]{1,0:T(8,128)S(1)}, s32[140]{0:T(256)S(1)}) custom-call(s32[4]{0:T(128)S(1)} %pad_add_fusion.facts, s32[5,64]{1,0:T(8,128)S(1)} %bitcast.7, f32[40960,128]{1,0:T(8,128)} %bitcast.9), custom_call_target="tpu_custom_call" | custom-call | flops 10000000 | bytes 18350080 | tf_op jit(solution)/shard_map/pallas_call | solution.py:374
  14.8 5.3 %collective-permute-done.2.refs_0_ = f32[2,16,4096]{2,1,0:T(8,128)S(1)} collective-permute-done((f32[2,16,4096]{2,1,0:T(8,128)S(1)}, f32[2,16,4096]{2,1,0:T(8,128)S(1)}, u32[]{:S(2)}, u32[]{:S(2)}) %collective-permute-start.2) | collective-permute-done | bytes 524320 | tf_op jit(solution)/shard_map/ppermute | solution.py:318
  20.0 1.3 %collective-permute-start.3 = (f32[2,16,4096]{2,1,0:T(8,128)S(1)}, f32[2,16,4096]{2,1,0:T(8,128)S(1)}, u32[]{:S(2)}, u32[]{:S(2)}) collective-permute-start(f32[2,16,4096]{2,1,0:T(8,128)S(1)} %shard_map.58.refs_2_), channel_id=1, source_target_pairs={{0,1},{1,0},{2,3},{3,2},{4,5},{5,4},{6,7},{7,6},{8,9},{9,8},{10,11... | collective-permute-start | bytes 1572872 | tf_op jit(solution)/shard_map/ppermute | solution.py:322
  21.3 0.0 collective-permute-done.1.refs_1_
  21.3 1.5 %collective-permute-done.3.refs_3_ = f32[2,16,4096]{2,1,0:T(8,128)S(1)} collective-permute-done((f32[2,16,4096]{2,1,0:T(8,128)S(1)}, f32[2,16,4096]{2,1,0:T(8,128)S(1)}, u32[]{:S(2)}, u32[]{:S(2)}) %collective-permute-start.3) | collective-permute-done | bytes 524320 | tf_op jit(solution)/shard_map/ppermute | solution.py:322
  22.9 0.0 copy-done.1
  22.9 1.5 %shard_map.59 = (f32[34,16,128]{2,1,0:T(8,128)S(1)}, f32[34,16,128]{2,1,0:T(8,128)S(1)}, f32[34,16,128]{2,1,0:T(8,128)S(1)}, bf16[34,32,128]{2,1,0:T(8,128)(2,1)...) custom-call(s32[4]{0:T(128)S(1)} %pad_add_fusion.facts, ...), custom_call_target="tpu_custom_call" | custom-call | tf_op jit(solution)/shard_map/pallas_call | solution.py:405
  24.4 0.4 collective-permute-start.4
  24.8 3.0 %collective-permute-start.5 = (f32[15,16,128]{2,1,0:T(8,128)S(1)}, f32[15,16,128]{2,1,0:T(8,128)S(1)}, u32[]{:S(2)}, u32[]{:S(2)}) collective-permute-start(f32[15,16,128]{2,1,0:T(8,128)S(1)} %get-tuple-element.75), channel_id=1, source_target_pairs={{1,2},{3,7},{6,5},{4,8},{9,10},{11,15},{14,13},{12,16},{17,18},{19... | collective-permute-start | bytes 368648 | tf_op jit(solution)/shard_map/ppermute | solution.py:427
  27.8 0.0 collective-permute-done.4.refs_5_
  27.9 2.9 %shard_map.60 = (f32[34,16,128]{2,1,0:T(8,128)S(1)}, f32[34,16,128]{2,1,0:T(8,128)S(1)}, f32[34,16,128]{2,1,0:T(8,128)S(1)}, bf16[34,32,128]{2,1,0:T(8,128)(2,1)S(1)}, bf16[34,32,128]{2,1,0:T(8,128)(2,1)S(1)}) custom-call(s32[4]{0:T(128)S(1)} %pad_add_fusion.facts, ...), custom_call_target="tpu_custom_call", output_to_operand_aliasing={{0}: (3, {}), {1}: (4, {}), {2}: (5, {}), {3}: (6, {}), {4}... | custom-call | tf_op jit(solution)/shard_map/pallas_call | solution.py:416
  30.7 0.0 collective-permute-done.raw
  30.8 1.2 %shard_map.61 = (bf16[28,640,256]{2,1,0:T(8,128)(2,1)S(1)}, s32[30]{0:T(128)S(1)}) custom-call(s32[4]{0:T(128)S(1)} %pad_add_fusion.facts, bf16[28,640,256]{2,1,0:T(8,128)(2,1)S(1)} %get-tuple-element.60.operator.prepared, f32[3848,128]{1,0:T(8,128)S(1)} %collective-permute-done.raw, ...), custom_call_target="tpu_custom_call", output_to_operand_aliasing={{0}: (1, {})} | custom-call | tf_op jit(solution)/shard_map/pallas_call | solution.py:431
  31.9 0.0 collective-permute-done.5.refs_5_
  31.9 2.4 %shard_map.62 = (f32[34,16,128]{2,1,0:T(8,128)S(1)}, f32[34,16,128]{2,1,0:T(8,128)S(1)}, f32[34,16,128]{2,1,0:T(8,128)S(1)}, bf16[34,32,128]{2,1,0:T(8,128)(2,1)...) custom-call(s32[4]{0:T(128)S(1)} %pad_add_fusion.facts, ...), custom_call_target="tpu_custom_call", output_to_operand_aliasing={{0}: (4, {}), {1}: (5, {}), {2}: (6, {}), {3}: (7, {}), {4}... | custom-call | tf_op jit(solution)/shard_map/pallas_call | solution.py:416
  34.3 1.5 %collective-permute-start.6 = (f32[15,16,128]{2,1,0:T(8,128)S(1)}, f32[15,16,128]{2,1,0:T(8,128)S(1)}, u32[]{:S(2)}, u32[]{:S(2)}) collective-permute-start(f32[15,16,128]{2,1,0:T(8,128)S(1)} %get-tuple-element.81), channel_id=1, source_target_pairs={{0,1},{2,3},{7,6},{5,4},{8,9},{10,11},{15,14},{13,12},{16,17},{18,... | collective-permute-start | bytes 368648 | tf_op jit(solution)/shard_map/ppermute | solution.py:428
  35.8 2.5 %collective-permute-start.7 = (f32[15,16,128]{2,1,0:T(8,128)S(1)}, f32[15,16,128]{2,1,0:T(8,128)S(1)}, u32[]{:S(2)}, u32[]{:S(2)}) collective-permute-start(f32[15,16,128]{2,1,0:T(8,128)S(1)} %get-tuple-element.87), channel_id=1, source_target_pairs={{1,2},{3,7},{6,5},{4,8},{9,10},{11,15},{14,13},{12,16},{17,18},{19... | collective-permute-start | bytes 368648 | tf_op jit(solution)/shard_map/ppermute | solution.py:427
  38.4 0.0 collective-permute-done.6.refs_5_
  38.4 2.9 %shard_map.63 = (f32[34,16,128]{2,1,0:T(8,128)S(1)}, f32[34,16,128]{2,1,0:T(8,128)S(1)}, f32[34,16,128]{2,1,0:T(8,128)S(1)}, bf16[34,32,128]{2,1,0:T(8,128)(2,1)S(1)}, bf16[34,32,128]{2,1,0:T(8,128)(2,1)S(1)}) custom-call(s32[4]{0:T(128)S(1)} %pad_add_fusion.facts, ...), custom_call_target="tpu_custom_call", output_to_operand_aliasing={{0}: (3, {}), {1}: (4, {}), {2}: (5, {}), {3}: (6, {}), {4}... | custom-call | tf_op jit(solution)/shard_map/pallas_call | solution.py:416
  41.3 1.0 %collective-permute-done.7.refs_5_ = f32[15,16,128]{2,1,0:T(8,128)S(1)} collective-permute-done((f32[15,16,128]{2,1,0:T(8,128)S(1)}, f32[15,16,128]{2,1,0:T(8,128)S(1)}, u32[]{:S(2)}, u32[]{:S(2)}) %collective-permute-start.7) | collective-permute-done | bytes 122912 | tf_op jit(solution)/shard_map/ppermute | solution.py:427
  42.3 2.3 %shard_map.64 = (f32[34,16,128]{2,1,0:T(8,128)S(1)}, f32[34,16,128]{2,1,0:T(8,128)S(1)}, f32[34,16,128]{2,1,0:T(8,128)S(1)}, bf16[34,32,128]{2,1,0:T(8,128)(2,1)...) custom-call(s32[4]{0:T(128)S(1)} %pad_add_fusion.facts, ...), custom_call_target="tpu_custom_call", output_to_operand_aliasing={{0}: (4, {}), {1}: (5, {}), {2}: (6, {}), {3}: (7, {}), {4}... | custom-call | tf_op jit(solution)/shard_map/pallas_call | solution.py:416
  44.7 1.3 %collective-permute-start.8 = (f32[15,16,128]{2,1,0:T(8,128)S(1)}, f32[15,16,128]{2,1,0:T(8,128)S(1)}, u32[]{:S(2)}, u32[]{:S(2)}) collective-permute-start(f32[15,16,128]{2,1,0:T(8,128)S(1)} %get-tuple-element.93), channel_id=1, source_target_pairs={{0,1},{2,3},{7,6},{5,4},{8,9},{10,11},{15,14},{13,12},{16,17},{18,... | collective-permute-start | bytes 368648 | tf_op jit(solution)/shard_map/ppermute | solution.py:428
  45.9 1.9 %collective-permute-start.9 = (f32[15,16,128]{2,1,0:T(8,128)S(1)}, f32[15,16,128]{2,1,0:T(8,128)S(1)}, u32[]{:S(2)}, u32[]{:S(2)}) collective-permute-start(f32[15,16,128]{2,1,0:T(8,128)S(1)} %get-tuple-element.99), channel_id=1, source_target_pairs={{1,2},{3,7},{6,5},{4,8},{9,10},{11,15},{14,13},{12,16},{17,18},{19... | collective-permute-start | bytes 368648 | tf_op jit(solution)/shard_map/ppermute | solution.py:427
  47.9 0.0 collective-permute-done.8.refs_5_
  47.9 2.9 %shard_map.65 = (f32[34,16,128]{2,1,0:T(8,128)S(1)}, f32[34,16,128]{2,1,0:T(8,128)S(1)}, f32[34,16,128]{2,1,0:T(8,128)S(1)}, bf16[34,32,128]{2,1,0:T(8,128)(2,1)S(1)}, bf16[34,32,128]{2,1,0:T(8,128)(2,1)S(1)}) custom-call(s32[4]{0:T(128)S(1)} %pad_add_fusion.facts, ...), custom_call_target="tpu_custom_call", output_to_operand_aliasing={{0}: (3, {}), {1}: (4, {}), {2}: (5, {}), {3}: (6, {}), {4}... | custom-call | tf_op jit(solution)/shard_map/pallas_call | solution.py:416
  50.8 1.7 %collective-permute-done.9.refs_5_ = f32[15,16,128]{2,1,0:T(8,128)S(1)} collective-permute-done((f32[15,16,128]{2,1,0:T(8,128)S(1)}, f32[15,16,128]{2,1,0:T(8,128)S(1)}, u32[]{:S(2)}, u32[]{:S(2)}) %collective-permute-start.9) | collective-permute-done | bytes 122912 | tf_op jit(solution)/shard_map/ppermute | solution.py:427
  52.4 2.4 %shard_map.66 = (f32[34,16,128]{2,1,0:T(8,128)S(1)}, f32[34,16,128]{2,1,0:T(8,128)S(1)}, f32[34,16,128]{2,1,0:T(8,128)S(1)}, bf16[34,32,128]{2,1,0:T(8,128)(2,1)...) custom-call(s32[4]{0:T(128)S(1)} %pad_add_fusion.facts, ...), custom_call_target="tpu_custom_call", output_to_operand_aliasing={{0}: (4, {}), {1}: (5, {}), {2}: (6, {}), {3}: (7, {}), {4}... | custom-call | tf_op jit(solution)/shard_map/pallas_call | solution.py:416
  54.8 1.3 %collective-permute-start.10 = (f32[15,16,128]{2,1,0:T(8,128)S(1)}, f32[15,16,128]{2,1,0:T(8,128)S(1)}, u32[]{:S(2)}, u32[]{:S(2)}) collective-permute-start(f32[15,16,128]{2,1,0:T(8,128)S(1)} %get-tuple-element.105), channel_id=1, source_target_pairs={{0,1},{2,3},{7,6},{5,4},{8,9},{10,11},{15,14},{13,12},{16,17},{18,... | collective-permute-start | bytes 368648 | tf_op jit(solution)/shard_map/ppermute | solution.py:428
  56.1 2.1 %collective-permute-start.11 = (f32[15,16,128]{2,1,0:T(8,128)S(1)}, f32[15,16,128]{2,1,0:T(8,128)S(1)}, u32[]{:S(2)}, u32[]{:S(2)}) collective-permute-start(f32[15,16,128]{2,1,0:T(8,128)S(1)} %get-tuple-element.111), channel_id=1, source_target_pairs={{1,2},{3,7},{6,5},{4,8},{9,10},{11,15},{14,13},{12,16},{17,18},{19... | collective-permute-start | bytes 368648 | tf_op jit(solution)/shard_map/ppermute | solution.py:427
  58.2 0.0 collective-permute-done.10.refs_5_
  58.2 2.9 %shard_map.67 = (f32[34,16,128]{2,1,0:T(8,128)S(1)}, f32[34,16,128]{2,1,0:T(8,128)S(1)}, f32[34,16,128]{2,1,0:T(8,128)S(1)}, bf16[34,32,128]{2,1,0:T(8,128)(2,1)S(1)}, bf16[34,32,128]{2,1,0:T(8,128)(2,1)S(1)}) custom-call(s32[4]{0:T(128)S(1)} %pad_add_fusion.facts, ...), custom_call_target="tpu_custom_call", output_to_operand_aliasing={{0}: (3, {}), {1}: (4, {}), {2}: (5, {}), {3}: (6, {}), {4}... | custom-call | tf_op jit(solution)/shard_map/pallas_call | solution.py:416
  61.0 1.5 %collective-permute-done.11.refs_5_ = f32[15,16,128]{2,1,0:T(8,128)S(1)} collective-permute-done((f32[15,16,128]{2,1,0:T(8,128)S(1)}, f32[15,16,128]{2,1,0:T(8,128)S(1)}, u32[]{:S(2)}, u32[]{:S(2)}) %collective-permute-start.11) | collective-permute-done | bytes 122912 | tf_op jit(solution)/shard_map/ppermute | solution.py:427
  62.5 2.3 %shard_map.68 = (f32[34,16,128]{2,1,0:T(8,128)S(1)}, f32[34,16,128]{2,1,0:T(8,128)S(1)}, f32[34,16,128]{2,1,0:T(8,128)S(1)}, bf16[34,32,128]{2,1,0:T(8,128)(2,1)...) custom-call(s32[4]{0:T(128)S(1)} %pad_add_fusion.facts, ...), custom_call_target="tpu_custom_call", output_to_operand_aliasing={{0}: (4, {}), {1}: (5, {}), {2}: (6, {}), {3}: (7, {}), {4}... | custom-call | tf_op jit(solution)/shard_map/pallas_call | solution.py:416
  64.9 0.0 collective-permute-start.13
  64.9 1.3 %collective-permute-start.12 = (f32[16,16,128]{2,1,0:T(8,128)S(1)}, f32[16,16,128]{2,1,0:T(8,128)S(1)}, u32[]{:S(2)}, u32[]{:S(2)}) collective-permute-start(f32[16,16,128]{2,1,0:T(8,128)S(1)} %get-tuple-element.112.refs_0_), channel_id=1, source_target_pairs={{0,1},{1,0},{2,3},{3,2},{4,5},{5,4},{6,7},{7,6},{8,9},{9,8},{10,11... | collective-permute-start | bytes 393224 | tf_op jit(solution)/shard_map/ppermute | solution.py:322
  66.2 2.5 %collective-permute-done.13.refs_2_ = f32[16,16,128]{2,1,0:T(8,128)S(1)} collective-permute-done((f32[16,16,128]{2,1,0:T(8,128)S(1)}, f32[16,16,128]{2,1,0:T(8,128)S(1)}, u32[]{:S(2)}, u32[]{:S(2)}) %collective-permute-start.13) | collective-permute-done | bytes 131104 | tf_op jit(solution)/shard_map/ppermute | solution.py:318
  68.7 2.4 %collective-permute-start.14 = (f32[16,16,128]{2,1,0:T(8,128)S(1)}, f32[16,16,128]{2,1,0:T(8,128)S(1)}, u32[]{:S(2)}, u32[]{:S(2)}) collective-permute-start(f32[16,16,128]{2,1,0:T(8,128)S(1)} %collective-permute-done.13.refs_2_), channel_id=1, source_target_pairs={{0,1},{1,0},{2,3},{3,2},{4,5},{5,4},{6,7},{7,6},{8,9},{9,8},{10,11... | collective-permute-start | bytes 393224 | tf_op jit(solution)/shard_map/ppermute | solution.py:322
  71.1 0.0 collective-permute-done.12.refs_1_
  71.1 1.0 %collective-permute-done.14.refs_3_ = f32[16,16,128]{2,1,0:T(8,128)S(1)} collective-permute-done((f32[16,16,128]{2,1,0:T(8,128)S(1)}, f32[16,16,128]{2,1,0:T(8,128)S(1)}, u32[]{:S(2)}, u32[]{:S(2)}) %collective-permute-start.14) | collective-permute-done | bytes 131104 | tf_op jit(solution)/shard_map/ppermute | solution.py:322
  72.1 1.7 %shard_map.69 = f32[16,4096]{1,0:T(8,128)} custom-call(s32[4]{0:T(128)S(1)} %pad_add_fusion.facts, s32[1,4]{1,0:T(1,128)S(1)} %copy-done.1, f32[16,16,128]{2,1,0:T(8,128)S(1)} %get-tuple-element.112.refs_0_, f32[16,16,128]{2,1,0:T(8,128)S(1)} %collective-permute-done.12.refs_1_, f32[16,16,128]{2,1,0:T(8,128)S(1)} %collective-permute-done.13.refs_2_, ...), custom_call_target="tpu_custom_call" | custom-call | tf_op jit(solution)/shard_map/pallas_call | solution.py:458
  (2 shorter events, 0.0 us)
Async XLA Ops:
  0.1 0.7 copy-start
  1.4 29.4 %collective-permute-start = (f32[3848,128]{1,0:T(8,128)S(1)}, f32[3848,128]{1,0:T(8,128)S(1)}, u32[]{:S(2)}, u32[]{:S(2)}) collective-permute-start(f32[3848,128]{1,0:T(8,128)S(1)} %shard_map.56), channel_id=1, source_target_pairs={{3,7},{4,8},{11,15},{12,16},{19,23},{20,24},{27,31},{7,3},{8,4},{1... | collective-permute-start | bytes 5910536 | tf_op jit(solution)/shard_map/ppermute | solution.py:372
  3.2 19.6 %copy-start.1 = (s32[1,4]{1,0:T(1,128)S(1)}, s32[1,4]{1,0:T(1,128)}, u32[]{:S(2)}) copy-start(s32[1,4]{1,0:T(1,128)} %counts.3) | copy-start | bytes 52
  3.3 16.8 %collective-permute-start.2 = (f32[2,16,4096]{2,1,0:T(8,128)S(1)}, f32[2,16,4096]{2,1,0:T(8,128)S(1)}, u32[]{:S(2)}, u32[]{:S(2)}) collective-permute-start(f32[2,16,4096]{2,1,0:T(8,128)S(1)} %shard_map.57.refs_0_), channel_id=1, source_target_pairs={{2,0},{3,1},{0,2},{1,3},{6,4},{7,5},{4,6},{5,7},{10,8},{11,9},{8,1... | collective-permute-start | bytes 1572872 | tf_op jit(solution)/shard_map/ppermute | solution.py:318
  8.4 12.9 %collective-permute-start.1 = (f32[2,16,4096]{2,1,0:T(8,128)S(1)}, f32[2,16,4096]{2,1,0:T(8,128)S(1)}, u32[]{:S(2)}, u32[]{:S(2)}) collective-permute-start(f32[2,16,4096]{2,1,0:T(8,128)S(1)} %shard_map.57.refs_0_), channel_id=1, source_target_pairs={{0,1},{1,0},{2,3},{3,2},{4,5},{5,4},{6,7},{7,6},{8,9},{9,8},{10,11... | collective-permute-start | bytes 1572872 | tf_op jit(solution)/shard_map/ppermute | solution.py:322
  20.0 2.8 %collective-permute-start.3 = (f32[2,16,4096]{2,1,0:T(8,128)S(1)}, f32[2,16,4096]{2,1,0:T(8,128)S(1)}, u32[]{:S(2)}, u32[]{:S(2)}) collective-permute-start(f32[2,16,4096]{2,1,0:T(8,128)S(1)} %shard_map.58.refs_2_), channel_id=1, source_target_pairs={{0,1},{1,0},{2,3},{3,2},{4,5},{5,4},{6,7},{7,6},{8,9},{9,8},{10,11... | collective-permute-start | bytes 1572872 | tf_op jit(solution)/shard_map/ppermute | solution.py:322
  24.4 3.5 %collective-permute-start.4 = (f32[15,16,128]{2,1,0:T(8,128)S(1)}, f32[15,16,128]{2,1,0:T(8,128)S(1)}, u32[]{:S(2)}, u32[]{:S(2)}) collective-permute-start(f32[15,16,128]{2,1,0:T(8,128)S(1)} %get-tuple-element.67), channel_id=1, source_target_pairs={{0,1},{2,3},{7,6},{5,4},{8,9},{10,11},{15,14},{13,12},{16,17},{18,... | collective-permute-start | bytes 368648 | tf_op jit(solution)/shard_map/ppermute | solution.py:428
  24.8 7.1 %collective-permute-start.5 = (f32[15,16,128]{2,1,0:T(8,128)S(1)}, f32[15,16,128]{2,1,0:T(8,128)S(1)}, u32[]{:S(2)}, u32[]{:S(2)}) collective-permute-start(f32[15,16,128]{2,1,0:T(8,128)S(1)} %get-tuple-element.75), channel_id=1, source_target_pairs={{1,2},{3,7},{6,5},{4,8},{9,10},{11,15},{14,13},{12,16},{17,18},{19... | collective-permute-start | bytes 368648 | tf_op jit(solution)/shard_map/ppermute | solution.py:427
  34.3 4.1 %collective-permute-start.6 = (f32[15,16,128]{2,1,0:T(8,128)S(1)}, f32[15,16,128]{2,1,0:T(8,128)S(1)}, u32[]{:S(2)}, u32[]{:S(2)}) collective-permute-start(f32[15,16,128]{2,1,0:T(8,128)S(1)} %get-tuple-element.81), channel_id=1, source_target_pairs={{0,1},{2,3},{7,6},{5,4},{8,9},{10,11},{15,14},{13,12},{16,17},{18,... | collective-permute-start | bytes 368648 | tf_op jit(solution)/shard_map/ppermute | solution.py:428
  35.8 6.5 %collective-permute-start.7 = (f32[15,16,128]{2,1,0:T(8,128)S(1)}, f32[15,16,128]{2,1,0:T(8,128)S(1)}, u32[]{:S(2)}, u32[]{:S(2)}) collective-permute-start(f32[15,16,128]{2,1,0:T(8,128)S(1)} %get-tuple-element.87), channel_id=1, source_target_pairs={{1,2},{3,7},{6,5},{4,8},{9,10},{11,15},{14,13},{12,16},{17,18},{19... | collective-permute-start | bytes 368648 | tf_op jit(solution)/shard_map/ppermute | solution.py:427
  44.7 3.2 %collective-permute-start.8 = (f32[15,16,128]{2,1,0:T(8,128)S(1)}, f32[15,16,128]{2,1,0:T(8,128)S(1)}, u32[]{:S(2)}, u32[]{:S(2)}) collective-permute-start(f32[15,16,128]{2,1,0:T(8,128)S(1)} %get-tuple-element.93), channel_id=1, source_target_pairs={{0,1},{2,3},{7,6},{5,4},{8,9},{10,11},{15,14},{13,12},{16,17},{18,... | collective-permute-start | bytes 368648 | tf_op jit(solution)/shard_map/ppermute | solution.py:428
  45.9 6.5 %collective-permute-start.9 = (f32[15,16,128]{2,1,0:T(8,128)S(1)}, f32[15,16,128]{2,1,0:T(8,128)S(1)}, u32[]{:S(2)}, u32[]{:S(2)}) collective-permute-start(f32[15,16,128]{2,1,0:T(8,128)S(1)} %get-tuple-element.99), channel_id=1, source_target_pairs={{1,2},{3,7},{6,5},{4,8},{9,10},{11,15},{14,13},{12,16},{17,18},{19... | collective-permute-start | bytes 368648 | tf_op jit(solution)/shard_map/ppermute | solution.py:427
  54.8 3.4 %collective-permute-start.10 = (f32[15,16,128]{2,1,0:T(8,128)S(1)}, f32[15,16,128]{2,1,0:T(8,128)S(1)}, u32[]{:S(2)}, u32[]{:S(2)}) collective-permute-start(f32[15,16,128]{2,1,0:T(8,128)S(1)} %get-tuple-element.105), channel_id=1, source_target_pairs={{0,1},{2,3},{7,6},{5,4},{8,9},{10,11},{15,14},{13,12},{16,17},{18,... | collective-permute-start | bytes 368648 | tf_op jit(solution)/shard_map/ppermute | solution.py:428
  56.1 6.5 %collective-permute-start.11 = (f32[15,16,128]{2,1,0:T(8,128)S(1)}, f32[15,16,128]{2,1,0:T(8,128)S(1)}, u32[]{:S(2)}, u32[]{:S(2)}) collective-permute-start(f32[15,16,128]{2,1,0:T(8,128)S(1)} %get-tuple-element.111), channel_id=1, source_target_pairs={{1,2},{3,7},{6,5},{4,8},{9,10},{11,15},{14,13},{12,16},{17,18},{19... | collective-permute-start | bytes 368648 | tf_op jit(solution)/shard_map/ppermute | solution.py:427
  64.9 3.9 %collective-permute-start.13 = (f32[16,16,128]{2,1,0:T(8,128)S(1)}, f32[16,16,128]{2,1,0:T(8,128)S(1)}, u32[]{:S(2)}, u32[]{:S(2)}) collective-permute-start(f32[16,16,128]{2,1,0:T(8,128)S(1)} %get-tuple-element.112.refs_0_), channel_id=1, source_target_pairs={{2,0},{3,1},{0,2},{1,3},{6,4},{7,5},{4,6},{5,7},{10,8},{11,9},{8,1... | collective-permute-start | bytes 393224 | tf_op jit(solution)/shard_map/ppermute | solution.py:318
  64.9 6.2 %collective-permute-start.12 = (f32[16,16,128]{2,1,0:T(8,128)S(1)}, f32[16,16,128]{2,1,0:T(8,128)S(1)}, u32[]{:S(2)}, u32[]{:S(2)}) collective-permute-start(f32[16,16,128]{2,1,0:T(8,128)S(1)} %get-tuple-element.112.refs_0_), channel_id=1, source_target_pairs={{0,1},{1,0},{2,3},{3,2},{4,5},{5,4},{6,7},{7,6},{8,9},{9,8},{10,11... | collective-permute-start | bytes 393224 | tf_op jit(solution)/shard_map/ppermute | solution.py:322
  68.7 3.4 %collective-permute-start.14 = (f32[16,16,128]{2,1,0:T(8,128)S(1)}, f32[16,16,128]{2,1,0:T(8,128)S(1)}, u32[]{:S(2)}, u32[]{:S(2)}) collective-permute-start(f32[16,16,128]{2,1,0:T(8,128)S(1)} %collective-permute-done.13.refs_2_), channel_id=1, source_target_pairs={{0,1},{1,0},{2,3},{3,2},{4,5},{5,4},{6,7},{7,6},{8,9},{9,8},{10,11... | collective-permute-start | bytes 393224 | tf_op jit(solution)/shard_map/ppermute | solution.py:322

commit v6 on v5

--- a/solution.py
+++ b/solution.py
@@ -78,10 +78,13 @@
     now[pl.ds(at, h), 16:] = low
 
 
-def begin_of(counts, j):
+COUNTS = 4
+
+
+def begin_of(facts, folds, j):
     total = 0
-    for i in range(counts.shape[1]):
-        total = total + jnp.where(i < j, counts[0, i], 0)
+    for i in range(folds):
+        total = total + jnp.where(i < j, facts[COUNTS + i], 0)
     return total
 
 
@@ -93,7 +96,7 @@
     return jnp.where(backwards == 1, folds - 1 - fold, fold)
 
 
-def align_kernel(ob, steps, keys, facts, counts, *refs):
+def align_kernel(ob, steps, keys, facts, *refs):
     folds = len(keys)
     sources, (x, u, r, now, later, pay_a, pay_b) = refs[:folds], refs[folds:]
     del x, later
@@ -104,7 +107,7 @@
     spans = []
     for d, c in keys:
         owner = holder(facts[2], folds, d, c)
-        spans.append((begin_of(counts, owner), counts[0, owner]))
+        spans.append((begin_of(facts, folds, owner), facts[COUNTS + owner]))
 
     def block(e, carry):
         row = base + e * 128
@@ -135,31 +138,49 @@
     put_payload(ob, steps, sides(even, False), u, r, pay_b)
 
 
-def stack_kernel(initial, right_side, stacked, sem):
-    pair = [pltpu.make_async_copy(array, stacked.at[i], sem.at[i]) for i, array in enumerate((initial, right_side))]
+def first_kernel(folds, halo, width, counts, columns, initial, right_side, blocks, facts, held, stacked, border, live, sem):
+    own = columns.shape[1]
+    size = blocks.shape[0] // own
+    fold = lax.axis_index("fold")
+    backwards = lax.rem(lax.axis_index("group"), 2)
+    part = part_of(fold, folds, backwards)
+    edge = (part == 0) | (part == folds - 1)
+    first = jnp.where(part == 0, 0, own - halo)
+    small = [pltpu.make_async_copy(columns, held, sem.at[0]), pltpu.make_async_copy(counts, live, sem.at[1])]
+    pair = [pltpu.make_async_copy(array, stacked.at[i], sem.at[2 + i]) for i, array in enumerate((initial, right_side))]
+    rows = []
+    for i in range(halo):
+        row = blocks.at[pl.ds(pl.multiple_of((first + i) * size, size), size)]
+        rows.append(pltpu.make_async_copy(row, border.at[i * size : (i + 1) * size], sem.at[4 + i]))
+    for copy in small:
+        copy.start()
+
+    @pl.when(edge)
+    def _():
+        for copy in rows:
+            copy.start()
+
     for copy in pair:
         copy.start()
-    for copy in pair:
+    for copy in small:
         copy.wait()
-
-
-def outward_kernel(folds, halo, width, facts, columns, blocks, border, sem):
-    own = columns.shape[1]
-    size = blocks.shape[0] // own
-    part = facts[0]
-    first = jnp.where(part == 0, 0, own - halo)
-
-    @pl.when((part == 0) | (part == folds - 1))
+    for i, fact in enumerate((part, lax.rem(part, 2), fold, backwards)):
+        facts[i] = fact
+    for i in range(folds):
+        facts[COUNTS + i] = live[0, i]
+
+    @pl.when(edge)
     def _():
-        rows = blocks.at[pl.ds(pl.multiple_of(first * size, size), halo * size)]
-        copy = pltpu.make_async_copy(rows, border.at[: halo * size], sem)
-        copy.start()
         lane = lax.broadcasted_iota(jnp.int32, (8, 128), 1)
         indices = jnp.zeros((8, 128), jnp.int32)
         for i in range(halo):
             for k in range(width):
-                indices = jnp.where(lane == i * width + k, columns[k, first + i], indices)
+                indices = jnp.where(lane == i * width + k, held[k, first + i], indices)
         border[halo * size :] = indices.astype(F32)
+        for copy in rows:
+            copy.wait()
+
+    for copy in pair:
         copy.wait()
 
 
@@ -295,13 +316,13 @@
         put_payload(ob, steps, sides(even, False), u, r, outs[1])
 
 
-def finish_kernel(ob, keys, facts, counts, *refs):
+def finish_kernel(ob, keys, facts, *refs):
     parts, (out, whole) = refs[:-2], refs[-2:]
     total = whole.shape[0]
     for (d, c), part in zip(keys, parts):
         theirs = part_of(holder(facts[2], len(keys), d, c), len(keys), facts[3])
         whole[pl.ds(theirs * ob, ob)] = part[...]
-    start, count = begin_of(counts, facts[2]), counts[0, facts[2]]
+    start, count = begin_of(facts, len(keys), facts[2]), facts[COUNTS + facts[2]]
     lane = lax.broadcasted_iota(jnp.int32, (16, 128), 1)
     low, shift = start >> 7, start & 127
 
@@ -332,11 +353,7 @@
     halo = HB * (steps - 1)
     rows = ob + 2 * halo
     pairs = coefficients()
-    fold = lax.axis_index("fold")
-    backwards = lax.axis_index("group") % 2
-    part = part_of(fold, folds, backwards)
     devices = groups * folds
-    facts = jnp.stack([part, part % 2, fold, backwards]).astype(jnp.int32)
     operator_shape = pltpu.VMEM((rows, size, 2 * side), BF16)
 
     payload = jax.ShapeDtypeStruct((2 * HB * steps - HB, vectors, side), F32)
@@ -349,31 +366,30 @@
 
     swap_a, swap_b, swap_border = swap(0, 2), swap(1, 2), swap(folds - 1, folds)
 
-    near = [pltpu.with_memory_space_constraint(array, pltpu.HBM) for array in (initial, right_side)]
-    stacked = pl.pallas_call(
-        stack_kernel,
-        out_shape=pltpu.VMEM((2, vectors, capacity), F32),
-        in_specs=[HBM, HBM],
-        out_specs=VMEM,
-        scratch_shapes=[pltpu.SemaphoreType.DMA((2,))],
+    def fixed(array, space=pltpu.HBM):
+        return pltpu.with_memory_space_constraint(array, space)
+
+    flat = fixed(blocks.reshape(own * size, side))
+    facts, indices, stacked, border = pl.pallas_call(
+        functools.partial(first_kernel, folds, halo, width),
+        out_shape=(
+            pltpu.SMEM((COUNTS + folds,), jnp.int32),
+            pltpu.SMEM((width, own), jnp.int32),
+            pltpu.VMEM((2, vectors, capacity), F32),
+            pltpu.VMEM((halo * size + 8, side), F32),
+        ),
+        in_specs=[HBM] * 5,
+        out_specs=(SMEM, SMEM, VMEM, VMEM),
+        scratch_shapes=[pltpu.SMEM((1, folds), jnp.int32), pltpu.SemaphoreType.DMA((4 + halo,))],
         compiler_params=params(),
-    )(*near)
+    )(fixed(counts), fixed(columns.T), fixed(initial), fixed(right_side), flat)
+    facts, indices = fixed(facts, pltpu.SMEM), fixed(indices, pltpu.SMEM)
+    border = lax.ppermute(border, AXES, swap_border)
     far = [over_chips(stacked, d, folds) for d in range(1, folds // 2)]
-    turned = columns.T
-    flat = pltpu.with_memory_space_constraint(blocks.reshape(own * size, side), pltpu.HBM)
-    border = pl.pallas_call(
-        functools.partial(outward_kernel, folds, halo, width),
-        out_shape=pltpu.VMEM((halo * size + 8, side), F32),
-        in_specs=[SMEM, SMEM, HBM],
-        out_specs=VMEM,
-        scratch_shapes=[pltpu.SemaphoreType.DMA(())],
-        compiler_params=params(),
-    )(facts, turned, flat)
-    border = lax.ppermute(border, AXES, swap_border)
 
     operator, token, offsets = pl.pallas_call(
         functools.partial(prepare_kernel, ob, halo, width),
-        out_shape=(operator_shape, jax.ShapeDtypeStruct((8, 128), F32), jax.ShapeDtypeStruct((rows * width,), jnp.int32)),
+        out_shape=(operator_shape, jax.ShapeDtypeStruct((8, 128), F32), pltpu.SMEM((rows * width,), jnp.int32)),
         in_specs=[SMEM, SMEM, HBM],
         out_specs=(VMEM, VMEM, SMEM),
         scratch_shapes=[
@@ -382,7 +398,8 @@
         ],
         compiler_params=params(),
         cost_estimate=pl.CostEstimate(flops=10**7, bytes_accessed=2 * rows * size * side * 4, transcendentals=0),
-    )(facts, turned, flat)
+    )(facts, indices, flat)
+    offsets = fixed(offsets, pltpu.SMEM)
 
     def gate(arrays, spaces, token):
         return pl.pallas_call(
@@ -405,10 +422,10 @@
     *held, pay_a, pay_b = pl.pallas_call(
         functools.partial(align_kernel, ob, steps, keys),
         out_shape=(*state, payload, payload),
-        in_specs=[SMEM, SMEM] + [VMEM] * folds,
+        in_specs=[SMEM] + [VMEM] * folds,
         out_specs=(VMEM,) * 7,
         compiler_params=params(),
-    )(facts, counts, *[pltpu.with_memory_space_constraint(array, pltpu.VMEM) for array in arrays])
+    )(facts, *[fixed(array, pltpu.VMEM) for array in arrays])
 
     def part_of_phase(kernel, operator, indices, held, got, outs):
         held = [pltpu.with_memory_space_constraint(array, pltpu.VMEM) for array in held]
@@ -430,7 +447,7 @@
         if done == 0:
             operator, lent = pl.pallas_call(
                 functools.partial(border_kernel, ob, folds, halo, width),
-                out_shape=(operator_shape, jax.ShapeDtypeStruct((halo * width,), jnp.int32)),
+                out_shape=(operator_shape, pltpu.SMEM((halo * width,), jnp.int32)),
                 in_specs=[SMEM, VMEM, VMEM, pl.BlockSpec(memory_space=pl.ANY)],
                 out_specs=(VMEM, SMEM),
                 input_output_aliases={1: 0},
@@ -441,6 +458,7 @@
                 ],
                 compiler_params=params(),
             )(facts, pltpu.with_memory_space_constraint(operator, pltpu.VMEM), border, held[0])
+            lent = fixed(lent, pltpu.SMEM)
         if done + steps < APPLIES:
             held, (pay_a, pay_b) = part_of_phase(
                 outer_kernel, operator, [offsets, lent], held, got_b, (payload, payload)
@@ -458,11 +476,11 @@
     return pl.pallas_call(
         functools.partial(finish_kernel, ob, keys),
         out_shape=jax.ShapeDtypeStruct((vectors, capacity), F32),
-        in_specs=[SMEM, SMEM] + [VMEM] * folds,
+        in_specs=[SMEM] + [VMEM] * folds,
         out_specs=VMEM,
         scratch_shapes=[pltpu.VMEM((own, vectors, side), F32)],
         compiler_params=params(),
-    )(facts, counts, *parts)
+    )(facts, *parts)
 
 
 def solution(mesh):

time: 74.3 us -> 68.9 us (0.927)
  Pallas kernels: 33.3 us -> 24.9 us
  waiting for transfers between devices: 14.6 us -> 19 us
    pallas_call x8, Pallas kernels: 20.9 us -> 16.4 us  [part_of_phase(): pl.pallas_call(functools.partial(kernel, ob, folds, steps, done == 0, don...]
    ppermute x4, waiting for transfers between devices: 4.23 us -> 7.59 us  [on_device(): got_b = lax.ppermute(pay_b, AXES, swap_b)]
    ppermute x4, starting transfers between devices: 4.53 us -> 5.79 us  [on_device(): got_a = lax.ppermute(pay_a, AXES, swap_a)]
    pallas_call x1, Pallas kernels: 1.15 us -> 0.02 us  [on_device(): pl.pallas_call(functools.partial(border_kernel, ob, folds, halo, width),...]
    ppermute x2, waiting for transfers between devices: 7.8 us -> 8.88 us  [over_chips(): lax.ppermute(array, 'fold', [((i + 2 * d) % folds, i) for i in range(fold...]
    pallas_call x1, Pallas kernels: 6.31 us -> 5.24 us  [on_device(): pl.pallas_call(functools.partial(prepare_kernel, ob, halo, width), out_sh...]
    ppermute x2, starting transfers between devices: 5.22 us -> 4.24 us  [over_chips(): lax.ppermute(array, 'fold', [((i + 2 * d) % folds, i) for i in range(fold...]
    pallas_call x2 -> x1, Pallas kernels: 1.67 us -> 1.12 us  [on_device(): pl.pallas_call(functools.partial(first_kernel, folds, halo, width), out_s...]
  transfers between devices with their start and end apart: 15 -> 15, of which waited for: 7 -> 8; matrix products, arithmetic and copies ran while one was open for 0% -> 0% of each run, Pallas kernels for 29% -> 23%
where the time goes in v6:
time: 68.9 us; the launch traced here: 68.7 us
  Pallas kernels  24.9 us (36%)
  starting transfers between devices  24.7 us (36%)
  waiting for transfers between devices  19 us (28%)
    pallas_call x8, Pallas kernels, part_of_phase(): pl.pallas_call(functools.partial(kernel, ob, folds, steps, done == 0, don...  16.4 us
    ppermute x4, starting transfers between devices, on_device(): got_b = lax.ppermute(pay_b, AXES, swap_b)  8.91 us
    ppermute x2, waiting for transfers between devices, over_chips(): lax.ppermute(array, 'fold', [((i + 2 * d) % folds, i) for i in range(fold...  8.88 us
    ppermute x4, waiting for transfers between devices, on_device(): got_b = lax.ppermute(pay_b, AXES, swap_b)  7.59 us
    ppermute x4, starting transfers between devices, on_device(): got_a = lax.ppermute(pay_a, AXES, swap_a)  5.79 us
    pallas_call x1, Pallas kernels, on_device(): pl.pallas_call(functools.partial(prepare_kernel, ob, halo, width), out_sh...  5.24 us
    ppermute x4, starting transfers between devices, other_core(): return lax.ppermute(array, 'fold', [(i, i ^ 1) for i in range(folds)])  4.92 us
    ppermute x2, starting transfers between devices, over_chips(): lax.ppermute(array, 'fold', [((i + 2 * d) % folds, i) for i in range(fold...  4.24 us
  transfers between devices with their start and end apart: 15, of which 8 were waited for; matrix products, arithmetic and copies ran while one was open for 0% of the time, Pallas kernels for 23%

profile of v6, /device:TPU:9, one launch (start us, length us, event | category | flops | bytes accessed | tf_op | source)
XLA Modules:
  0.0 68.7 jit_solution(5127473509433976979)
XLA Ops:
  0.0 1.1 %shard_map.55 = (s32[8]{0:T(128)S(4)}, s32[5,64]{1,0:T(8,128)S(4)}, f32[2,16,4096]{2,1,0:T(8,128)S(1)}, f32[3848,128]{1,0:T(8,128)S(1)}) custom-call(s32[1,4]{1,0:T(1,128)} %counts.1, s32[5,64]{1,0:T(8,128)} %bitcast.4, f32[16,4096]{1,0:T(8,128)} %initial.1, f32[16,4096]{1,0:T(8,128)} %right_side.1, f32[40960,128]{1,0:T(8,128)} %bitcast.2), custom_call_target="tpu_custom_call" | custom-call | tf_op jit(solution)/shard_map/pallas_call | solution.py:373
  1.1 0.8 %collective-permute-start = (f32[3848,128]{1,0:T(8,128)S(1)}, f32[3848,128]{1,0:T(8,128)S(1)}, u32[]{:S(2)}, u32[]{:S(2)}) collective-permute-start(f32[3848,128]{1,0:T(8,128)S(1)} %get-tuple-element.67), channel_id=1, source_target_pairs={{3,7},{4,8},{11,15},{12,16},{19,23},{20,24},{27,31},{7,3},{8,4},{1... | collective-permute-start | bytes 5910536 | tf_op jit(solution)/shard_map/ppermute | solution.py:387
  1.9 4.2 %collective-permute-start.2 = (f32[2,16,4096]{2,1,0:T(8,128)S(1)}, f32[2,16,4096]{2,1,0:T(8,128)S(1)}, u32[]{:S(2)}, u32[]{:S(2)}) collective-permute-start(f32[2,16,4096]{2,1,0:T(8,128)S(1)} %get-tuple-element.68.refs_0_), channel_id=1, source_target_pairs={{2,0},{3,1},{0,2},{1,3},{6,4},{7,5},{4,6},{5,7},{10,8},{11,9},{8,1... | collective-permute-start | bytes 1572872 | tf_op jit(solution)/shard_map/ppermute | solution.py:339
  6.1 0.0 collective-permute-start.1
  6.2 5.2 %shard_map.56 = (bf16[28,640,256]{2,1,0:T(8,128)(2,1)S(1)}, f32[8,128]{1,0:T(8,128)S(1)}, s32[140]{0:T(256)S(4)}) custom-call(s32[8]{0:T(128)S(4)} %get-tuple-element.63.facts, s32[5,64]{1,0:T(8,128)S(4)} %get-tuple-element.64.columns, f32[40960,128]{1,0:T(8,128)} %bitcast.3), custom_call_target="tpu_custom_call" | custom-call | flops 10000000 | bytes 18350080 | tf_op jit(solution)/shard_map/pallas_call | solution.py:390
  11.4 6.3 %collective-permute-done.2.refs_0_ = f32[2,16,4096]{2,1,0:T(8,128)S(1)} collective-permute-done((f32[2,16,4096]{2,1,0:T(8,128)S(1)}, f32[2,16,4096]{2,1,0:T(8,128)S(1)}, u32[]{:S(2)}, u32[]{:S(2)}) %collective-permute-start.2) | collective-permute-done | bytes 524320 | tf_op jit(solution)/shard_map/ppermute | solution.py:339
  17.8 1.3 %collective-permute-start.3 = (f32[2,16,4096]{2,1,0:T(8,128)S(1)}, f32[2,16,4096]{2,1,0:T(8,128)S(1)}, u32[]{:S(2)}, u32[]{:S(2)}) collective-permute-start(f32[2,16,4096]{2,1,0:T(8,128)S(1)} %shard_map.57.refs_2_), channel_id=1, source_target_pairs={{0,1},{1,0},{2,3},{3,2},{4,5},{5,4},{6,7},{7,6},{8,9},{9,8},{10,11... | collective-permute-start | bytes 1572872 | tf_op jit(solution)/shard_map/ppermute | solution.py:343
  19.0 0.0 collective-permute-done.1.refs_1_
  19.0 1.5 %collective-permute-done.3.refs_3_ = f32[2,16,4096]{2,1,0:T(8,128)S(1)} collective-permute-done((f32[2,16,4096]{2,1,0:T(8,128)S(1)}, f32[2,16,4096]{2,1,0:T(8,128)S(1)}, u32[]{:S(2)}, u32[]{:S(2)}) %collective-permute-start.3) | collective-permute-done | bytes 524320 | tf_op jit(solution)/shard_map/ppermute | solution.py:343
  20.6 0.9 %shard_map.58 = (f32[34,16,128]{2,1,0:T(8,128)S(1)}, f32[34,16,128]{2,1,0:T(8,128)S(1)}, f32[34,16,128]{2,1,0:T(8,128)S(1)}, bf16[34,32,128]{2,1,0:T(8,128)(2,1)...) custom-call(s32[8]{0:T(128)S(4)} %get-tuple-element.63.facts, ...), custom_call_target="tpu_custom_call" | custom-call | tf_op jit(solution)/shard_map/pallas_call | solution.py:422
  21.5 0.4 collective-permute-start.4
  22.0 3.0 %collective-permute-start.5 = (f32[15,16,128]{2,1,0:T(8,128)S(1)}, f32[15,16,128]{2,1,0:T(8,128)S(1)}, u32[]{:S(2)}, u32[]{:S(2)}) collective-permute-start(f32[15,16,128]{2,1,0:T(8,128)S(1)} %get-tuple-element.83), channel_id=1, source_target_pairs={{1,2},{3,7},{6,5},{4,8},{9,10},{11,15},{14,13},{12,16},{17,18},{19... | collective-permute-start | bytes 368648 | tf_op jit(solution)/shard_map/ppermute | solution.py:444
  25.0 0.0 collective-permute-done.4.refs_5_
  25.0 2.3 %shard_map.59 = (f32[34,16,128]{2,1,0:T(8,128)S(1)}, f32[34,16,128]{2,1,0:T(8,128)S(1)}, f32[34,16,128]{2,1,0:T(8,128)S(1)}, bf16[34,32,128]{2,1,0:T(8,128)(2,1)S(1)}, bf16[34,32,128]{2,1,0:T(8,128)(2,1)S(1)}) custom-call(s32[8]{0:T(128)S(4)} %get-tuple-element.63.facts, ...), custom_call_target="tpu_custom_call", output_to_operand_aliasing={{0}: (3, {}), {1}: (4, {}), {2}: (5, {}), {3}: (6, {}), {4}... | custom-call | tf_op jit(solution)/shard_map/pallas_call | solution.py:433
  27.3 0.0 collective-permute-done.raw
  27.3 1.1 %collective-permute-done.5.refs_5_ = f32[15,16,128]{2,1,0:T(8,128)S(1)} collective-permute-done((f32[15,16,128]{2,1,0:T(8,128)S(1)}, f32[15,16,128]{2,1,0:T(8,128)S(1)}, u32[]{:S(2)}, u32[]{:S(2)}) %collective-permute-start.5) | collective-permute-done | bytes 122912 | tf_op jit(solution)/shard_map/ppermute | solution.py:444
  28.4 1.8 %shard_map.61 = (f32[34,16,128]{2,1,0:T(8,128)S(1)}, f32[34,16,128]{2,1,0:T(8,128)S(1)}, f32[34,16,128]{2,1,0:T(8,128)S(1)}, bf16[34,32,128]{2,1,0:T(8,128)(2,1)...) custom-call(s32[8]{0:T(128)S(4)} %get-tuple-element.63.facts, ...), custom_call_target="tpu_custom_call", output_to_operand_aliasing={{0}: (4, {}), {1}: (5, {}), {2}: (6, {}), {3}: (7, {}), {4}... | custom-call | tf_op jit(solution)/shard_map/pallas_call | solution.py:433
  30.2 2.8 %collective-permute-start.6 = (f32[15,16,128]{2,1,0:T(8,128)S(1)}, f32[15,16,128]{2,1,0:T(8,128)S(1)}, u32[]{:S(2)}, u32[]{:S(2)}) collective-permute-start(f32[15,16,128]{2,1,0:T(8,128)S(1)} %get-tuple-element.89), channel_id=1, source_target_pairs={{0,1},{2,3},{7,6},{5,4},{8,9},{10,11},{15,14},{13,12},{16,17},{18,... | collective-permute-start | bytes 368648 | tf_op jit(solution)/shard_map/ppermute | solution.py:445
  33.0 1.9 %collective-permute-start.7 = (f32[15,16,128]{2,1,0:T(8,128)S(1)}, f32[15,16,128]{2,1,0:T(8,128)S(1)}, u32[]{:S(2)}, u32[]{:S(2)}) collective-permute-start(f32[15,16,128]{2,1,0:T(8,128)S(1)} %get-tuple-element.95), channel_id=1, source_target_pairs={{1,2},{3,7},{6,5},{4,8},{9,10},{11,15},{14,13},{12,16},{17,18},{19... | collective-permute-start | bytes 368648 | tf_op jit(solution)/shard_map/ppermute | solution.py:444
  35.0 0.0 collective-permute-done.6.refs_5_
  35.0 2.3 %shard_map.62 = (f32[34,16,128]{2,1,0:T(8,128)S(1)}, f32[34,16,128]{2,1,0:T(8,128)S(1)}, f32[34,16,128]{2,1,0:T(8,128)S(1)}, bf16[34,32,128]{2,1,0:T(8,128)(2,1)S(1)}, bf16[34,32,128]{2,1,0:T(8,128)(2,1)S(1)}) custom-call(s32[8]{0:T(128)S(4)} %get-tuple-element.63.facts, ...), custom_call_target="tpu_custom_call", output_to_operand_aliasing={{0}: (3, {}), {1}: (4, {}), {2}: (5, {}), {3}: (6, {}), {4}... | custom-call | tf_op jit(solution)/shard_map/pallas_call | solution.py:433
  37.3 2.2 %collective-permute-done.7.refs_5_ = f32[15,16,128]{2,1,0:T(8,128)S(1)} collective-permute-done((f32[15,16,128]{2,1,0:T(8,128)S(1)}, f32[15,16,128]{2,1,0:T(8,128)S(1)}, u32[]{:S(2)}, u32[]{:S(2)}) %collective-permute-start.7) | collective-permute-done | bytes 122912 | tf_op jit(solution)/shard_map/ppermute | solution.py:444
  39.5 1.8 %shard_map.63 = (f32[34,16,128]{2,1,0:T(8,128)S(1)}, f32[34,16,128]{2,1,0:T(8,128)S(1)}, f32[34,16,128]{2,1,0:T(8,128)S(1)}, bf16[34,32,128]{2,1,0:T(8,128)(2,1)...) custom-call(s32[8]{0:T(128)S(4)} %get-tuple-element.63.facts, ...), custom_call_target="tpu_custom_call", output_to_operand_aliasing={{0}: (4, {}), {1}: (5, {}), {2}: (6, {}), {3}: (7, {}), {4}... | custom-call | tf_op jit(solution)/shard_map/pallas_call | solution.py:433
  41.3 1.3 %collective-permute-start.8 = (f32[15,16,128]{2,1,0:T(8,128)S(1)}, f32[15,16,128]{2,1,0:T(8,128)S(1)}, u32[]{:S(2)}, u32[]{:S(2)}) collective-permute-start(f32[15,16,128]{2,1,0:T(8,128)S(1)} %get-tuple-element.101), channel_id=1, source_target_pairs={{0,1},{2,3},{7,6},{5,4},{8,9},{10,11},{15,14},{13,12},{16,17},{18,... | collective-permute-start | bytes 368648 | tf_op jit(solution)/shard_map/ppermute | solution.py:445
  42.6 1.9 %collective-permute-start.9 = (f32[15,16,128]{2,1,0:T(8,128)S(1)}, f32[15,16,128]{2,1,0:T(8,128)S(1)}, u32[]{:S(2)}, u32[]{:S(2)}) collective-permute-start(f32[15,16,128]{2,1,0:T(8,128)S(1)} %get-tuple-element.107), channel_id=1, source_target_pairs={{1,2},{3,7},{6,5},{4,8},{9,10},{11,15},{14,13},{12,16},{17,18},{19... | collective-permute-start | bytes 368648 | tf_op jit(solution)/shard_map/ppermute | solution.py:444
  44.5 0.0 collective-permute-done.8.refs_5_
  44.5 2.3 %shard_map.64 = (f32[34,16,128]{2,1,0:T(8,128)S(1)}, f32[34,16,128]{2,1,0:T(8,128)S(1)}, f32[34,16,128]{2,1,0:T(8,128)S(1)}, bf16[34,32,128]{2,1,0:T(8,128)(2,1)S(1)}, bf16[34,32,128]{2,1,0:T(8,128)(2,1)S(1)}) custom-call(s32[8]{0:T(128)S(4)} %get-tuple-element.63.facts, ...), custom_call_target="tpu_custom_call", output_to_operand_aliasing={{0}: (3, {}), {1}: (4, {}), {2}: (5, {}), {3}: (6, {}), {4}... | custom-call | tf_op jit(solution)/shard_map/pallas_call | solution.py:433
  46.8 2.2 %collective-permute-done.9.refs_5_ = f32[15,16,128]{2,1,0:T(8,128)S(1)} collective-permute-done((f32[15,16,128]{2,1,0:T(8,128)S(1)}, f32[15,16,128]{2,1,0:T(8,128)S(1)}, u32[]{:S(2)}, u32[]{:S(2)}) %collective-permute-start.9) | collective-permute-done | bytes 122912 | tf_op jit(solution)/shard_map/ppermute | solution.py:444
  49.0 1.8 %shard_map.65 = (f32[34,16,128]{2,1,0:T(8,128)S(1)}, f32[34,16,128]{2,1,0:T(8,128)S(1)}, f32[34,16,128]{2,1,0:T(8,128)S(1)}, bf16[34,32,128]{2,1,0:T(8,128)(2,1)...) custom-call(s32[8]{0:T(128)S(4)} %get-tuple-element.63.facts, ...), custom_call_target="tpu_custom_call", output_to_operand_aliasing={{0}: (4, {}), {1}: (5, {}), {2}: (6, {}), {3}: (7, {}), {4}... | custom-call | tf_op jit(solution)/shard_map/pallas_call | solution.py:433
  50.8 1.3 %collective-permute-start.10 = (f32[15,16,128]{2,1,0:T(8,128)S(1)}, f32[15,16,128]{2,1,0:T(8,128)S(1)}, u32[]{:S(2)}, u32[]{:S(2)}) collective-permute-start(f32[15,16,128]{2,1,0:T(8,128)S(1)} %get-tuple-element.113), channel_id=1, source_target_pairs={{0,1},{2,3},{7,6},{5,4},{8,9},{10,11},{15,14},{13,12},{16,17},{18,... | collective-permute-start | bytes 368648 | tf_op jit(solution)/shard_map/ppermute | solution.py:445
  52.1 2.1 %collective-permute-start.11 = (f32[15,16,128]{2,1,0:T(8,128)S(1)}, f32[15,16,128]{2,1,0:T(8,128)S(1)}, u32[]{:S(2)}, u32[]{:S(2)}) collective-permute-start(f32[15,16,128]{2,1,0:T(8,128)S(1)} %get-tuple-element.119), channel_id=1, source_target_pairs={{1,2},{3,7},{6,5},{4,8},{9,10},{11,15},{14,13},{12,16},{17,18},{19... | collective-permute-start | bytes 368648 | tf_op jit(solution)/shard_map/ppermute | solution.py:444
  54.2 0.0 collective-permute-done.10.refs_5_
  54.2 2.3 %shard_map.66 = (f32[34,16,128]{2,1,0:T(8,128)S(1)}, f32[34,16,128]{2,1,0:T(8,128)S(1)}, f32[34,16,128]{2,1,0:T(8,128)S(1)}, bf16[34,32,128]{2,1,0:T(8,128)(2,1)S(1)}, bf16[34,32,128]{2,1,0:T(8,128)(2,1)S(1)}) custom-call(s32[8]{0:T(128)S(4)} %get-tuple-element.63.facts, ...), custom_call_target="tpu_custom_call", output_to_operand_aliasing={{0}: (3, {}), {1}: (4, {}), {2}: (5, {}), {3}: (6, {}), {4}... | custom-call | tf_op jit(solution)/shard_map/pallas_call | solution.py:433
  56.5 2.1 %collective-permute-done.11.refs_5_ = f32[15,16,128]{2,1,0:T(8,128)S(1)} collective-permute-done((f32[15,16,128]{2,1,0:T(8,128)S(1)}, f32[15,16,128]{2,1,0:T(8,128)S(1)}, u32[]{:S(2)}, u32[]{:S(2)}) %collective-permute-start.11) | collective-permute-done | bytes 122912 | tf_op jit(solution)/shard_map/ppermute | solution.py:444
  58.6 1.8 %shard_map.67 = (f32[34,16,128]{2,1,0:T(8,128)S(1)}, f32[34,16,128]{2,1,0:T(8,128)S(1)}, f32[34,16,128]{2,1,0:T(8,128)S(1)}, bf16[34,32,128]{2,1,0:T(8,128)(2,1)...) custom-call(s32[8]{0:T(128)S(4)} %get-tuple-element.63.facts, ...), custom_call_target="tpu_custom_call", output_to_operand_aliasing={{0}: (4, {}), {1}: (5, {}), {2}: (6, {}), {3}: (7, {}), {4}... | custom-call | tf_op jit(solution)/shard_map/pallas_call | solution.py:433
  60.3 0.0 collective-permute-start.13
  60.4 1.3 %collective-permute-start.12 = (f32[16,16,128]{2,1,0:T(8,128)S(1)}, f32[16,16,128]{2,1,0:T(8,128)S(1)}, u32[]{:S(2)}, u32[]{:S(2)}) collective-permute-start(f32[16,16,128]{2,1,0:T(8,128)S(1)} %get-tuple-element.120.refs_0_), channel_id=1, source_target_pairs={{0,1},{1,0},{2,3},{3,2},{4,5},{5,4},{6,7},{7,6},{8,9},{9,8},{10,11... | collective-permute-start | bytes 393224 | tf_op jit(solution)/shard_map/ppermute | solution.py:343
  61.6 2.5 %collective-permute-done.13.refs_2_ = f32[16,16,128]{2,1,0:T(8,128)S(1)} collective-permute-done((f32[16,16,128]{2,1,0:T(8,128)S(1)}, f32[16,16,128]{2,1,0:T(8,128)S(1)}, u32[]{:S(2)}, u32[]{:S(2)}) %collective-permute-start.13) | collective-permute-done | bytes 131104 | tf_op jit(solution)/shard_map/ppermute | solution.py:339
  64.2 2.4 %collective-permute-start.14 = (f32[16,16,128]{2,1,0:T(8,128)S(1)}, f32[16,16,128]{2,1,0:T(8,128)S(1)}, u32[]{:S(2)}, u32[]{:S(2)}) collective-permute-start(f32[16,16,128]{2,1,0:T(8,128)S(1)} %collective-permute-done.13.refs_2_), channel_id=1, source_target_pairs={{0,1},{1,0},{2,3},{3,2},{4,5},{5,4},{6,7},{7,6},{8,9},{9,8},{10,11... | collective-permute-start | bytes 393224 | tf_op jit(solution)/shard_map/ppermute | solution.py:343
  66.5 0.0 collective-permute-done.12.refs_1_
  66.5 1.0 %collective-permute-done.14.refs_3_ = f32[16,16,128]{2,1,0:T(8,128)S(1)} collective-permute-done((f32[16,16,128]{2,1,0:T(8,128)S(1)}, f32[16,16,128]{2,1,0:T(8,128)S(1)}, u32[]{:S(2)}, u32[]{:S(2)}) %collective-permute-start.14) | collective-permute-done | bytes 131104 | tf_op jit(solution)/shard_map/ppermute | solution.py:343
  67.5 1.2 %shard_map.68 = f32[16,4096]{1,0:T(8,128)} custom-call(s32[8]{0:T(128)S(4)} %get-tuple-element.63.facts, f32[16,16,128]{2,1,0:T(8,128)S(1)} %get-tuple-element.120.refs_0_, f32[16,16,128]{2,1,0:T(8,128)S(1)} %collective-permute-done.12.refs_1_, f32[16,16,128]{2,1,0:T(8,128)S(1)} %collective-permute-done.13.refs_2_, ...), custom_call_target="tpu_custom_call" | custom-call | tf_op jit(solution)/shard_map/pallas_call | solution.py:476
  (2 shorter events, 0.0 us)
Async XLA Ops:
  1.1 26.2 %collective-permute-start = (f32[3848,128]{1,0:T(8,128)S(1)}, f32[3848,128]{1,0:T(8,128)S(1)}, u32[]{:S(2)}, u32[]{:S(2)}) collective-permute-start(f32[3848,128]{1,0:T(8,128)S(1)} %get-tuple-element.67), channel_id=1, source_target_pairs={{3,7},{4,8},{11,15},{12,16},{19,23},{20,24},{27,31},{7,3},{8,4},{1... | collective-permute-start | bytes 5910536 | tf_op jit(solution)/shard_map/ppermute | solution.py:387
  1.9 15.8 %collective-permute-start.2 = (f32[2,16,4096]{2,1,0:T(8,128)S(1)}, f32[2,16,4096]{2,1,0:T(8,128)S(1)}, u32[]{:S(2)}, u32[]{:S(2)}) collective-permute-start(f32[2,16,4096]{2,1,0:T(8,128)S(1)} %get-tuple-element.68.refs_0_), channel_id=1, source_target_pairs={{2,0},{3,1},{0,2},{1,3},{6,4},{7,5},{4,6},{5,7},{10,8},{11,9},{8,1... | collective-permute-start | bytes 1572872 | tf_op jit(solution)/shard_map/ppermute | solution.py:339
  6.1 12.9 %collective-permute-start.1 = (f32[2,16,4096]{2,1,0:T(8,128)S(1)}, f32[2,16,4096]{2,1,0:T(8,128)S(1)}, u32[]{:S(2)}, u32[]{:S(2)}) collective-permute-start(f32[2,16,4096]{2,1,0:T(8,128)S(1)} %get-tuple-element.68.refs_0_), channel_id=1, source_target_pairs={{0,1},{1,0},{2,3},{3,2},{4,5},{5,4},{6,7},{7,6},{8,9},{9,8},{10,11... | collective-permute-start | bytes 1572872 | tf_op jit(solution)/shard_map/ppermute | solution.py:343
  17.8 2.8 %collective-permute-start.3 = (f32[2,16,4096]{2,1,0:T(8,128)S(1)}, f32[2,16,4096]{2,1,0:T(8,128)S(1)}, u32[]{:S(2)}, u32[]{:S(2)}) collective-permute-start(f32[2,16,4096]{2,1,0:T(8,128)S(1)} %shard_map.57.refs_2_), channel_id=1, source_target_pairs={{0,1},{1,0},{2,3},{3,2},{4,5},{5,4},{6,7},{7,6},{8,9},{9,8},{10,11... | collective-permute-start | bytes 1572872 | tf_op jit(solution)/shard_map/ppermute | solution.py:343
  21.5 3.5 %collective-permute-start.4 = (f32[15,16,128]{2,1,0:T(8,128)S(1)}, f32[15,16,128]{2,1,0:T(8,128)S(1)}, u32[]{:S(2)}, u32[]{:S(2)}) collective-permute-start(f32[15,16,128]{2,1,0:T(8,128)S(1)} %get-tuple-element.75), channel_id=1, source_target_pairs={{0,1},{2,3},{7,6},{5,4},{8,9},{10,11},{15,14},{13,12},{16,17},{18,... | collective-permute-start | bytes 368648 | tf_op jit(solution)/shard_map/ppermute | solution.py:445
  22.0 6.5 %collective-permute-start.5 = (f32[15,16,128]{2,1,0:T(8,128)S(1)}, f32[15,16,128]{2,1,0:T(8,128)S(1)}, u32[]{:S(2)}, u32[]{:S(2)}) collective-permute-start(f32[15,16,128]{2,1,0:T(8,128)S(1)} %get-tuple-element.83), channel_id=1, source_target_pairs={{1,2},{3,7},{6,5},{4,8},{9,10},{11,15},{14,13},{12,16},{17,18},{19... | collective-permute-start | bytes 368648 | tf_op jit(solution)/shard_map/ppermute | solution.py:444
  30.2 4.7 %collective-permute-start.6 = (f32[15,16,128]{2,1,0:T(8,128)S(1)}, f32[15,16,128]{2,1,0:T(8,128)S(1)}, u32[]{:S(2)}, u32[]{:S(2)}) collective-permute-start(f32[15,16,128]{2,1,0:T(8,128)S(1)} %get-tuple-element.89), channel_id=1, source_target_pairs={{0,1},{2,3},{7,6},{5,4},{8,9},{10,11},{15,14},{13,12},{16,17},{18,... | collective-permute-start | bytes 368648 | tf_op jit(solution)/shard_map/ppermute | solution.py:445
  33.0 6.5 %collective-permute-start.7 = (f32[15,16,128]{2,1,0:T(8,128)S(1)}, f32[15,16,128]{2,1,0:T(8,128)S(1)}, u32[]{:S(2)}, u32[]{:S(2)}) collective-permute-start(f32[15,16,128]{2,1,0:T(8,128)S(1)} %get-tuple-element.95), channel_id=1, source_target_pairs={{1,2},{3,7},{6,5},{4,8},{9,10},{11,15},{14,13},{12,16},{17,18},{19... | collective-permute-start | bytes 368648 | tf_op jit(solution)/shard_map/ppermute | solution.py:444
  41.3 3.2 %collective-permute-start.8 = (f32[15,16,128]{2,1,0:T(8,128)S(1)}, f32[15,16,128]{2,1,0:T(8,128)S(1)}, u32[]{:S(2)}, u32[]{:S(2)}) collective-permute-start(f32[15,16,128]{2,1,0:T(8,128)S(1)} %get-tuple-element.101), channel_id=1, source_target_pairs={{0,1},{2,3},{7,6},{5,4},{8,9},{10,11},{15,14},{13,12},{16,17},{18,... | collective-permute-start | bytes 368648 | tf_op jit(solution)/shard_map/ppermute | solution.py:445
  42.6 6.5 %collective-permute-start.9 = (f32[15,16,128]{2,1,0:T(8,128)S(1)}, f32[15,16,128]{2,1,0:T(8,128)S(1)}, u32[]{:S(2)}, u32[]{:S(2)}) collective-permute-start(f32[15,16,128]{2,1,0:T(8,128)S(1)} %get-tuple-element.107), channel_id=1, source_target_pairs={{1,2},{3,7},{6,5},{4,8},{9,10},{11,15},{14,13},{12,16},{17,18},{19... | collective-permute-start | bytes 368648 | tf_op jit(solution)/shard_map/ppermute | solution.py:444
  50.8 3.4 %collective-permute-start.10 = (f32[15,16,128]{2,1,0:T(8,128)S(1)}, f32[15,16,128]{2,1,0:T(8,128)S(1)}, u32[]{:S(2)}, u32[]{:S(2)}) collective-permute-start(f32[15,16,128]{2,1,0:T(8,128)S(1)} %get-tuple-element.113), channel_id=1, source_target_pairs={{0,1},{2,3},{7,6},{5,4},{8,9},{10,11},{15,14},{13,12},{16,17},{18,... | collective-permute-start | bytes 368648 | tf_op jit(solution)/shard_map/ppermute | solution.py:445
  52.1 6.5 %collective-permute-start.11 = (f32[15,16,128]{2,1,0:T(8,128)S(1)}, f32[15,16,128]{2,1,0:T(8,128)S(1)}, u32[]{:S(2)}, u32[]{:S(2)}) collective-permute-start(f32[15,16,128]{2,1,0:T(8,128)S(1)} %get-tuple-element.119), channel_id=1, source_target_pairs={{1,2},{3,7},{6,5},{4,8},{9,10},{11,15},{14,13},{12,16},{17,18},{19... | collective-permute-start | bytes 368648 | tf_op jit(solution)/shard_map/ppermute | solution.py:444
  60.3 3.8 %collective-permute-start.13 = (f32[16,16,128]{2,1,0:T(8,128)S(1)}, f32[16,16,128]{2,1,0:T(8,128)S(1)}, u32[]{:S(2)}, u32[]{:S(2)}) collective-permute-start(f32[16,16,128]{2,1,0:T(8,128)S(1)} %get-tuple-element.120.refs_0_), channel_id=1, source_target_pairs={{2,0},{3,1},{0,2},{1,3},{6,4},{7,5},{4,6},{5,7},{10,8},{11,9},{8,1... | collective-permute-start | bytes 393224 | tf_op jit(solution)/shard_map/ppermute | solution.py:339
  60.4 6.2 %collective-permute-start.12 = (f32[16,16,128]{2,1,0:T(8,128)S(1)}, f32[16,16,128]{2,1,0:T(8,128)S(1)}, u32[]{:S(2)}, u32[]{:S(2)}) collective-permute-start(f32[16,16,128]{2,1,0:T(8,128)S(1)} %get-tuple-element.120.refs_0_), channel_id=1, source_target_pairs={{0,1},{1,0},{2,3},{3,2},{4,5},{5,4},{6,7},{7,6},{8,9},{9,8},{10,11... | collective-permute-start | bytes 393224 | tf_op jit(solution)/shard_map/ppermute | solution.py:343
  64.2 3.4 %collective-permute-start.14 = (f32[16,16,128]{2,1,0:T(8,128)S(1)}, f32[16,16,128]{2,1,0:T(8,128)S(1)}, u32[]{:S(2)}, u32[]{:S(2)}) collective-permute-start(f32[16,16,128]{2,1,0:T(8,128)S(1)} %collective-permute-done.13.refs_2_), channel_id=1, source_target_pairs={{0,1},{1,0},{2,3},{3,2},{4,5},{5,4},{6,7},{7,6},{8,9},{9,8},{10,11... | collective-permute-start | bytes 393224 | tf_op jit(solution)/shard_map/ppermute | solution.py:343

commit v7 on v6

--- a/solution.py
+++ b/solution.py
@@ -14,6 +14,7 @@
 
 upper_bound = 4.5
 lower_bound = 1.35
+THETA = (upper_bound + lower_bound) / 2.0
 
 AXES = ("group", "fold")
 F32 = jnp.float32
@@ -24,7 +25,7 @@
 
 
 def coefficients():
-    theta = (upper_bound + lower_bound) / 2.0
+    theta = THETA
     delta = (upper_bound - lower_bound) / 2.0
     pairs = []
     for sweep in range(SWEEPS):
@@ -54,28 +55,58 @@
     return jnp.where(lane < 128 - shift, first, second)
 
 
-def sides(even, right_is_a):
-    return even if right_is_a else jnp.logical_not(even)
-
-
-def put_payload(ob, steps, right, u, r, pay):
+def put_near(ob, steps, even, u, r, pay):
     h = HB * steps
     inner = h - HB
-    pay[:h] = u[pl.ds(h + jnp.where(right, ob - h, 0), h)]
+    pay[:h] = u[pl.ds(jnp.where(even, ob, h), h)]
     if inner:
-        pay[h:] = r[pl.ds(h + jnp.where(right, ob - inner, 0), inner)]
-
-
-def take_payload(ob, steps, right, got, u, r, now):
+        pay[h:] = r[pl.ds(jnp.where(even, h + ob - inner, h), inner)]
+
+
+def take_near(ob, steps, even, got, u, r, now):
     h = HB * steps
     inner = h - HB
-    at = jnp.where(right, h + ob, 0)
+    at = jnp.where(even, h + ob, 0)
     u[pl.ds(at, h)] = got[:h]
     if inner:
-        r[pl.ds(jnp.where(right, h + ob, HB), inner)] = got[h:]
+        r[pl.ds(jnp.where(even, h + ob, HB), inner)] = got[h:]
     high, low = split(got[:h])
     now[pl.ds(at, h), :16] = high
     now[pl.ds(at, h), 16:] = low
+
+
+def sent_blocks(steps):
+    return HB * (steps - 2)
+
+
+def put_far(ob, steps, even, u, r, pay):
+    h = HB * steps
+    pay[: 2 * HB] = u[pl.ds(jnp.where(even, h, h + ob - 2 * HB), 2 * HB)]
+    pay[2 * HB : 3 * HB] = r[pl.ds(jnp.where(even, h, h + ob - HB), HB)]
+
+
+def put_far_ahead(ob, steps, even, u, pay):
+    h, n = HB * steps, sent_blocks(steps)
+    pay[3 * HB :] = u[pl.ds(jnp.where(even, h + HB, h + ob - HB - n), n)]
+
+
+def take_far(ob, steps, even, got, u, r, now, later):
+    h, n = HB * steps, sent_blocks(steps)
+    high, low = split(got[: 2 * HB])
+    at = jnp.where(even, h - 2 * HB, h + ob)
+    now[pl.ds(at, 2 * HB), :16] = high
+    now[pl.ds(at, 2 * HB), 16:] = low
+    at = jnp.where(even, h - HB, h + ob)
+    u[pl.ds(at, HB)] = got[pl.ds(jnp.where(even, HB, 0), HB)]
+    r[pl.ds(at, HB)] = got[2 * HB : 3 * HB]
+    if n:
+        ahead = got[3 * HB :]
+        at = jnp.where(even, h - HB - n, h + ob + HB)
+        u[pl.ds(at, n)] = ahead
+        r[pl.ds(at, n)] = ahead * THETA
+        high, low = split(ahead)
+        later[pl.ds(at, n), :16] = high
+        later[pl.ds(at, n), 16:] = low
 
 
 COUNTS = 4
@@ -98,7 +129,7 @@
 
 def align_kernel(ob, steps, keys, facts, *refs):
     folds = len(keys)
-    sources, (x, u, r, now, later, pay_a, pay_b) = refs[:folds], refs[folds:]
+    sources, (x, u, r, now, later, pay_a) = refs[:folds], refs[folds:]
     del x, later
     h = HB * steps
     capacity = sources[0].shape[-1]
@@ -133,23 +164,21 @@
         return carry
 
     lax.fori_loop(0, ob, block, 0, unroll=4)
-    even = facts[1] == 0
-    put_payload(ob, steps, sides(even, True), u, r, pay_a)
-    put_payload(ob, steps, sides(even, False), u, r, pay_b)
-
-
-def first_kernel(folds, halo, width, counts, columns, initial, right_side, blocks, facts, held, stacked, border, live, sem):
+    put_near(ob, steps, facts[1] == 0, u, r, pay_a)
+
+
+def first_kernel(folds, lend, width, counts, columns, initial, right_side, blocks, facts, held, stacked, border, live, sem):
     own = columns.shape[1]
     size = blocks.shape[0] // own
     fold = lax.axis_index("fold")
     backwards = lax.rem(lax.axis_index("group"), 2)
     part = part_of(fold, folds, backwards)
     edge = (part == 0) | (part == folds - 1)
-    first = jnp.where(part == 0, 0, own - halo)
+    first = jnp.where(part == 0, 0, own - lend)
     small = [pltpu.make_async_copy(columns, held, sem.at[0]), pltpu.make_async_copy(counts, live, sem.at[1])]
     pair = [pltpu.make_async_copy(array, stacked.at[i], sem.at[2 + i]) for i, array in enumerate((initial, right_side))]
     rows = []
-    for i in range(halo):
+    for i in range(lend):
         row = blocks.at[pl.ds(pl.multiple_of((first + i) * size, size), size)]
         rows.append(pltpu.make_async_copy(row, border.at[i * size : (i + 1) * size], sem.at[4 + i]))
     for copy in small:
@@ -173,10 +202,10 @@
     def _():
         lane = lax.broadcasted_iota(jnp.int32, (8, 128), 1)
         indices = jnp.zeros((8, 128), jnp.int32)
-        for i in range(halo):
+        for i in range(lend):
             for k in range(width):
                 indices = jnp.where(lane == i * width + k, held[k, first + i], indices)
-        border[halo * size :] = indices.astype(F32)
+        border[lend * size :] = indices.astype(F32)
         for copy in rows:
             copy.wait()
 
@@ -228,22 +257,22 @@
     lax.fori_loop(0, rows // group, several, 0)
 
 
-def border_kernel(ob, folds, halo, width, facts, prepared, raw, before, out, offsets, vector, scalars, sem):
+def border_kernel(ob, folds, halo, lend, width, facts, prepared, raw, before, out, offsets, vector, scalars, sem):
     del prepared, before
     part = facts[0]
     size = out.shape[1]
 
     @pl.when((part == 0) | (part == folds - 1))
     def _():
-        vector[...] = raw[halo * size :].astype(jnp.int32)
+        vector[...] = raw[lend * size :].astype(jnp.int32)
         copy = pltpu.make_async_copy(vector, scalars, sem)
         copy.start()
-        first = jnp.where(part == 0, 0, halo + ob)
-        for a in range(halo):
+        first = jnp.where(part == 0, halo - lend, halo + ob)
+        for a in range(lend):
             put_row(out, first + a, raw.at[a * size : (a + 1) * size])
         copy.wait()
-        for i in range(halo):
-            local = jnp.where(part == 0, ob * folds - halo + i, i)
+        for i in range(lend):
+            local = jnp.where(part == 0, ob * folds - lend + i, i)
             for k in range(width):
                 offsets[i * width + k] = jnp.clip(scalars[0, i * width + k] - HB - local, -HB, HB)
 
@@ -276,19 +305,35 @@
     lax.fori_loop(0, count, row, 0, unroll=True)
 
 
+def look_up(offsets, width):
+    return lambda a, k: offsets[a * width + k]
+
+
+def ahead(ob, steps, even, first, pair, offset, operator, x, u, r, pieces):
+    h, n = HB * steps, sent_blocks(steps)
+    starts = jnp.where(even, h + HB, h + ob - HB - n)
+    apply_rows(0, steps, starts, n, first, False, pair, offset, operator, x, u, r, pieces)
+
+
+def begin_kernel(ob, steps, pair, facts, offsets, operator, *refs):
+    (x, u, r, *pieces), pay_b = refs[5:10], refs[10]
+    even = facts[1] == 0
+    put_far(ob, steps, even, u, r, pay_b)
+    if sent_blocks(steps):
+        ahead(ob, steps, even, True, pair, look_up(offsets, operator.shape[1] // 128), operator, x, u, r, pieces)
+        put_far_ahead(ob, steps, even, u, pay_b)
+
+
 def inner_kernel(ob, folds, steps, first, last, pairs, facts, offsets, operator, *refs):
     got_a, (x, u, r, *pieces) = refs[5], refs[6:]
     h = HB * steps
-    width = operator.shape[1] // 128
     even = facts[1] == 0
-    take_payload(ob, steps, sides(even, True), got_a, u, r, pieces[0])
-
-    def offset(a, k):
-        return offsets[a * width + k]
-
+    offset = look_up(offsets, operator.shape[1] // 128)
+    take_near(ob, steps, even, got_a, u, r, pieces[0])
     for t in range(steps):
-        starts = jnp.where(even, h + HB + HB * t, HB + HB * t)
-        count = ob + h - 2 * HB - 2 * HB * t
+        done = HB + (HB * t if t else sent_blocks(steps))
+        starts = jnp.where(even, h + done, HB + HB * t)
+        count = ob + h - HB - HB * t - done
         apply_rows(t, steps, starts, count, first, last, pairs[t], offset, operator, x, u, r, pieces)
 
 
@@ -297,23 +342,29 @@
     h = HB * steps
     inner = h - HB
     width = operator.shape[1] // 128
+    lend = lent.shape[0] // width
     even = facts[1] == 0
     edge = (facts[0] == 0) | (facts[0] == folds - 1)
-    take_payload(ob, steps, sides(even, False), got_b, u, r, pieces[0])
+    take_far(ob, steps, even, got_b, u, r, *pieces)
 
     def offset(a, k):
-        i = jnp.where(even, a, a - inner - ob)
-        outside = edge & (i >= 0) & (i < inner)
-        return jnp.where(outside, lent[jnp.clip(i, 0, inner - 1) * width + k], offsets[a * width + k])
+        i = a - jnp.where(even, inner - lend, inner + ob)
+        outside = edge & (i >= 0) & (i < lend)
+        return jnp.where(outside, lent[jnp.clip(i, 0, lend - 1) * width + k], offsets[a * width + k])
 
     for t in range(steps):
-        starts = jnp.where(even, HB + HB * t, h + ob - HB - HB * t)
-        apply_rows(t, steps, starts, h, first, last, pairs[t], offset, operator, x, u, r, pieces)
+        count = h if t else 2 * HB
+        starts = jnp.where(even, HB + HB * t + h - count if not t else HB + HB * t, h + ob - HB - HB * t)
+        apply_rows(t, steps, starts, count, first, last, pairs[t], offset, operator, x, u, r, pieces)
     if last:
         outs[0][...] = x[h : h + ob]
-    else:
-        put_payload(ob, steps, sides(even, True), u, r, outs[0])
-        put_payload(ob, steps, sides(even, False), u, r, outs[1])
+        return
+    put_near(ob, steps, even, u, r, outs[0])
+    put_far(ob, steps, even, u, r, outs[1])
+    if sent_blocks(steps):
+        pieces = pieces[::-1] if steps % 2 else pieces
+        ahead(ob, steps, even, False, pairs[steps], look_up(offsets, width), operator, x, u, r, pieces)
+        put_far_ahead(ob, steps, even, u, outs[1])
 
 
 def finish_kernel(ob, keys, facts, *refs):
@@ -349,14 +400,17 @@
     own, width, side = blocks.shape[0], blocks.shape[1], blocks.shape[2]
     size = width * side
     ob = own // folds
-    steps = 3 if ob >= 9 else 2
+    steps = 4 if ob >= 12 else 2
     halo = HB * (steps - 1)
+    lend = max(HB, sent_blocks(steps))
     rows = ob + 2 * halo
     pairs = coefficients()
     devices = groups * folds
     operator_shape = pltpu.VMEM((rows, size, 2 * side), BF16)
 
-    payload = jax.ShapeDtypeStruct((2 * HB * steps - HB, vectors, side), F32)
+
+    payload_a = jax.ShapeDtypeStruct((2 * HB * steps - HB, vectors, side), F32)
+    payload_b = jax.ShapeDtypeStruct((3 * HB + sent_blocks(steps), vectors, side), F32)
 
     line = [g * folds + (folds - 1 - p if g % 2 else p) for g in range(groups) for p in range(folds)]
 
@@ -371,16 +425,16 @@
 
     flat = fixed(blocks.reshape(own * size, side))
     facts, indices, stacked, border = pl.pallas_call(
-        functools.partial(first_kernel, folds, halo, width),
+        functools.partial(first_kernel, folds, lend, width),
         out_shape=(
             pltpu.SMEM((COUNTS + folds,), jnp.int32),
             pltpu.SMEM((width, own), jnp.int32),
             pltpu.VMEM((2, vectors, capacity), F32),
-            pltpu.VMEM((halo * size + 8, side), F32),
+            pltpu.VMEM((lend * size + 8, side), F32),
         ),
         in_specs=[HBM] * 5,
         out_specs=(SMEM, SMEM, VMEM, VMEM),
-        scratch_shapes=[pltpu.SMEM((1, folds), jnp.int32), pltpu.SemaphoreType.DMA((4 + halo,))],
+        scratch_shapes=[pltpu.SMEM((1, folds), jnp.int32), pltpu.SemaphoreType.DMA((4 + lend,))],
         compiler_params=params(),
     )(fixed(counts), fixed(columns.T), fixed(initial), fixed(right_side), flat)
     facts, indices = fixed(facts, pltpu.SMEM), fixed(indices, pltpu.SMEM)
@@ -419,19 +473,28 @@
         arrays += [array, other_core(array, folds)]
     extent = ob + 2 * HB * steps
     state = (pltpu.VMEM((extent, vectors, side), F32),) * 3 + (pltpu.VMEM((extent, 2 * vectors, side), BF16),) * 2
-    *held, pay_a, pay_b = pl.pallas_call(
+    *held, pay_a = pl.pallas_call(
         functools.partial(align_kernel, ob, steps, keys),
-        out_shape=(*state, payload, payload),
+        out_shape=(*state, payload_a),
         in_specs=[SMEM] + [VMEM] * folds,
-        out_specs=(VMEM,) * 7,
+        out_specs=(VMEM,) * 6,
         compiler_params=params(),
     )(facts, *[fixed(array, pltpu.VMEM) for array in arrays])
+
+    *held, pay_b = pl.pallas_call(
+        functools.partial(begin_kernel, ob, steps, pairs[0]),
+        out_shape=(*state, payload_b),
+        in_specs=[SMEM, SMEM] + [VMEM] * 6,
+        out_specs=(VMEM,) * 6,
+        input_output_aliases={3 + i: i for i in range(5)},
+        compiler_params=params(),
+    )(facts, offsets, fixed(operator, pltpu.VMEM), *[fixed(array, pltpu.VMEM) for array in held])
 
     def part_of_phase(kernel, operator, indices, held, got, outs):
         held = [pltpu.with_memory_space_constraint(array, pltpu.VMEM) for array in held]
         n = len(indices)
         results = pl.pallas_call(
-            functools.partial(kernel, ob, folds, steps, done == 0, done + steps == APPLIES, pairs[done : done + steps]),
+            functools.partial(kernel, ob, folds, steps, done == 0, done + steps == APPLIES, pairs[done : done + steps + 1]),
             out_shape=(*state, *outs),
             in_specs=[SMEM] * (1 + n) + [VMEM] * 7,
             out_specs=(VMEM,) * (5 + len(outs)),
@@ -446,8 +509,8 @@
         held, _ = part_of_phase(inner_kernel, operator, [offsets], held, got_a, ())
         if done == 0:
             operator, lent = pl.pallas_call(
-                functools.partial(border_kernel, ob, folds, halo, width),
-                out_shape=(operator_shape, pltpu.SMEM((halo * width,), jnp.int32)),
+                functools.partial(border_kernel, ob, folds, halo, lend, width),
+                out_shape=(operator_shape, pltpu.SMEM((lend * width,), jnp.int32)),
                 in_specs=[SMEM, VMEM, VMEM, pl.BlockSpec(memory_space=pl.ANY)],
                 out_specs=(VMEM, SMEM),
                 input_output_aliases={1: 0},
@@ -461,7 +524,7 @@
             lent = fixed(lent, pltpu.SMEM)
         if done + steps < APPLIES:
             held, (pay_a, pay_b) = part_of_phase(
-                outer_kernel, operator, [offsets, lent], held, got_b, (payload, payload)
+                outer_kernel, operator, [offsets, lent], held, got_b, (payload_a, payload_b)
             )
         else:
             result = jax.ShapeDtypeStruct((ob, vectors, side), F32)

time: 68.9 us -> 62.7 us (0.910)
  waiting for transfers between devices: 19 us -> 14.2 us
  starting transfers between devices: 24.7 us -> 20.9 us
  Pallas kernels: 24.9 us -> 27.3 us
    ppermute x4 -> x3, waiting for transfers between devices: 7.59 us -> 3.7 us  [on_device(): got_b = lax.ppermute(pay_b, AXES, swap_b)]
    ppermute x4 -> x3, starting transfers between devices: 8.91 us -> 7.02 us  [on_device(): got_b = lax.ppermute(pay_b, AXES, swap_b)]
    ppermute x4 -> x3, starting transfers between devices: 5.79 us -> 3.94 us  [on_device(): got_a = lax.ppermute(pay_a, AXES, swap_a)]
    pallas_call x8 -> x6, Pallas kernels: 16.4 us -> 17.4 us  [part_of_phase(): pl.pallas_call(functools.partial(kernel, ob, folds, steps, done == 0, don...]
    pallas_call x1, Pallas kernels: 5.24 us -> 6.16 us  [on_device(): pl.pallas_call(functools.partial(prepare_kernel, ob, halo, width), out_sh...]
    ppermute x2, waiting for transfers between devices: 8.88 us -> 7.98 us  [over_chips(): lax.ppermute(array, 'fold', [((i + 2 * d) % folds, i) for i in range(fold...]
    pallas_call x2 -> x3, Pallas kernels: 1.14 us -> 1.57 us  [the longest x1 1.12 us: on_device(): pl.pallas_call(functools.partial(first_kernel, folds, lend, width), out_s...]
  transfers between devices with their start and end apart: 15 -> 13, of which waited for: 8 -> 7; matrix products, arithmetic and copies ran while one was open for 0% -> 0% of each run, Pallas kernels for 23% -> 26%
where the time goes in v7:
time: 62.7 us; the launch traced here: 62.5 us
  Pallas kernels  27.3 us (44%)
  starting transfers between devices  20.9 us (33%)
  waiting for transfers between devices  14.2 us (23%)
    pallas_call x6, Pallas kernels, part_of_phase(): pl.pallas_call(functools.partial(kernel, ob, folds, steps, done == 0, don...  17.4 us
    ppermute x2, waiting for transfers between devices, over_chips(): lax.ppermute(array, 'fold', [((i + 2 * d) % folds, i) for i in range(fold...  7.98 us
    ppermute x3, starting transfers between devices, on_device(): got_b = lax.ppermute(pay_b, AXES, swap_b)  7.02 us
    pallas_call x1, Pallas kernels, on_device(): pl.pallas_call(functools.partial(prepare_kernel, ob, halo, width), out_sh...  6.16 us
    ppermute x4, starting transfers between devices, other_core(): return lax.ppermute(array, 'fold', [(i, i ^ 1) for i in range(folds)])  4.89 us
    ppermute x2, starting transfers between devices, over_chips(): lax.ppermute(array, 'fold', [((i + 2 * d) % folds, i) for i in range(fold...  4.24 us
    ppermute x3, starting transfers between devices, on_device(): got_a = lax.ppermute(pay_a, AXES, swap_a)  3.94 us
    ppermute x3, waiting for transfers between devices, on_device(): got_b = lax.ppermute(pay_b, AXES, swap_b)  3.7 us
  transfers between devices with their start and end apart: 13, of which 7 were waited for; matrix products, arithmetic and copies ran while one was open for 0% of the time, Pallas kernels for 26%

profile of v7, /device:TPU:9, one launch (start us, length us, event | category | flops | bytes accessed | tf_op | source)
XLA Modules:
  0.0 62.5 jit_solution(3883113670600903122)
XLA Ops:
  0.0 1.1 %shard_map.55 = (s32[8]{0:T(128)S(4)}, s32[5,64]{1,0:T(8,128)S(4)}, f32[2,16,4096]{2,1,0:T(8,128)S(1)}, f32[3848,128]{1,0:T(8,128)S(1)}) custom-call(s32[1,4]{1,0:T(1,128)} %counts.1, s32[5,64]{1,0:T(8,128)} %bitcast.4, f32[16,4096]{1,0:T(8,128)} %initial.1, f32[16,4096]{1,0:T(8,128)} %right_side.1, f32[40960,128]{1,0:T(8,128)} %bitcast.2), custom_call_target="tpu_custom_call" | custom-call | tf_op jit(solution)/shard_map/pallas_call | solution.py:427
  1.1 0.8 %collective-permute-start = (f32[3848,128]{1,0:T(8,128)S(1)}, f32[3848,128]{1,0:T(8,128)S(1)}, u32[]{:S(2)}, u32[]{:S(2)}) collective-permute-start(f32[3848,128]{1,0:T(8,128)S(1)} %get-tuple-element.60), channel_id=1, source_target_pairs={{3,7},{4,8},{11,15},{12,16},{19,23},{20,24},{27,31},{7,3},{8,4},{1... | collective-permute-start | bytes 5910536 | tf_op jit(solution)/shard_map/ppermute | solution.py:441
  1.9 4.2 %collective-permute-start.2 = (f32[2,16,4096]{2,1,0:T(8,128)S(1)}, f32[2,16,4096]{2,1,0:T(8,128)S(1)}, u32[]{:S(2)}, u32[]{:S(2)}) collective-permute-start(f32[2,16,4096]{2,1,0:T(8,128)S(1)} %get-tuple-element.61.refs_0_), channel_id=1, source_target_pairs={{2,0},{3,1},{0,2},{1,3},{6,4},{7,5},{4,6},{5,7},{10,8},{11,9},{8,1... | collective-permute-start | bytes 1572872 | tf_op jit(solution)/shard_map/ppermute | solution.py:390
  6.1 0.0 collective-permute-start.1
  6.2 6.2 %shard_map.56 = (bf16[34,640,256]{2,1,0:T(8,128)(2,1)S(1)}, f32[8,128]{1,0:T(8,128)S(1)}, s32[170]{0:T(256)S(4)}) custom-call(s32[8]{0:T(128)S(4)} %get-tuple-element.56.facts, s32[5,64]{1,0:T(8,128)S(4)} %get-tuple-element.57.columns, f32[40960,128]{1,0:T(8,128)} %bitcast.3), custom_call_target="tpu_custom_call" | custom-call | flops 10000000 | bytes 22282240 | tf_op jit(solution)/shard_map/pallas_call | solution.py:444
  12.3 5.4 %collective-permute-done.2.refs_0_ = f32[2,16,4096]{2,1,0:T(8,128)S(1)} collective-permute-done((f32[2,16,4096]{2,1,0:T(8,128)S(1)}, f32[2,16,4096]{2,1,0:T(8,128)S(1)}, u32[]{:S(2)}, u32[]{:S(2)}) %collective-permute-start.2) | collective-permute-done | bytes 524320 | tf_op jit(solution)/shard_map/ppermute | solution.py:390
  17.8 1.3 %collective-permute-start.3 = (f32[2,16,4096]{2,1,0:T(8,128)S(1)}, f32[2,16,4096]{2,1,0:T(8,128)S(1)}, u32[]{:S(2)}, u32[]{:S(2)}) collective-permute-start(f32[2,16,4096]{2,1,0:T(8,128)S(1)} %shard_map.57.refs_2_), channel_id=1, source_target_pairs={{0,1},{1,0},{2,3},{3,2},{4,5},{5,4},{6,7},{7,6},{8,9},{9,8},{10,11... | collective-permute-start | bytes 1572872 | tf_op jit(solution)/shard_map/ppermute | solution.py:394
  19.0 0.0 collective-permute-done.1.refs_1_
  19.0 1.5 %collective-permute-done.3.refs_3_ = f32[2,16,4096]{2,1,0:T(8,128)S(1)} collective-permute-done((f32[2,16,4096]{2,1,0:T(8,128)S(1)}, f32[2,16,4096]{2,1,0:T(8,128)S(1)}, u32[]{:S(2)}, u32[]{:S(2)}) %collective-permute-start.3) | collective-permute-done | bytes 524320 | tf_op jit(solution)/shard_map/ppermute | solution.py:394
  20.6 0.9 %shard_map.58 = (f32[40,16,128]{2,1,0:T(8,128)S(1)}, f32[40,16,128]{2,1,0:T(8,128)S(1)}, f32[40,16,128]{2,1,0:T(8,128)S(1)}, bf16[40,32,128]{2,1,0:T(8,128)(2,1)...) custom-call(s32[8]{0:T(128)S(4)} %get-tuple-element.56.facts, ...), custom_call_target="tpu_custom_call" | custom-call | tf_op jit(solution)/shard_map/pallas_call | solution.py:476
  21.5 0.4 collective-permute-start.4
  22.0 0.4 shard_map.59
  22.4 3.0 %collective-permute-start.5 = (f32[15,16,128]{2,1,0:T(8,128)S(1)}, f32[15,16,128]{2,1,0:T(8,128)S(1)}, u32[]{:S(2)}, u32[]{:S(2)}) collective-permute-start(f32[15,16,128]{2,1,0:T(8,128)S(1)} %get-tuple-element.81), channel_id=1, source_target_pairs={{1,2},{3,7},{6,5},{4,8},{9,10},{11,15},{14,13},{12,16},{17,18},{19... | collective-permute-start | bytes 368648 | tf_op jit(solution)/shard_map/ppermute | solution.py:507
  25.4 0.0 collective-permute-done.4.refs_5_
  25.4 2.9 %shard_map.60 = (f32[40,16,128]{2,1,0:T(8,128)S(1)}, f32[40,16,128]{2,1,0:T(8,128)S(1)}, f32[40,16,128]{2,1,0:T(8,128)S(1)}, bf16[40,32,128]{2,1,0:T(8,128)(2,1)S(1)}, bf16[40,32,128]{2,1,0:T(8,128)(2,1)S(1)}) custom-call(s32[8]{0:T(128)S(4)} %get-tuple-element.56.facts, ...), custom_call_target="tpu_custom_call", output_to_operand_aliasing={{0}: (3, {}), {1}: (4, {}), {2}: (5, {}), {3}: (6, {}), {4}... | custom-call | tf_op jit(solution)/shard_map/pallas_call | solution.py:496
  28.3 0.0 collective-permute-done.raw
  28.4 0.5 collective-permute-done.5.refs_5_
  28.9 3.1 %shard_map.62 = (f32[40,16,128]{2,1,0:T(8,128)S(1)}, f32[40,16,128]{2,1,0:T(8,128)S(1)}, f32[40,16,128]{2,1,0:T(8,128)S(1)}, bf16[40,32,128]{2,1,0:T(8,128)(2,1)...) custom-call(s32[8]{0:T(128)S(4)} %get-tuple-element.56.facts, ...), custom_call_target="tpu_custom_call", output_to_operand_aliasing={{0}: (4, {}), {1}: (5, {}), {2}: (6, {}), {3}: (7, {}), {4}... | custom-call | tf_op jit(solution)/shard_map/pallas_call | solution.py:496
  31.9 2.3 %collective-permute-start.6 = (f32[21,16,128]{2,1,0:T(8,128)S(1)}, f32[21,16,128]{2,1,0:T(8,128)S(1)}, u32[]{:S(2)}, u32[]{:S(2)}) collective-permute-start(f32[21,16,128]{2,1,0:T(8,128)S(1)} %get-tuple-element.87), channel_id=1, source_target_pairs={{0,1},{2,3},{7,6},{5,4},{8,9},{10,11},{15,14},{13,12},{16,17},{18,... | collective-permute-start | bytes 516104 | tf_op jit(solution)/shard_map/ppermute | solution.py:508
  34.2 1.9 %collective-permute-start.7 = (f32[15,16,128]{2,1,0:T(8,128)S(1)}, f32[15,16,128]{2,1,0:T(8,128)S(1)}, u32[]{:S(2)}, u32[]{:S(2)}) collective-permute-start(f32[15,16,128]{2,1,0:T(8,128)S(1)} %get-tuple-element.93), channel_id=1, source_target_pairs={{1,2},{3,7},{6,5},{4,8},{9,10},{11,15},{14,13},{12,16},{17,18},{19... | collective-permute-start | bytes 368648 | tf_op jit(solution)/shard_map/ppermute | solution.py:507
  36.2 0.0 collective-permute-done.6.refs_5_
  36.2 2.9 %shard_map.63 = (f32[40,16,128]{2,1,0:T(8,128)S(1)}, f32[40,16,128]{2,1,0:T(8,128)S(1)}, f32[40,16,128]{2,1,0:T(8,128)S(1)}, bf16[40,32,128]{2,1,0:T(8,128)(2,1)S(1)}, bf16[40,32,128]{2,1,0:T(8,128)(2,1)S(1)}) custom-call(s32[8]{0:T(128)S(4)} %get-tuple-element.56.facts, ...), custom_call_target="tpu_custom_call", output_to_operand_aliasing={{0}: (3, {}), {1}: (4, {}), {2}: (5, {}), {3}: (6, {}), {4}... | custom-call | tf_op jit(solution)/shard_map/pallas_call | solution.py:496
  39.0 1.7 %collective-permute-done.7.refs_5_ = f32[15,16,128]{2,1,0:T(8,128)S(1)} collective-permute-done((f32[15,16,128]{2,1,0:T(8,128)S(1)}, f32[15,16,128]{2,1,0:T(8,128)S(1)}, u32[]{:S(2)}, u32[]{:S(2)}) %collective-permute-start.7) | collective-permute-done | bytes 122912 | tf_op jit(solution)/shard_map/ppermute | solution.py:507
  40.7 3.1 %shard_map.64 = (f32[40,16,128]{2,1,0:T(8,128)S(1)}, f32[40,16,128]{2,1,0:T(8,128)S(1)}, f32[40,16,128]{2,1,0:T(8,128)S(1)}, bf16[40,32,128]{2,1,0:T(8,128)(2,1)...) custom-call(s32[8]{0:T(128)S(4)} %get-tuple-element.56.facts, ...), custom_call_target="tpu_custom_call", output_to_operand_aliasing={{0}: (4, {}), {1}: (5, {}), {2}: (6, {}), {3}: (7, {}), {4}... | custom-call | tf_op jit(solution)/shard_map/pallas_call | solution.py:496
  43.8 1.2 %collective-permute-start.8 = (f32[21,16,128]{2,1,0:T(8,128)S(1)}, f32[21,16,128]{2,1,0:T(8,128)S(1)}, u32[]{:S(2)}, u32[]{:S(2)}) collective-permute-start(f32[21,16,128]{2,1,0:T(8,128)S(1)} %get-tuple-element.99), channel_id=1, source_target_pairs={{0,1},{2,3},{7,6},{5,4},{8,9},{10,11},{15,14},{13,12},{16,17},{18,... | collective-permute-start | bytes 516104 | tf_op jit(solution)/shard_map/ppermute | solution.py:508
  45.0 2.1 %collective-permute-start.9 = (f32[15,16,128]{2,1,0:T(8,128)S(1)}, f32[15,16,128]{2,1,0:T(8,128)S(1)}, u32[]{:S(2)}, u32[]{:S(2)}) collective-permute-start(f32[15,16,128]{2,1,0:T(8,128)S(1)} %get-tuple-element.105), channel_id=1, source_target_pairs={{1,2},{3,7},{6,5},{4,8},{9,10},{11,15},{14,13},{12,16},{17,18},{19... | collective-permute-start | bytes 368648 | tf_op jit(solution)/shard_map/ppermute | solution.py:507
  47.1 0.0 collective-permute-done.8.refs_5_
  47.1 2.9 %shard_map.65 = (f32[40,16,128]{2,1,0:T(8,128)S(1)}, f32[40,16,128]{2,1,0:T(8,128)S(1)}, f32[40,16,128]{2,1,0:T(8,128)S(1)}, bf16[40,32,128]{2,1,0:T(8,128)(2,1)S(1)}, bf16[40,32,128]{2,1,0:T(8,128)(2,1)S(1)}) custom-call(s32[8]{0:T(128)S(4)} %get-tuple-element.56.facts, ...), custom_call_target="tpu_custom_call", output_to_operand_aliasing={{0}: (3, {}), {1}: (4, {}), {2}: (5, {}), {3}: (6, {}), {4}... | custom-call | tf_op jit(solution)/shard_map/pallas_call | solution.py:496
  50.0 1.5 %collective-permute-done.9.refs_5_ = f32[15,16,128]{2,1,0:T(8,128)S(1)} collective-permute-done((f32[15,16,128]{2,1,0:T(8,128)S(1)}, f32[15,16,128]{2,1,0:T(8,128)S(1)}, u32[]{:S(2)}, u32[]{:S(2)}) %collective-permute-start.9) | collective-permute-done | bytes 122912 | tf_op jit(solution)/shard_map/ppermute | solution.py:507
  51.5 2.7 %shard_map.66 = (f32[40,16,128]{2,1,0:T(8,128)S(1)}, f32[40,16,128]{2,1,0:T(8,128)S(1)}, f32[40,16,128]{2,1,0:T(8,128)S(1)}, bf16[40,32,128]{2,1,0:T(8,128)(2,1)...) custom-call(s32[8]{0:T(128)S(4)} %get-tuple-element.56.facts, ...), custom_call_target="tpu_custom_call", output_to_operand_aliasing={{0}: (4, {}), {1}: (5, {}), {2}: (6, {}), {3}: (7, {}), {4}... | custom-call | tf_op jit(solution)/shard_map/pallas_call | solution.py:496
  54.1 0.0 collective-permute-start.11
  54.1 1.3 %collective-permute-start.10 = (f32[16,16,128]{2,1,0:T(8,128)S(1)}, f32[16,16,128]{2,1,0:T(8,128)S(1)}, u32[]{:S(2)}, u32[]{:S(2)}) collective-permute-start(f32[16,16,128]{2,1,0:T(8,128)S(1)} %get-tuple-element.106.refs_0_), channel_id=1, source_target_pairs={{0,1},{1,0},{2,3},{3,2},{4,5},{5,4},{6,7},{7,6},{8,9},{9,8},{10,11... | collective-permute-start | bytes 393224 | tf_op jit(solution)/shard_map/ppermute | solution.py:394
  55.4 2.6 %collective-permute-done.11.refs_2_ = f32[16,16,128]{2,1,0:T(8,128)S(1)} collective-permute-done((f32[16,16,128]{2,1,0:T(8,128)S(1)}, f32[16,16,128]{2,1,0:T(8,128)S(1)}, u32[]{:S(2)}, u32[]{:S(2)}) %collective-permute-start.11) | collective-permute-done | bytes 131104 | tf_op jit(solution)/shard_map/ppermute | solution.py:390
  58.0 2.3 %collective-permute-start.12 = (f32[16,16,128]{2,1,0:T(8,128)S(1)}, f32[16,16,128]{2,1,0:T(8,128)S(1)}, u32[]{:S(2)}, u32[]{:S(2)}) collective-permute-start(f32[16,16,128]{2,1,0:T(8,128)S(1)} %collective-permute-done.11.refs_2_), channel_id=1, source_target_pairs={{0,1},{1,0},{2,3},{3,2},{4,5},{5,4},{6,7},{7,6},{8,9},{9,8},{10,11... | collective-permute-start | bytes 393224 | tf_op jit(solution)/shard_map/ppermute | solution.py:394
  60.3 0.0 collective-permute-done.10.refs_1_
  60.3 1.0 %collective-permute-done.12.refs_3_ = f32[16,16,128]{2,1,0:T(8,128)S(1)} collective-permute-done((f32[16,16,128]{2,1,0:T(8,128)S(1)}, f32[16,16,128]{2,1,0:T(8,128)S(1)}, u32[]{:S(2)}, u32[]{:S(2)}) %collective-permute-start.12) | collective-permute-done | bytes 131104 | tf_op jit(solution)/shard_map/ppermute | solution.py:394
  61.3 1.2 %shard_map.67 = f32[16,4096]{1,0:T(8,128)} custom-call(s32[8]{0:T(128)S(4)} %get-tuple-element.56.facts, f32[16,16,128]{2,1,0:T(8,128)S(1)} %get-tuple-element.106.refs_0_, f32[16,16,128]{2,1,0:T(8,128)S(1)} %collective-permute-done.10.refs_1_, f32[16,16,128]{2,1,0:T(8,128)S(1)} %collective-permute-done.11.refs_2_, ...), custom_call_target="tpu_custom_call" | custom-call | tf_op jit(solution)/shard_map/pallas_call | solution.py:539
  (2 shorter events, 0.0 us)
Async XLA Ops:
  1.1 27.2 %collective-permute-start = (f32[3848,128]{1,0:T(8,128)S(1)}, f32[3848,128]{1,0:T(8,128)S(1)}, u32[]{:S(2)}, u32[]{:S(2)}) collective-permute-start(f32[3848,128]{1,0:T(8,128)S(1)} %get-tuple-element.60), channel_id=1, source_target_pairs={{3,7},{4,8},{11,15},{12,16},{19,23},{20,24},{27,31},{7,3},{8,4},{1... | collective-permute-start | bytes 5910536 | tf_op jit(solution)/shard_map/ppermute | solution.py:441
  1.9 15.8 %collective-permute-start.2 = (f32[2,16,4096]{2,1,0:T(8,128)S(1)}, f32[2,16,4096]{2,1,0:T(8,128)S(1)}, u32[]{:S(2)}, u32[]{:S(2)}) collective-permute-start(f32[2,16,4096]{2,1,0:T(8,128)S(1)} %get-tuple-element.61.refs_0_), channel_id=1, source_target_pairs={{2,0},{3,1},{0,2},{1,3},{6,4},{7,5},{4,6},{5,7},{10,8},{11,9},{8,1... | collective-permute-start | bytes 1572872 | tf_op jit(solution)/shard_map/ppermute | solution.py:390
  6.1 12.9 %collective-permute-start.1 = (f32[2,16,4096]{2,1,0:T(8,128)S(1)}, f32[2,16,4096]{2,1,0:T(8,128)S(1)}, u32[]{:S(2)}, u32[]{:S(2)}) collective-permute-start(f32[2,16,4096]{2,1,0:T(8,128)S(1)} %get-tuple-element.61.refs_0_), channel_id=1, source_target_pairs={{0,1},{1,0},{2,3},{3,2},{4,5},{5,4},{6,7},{7,6},{8,9},{9,8},{10,11... | collective-permute-start | bytes 1572872 | tf_op jit(solution)/shard_map/ppermute | solution.py:394
  17.8 2.8 %collective-permute-start.3 = (f32[2,16,4096]{2,1,0:T(8,128)S(1)}, f32[2,16,4096]{2,1,0:T(8,128)S(1)}, u32[]{:S(2)}, u32[]{:S(2)}) collective-permute-start(f32[2,16,4096]{2,1,0:T(8,128)S(1)} %shard_map.57.refs_2_), channel_id=1, source_target_pairs={{0,1},{1,0},{2,3},{3,2},{4,5},{5,4},{6,7},{7,6},{8,9},{9,8},{10,11... | collective-permute-start | bytes 1572872 | tf_op jit(solution)/shard_map/ppermute | solution.py:394
  21.5 3.9 %collective-permute-start.4 = (f32[21,16,128]{2,1,0:T(8,128)S(1)}, f32[21,16,128]{2,1,0:T(8,128)S(1)}, u32[]{:S(2)}, u32[]{:S(2)}) collective-permute-start(f32[21,16,128]{2,1,0:T(8,128)S(1)} %get-tuple-element.73), channel_id=1, source_target_pairs={{0,1},{2,3},{7,6},{5,4},{8,9},{10,11},{15,14},{13,12},{16,17},{18,... | collective-permute-start | bytes 516104 | tf_op jit(solution)/shard_map/ppermute | solution.py:508
  22.4 6.5 %collective-permute-start.5 = (f32[15,16,128]{2,1,0:T(8,128)S(1)}, f32[15,16,128]{2,1,0:T(8,128)S(1)}, u32[]{:S(2)}, u32[]{:S(2)}) collective-permute-start(f32[15,16,128]{2,1,0:T(8,128)S(1)} %get-tuple-element.81), channel_id=1, source_target_pairs={{1,2},{3,7},{6,5},{4,8},{9,10},{11,15},{14,13},{12,16},{17,18},{19... | collective-permute-start | bytes 368648 | tf_op jit(solution)/shard_map/ppermute | solution.py:507
  31.9 4.2 %collective-permute-start.6 = (f32[21,16,128]{2,1,0:T(8,128)S(1)}, f32[21,16,128]{2,1,0:T(8,128)S(1)}, u32[]{:S(2)}, u32[]{:S(2)}) collective-permute-start(f32[21,16,128]{2,1,0:T(8,128)S(1)} %get-tuple-element.87), channel_id=1, source_target_pairs={{0,1},{2,3},{7,6},{5,4},{8,9},{10,11},{15,14},{13,12},{16,17},{18,... | collective-permute-start | bytes 516104 | tf_op jit(solution)/shard_map/ppermute | solution.py:508
  34.2 6.5 %collective-permute-start.7 = (f32[15,16,128]{2,1,0:T(8,128)S(1)}, f32[15,16,128]{2,1,0:T(8,128)S(1)}, u32[]{:S(2)}, u32[]{:S(2)}) collective-permute-start(f32[15,16,128]{2,1,0:T(8,128)S(1)} %get-tuple-element.93), channel_id=1, source_target_pairs={{1,2},{3,7},{6,5},{4,8},{9,10},{11,15},{14,13},{12,16},{17,18},{19... | collective-permute-start | bytes 368648 | tf_op jit(solution)/shard_map/ppermute | solution.py:507
  43.8 3.3 %collective-permute-start.8 = (f32[21,16,128]{2,1,0:T(8,128)S(1)}, f32[21,16,128]{2,1,0:T(8,128)S(1)}, u32[]{:S(2)}, u32[]{:S(2)}) collective-permute-start(f32[21,16,128]{2,1,0:T(8,128)S(1)} %get-tuple-element.99), channel_id=1, source_target_pairs={{0,1},{2,3},{7,6},{5,4},{8,9},{10,11},{15,14},{13,12},{16,17},{18,... | collective-permute-start | bytes 516104 | tf_op jit(solution)/shard_map/ppermute | solution.py:508
  45.0 6.5 %collective-permute-start.9 = (f32[15,16,128]{2,1,0:T(8,128)S(1)}, f32[15,16,128]{2,1,0:T(8,128)S(1)}, u32[]{:S(2)}, u32[]{:S(2)}) collective-permute-start(f32[15,16,128]{2,1,0:T(8,128)S(1)} %get-tuple-element.105), channel_id=1, source_target_pairs={{1,2},{3,7},{6,5},{4,8},{9,10},{11,15},{14,13},{12,16},{17,18},{19... | collective-permute-start | bytes 368648 | tf_op jit(solution)/shard_map/ppermute | solution.py:507
  54.1 3.8 %collective-permute-start.11 = (f32[16,16,128]{2,1,0:T(8,128)S(1)}, f32[16,16,128]{2,1,0:T(8,128)S(1)}, u32[]{:S(2)}, u32[]{:S(2)}) collective-permute-start(f32[16,16,128]{2,1,0:T(8,128)S(1)} %get-tuple-element.106.refs_0_), channel_id=1, source_target_pairs={{2,0},{3,1},{0,2},{1,3},{6,4},{7,5},{4,6},{5,7},{10,8},{11,9},{8,1... | collective-permute-start | bytes 393224 | tf_op jit(solution)/shard_map/ppermute | solution.py:390
  54.1 6.2 %collective-permute-start.10 = (f32[16,16,128]{2,1,0:T(8,128)S(1)}, f32[16,16,128]{2,1,0:T(8,128)S(1)}, u32[]{:S(2)}, u32[]{:S(2)}) collective-permute-start(f32[16,16,128]{2,1,0:T(8,128)S(1)} %get-tuple-element.106.refs_0_), channel_id=1, source_target_pairs={{0,1},{1,0},{2,3},{3,2},{4,5},{5,4},{6,7},{7,6},{8,9},{9,8},{10,11... | collective-permute-start | bytes 393224 | tf_op jit(solution)/shard_map/ppermute | solution.py:394
  58.0 3.3 %collective-permute-start.12 = (f32[16,16,128]{2,1,0:T(8,128)S(1)}, f32[16,16,128]{2,1,0:T(8,128)S(1)}, u32[]{:S(2)}, u32[]{:S(2)}) collective-permute-start(f32[16,16,128]{2,1,0:T(8,128)S(1)} %collective-permute-done.11.refs_2_), channel_id=1, source_target_pairs={{0,1},{1,0},{2,3},{3,2},{4,5},{5,4},{6,7},{7,6},{8,9},{9,8},{10,11... | collective-permute-start | bytes 393224 | tf_op jit(solution)/shard_map/ppermute | solution.py:394

commit v8 on v7

--- a/solution.py
+++ b/solution.py
@@ -127,44 +127,38 @@
     return jnp.where(backwards == 1, folds - 1 - fold, fold)
 
 
-def align_kernel(ob, steps, keys, facts, *refs):
-    folds = len(keys)
-    sources, (x, u, r, now, later, pay_a) = refs[:folds], refs[folds:]
-    del x, later
-    h = HB * steps
+def align_kernel(ob, folds, facts, *refs):
+    sources, outs = refs[:2], refs[2:]
     capacity = sources[0].shape[-1]
     lane = lax.broadcasted_iota(jnp.int32, (16, 128), 1)
-    base = facts[0] * (ob * 128)
     spans = []
-    for d, c in keys:
-        owner = holder(facts[2], folds, d, c)
+    for c in (False, True):
+        owner = holder(facts[2], folds, 0, c)
         spans.append((begin_of(facts, folds, owner), facts[COUNTS + owner]))
-
-    def block(e, carry):
-        row = base + e * 128
-        totals = [jnp.zeros((16, 128), F32), jnp.zeros((16, 128), F32)]
-        for source, (start, count) in zip(sources, spans):
-            at = row - start
-            low = at >> 7
-            shift = at & 127
-            index = at + lane
-            valid = (index >= 0) & (index < count)
-            for a in range(2):
-
-                def window(b, a=a, source=source):
-                    b = jnp.clip(b, 0, capacity // 128 - 1)
-                    return source[a, :, pl.ds(pl.multiple_of(b * 128, 128), 128)]
-
-                totals[a] = jnp.where(valid, pick_lanes(window, low, shift), totals[a])
-        u[h + e] = totals[0]
-        r[h + e] = totals[1]
-        high, low = split(totals[0])
-        now[h + e, :16] = high
-        now[h + e, 16:] = low
-        return carry
-
-    lax.fori_loop(0, ob, block, 0, unroll=4)
-    put_near(ob, steps, facts[1] == 0, u, r, pay_a)
+    for d, out in enumerate(outs):
+        base = part_of(holder(facts[2], folds, d, False), folds, facts[3]) * (ob * 128)
+
+        def block(e, carry, out=out, base=base):
+            row = base + e * 128
+            totals = [jnp.zeros((16, 128), F32), jnp.zeros((16, 128), F32)]
+            for source, (start, count) in zip(sources, spans):
+                at = row - start
+                low = at >> 7
+                shift = at & 127
+                index = at + lane
+                valid = (index >= 0) & (index < count)
+                for a in range(2):
+
+                    def window(b, a=a, source=source):
+                        b = jnp.clip(b, 0, capacity // 128 - 1)
+                        return source[a, :, pl.ds(pl.multiple_of(b * 128, 128), 128)]
+
+                    totals[a] = jnp.where(valid, pick_lanes(window, low, shift), totals[a])
+            out[0, e] = totals[0]
+            out[1, e] = totals[1]
+            return carry
+
+        lax.fori_loop(0, ob, block, 0, unroll=4)
 
 
 def first_kernel(folds, lend, width, counts, columns, initial, right_side, blocks, facts, held, stacked, border, live, sem):
@@ -213,10 +207,6 @@
         copy.wait()
 
 
-def gate_kernel(n, *refs):
-    del n, refs
-
-
 def put_row(out, a, raw):
     side = raw.shape[-1]
     for k in range(out.shape[1] // side):
@@ -225,7 +215,8 @@
         out[a, k * side : (k + 1) * side, side:] = low.T
 
 
-def prepare_kernel(ob, halo, width, facts, columns, blocks, out, token, offsets, raw, sem):
+def prepare_kernel(ob, halo, width, facts, columns, blocks, token, out, offsets, raw, sem):
+    del token
     rows, size = raw.shape[0], raw.shape[1]
     own = blocks.shape[0] // size
     first = facts[0] * ob - halo
@@ -244,7 +235,6 @@
         return carry
 
     lax.fori_loop(0, rows, indices, 0)
-    token[...] = jnp.zeros_like(token)
     group = 4 if rows % 4 == 0 else 2
 
     def several(g, carry):
@@ -316,8 +306,18 @@
 
 
 def begin_kernel(ob, steps, pair, facts, offsets, operator, *refs):
-    (x, u, r, *pieces), pay_b = refs[5:10], refs[10]
+    partial, (x, u, r, *pieces), (pay_a, pay_b) = refs[:-7], refs[-7:-2], refs[-2:]
+    h = HB * steps
+    total = partial[0][...]
+    for other in partial[1:]:
+        total = total + other[...]
+    u[h : h + ob] = total[0]
+    r[h : h + ob] = total[1]
+    high, low = split(total[0])
+    pieces[0][h : h + ob, :16] = high
+    pieces[0][h : h + ob, 16:] = low
     even = facts[1] == 0
+    put_near(ob, steps, even, u, r, pay_a)
     put_far(ob, steps, even, u, r, pay_b)
     if sent_blocks(steps):
         ahead(ob, steps, even, True, pair, look_up(offsets, operator.shape[1] // 128), operator, x, u, r, pieces)
@@ -400,7 +400,7 @@
     own, width, side = blocks.shape[0], blocks.shape[1], blocks.shape[2]
     size = width * side
     ob = own // folds
-    steps = 4 if ob >= 12 else 2
+    steps = 3 if ob >= 9 else 2
     halo = HB * (steps - 1)
     lend = max(HB, sent_blocks(steps))
     rows = ob + 2 * halo
@@ -439,56 +439,37 @@
     )(fixed(counts), fixed(columns.T), fixed(initial), fixed(right_side), flat)
     facts, indices = fixed(facts, pltpu.SMEM), fixed(indices, pltpu.SMEM)
     border = lax.ppermute(border, AXES, swap_border)
-    far = [over_chips(stacked, d, folds) for d in range(1, folds // 2)]
-
-    operator, token, offsets = pl.pallas_call(
+    mate = other_core(stacked, folds)
+    rows_of = jax.ShapeDtypeStruct((2, ob, vectors, side), F32)
+    partial = pl.pallas_call(
+        functools.partial(align_kernel, ob, folds),
+        out_shape=(rows_of,) * (folds // 2),
+        in_specs=[SMEM, VMEM, VMEM],
+        out_specs=(VMEM,) * (folds // 2),
+        compiler_params=params(),
+    )(facts, fixed(stacked, pltpu.VMEM), fixed(mate, pltpu.VMEM))
+    sent = [over_chips(partial[d], folds // 2 - d, folds) for d in range(1, folds // 2)]
+
+    operator, offsets = pl.pallas_call(
         functools.partial(prepare_kernel, ob, halo, width),
-        out_shape=(operator_shape, jax.ShapeDtypeStruct((8, 128), F32), pltpu.SMEM((rows * width,), jnp.int32)),
-        in_specs=[SMEM, SMEM, HBM],
-        out_specs=(VMEM, VMEM, SMEM),
-        scratch_shapes=[
-            pltpu.VMEM((rows, size, side), F32),
-            pltpu.SemaphoreType.DMA((rows,)),
-        ],
-        compiler_params=params(),
+        out_shape=(operator_shape, pltpu.SMEM((rows * width,), jnp.int32)),
+        in_specs=[SMEM, SMEM, HBM, pl.BlockSpec(memory_space=pl.ANY)],
+        out_specs=(VMEM, SMEM),
+        scratch_shapes=[pltpu.VMEM((rows, size, side), F32), pltpu.SemaphoreType.DMA((rows,))],
+        compiler_params=params(32),
         cost_estimate=pl.CostEstimate(flops=10**7, bytes_accessed=2 * rows * size * side * 4, transcendentals=0),
-    )(facts, indices, flat)
+    )(facts, indices, flat, partial[0])
     offsets = fixed(offsets, pltpu.SMEM)
 
-    def gate(arrays, spaces, token):
-        return pl.pallas_call(
-            functools.partial(gate_kernel, len(arrays)),
-            out_shape=tuple(space(array.shape, F32) for array, space in zip(arrays, spaces)),
-            in_specs=[pl.BlockSpec(memory_space=space) for space in spaces] + [pl.BlockSpec(memory_space=pl.ANY)],
-            out_specs=tuple(pl.BlockSpec(memory_space=space) for space in spaces),
-            input_output_aliases={i: i for i in range(len(arrays))},
-            compiler_params=params(),
-        )(*[pltpu.with_memory_space_constraint(array, space) for array, space in zip(arrays, spaces)], token)
-
-    far = gate(far, [pltpu.VMEM] * len(far), token)
-
-    keys, arrays = [], []
-    for d, array in enumerate([stacked, *far]):
-        keys += [(d, False), (d, True)]
-        arrays += [array, other_core(array, folds)]
     extent = ob + 2 * HB * steps
     state = (pltpu.VMEM((extent, vectors, side), F32),) * 3 + (pltpu.VMEM((extent, 2 * vectors, side), BF16),) * 2
-    *held, pay_a = pl.pallas_call(
-        functools.partial(align_kernel, ob, steps, keys),
-        out_shape=(*state, payload_a),
-        in_specs=[SMEM] + [VMEM] * folds,
-        out_specs=(VMEM,) * 6,
+    *held, pay_a, pay_b = pl.pallas_call(
+        functools.partial(begin_kernel, ob, steps, pairs[0]),
+        out_shape=(*state, payload_a, payload_b),
+        in_specs=[SMEM, SMEM] + [VMEM] * (1 + folds // 2),
+        out_specs=(VMEM,) * 7,
         compiler_params=params(),
-    )(facts, *[fixed(array, pltpu.VMEM) for array in arrays])
-
-    *held, pay_b = pl.pallas_call(
-        functools.partial(begin_kernel, ob, steps, pairs[0]),
-        out_shape=(*state, payload_b),
-        in_specs=[SMEM, SMEM] + [VMEM] * 6,
-        out_specs=(VMEM,) * 6,
-        input_output_aliases={3 + i: i for i in range(5)},
-        compiler_params=params(),
-    )(facts, offsets, fixed(operator, pltpu.VMEM), *[fixed(array, pltpu.VMEM) for array in held])
+    )(facts, offsets, fixed(operator, pltpu.VMEM), partial[0], *sent)
 
     def part_of_phase(kernel, operator, indices, held, got, outs):
         held = [pltpu.with_memory_space_constraint(array, pltpu.VMEM) for array in held]
@@ -533,6 +514,7 @@
             held = [*held[:3], held[4], held[3]]
 
     parts = []
+    keys = [(d, c) for d in range(folds // 2) for c in (False, True)]
     for d in range(folds // 2):
         piece = over_chips(x, d, folds) if d else x
         parts += [piece, other_core(piece, folds)]

time: 62.7 us -> 62.1 us (level)
  Pallas kernels: 27.3 us -> 25.8 us
  starting transfers between devices: 20.9 us -> 22.1 us
    ppermute x2, waiting for transfers between devices: 7.98 us -> 4.09 us  [over_chips(): lax.ppermute(array, 'fold', [((i + 2 * d) % folds, i) for i in range(fold...]
    ppermute x2, starting transfers between devices: 4.24 us -> 0.82 us  [over_chips(): lax.ppermute(array, 'fold', [((i + 2 * d) % folds, i) for i in range(fold...]
    ppermute x3 -> x4, waiting for transfers between devices: 3.7 us -> 7.09 us  [on_device(): got_b = lax.ppermute(pay_b, AXES, swap_b)]
    ppermute x4 -> x3, starting transfers between devices: 4.89 us -> 7.22 us  [other_core(): return lax.ppermute(array, 'fold', [(i, i ^ 1) for i in range(folds)])]
    ppermute x3 -> x4, starting transfers between devices: 7.02 us -> 8.46 us  [on_device(): got_b = lax.ppermute(pay_b, AXES, swap_b)]
    ppermute x3 -> x4, starting transfers between devices: 3.94 us -> 4.88 us  [on_device(): got_a = lax.ppermute(pay_a, AXES, swap_a)]
    pallas_call x1, Pallas kernels: 6.16 us -> 5.24 us  [on_device(): pl.pallas_call(functools.partial(prepare_kernel, ob, halo, width), out_sh...]
    pallas_call x6 -> x8, Pallas kernels: 17.4 us -> 16.8 us  [part_of_phase(): pl.pallas_call(functools.partial(kernel, ob, folds, steps, done == 0, don...]
  transfers between devices with their start and end apart: 13 -> 14, of which waited for: 7 -> 8; matrix products, arithmetic and copies ran while one was open for 0% -> 0% of each run, Pallas kernels for 26% -> 26%
where the time goes in v8:
time: 62.1 us; the launch traced here: 61.7 us
  Pallas kernels  25.8 us (42%)
  starting transfers between devices  22.1 us (36%)
  waiting for transfers between devices  13.7 us (22%)
    pallas_call x8, Pallas kernels, part_of_phase(): pl.pallas_call(functools.partial(kernel, ob, folds, steps, done == 0, don...  16.8 us
    ppermute x4, starting transfers between devices, on_device(): got_b = lax.ppermute(pay_b, AXES, swap_b)  8.46 us
    ppermute x3, starting transfers between devices, other_core(): return lax.ppermute(array, 'fold', [(i, i ^ 1) for i in range(folds)])  7.22 us
    ppermute x4, waiting for transfers between devices, on_device(): got_b = lax.ppermute(pay_b, AXES, swap_b)  7.09 us
    pallas_call x1, Pallas kernels, on_device(): pl.pallas_call(functools.partial(prepare_kernel, ob, halo, width), out_sh...  5.24 us
    ppermute x4, starting transfers between devices, on_device(): got_a = lax.ppermute(pay_a, AXES, swap_a)  4.88 us
    ppermute x2, waiting for transfers between devices, over_chips(): lax.ppermute(array, 'fold', [((i + 2 * d) % folds, i) for i in range(fold...  4.09 us
    ppermute x3, waiting for transfers between devices, other_core(): return lax.ppermute(array, 'fold', [(i, i ^ 1) for i in range(folds)])  2.52 us
  transfers between devices with their start and end apart: 14, of which 8 were waited for; matrix products, arithmetic and copies ran while one was open for 0% of the time, Pallas kernels for 26%

profile of v8, /device:TPU:9, one launch (start us, length us, event | category | flops | bytes accessed | tf_op | source)
XLA Modules:
  0.0 61.7 jit_solution(16614395871705789967)
XLA Ops:
  0.0 1.1 %shard_map.55 = (s32[8]{0:T(128)S(4)}, s32[5,64]{1,0:T(8,128)S(4)}, f32[2,16,4096]{2,1,0:T(8,128)S(1)}, f32[1928,128]{1,0:T(8,128)S(1)}) custom-call(s32[1,4]{1,0:T(1,128)} %counts.1, s32[5,64]{1,0:T(8,128)} %bitcast.4, f32[16,4096]{1,0:T(8,128)} %initial.1, f32[16,4096]{1,0:T(8,128)} %right_side.1, f32[40960,128]{1,0:T(8,128)} %bitcast.2), custom_call_target="tpu_custom_call" | custom-call | tf_op jit(solution)/shard_map/pallas_call | solution.py:427
  1.1 0.7 %collective-permute-start.1 = (f32[1928,128]{1,0:T(8,128)S(1)}, f32[1928,128]{1,0:T(8,128)S(1)}, u32[]{:S(2)}, u32[]{:S(2)}) collective-permute-start(f32[1928,128]{1,0:T(8,128)S(1)} %get-tuple-element.70), channel_id=1, source_target_pairs={{3,7},{4,8},{11,15},{12,16},{19,23},{20,24},{27,31},{7,3},{8,4},{1... | collective-permute-start | bytes 2961416 | tf_op jit(solution)/shard_map/ppermute | solution.py:441
  1.8 3.6 %collective-permute-start = (f32[2,16,4096]{2,1,0:T(8,128)S(1)}, f32[2,16,4096]{2,1,0:T(8,128)S(1)}, u32[]{:S(2)}, u32[]{:S(2)}) collective-permute-start(f32[2,16,4096]{2,1,0:T(8,128)S(1)} %get-tuple-element.66.refs_0_), channel_id=1, source_target_pairs={{0,1},{1,0},{2,3},{3,2},{4,5},{5,4},{6,7},{7,6},{8,9},{9,8},{10,11... | collective-permute-start | bytes 1572872 | tf_op jit(solution)/shard_map/ppermute | solution.py:394
  5.5 1.5 %collective-permute-done.refs_1_ = f32[2,16,4096]{2,1,0:T(8,128)S(1)} collective-permute-done((f32[2,16,4096]{2,1,0:T(8,128)S(1)}, f32[2,16,4096]{2,1,0:T(8,128)S(1)}, u32[]{:S(2)}, u32[]{:S(2)}) %collective-permute-start) | collective-permute-done | bytes 524320 | tf_op jit(solution)/shard_map/ppermute | solution.py:394
  7.0 1.2 %shard_map.56 = (f32[2,16,16,128]{3,2,1,0:T(8,128)S(1)}, f32[2,16,16,128]{3,2,1,0:T(8,128)S(1)}) custom-call(s32[8]{0:T(128)S(4)} %get-tuple-element.64.facts, f32[2,16,4096]{2,1,0:T(8,128)S(1)} %get-tuple-element.66.refs_0_, f32[2,16,4096]{2,1,0:T(8,128)S(1)} %collective-permute-done.refs_1_), custom_call_target="tpu_custom_call" | custom-call | tf_op jit(solution)/shard_map/pallas_call | solution.py:444
  8.2 0.8 %collective-permute-start.2 = (f32[2,16,16,128]{3,2,1,0:T(8,128)S(1)}, f32[2,16,16,128]{3,2,1,0:T(8,128)S(1)}, u32[]{:S(2)}, u32[]{:S(2)}) collective-permute-start(f32[2,16,16,128]{3,2,1,0:T(8,128)S(1)} %get-tuple-element.71), channel_id=1, source_target_pairs={{2,0},{3,1},{0,2},{1,3},{6,4},{7,5},{4,6},{5,7},{10,8},{11,9},{8,1... | collective-permute-start | bytes 786440 | tf_op jit(solution)/shard_map/ppermute | solution.py:390
  9.0 5.2 %shard_map.57 = (bf16[28,640,256]{2,1,0:T(8,128)(2,1)S(1)}, s32[140]{0:T(256)S(4)}) custom-call(s32[8]{0:T(128)S(4)} %get-tuple-element.64.facts, s32[5,64]{1,0:T(8,128)S(4)} %get-tuple-element.65.columns, f32[40960,128]{1,0:T(8,128)} %bitcast.3, f32[2,16,16,128]{3,2,1,0:T(8,128)S(1)} %get-tuple-element.67.token.refs_0_), custom_call_target="tpu_custom_call" | custom-call | flops 10000000 | bytes 18350080 | tf_op jit(solution)/shard_map/pallas_call | solution.py:453
  14.2 1.5 %collective-permute-done.2.refs_1_ = f32[2,16,16,128]{3,2,1,0:T(8,128)S(1)} collective-permute-done((f32[2,16,16,128]{3,2,1,0:T(8,128)S(1)}, f32[2,16,16,128]{3,2,1,0:T(8,128)S(1)}, u32[]{:S(2)}, u32[]{:S(2)}) %collective-permute-start.2) | collective-permute-done | bytes 262176 | tf_op jit(solution)/shard_map/ppermute | solution.py:390
  15.7 0.3 shard_map.58
  16.0 1.3 %collective-permute-start.3 = (f32[15,16,128]{2,1,0:T(8,128)S(1)}, f32[15,16,128]{2,1,0:T(8,128)S(1)}, u32[]{:S(2)}, u32[]{:S(2)}) collective-permute-start(f32[15,16,128]{2,1,0:T(8,128)S(1)} %get-tuple-element.77), channel_id=1, source_target_pairs={{0,1},{2,3},{7,6},{5,4},{8,9},{10,11},{15,14},{13,12},{16,17},{18,... | collective-permute-start | bytes 368648 | tf_op jit(solution)/shard_map/ppermute | solution.py:489
  17.3 2.6 %collective-permute-start.4 = (f32[12,16,128]{2,1,0:T(8,128)S(1)}, f32[12,16,128]{2,1,0:T(8,128)S(1)}, u32[]{:S(2)}, u32[]{:S(2)}) collective-permute-start(f32[12,16,128]{2,1,0:T(8,128)S(1)} %get-tuple-element.85), channel_id=1, source_target_pairs={{1,2},{3,7},{6,5},{4,8},{9,10},{11,15},{14,13},{12,16},{17,18},{19... | collective-permute-start | bytes 294920 | tf_op jit(solution)/shard_map/ppermute | solution.py:488
  19.9 0.0 collective-permute-done.3.refs_5_
  19.9 2.3 %shard_map.59 = (f32[34,16,128]{2,1,0:T(8,128)S(1)}, f32[34,16,128]{2,1,0:T(8,128)S(1)}, f32[34,16,128]{2,1,0:T(8,128)S(1)}, bf16[34,32,128]{2,1,0:T(8,128)(2,1)S(1)}, bf16[34,32,128]{2,1,0:T(8,128)(2,1)S(1)}) custom-call(s32[8]{0:T(128)S(4)} %get-tuple-element.64.facts, ...), custom_call_target="tpu_custom_call", output_to_operand_aliasing={{0}: (3, {}), {1}: (4, {}), {2}: (5, {}), {3}: (6, {}), {4}... | custom-call | tf_op jit(solution)/shard_map/pallas_call | solution.py:477
  22.2 0.0 collective-permute-done.1.raw
  22.2 1.3 %collective-permute-done.4.refs_5_ = f32[12,16,128]{2,1,0:T(8,128)S(1)} collective-permute-done((f32[12,16,128]{2,1,0:T(8,128)S(1)}, f32[12,16,128]{2,1,0:T(8,128)S(1)}, u32[]{:S(2)}, u32[]{:S(2)}) %collective-permute-start.4) | collective-permute-done | bytes 98336 | tf_op jit(solution)/shard_map/ppermute | solution.py:488
  23.5 2.0 %shard_map.61 = (f32[34,16,128]{2,1,0:T(8,128)S(1)}, f32[34,16,128]{2,1,0:T(8,128)S(1)}, f32[34,16,128]{2,1,0:T(8,128)S(1)}, bf16[34,32,128]{2,1,0:T(8,128)(2,1)...) custom-call(s32[8]{0:T(128)S(4)} %get-tuple-element.64.facts, ...), custom_call_target="tpu_custom_call", output_to_operand_aliasing={{0}: (4, {}), {1}: (5, {}), {2}: (6, {}), {3}: (7, {}), {4}... | custom-call | tf_op jit(solution)/shard_map/pallas_call | solution.py:477
  25.5 1.2 %collective-permute-start.5 = (f32[15,16,128]{2,1,0:T(8,128)S(1)}, f32[15,16,128]{2,1,0:T(8,128)S(1)}, u32[]{:S(2)}, u32[]{:S(2)}) collective-permute-start(f32[15,16,128]{2,1,0:T(8,128)S(1)} %get-tuple-element.91), channel_id=1, source_target_pairs={{0,1},{2,3},{7,6},{5,4},{8,9},{10,11},{15,14},{13,12},{16,17},{18,... | collective-permute-start | bytes 368648 | tf_op jit(solution)/shard_map/ppermute | solution.py:489
  26.7 1.9 %collective-permute-start.6 = (f32[12,16,128]{2,1,0:T(8,128)S(1)}, f32[12,16,128]{2,1,0:T(8,128)S(1)}, u32[]{:S(2)}, u32[]{:S(2)}) collective-permute-start(f32[12,16,128]{2,1,0:T(8,128)S(1)} %get-tuple-element.97), channel_id=1, source_target_pairs={{1,2},{3,7},{6,5},{4,8},{9,10},{11,15},{14,13},{12,16},{17,18},{19... | collective-permute-start | bytes 294920 | tf_op jit(solution)/shard_map/ppermute | solution.py:488
  28.6 0.0 collective-permute-done.5.refs_5_
  28.6 2.3 %shard_map.62 = (f32[34,16,128]{2,1,0:T(8,128)S(1)}, f32[34,16,128]{2,1,0:T(8,128)S(1)}, f32[34,16,128]{2,1,0:T(8,128)S(1)}, bf16[34,32,128]{2,1,0:T(8,128)(2,1)S(1)}, bf16[34,32,128]{2,1,0:T(8,128)(2,1)S(1)}) custom-call(s32[8]{0:T(128)S(4)} %get-tuple-element.64.facts, ...), custom_call_target="tpu_custom_call", output_to_operand_aliasing={{0}: (3, {}), {1}: (4, {}), {2}: (5, {}), {3}: (6, {}), {4}... | custom-call | tf_op jit(solution)/shard_map/pallas_call | solution.py:477
  30.9 2.0 %collective-permute-done.6.refs_5_ = f32[12,16,128]{2,1,0:T(8,128)S(1)} collective-permute-done((f32[12,16,128]{2,1,0:T(8,128)S(1)}, f32[12,16,128]{2,1,0:T(8,128)S(1)}, u32[]{:S(2)}, u32[]{:S(2)}) %collective-permute-start.6) | collective-permute-done | bytes 98336 | tf_op jit(solution)/shard_map/ppermute | solution.py:488
  32.9 2.0 %shard_map.63 = (f32[34,16,128]{2,1,0:T(8,128)S(1)}, f32[34,16,128]{2,1,0:T(8,128)S(1)}, f32[34,16,128]{2,1,0:T(8,128)S(1)}, bf16[34,32,128]{2,1,0:T(8,128)(2,1)...) custom-call(s32[8]{0:T(128)S(4)} %get-tuple-element.64.facts, ...), custom_call_target="tpu_custom_call", output_to_operand_aliasing={{0}: (4, {}), {1}: (5, {}), {2}: (6, {}), {3}: (7, {}), {4}... | custom-call | tf_op jit(solution)/shard_map/pallas_call | solution.py:477
  34.9 1.2 %collective-permute-start.7 = (f32[15,16,128]{2,1,0:T(8,128)S(1)}, f32[15,16,128]{2,1,0:T(8,128)S(1)}, u32[]{:S(2)}, u32[]{:S(2)}) collective-permute-start(f32[15,16,128]{2,1,0:T(8,128)S(1)} %get-tuple-element.103), channel_id=1, source_target_pairs={{0,1},{2,3},{7,6},{5,4},{8,9},{10,11},{15,14},{13,12},{16,17},{18,... | collective-permute-start | bytes 368648 | tf_op jit(solution)/shard_map/ppermute | solution.py:489
  36.1 1.9 %collective-permute-start.8 = (f32[12,16,128]{2,1,0:T(8,128)S(1)}, f32[12,16,128]{2,1,0:T(8,128)S(1)}, u32[]{:S(2)}, u32[]{:S(2)}) collective-permute-start(f32[12,16,128]{2,1,0:T(8,128)S(1)} %get-tuple-element.109), channel_id=1, source_target_pairs={{1,2},{3,7},{6,5},{4,8},{9,10},{11,15},{14,13},{12,16},{17,18},{19... | collective-permute-start | bytes 294920 | tf_op jit(solution)/shard_map/ppermute | solution.py:488
  38.0 0.0 collective-permute-done.7.refs_5_
  38.0 2.3 %shard_map.64 = (f32[34,16,128]{2,1,0:T(8,128)S(1)}, f32[34,16,128]{2,1,0:T(8,128)S(1)}, f32[34,16,128]{2,1,0:T(8,128)S(1)}, bf16[34,32,128]{2,1,0:T(8,128)(2,1)S(1)}, bf16[34,32,128]{2,1,0:T(8,128)(2,1)S(1)}) custom-call(s32[8]{0:T(128)S(4)} %get-tuple-element.64.facts, ...), custom_call_target="tpu_custom_call", output_to_operand_aliasing={{0}: (3, {}), {1}: (4, {}), {2}: (5, {}), {3}: (6, {}), {4}... | custom-call | tf_op jit(solution)/shard_map/pallas_call | solution.py:477
  40.3 2.0 %collective-permute-done.8.refs_5_ = f32[12,16,128]{2,1,0:T(8,128)S(1)} collective-permute-done((f32[12,16,128]{2,1,0:T(8,128)S(1)}, f32[12,16,128]{2,1,0:T(8,128)S(1)}, u32[]{:S(2)}, u32[]{:S(2)}) %collective-permute-start.8) | collective-permute-done | bytes 98336 | tf_op jit(solution)/shard_map/ppermute | solution.py:488
  42.3 2.0 %shard_map.65 = (f32[34,16,128]{2,1,0:T(8,128)S(1)}, f32[34,16,128]{2,1,0:T(8,128)S(1)}, f32[34,16,128]{2,1,0:T(8,128)S(1)}, bf16[34,32,128]{2,1,0:T(8,128)(2,1)...) custom-call(s32[8]{0:T(128)S(4)} %get-tuple-element.64.facts, ...), custom_call_target="tpu_custom_call", output_to_operand_aliasing={{0}: (4, {}), {1}: (5, {}), {2}: (6, {}), {3}: (7, {}), {4}... | custom-call | tf_op jit(solution)/shard_map/pallas_call | solution.py:477
  44.3 1.2 %collective-permute-start.9 = (f32[15,16,128]{2,1,0:T(8,128)S(1)}, f32[15,16,128]{2,1,0:T(8,128)S(1)}, u32[]{:S(2)}, u32[]{:S(2)}) collective-permute-start(f32[15,16,128]{2,1,0:T(8,128)S(1)} %get-tuple-element.115), channel_id=1, source_target_pairs={{0,1},{2,3},{7,6},{5,4},{8,9},{10,11},{15,14},{13,12},{16,17},{18,... | collective-permute-start | bytes 368648 | tf_op jit(solution)/shard_map/ppermute | solution.py:489
  45.5 2.1 %collective-permute-start.10 = (f32[12,16,128]{2,1,0:T(8,128)S(1)}, f32[12,16,128]{2,1,0:T(8,128)S(1)}, u32[]{:S(2)}, u32[]{:S(2)}) collective-permute-start(f32[12,16,128]{2,1,0:T(8,128)S(1)} %get-tuple-element.121), channel_id=1, source_target_pairs={{1,2},{3,7},{6,5},{4,8},{9,10},{11,15},{14,13},{12,16},{17,18},{19... | collective-permute-start | bytes 294920 | tf_op jit(solution)/shard_map/ppermute | solution.py:488
  47.6 0.0 collective-permute-done.9.refs_5_
  47.6 2.3 %shard_map.66 = (f32[34,16,128]{2,1,0:T(8,128)S(1)}, f32[34,16,128]{2,1,0:T(8,128)S(1)}, f32[34,16,128]{2,1,0:T(8,128)S(1)}, bf16[34,32,128]{2,1,0:T(8,128)(2,1)S(1)}, bf16[34,32,128]{2,1,0:T(8,128)(2,1)S(1)}) custom-call(s32[8]{0:T(128)S(4)} %get-tuple-element.64.facts, ...), custom_call_target="tpu_custom_call", output_to_operand_aliasing={{0}: (3, {}), {1}: (4, {}), {2}: (5, {}), {3}: (6, {}), {4}... | custom-call | tf_op jit(solution)/shard_map/pallas_call | solution.py:477
  49.9 1.8 %collective-permute-done.10.refs_5_ = f32[12,16,128]{2,1,0:T(8,128)S(1)} collective-permute-done((f32[12,16,128]{2,1,0:T(8,128)S(1)}, f32[12,16,128]{2,1,0:T(8,128)S(1)}, u32[]{:S(2)}, u32[]{:S(2)}) %collective-permute-start.10) | collective-permute-done | bytes 98336 | tf_op jit(solution)/shard_map/ppermute | solution.py:488
  51.7 1.7 %shard_map.67 = (f32[34,16,128]{2,1,0:T(8,128)S(1)}, f32[34,16,128]{2,1,0:T(8,128)S(1)}, f32[34,16,128]{2,1,0:T(8,128)S(1)}, bf16[34,32,128]{2,1,0:T(8,128)(2,1)...) custom-call(s32[8]{0:T(128)S(4)} %get-tuple-element.64.facts, ...), custom_call_target="tpu_custom_call", output_to_operand_aliasing={{0}: (4, {}), {1}: (5, {}), {2}: (6, {}), {3}: (7, {}), {4}... | custom-call | tf_op jit(solution)/shard_map/pallas_call | solution.py:477
  53.4 0.0 collective-permute-start.12
  53.4 1.3 %collective-permute-start.11 = (f32[16,16,128]{2,1,0:T(8,128)S(1)}, f32[16,16,128]{2,1,0:T(8,128)S(1)}, u32[]{:S(2)}, u32[]{:S(2)}) collective-permute-start(f32[16,16,128]{2,1,0:T(8,128)S(1)} %get-tuple-element.122.refs_0_), channel_id=1, source_target_pairs={{0,1},{1,0},{2,3},{3,2},{4,5},{5,4},{6,7},{7,6},{8,9},{9,8},{10,11... | collective-permute-start | bytes 393224 | tf_op jit(solution)/shard_map/ppermute | solution.py:394
  54.7 2.6 %collective-permute-done.12.refs_2_ = f32[16,16,128]{2,1,0:T(8,128)S(1)} collective-permute-done((f32[16,16,128]{2,1,0:T(8,128)S(1)}, f32[16,16,128]{2,1,0:T(8,128)S(1)}, u32[]{:S(2)}, u32[]{:S(2)}) %collective-permute-start.12) | collective-permute-done | bytes 131104 | tf_op jit(solution)/shard_map/ppermute | solution.py:390
  57.2 2.3 %collective-permute-start.13 = (f32[16,16,128]{2,1,0:T(8,128)S(1)}, f32[16,16,128]{2,1,0:T(8,128)S(1)}, u32[]{:S(2)}, u32[]{:S(2)}) collective-permute-start(f32[16,16,128]{2,1,0:T(8,128)S(1)} %collective-permute-done.12.refs_2_), channel_id=1, source_target_pairs={{0,1},{1,0},{2,3},{3,2},{4,5},{5,4},{6,7},{7,6},{8,9},{9,8},{10,11... | collective-permute-start | bytes 393224 | tf_op jit(solution)/shard_map/ppermute | solution.py:394
  59.6 0.0 collective-permute-done.11.refs_1_
  59.6 1.0 %collective-permute-done.13.refs_3_ = f32[16,16,128]{2,1,0:T(8,128)S(1)} collective-permute-done((f32[16,16,128]{2,1,0:T(8,128)S(1)}, f32[16,16,128]{2,1,0:T(8,128)S(1)}, u32[]{:S(2)}, u32[]{:S(2)}) %collective-permute-start.13) | collective-permute-done | bytes 131104 | tf_op jit(solution)/shard_map/ppermute | solution.py:394
  60.6 1.2 %shard_map.68 = f32[16,4096]{1,0:T(8,128)} custom-call(s32[8]{0:T(128)S(4)} %get-tuple-element.64.facts, f32[16,16,128]{2,1,0:T(8,128)S(1)} %get-tuple-element.122.refs_0_, f32[16,16,128]{2,1,0:T(8,128)S(1)} %collective-permute-done.11.refs_1_, f32[16,16,128]{2,1,0:T(8,128)S(1)} %collective-permute-done.12.refs_2_, ...), custom_call_target="tpu_custom_call" | custom-call | tf_op jit(solution)/shard_map/pallas_call | solution.py:521
  (1 shorter events, 0.0 us)
Async XLA Ops:
  1.1 21.1 %collective-permute-start.1 = (f32[1928,128]{1,0:T(8,128)S(1)}, f32[1928,128]{1,0:T(8,128)S(1)}, u32[]{:S(2)}, u32[]{:S(2)}) collective-permute-start(f32[1928,128]{1,0:T(8,128)S(1)} %get-tuple-element.70), channel_id=1, source_target_pairs={{3,7},{4,8},{11,15},{12,16},{19,23},{20,24},{27,31},{7,3},{8,4},{1... | collective-permute-start | bytes 2961416 | tf_op jit(solution)/shard_map/ppermute | solution.py:441
  1.8 5.2 %collective-permute-start = (f32[2,16,4096]{2,1,0:T(8,128)S(1)}, f32[2,16,4096]{2,1,0:T(8,128)S(1)}, u32[]{:S(2)}, u32[]{:S(2)}) collective-permute-start(f32[2,16,4096]{2,1,0:T(8,128)S(1)} %get-tuple-element.66.refs_0_), channel_id=1, source_target_pairs={{0,1},{1,0},{2,3},{3,2},{4,5},{5,4},{6,7},{7,6},{8,9},{9,8},{10,11... | collective-permute-start | bytes 1572872 | tf_op jit(solution)/shard_map/ppermute | solution.py:394
  8.2 7.6 %collective-permute-start.2 = (f32[2,16,16,128]{3,2,1,0:T(8,128)S(1)}, f32[2,16,16,128]{3,2,1,0:T(8,128)S(1)}, u32[]{:S(2)}, u32[]{:S(2)}) collective-permute-start(f32[2,16,16,128]{3,2,1,0:T(8,128)S(1)} %get-tuple-element.71), channel_id=1, source_target_pairs={{2,0},{3,1},{0,2},{1,3},{6,4},{7,5},{4,6},{5,7},{10,8},{11,9},{8,1... | collective-permute-start | bytes 786440 | tf_op jit(solution)/shard_map/ppermute | solution.py:390
  16.0 3.8 %collective-permute-start.3 = (f32[15,16,128]{2,1,0:T(8,128)S(1)}, f32[15,16,128]{2,1,0:T(8,128)S(1)}, u32[]{:S(2)}, u32[]{:S(2)}) collective-permute-start(f32[15,16,128]{2,1,0:T(8,128)S(1)} %get-tuple-element.77), channel_id=1, source_target_pairs={{0,1},{2,3},{7,6},{5,4},{8,9},{10,11},{15,14},{13,12},{16,17},{18,... | collective-permute-start | bytes 368648 | tf_op jit(solution)/shard_map/ppermute | solution.py:489
  17.3 6.2 %collective-permute-start.4 = (f32[12,16,128]{2,1,0:T(8,128)S(1)}, f32[12,16,128]{2,1,0:T(8,128)S(1)}, u32[]{:S(2)}, u32[]{:S(2)}) collective-permute-start(f32[12,16,128]{2,1,0:T(8,128)S(1)} %get-tuple-element.85), channel_id=1, source_target_pairs={{1,2},{3,7},{6,5},{4,8},{9,10},{11,15},{14,13},{12,16},{17,18},{19... | collective-permute-start | bytes 294920 | tf_op jit(solution)/shard_map/ppermute | solution.py:488
  25.5 3.1 %collective-permute-start.5 = (f32[15,16,128]{2,1,0:T(8,128)S(1)}, f32[15,16,128]{2,1,0:T(8,128)S(1)}, u32[]{:S(2)}, u32[]{:S(2)}) collective-permute-start(f32[15,16,128]{2,1,0:T(8,128)S(1)} %get-tuple-element.91), channel_id=1, source_target_pairs={{0,1},{2,3},{7,6},{5,4},{8,9},{10,11},{15,14},{13,12},{16,17},{18,... | collective-permute-start | bytes 368648 | tf_op jit(solution)/shard_map/ppermute | solution.py:489
  26.7 6.2 %collective-permute-start.6 = (f32[12,16,128]{2,1,0:T(8,128)S(1)}, f32[12,16,128]{2,1,0:T(8,128)S(1)}, u32[]{:S(2)}, u32[]{:S(2)}) collective-permute-start(f32[12,16,128]{2,1,0:T(8,128)S(1)} %get-tuple-element.97), channel_id=1, source_target_pairs={{1,2},{3,7},{6,5},{4,8},{9,10},{11,15},{14,13},{12,16},{17,18},{19... | collective-permute-start | bytes 294920 | tf_op jit(solution)/shard_map/ppermute | solution.py:488
  34.9 3.1 %collective-permute-start.7 = (f32[15,16,128]{2,1,0:T(8,128)S(1)}, f32[15,16,128]{2,1,0:T(8,128)S(1)}, u32[]{:S(2)}, u32[]{:S(2)}) collective-permute-start(f32[15,16,128]{2,1,0:T(8,128)S(1)} %get-tuple-element.103), channel_id=1, source_target_pairs={{0,1},{2,3},{7,6},{5,4},{8,9},{10,11},{15,14},{13,12},{16,17},{18,... | collective-permute-start | bytes 368648 | tf_op jit(solution)/shard_map/ppermute | solution.py:489
  36.1 6.2 %collective-permute-start.8 = (f32[12,16,128]{2,1,0:T(8,128)S(1)}, f32[12,16,128]{2,1,0:T(8,128)S(1)}, u32[]{:S(2)}, u32[]{:S(2)}) collective-permute-start(f32[12,16,128]{2,1,0:T(8,128)S(1)} %get-tuple-element.109), channel_id=1, source_target_pairs={{1,2},{3,7},{6,5},{4,8},{9,10},{11,15},{14,13},{12,16},{17,18},{19... | collective-permute-start | bytes 294920 | tf_op jit(solution)/shard_map/ppermute | solution.py:488
  44.3 3.3 %collective-permute-start.9 = (f32[15,16,128]{2,1,0:T(8,128)S(1)}, f32[15,16,128]{2,1,0:T(8,128)S(1)}, u32[]{:S(2)}, u32[]{:S(2)}) collective-permute-start(f32[15,16,128]{2,1,0:T(8,128)S(1)} %get-tuple-element.115), channel_id=1, source_target_pairs={{0,1},{2,3},{7,6},{5,4},{8,9},{10,11},{15,14},{13,12},{16,17},{18,... | collective-permute-start | bytes 368648 | tf_op jit(solution)/shard_map/ppermute | solution.py:489
  45.5 6.2 %collective-permute-start.10 = (f32[12,16,128]{2,1,0:T(8,128)S(1)}, f32[12,16,128]{2,1,0:T(8,128)S(1)}, u32[]{:S(2)}, u32[]{:S(2)}) collective-permute-start(f32[12,16,128]{2,1,0:T(8,128)S(1)} %get-tuple-element.121), channel_id=1, source_target_pairs={{1,2},{3,7},{6,5},{4,8},{9,10},{11,15},{14,13},{12,16},{17,18},{19... | collective-permute-start | bytes 294920 | tf_op jit(solution)/shard_map/ppermute | solution.py:488
  53.4 3.8 %collective-permute-start.12 = (f32[16,16,128]{2,1,0:T(8,128)S(1)}, f32[16,16,128]{2,1,0:T(8,128)S(1)}, u32[]{:S(2)}, u32[]{:S(2)}) collective-permute-start(f32[16,16,128]{2,1,0:T(8,128)S(1)} %get-tuple-element.122.refs_0_), channel_id=1, source_target_pairs={{2,0},{3,1},{0,2},{1,3},{6,4},{7,5},{4,6},{5,7},{10,8},{11,9},{8,1... | collective-permute-start | bytes 393224 | tf_op jit(solution)/shard_map/ppermute | solution.py:390
  53.4 6.2 %collective-permute-start.11 = (f32[16,16,128]{2,1,0:T(8,128)S(1)}, f32[16,16,128]{2,1,0:T(8,128)S(1)}, u32[]{:S(2)}, u32[]{:S(2)}) collective-permute-start(f32[16,16,128]{2,1,0:T(8,128)S(1)} %get-tuple-element.122.refs_0_), channel_id=1, source_target_pairs={{0,1},{1,0},{2,3},{3,2},{4,5},{5,4},{6,7},{7,6},{8,9},{9,8},{10,11... | collective-permute-start | bytes 393224 | tf_op jit(solution)/shard_map/ppermute | solution.py:394
  57.2 3.3 %collective-permute-start.13 = (f32[16,16,128]{2,1,0:T(8,128)S(1)}, f32[16,16,128]{2,1,0:T(8,128)S(1)}, u32[]{:S(2)}, u32[]{:S(2)}) collective-permute-start(f32[16,16,128]{2,1,0:T(8,128)S(1)} %collective-permute-done.12.refs_2_), channel_id=1, source_target_pairs={{0,1},{1,0},{2,3},{3,2},{4,5},{5,4},{6,7},{7,6},{8,9},{9,8},{10,11... | collective-permute-start | bytes 393224 | tf_op jit(solution)/shard_map/ppermute | solution.py:394

commit v9 on v8

--- a/solution.py
+++ b/solution.py
@@ -205,6 +205,10 @@
 
     for copy in pair:
         copy.wait()
+
+
+def gate_kernel(*refs):
+    del refs
 
 
 def put_row(out, a, raw):
@@ -438,7 +442,6 @@
         compiler_params=params(),
     )(fixed(counts), fixed(columns.T), fixed(initial), fixed(right_side), flat)
     facts, indices = fixed(facts, pltpu.SMEM), fixed(indices, pltpu.SMEM)
-    border = lax.ppermute(border, AXES, swap_border)
     mate = other_core(stacked, folds)
     rows_of = jax.ShapeDtypeStruct((2, ob, vectors, side), F32)
     partial = pl.pallas_call(
@@ -449,6 +452,15 @@
         compiler_params=params(),
     )(facts, fixed(stacked, pltpu.VMEM), fixed(mate, pltpu.VMEM))
     sent = [over_chips(partial[d], folds // 2 - d, folds) for d in range(1, folds // 2)]
+    border = pl.pallas_call(
+        gate_kernel,
+        out_shape=pltpu.VMEM(border.shape, F32),
+        in_specs=[VMEM, pl.BlockSpec(memory_space=pl.ANY)],
+        out_specs=VMEM,
+        input_output_aliases={0: 0},
+        compiler_params=params(),
+    )(fixed(border, pltpu.VMEM), partial[0])
+    border = lax.ppermute(border, AXES, swap_border)
 
     operator, offsets = pl.pallas_call(
         functools.partial(prepare_kernel, ob, halo, width),

time: 62.1 us -> 61.3 us (0.987)
  waiting for transfers between devices: 13.7 us -> 12.5 us
    ppermute x2, starting transfers between devices: 0.82 us -> 3.42 us  [over_chips(): lax.ppermute(array, 'fold', [((i + 2 * d) % folds, i) for i in range(fold...]
    ppermute x3, starting transfers between devices: 7.22 us -> 4.64 us  [other_core(): return lax.ppermute(array, 'fold', [(i, i ^ 1) for i in range(folds)])]
    ppermute x2, waiting for transfers between devices: 4.09 us -> 3.24 us  [over_chips(): lax.ppermute(array, 'fold', [((i + 2 * d) % folds, i) for i in range(fold...]
  transfers between devices with their start and end apart: 14 -> 14, of which waited for: 8 -> 8; matrix products, arithmetic and copies ran while one was open for 0% -> 0% of each run, Pallas kernels for 26% -> 24%
where the time goes in v9:
time: 61.3 us; the launch traced here: 61 us
  Pallas kernels  25.7 us (42%)
  starting transfers between devices  22.7 us (37%)
  waiting for transfers between devices  12.5 us (20%)
    pallas_call x8, Pallas kernels, part_of_phase(): pl.pallas_call(functools.partial(kernel, ob, folds, steps, done == 0, don...  16.8 us
    ppermute x4, starting transfers between devices, on_device(): got_b = lax.ppermute(pay_b, AXES, swap_b)  8.88 us
    ppermute x4, waiting for transfers between devices, on_device(): got_b = lax.ppermute(pay_b, AXES, swap_b)  6.69 us
    pallas_call x1, Pallas kernels, on_device(): pl.pallas_call(functools.partial(prepare_kernel, ob, halo, width), out_sh...  5.24 us
    ppermute x4, starting transfers between devices, on_device(): got_a = lax.ppermute(pay_a, AXES, swap_a)  4.99 us
    ppermute x3, starting transfers between devices, other_core(): return lax.ppermute(array, 'fold', [(i, i ^ 1) for i in range(folds)])  4.64 us
    ppermute x2, starting transfers between devices, over_chips(): lax.ppermute(array, 'fold', [((i + 2 * d) % folds, i) for i in range(fold...  3.42 us
    ppermute x2, waiting for transfers between devices, over_chips(): lax.ppermute(array, 'fold', [((i + 2 * d) % folds, i) for i in range(fold...  3.24 us
  transfers between devices with their start and end apart: 14, of which 8 were waited for; matrix products, arithmetic and copies ran while one was open for 0% of the time, Pallas kernels for 24%

profile of v9, /device:TPU:9, one launch (start us, length us, event | category | flops | bytes accessed | tf_op | source)
XLA Modules:
  0.0 61.0 jit_solution(10464495097035024674)
XLA Ops:
  0.0 1.1 %shard_map.55 = (s32[8]{0:T(128)S(4)}, s32[5,64]{1,0:T(8,128)S(4)}, f32[2,16,4096]{2,1,0:T(8,128)S(1)}, f32[1928,128]{1,0:T(8,128)S(1)}) custom-call(s32[1,4]{1,0:T(1,128)} %counts.1, s32[5,64]{1,0:T(8,128)} %bitcast.4, f32[16,4096]{1,0:T(8,128)} %initial.1, f32[16,4096]{1,0:T(8,128)} %right_side.1, f32[40960,128]{1,0:T(8,128)} %bitcast.2), custom_call_target="tpu_custom_call" | custom-call | tf_op jit(solution)/shard_map/pallas_call | solution.py:431
  1.1 1.0 %collective-permute-start = (f32[2,16,4096]{2,1,0:T(8,128)S(1)}, f32[2,16,4096]{2,1,0:T(8,128)S(1)}, u32[]{:S(2)}, u32[]{:S(2)}) collective-permute-start(f32[2,16,4096]{2,1,0:T(8,128)S(1)} %get-tuple-element.66.refs_0_), channel_id=1, source_target_pairs={{0,1},{1,0},{2,3},{3,2},{4,5},{5,4},{6,7},{7,6},{8,9},{9,8},{10,11... | collective-permute-start | bytes 1572872 | tf_op jit(solution)/shard_map/ppermute | solution.py:398
  2.1 1.5 %collective-permute-done.refs_1_ = f32[2,16,4096]{2,1,0:T(8,128)S(1)} collective-permute-done((f32[2,16,4096]{2,1,0:T(8,128)S(1)}, f32[2,16,4096]{2,1,0:T(8,128)S(1)}, u32[]{:S(2)}, u32[]{:S(2)}) %collective-permute-start) | collective-permute-done | bytes 524320 | tf_op jit(solution)/shard_map/ppermute | solution.py:398
  3.7 1.2 %shard_map.56 = (f32[2,16,16,128]{3,2,1,0:T(8,128)S(1)}, f32[2,16,16,128]{3,2,1,0:T(8,128)S(1)}) custom-call(s32[8]{0:T(128)S(4)} %get-tuple-element.64.facts, f32[2,16,4096]{2,1,0:T(8,128)S(1)} %get-tuple-element.66.refs_0_, f32[2,16,4096]{2,1,0:T(8,128)S(1)} %collective-permute-done.refs_1_), custom_call_target="tpu_custom_call" | custom-call | tf_op jit(solution)/shard_map/pallas_call | solution.py:447
  4.8 0.7 %collective-permute-start.1 = (f32[1928,128]{1,0:T(8,128)S(1)}, f32[1928,128]{1,0:T(8,128)S(1)}, u32[]{:S(2)}, u32[]{:S(2)}) collective-permute-start(f32[1928,128]{1,0:T(8,128)S(1)} %shard_map.58), channel_id=1, source_target_pairs={{3,7},{4,8},{11,15},{12,16},{19,23},{20,24},{27,31},{7,3},{8,4},{1... | collective-permute-start | bytes 2961416 | tf_op jit(solution)/shard_map/ppermute | solution.py:463
  5.6 3.4 %collective-permute-start.2 = (f32[2,16,16,128]{3,2,1,0:T(8,128)S(1)}, f32[2,16,16,128]{3,2,1,0:T(8,128)S(1)}, u32[]{:S(2)}, u32[]{:S(2)}) collective-permute-start(f32[2,16,16,128]{3,2,1,0:T(8,128)S(1)} %get-tuple-element.71), channel_id=1, source_target_pairs={{2,0},{3,1},{0,2},{1,3},{6,4},{7,5},{4,6},{5,7},{10,8},{11,9},{8,1... | collective-permute-start | bytes 786440 | tf_op jit(solution)/shard_map/ppermute | solution.py:394
  9.0 5.2 %shard_map.57 = (bf16[28,640,256]{2,1,0:T(8,128)(2,1)S(1)}, s32[140]{0:T(256)S(4)}) custom-call(s32[8]{0:T(128)S(4)} %get-tuple-element.64.facts, s32[5,64]{1,0:T(8,128)S(4)} %get-tuple-element.65.columns, f32[40960,128]{1,0:T(8,128)} %bitcast.3, f32[2,16,16,128]{3,2,1,0:T(8,128)S(1)} %get-tuple-element.67.token.refs_1_.refs_0_), custom_call_target="tpu_custom_call" | custom-call | flops 10000000 | bytes 18350080 | tf_op jit(solution)/shard_map/pallas_call | solution.py:465
  14.2 0.7 %collective-permute-done.2.refs_1_ = f32[2,16,16,128]{3,2,1,0:T(8,128)S(1)} collective-permute-done((f32[2,16,16,128]{3,2,1,0:T(8,128)S(1)}, f32[2,16,16,128]{3,2,1,0:T(8,128)S(1)}, u32[]{:S(2)}, u32[]{:S(2)}) %collective-permute-start.2) | collective-permute-done | bytes 262176 | tf_op jit(solution)/shard_map/ppermute | solution.py:394
  14.9 0.3 shard_map.59
  15.2 1.4 %collective-permute-start.3 = (f32[15,16,128]{2,1,0:T(8,128)S(1)}, f32[15,16,128]{2,1,0:T(8,128)S(1)}, u32[]{:S(2)}, u32[]{:S(2)}) collective-permute-start(f32[15,16,128]{2,1,0:T(8,128)S(1)} %get-tuple-element.77), channel_id=1, source_target_pairs={{0,1},{2,3},{7,6},{5,4},{8,9},{10,11},{15,14},{13,12},{16,17},{18,... | collective-permute-start | bytes 368648 | tf_op jit(solution)/shard_map/ppermute | solution.py:501
  16.6 3.0 %collective-permute-start.4 = (f32[12,16,128]{2,1,0:T(8,128)S(1)}, f32[12,16,128]{2,1,0:T(8,128)S(1)}, u32[]{:S(2)}, u32[]{:S(2)}) collective-permute-start(f32[12,16,128]{2,1,0:T(8,128)S(1)} %get-tuple-element.85), channel_id=1, source_target_pairs={{1,2},{3,7},{6,5},{4,8},{9,10},{11,15},{14,13},{12,16},{17,18},{19... | collective-permute-start | bytes 294920 | tf_op jit(solution)/shard_map/ppermute | solution.py:500
  19.6 0.0 collective-permute-done.3.refs_5_
  19.6 2.3 %shard_map.60 = (f32[34,16,128]{2,1,0:T(8,128)S(1)}, f32[34,16,128]{2,1,0:T(8,128)S(1)}, f32[34,16,128]{2,1,0:T(8,128)S(1)}, bf16[34,32,128]{2,1,0:T(8,128)(2,1)S(1)}, bf16[34,32,128]{2,1,0:T(8,128)(2,1)S(1)}) custom-call(s32[8]{0:T(128)S(4)} %get-tuple-element.64.facts, ...), custom_call_target="tpu_custom_call", output_to_operand_aliasing={{0}: (3, {}), {1}: (4, {}), {2}: (5, {}), {3}: (6, {}), {4}... | custom-call | tf_op jit(solution)/shard_map/pallas_call | solution.py:489
  21.9 0.0 collective-permute-done.1.raw
  21.9 0.9 %collective-permute-done.4.refs_5_ = f32[12,16,128]{2,1,0:T(8,128)S(1)} collective-permute-done((f32[12,16,128]{2,1,0:T(8,128)S(1)}, f32[12,16,128]{2,1,0:T(8,128)S(1)}, u32[]{:S(2)}, u32[]{:S(2)}) %collective-permute-start.4) | collective-permute-done | bytes 98336 | tf_op jit(solution)/shard_map/ppermute | solution.py:500
  22.8 2.0 %shard_map.62 = (f32[34,16,128]{2,1,0:T(8,128)S(1)}, f32[34,16,128]{2,1,0:T(8,128)S(1)}, f32[34,16,128]{2,1,0:T(8,128)S(1)}, bf16[34,32,128]{2,1,0:T(8,128)(2,1)...) custom-call(s32[8]{0:T(128)S(4)} %get-tuple-element.64.facts, ...), custom_call_target="tpu_custom_call", output_to_operand_aliasing={{0}: (4, {}), {1}: (5, {}), {2}: (6, {}), {3}: (7, {}), {4}... | custom-call | tf_op jit(solution)/shard_map/pallas_call | solution.py:489
  24.8 1.2 %collective-permute-start.5 = (f32[15,16,128]{2,1,0:T(8,128)S(1)}, f32[15,16,128]{2,1,0:T(8,128)S(1)}, u32[]{:S(2)}, u32[]{:S(2)}) collective-permute-start(f32[15,16,128]{2,1,0:T(8,128)S(1)} %get-tuple-element.91), channel_id=1, source_target_pairs={{0,1},{2,3},{7,6},{5,4},{8,9},{10,11},{15,14},{13,12},{16,17},{18,... | collective-permute-start | bytes 368648 | tf_op jit(solution)/shard_map/ppermute | solution.py:501
  26.0 1.9 %collective-permute-start.6 = (f32[12,16,128]{2,1,0:T(8,128)S(1)}, f32[12,16,128]{2,1,0:T(8,128)S(1)}, u32[]{:S(2)}, u32[]{:S(2)}) collective-permute-start(f32[12,16,128]{2,1,0:T(8,128)S(1)} %get-tuple-element.97), channel_id=1, source_target_pairs={{1,2},{3,7},{6,5},{4,8},{9,10},{11,15},{14,13},{12,16},{17,18},{19... | collective-permute-start | bytes 294920 | tf_op jit(solution)/shard_map/ppermute | solution.py:500
  27.9 0.0 collective-permute-done.5.refs_5_
  27.9 2.3 %shard_map.63 = (f32[34,16,128]{2,1,0:T(8,128)S(1)}, f32[34,16,128]{2,1,0:T(8,128)S(1)}, f32[34,16,128]{2,1,0:T(8,128)S(1)}, bf16[34,32,128]{2,1,0:T(8,128)(2,1)S(1)}, bf16[34,32,128]{2,1,0:T(8,128)(2,1)S(1)}) custom-call(s32[8]{0:T(128)S(4)} %get-tuple-element.64.facts, ...), custom_call_target="tpu_custom_call", output_to_operand_aliasing={{0}: (3, {}), {1}: (4, {}), {2}: (5, {}), {3}: (6, {}), {4}... | custom-call | tf_op jit(solution)/shard_map/pallas_call | solution.py:489
  30.2 2.0 %collective-permute-done.6.refs_5_ = f32[12,16,128]{2,1,0:T(8,128)S(1)} collective-permute-done((f32[12,16,128]{2,1,0:T(8,128)S(1)}, f32[12,16,128]{2,1,0:T(8,128)S(1)}, u32[]{:S(2)}, u32[]{:S(2)}) %collective-permute-start.6) | collective-permute-done | bytes 98336 | tf_op jit(solution)/shard_map/ppermute | solution.py:500
  32.2 2.0 %shard_map.64 = (f32[34,16,128]{2,1,0:T(8,128)S(1)}, f32[34,16,128]{2,1,0:T(8,128)S(1)}, f32[34,16,128]{2,1,0:T(8,128)S(1)}, bf16[34,32,128]{2,1,0:T(8,128)(2,1)...) custom-call(s32[8]{0:T(128)S(4)} %get-tuple-element.64.facts, ...), custom_call_target="tpu_custom_call", output_to_operand_aliasing={{0}: (4, {}), {1}: (5, {}), {2}: (6, {}), {3}: (7, {}), {4}... | custom-call | tf_op jit(solution)/shard_map/pallas_call | solution.py:489
  34.2 1.2 %collective-permute-start.7 = (f32[15,16,128]{2,1,0:T(8,128)S(1)}, f32[15,16,128]{2,1,0:T(8,128)S(1)}, u32[]{:S(2)}, u32[]{:S(2)}) collective-permute-start(f32[15,16,128]{2,1,0:T(8,128)S(1)} %get-tuple-element.103), channel_id=1, source_target_pairs={{0,1},{2,3},{7,6},{5,4},{8,9},{10,11},{15,14},{13,12},{16,17},{18,... | collective-permute-start | bytes 368648 | tf_op jit(solution)/shard_map/ppermute | solution.py:501
  35.4 1.9 %collective-permute-start.8 = (f32[12,16,128]{2,1,0:T(8,128)S(1)}, f32[12,16,128]{2,1,0:T(8,128)S(1)}, u32[]{:S(2)}, u32[]{:S(2)}) collective-permute-start(f32[12,16,128]{2,1,0:T(8,128)S(1)} %get-tuple-element.109), channel_id=1, source_target_pairs={{1,2},{3,7},{6,5},{4,8},{9,10},{11,15},{14,13},{12,16},{17,18},{19... | collective-permute-start | bytes 294920 | tf_op jit(solution)/shard_map/ppermute | solution.py:500
  37.3 0.0 collective-permute-done.7.refs_5_
  37.3 2.3 %shard_map.65 = (f32[34,16,128]{2,1,0:T(8,128)S(1)}, f32[34,16,128]{2,1,0:T(8,128)S(1)}, f32[34,16,128]{2,1,0:T(8,128)S(1)}, bf16[34,32,128]{2,1,0:T(8,128)(2,1)S(1)}, bf16[34,32,128]{2,1,0:T(8,128)(2,1)S(1)}) custom-call(s32[8]{0:T(128)S(4)} %get-tuple-element.64.facts, ...), custom_call_target="tpu_custom_call", output_to_operand_aliasing={{0}: (3, {}), {1}: (4, {}), {2}: (5, {}), {3}: (6, {}), {4}... | custom-call | tf_op jit(solution)/shard_map/pallas_call | solution.py:489
  39.6 2.0 %collective-permute-done.8.refs_5_ = f32[12,16,128]{2,1,0:T(8,128)S(1)} collective-permute-done((f32[12,16,128]{2,1,0:T(8,128)S(1)}, f32[12,16,128]{2,1,0:T(8,128)S(1)}, u32[]{:S(2)}, u32[]{:S(2)}) %collective-permute-start.8) | collective-permute-done | bytes 98336 | tf_op jit(solution)/shard_map/ppermute | solution.py:500
  41.6 2.0 %shard_map.66 = (f32[34,16,128]{2,1,0:T(8,128)S(1)}, f32[34,16,128]{2,1,0:T(8,128)S(1)}, f32[34,16,128]{2,1,0:T(8,128)S(1)}, bf16[34,32,128]{2,1,0:T(8,128)(2,1)...) custom-call(s32[8]{0:T(128)S(4)} %get-tuple-element.64.facts, ...), custom_call_target="tpu_custom_call", output_to_operand_aliasing={{0}: (4, {}), {1}: (5, {}), {2}: (6, {}), {3}: (7, {}), {4}... | custom-call | tf_op jit(solution)/shard_map/pallas_call | solution.py:489
  43.6 1.2 %collective-permute-start.9 = (f32[15,16,128]{2,1,0:T(8,128)S(1)}, f32[15,16,128]{2,1,0:T(8,128)S(1)}, u32[]{:S(2)}, u32[]{:S(2)}) collective-permute-start(f32[15,16,128]{2,1,0:T(8,128)S(1)} %get-tuple-element.115), channel_id=1, source_target_pairs={{0,1},{2,3},{7,6},{5,4},{8,9},{10,11},{15,14},{13,12},{16,17},{18,... | collective-permute-start | bytes 368648 | tf_op jit(solution)/shard_map/ppermute | solution.py:501
  44.8 2.1 %collective-permute-start.10 = (f32[12,16,128]{2,1,0:T(8,128)S(1)}, f32[12,16,128]{2,1,0:T(8,128)S(1)}, u32[]{:S(2)}, u32[]{:S(2)}) collective-permute-start(f32[12,16,128]{2,1,0:T(8,128)S(1)} %get-tuple-element.121), channel_id=1, source_target_pairs={{1,2},{3,7},{6,5},{4,8},{9,10},{11,15},{14,13},{12,16},{17,18},{19... | collective-permute-start | bytes 294920 | tf_op jit(solution)/shard_map/ppermute | solution.py:500
  46.9 0.0 collective-permute-done.9.refs_5_
  46.9 2.3 %shard_map.67 = (f32[34,16,128]{2,1,0:T(8,128)S(1)}, f32[34,16,128]{2,1,0:T(8,128)S(1)}, f32[34,16,128]{2,1,0:T(8,128)S(1)}, bf16[34,32,128]{2,1,0:T(8,128)(2,1)S(1)}, bf16[34,32,128]{2,1,0:T(8,128)(2,1)S(1)}) custom-call(s32[8]{0:T(128)S(4)} %get-tuple-element.64.facts, ...), custom_call_target="tpu_custom_call", output_to_operand_aliasing={{0}: (3, {}), {1}: (4, {}), {2}: (5, {}), {3}: (6, {}), {4}... | custom-call | tf_op jit(solution)/shard_map/pallas_call | solution.py:489
  49.2 1.8 %collective-permute-done.10.refs_5_ = f32[12,16,128]{2,1,0:T(8,128)S(1)} collective-permute-done((f32[12,16,128]{2,1,0:T(8,128)S(1)}, f32[12,16,128]{2,1,0:T(8,128)S(1)}, u32[]{:S(2)}, u32[]{:S(2)}) %collective-permute-start.10) | collective-permute-done | bytes 98336 | tf_op jit(solution)/shard_map/ppermute | solution.py:500
  51.0 1.7 %shard_map.68 = (f32[34,16,128]{2,1,0:T(8,128)S(1)}, f32[34,16,128]{2,1,0:T(8,128)S(1)}, f32[34,16,128]{2,1,0:T(8,128)S(1)}, bf16[34,32,128]{2,1,0:T(8,128)(2,1)...) custom-call(s32[8]{0:T(128)S(4)} %get-tuple-element.64.facts, ...), custom_call_target="tpu_custom_call", output_to_operand_aliasing={{0}: (4, {}), {1}: (5, {}), {2}: (6, {}), {3}: (7, {}), {4}... | custom-call | tf_op jit(solution)/shard_map/pallas_call | solution.py:489
  52.7 0.0 collective-permute-start.12
  52.7 1.3 %collective-permute-start.11 = (f32[16,16,128]{2,1,0:T(8,128)S(1)}, f32[16,16,128]{2,1,0:T(8,128)S(1)}, u32[]{:S(2)}, u32[]{:S(2)}) collective-permute-start(f32[16,16,128]{2,1,0:T(8,128)S(1)} %get-tuple-element.122.refs_0_), channel_id=1, source_target_pairs={{0,1},{1,0},{2,3},{3,2},{4,5},{5,4},{6,7},{7,6},{8,9},{9,8},{10,11... | collective-permute-start | bytes 393224 | tf_op jit(solution)/shard_map/ppermute | solution.py:398
  54.0 2.6 %collective-permute-done.12.refs_2_ = f32[16,16,128]{2,1,0:T(8,128)S(1)} collective-permute-done((f32[16,16,128]{2,1,0:T(8,128)S(1)}, f32[16,16,128]{2,1,0:T(8,128)S(1)}, u32[]{:S(2)}, u32[]{:S(2)}) %collective-permute-start.12) | collective-permute-done | bytes 131104 | tf_op jit(solution)/shard_map/ppermute | solution.py:394
  56.5 2.3 %collective-permute-start.13 = (f32[16,16,128]{2,1,0:T(8,128)S(1)}, f32[16,16,128]{2,1,0:T(8,128)S(1)}, u32[]{:S(2)}, u32[]{:S(2)}) collective-permute-start(f32[16,16,128]{2,1,0:T(8,128)S(1)} %collective-permute-done.12.refs_2_), channel_id=1, source_target_pairs={{0,1},{1,0},{2,3},{3,2},{4,5},{5,4},{6,7},{7,6},{8,9},{9,8},{10,11... | collective-permute-start | bytes 393224 | tf_op jit(solution)/shard_map/ppermute | solution.py:398
  58.9 0.0 collective-permute-done.11.refs_1_
  58.9 1.0 %collective-permute-done.13.refs_3_ = f32[16,16,128]{2,1,0:T(8,128)S(1)} collective-permute-done((f32[16,16,128]{2,1,0:T(8,128)S(1)}, f32[16,16,128]{2,1,0:T(8,128)S(1)}, u32[]{:S(2)}, u32[]{:S(2)}) %collective-permute-start.13) | collective-permute-done | bytes 131104 | tf_op jit(solution)/shard_map/ppermute | solution.py:398
  59.8 1.2 %shard_map.69 = f32[16,4096]{1,0:T(8,128)} custom-call(s32[8]{0:T(128)S(4)} %get-tuple-element.64.facts, f32[16,16,128]{2,1,0:T(8,128)S(1)} %get-tuple-element.122.refs_0_, f32[16,16,128]{2,1,0:T(8,128)S(1)} %collective-permute-done.11.refs_1_, f32[16,16,128]{2,1,0:T(8,128)S(1)} %collective-permute-done.12.refs_2_, ...), custom_call_target="tpu_custom_call" | custom-call | tf_op jit(solution)/shard_map/pallas_call | solution.py:533
  (2 shorter events, 0.0 us)
Async XLA Ops:
  1.1 2.6 %collective-permute-start = (f32[2,16,4096]{2,1,0:T(8,128)S(1)}, f32[2,16,4096]{2,1,0:T(8,128)S(1)}, u32[]{:S(2)}, u32[]{:S(2)}) collective-permute-start(f32[2,16,4096]{2,1,0:T(8,128)S(1)} %get-tuple-element.66.refs_0_), channel_id=1, source_target_pairs={{0,1},{1,0},{2,3},{3,2},{4,5},{5,4},{6,7},{7,6},{8,9},{9,8},{10,11... | collective-permute-start | bytes 1572872 | tf_op jit(solution)/shard_map/ppermute | solution.py:398
  4.8 17.1 %collective-permute-start.1 = (f32[1928,128]{1,0:T(8,128)S(1)}, f32[1928,128]{1,0:T(8,128)S(1)}, u32[]{:S(2)}, u32[]{:S(2)}) collective-permute-start(f32[1928,128]{1,0:T(8,128)S(1)} %shard_map.58), channel_id=1, source_target_pairs={{3,7},{4,8},{11,15},{12,16},{19,23},{20,24},{27,31},{7,3},{8,4},{1... | collective-permute-start | bytes 2961416 | tf_op jit(solution)/shard_map/ppermute | solution.py:463
  5.6 9.3 %collective-permute-start.2 = (f32[2,16,16,128]{3,2,1,0:T(8,128)S(1)}, f32[2,16,16,128]{3,2,1,0:T(8,128)S(1)}, u32[]{:S(2)}, u32[]{:S(2)}) collective-permute-start(f32[2,16,16,128]{3,2,1,0:T(8,128)S(1)} %get-tuple-element.71), channel_id=1, source_target_pairs={{2,0},{3,1},{0,2},{1,3},{6,4},{7,5},{4,6},{5,7},{10,8},{11,9},{8,1... | collective-permute-start | bytes 786440 | tf_op jit(solution)/shard_map/ppermute | solution.py:394
  15.2 4.4 %collective-permute-start.3 = (f32[15,16,128]{2,1,0:T(8,128)S(1)}, f32[15,16,128]{2,1,0:T(8,128)S(1)}, u32[]{:S(2)}, u32[]{:S(2)}) collective-permute-start(f32[15,16,128]{2,1,0:T(8,128)S(1)} %get-tuple-element.77), channel_id=1, source_target_pairs={{0,1},{2,3},{7,6},{5,4},{8,9},{10,11},{15,14},{13,12},{16,17},{18,... | collective-permute-start | bytes 368648 | tf_op jit(solution)/shard_map/ppermute | solution.py:501
  16.6 6.2 %collective-permute-start.4 = (f32[12,16,128]{2,1,0:T(8,128)S(1)}, f32[12,16,128]{2,1,0:T(8,128)S(1)}, u32[]{:S(2)}, u32[]{:S(2)}) collective-permute-start(f32[12,16,128]{2,1,0:T(8,128)S(1)} %get-tuple-element.85), channel_id=1, source_target_pairs={{1,2},{3,7},{6,5},{4,8},{9,10},{11,15},{14,13},{12,16},{17,18},{19... | collective-permute-start | bytes 294920 | tf_op jit(solution)/shard_map/ppermute | solution.py:500
  24.8 3.1 %collective-permute-start.5 = (f32[15,16,128]{2,1,0:T(8,128)S(1)}, f32[15,16,128]{2,1,0:T(8,128)S(1)}, u32[]{:S(2)}, u32[]{:S(2)}) collective-permute-start(f32[15,16,128]{2,1,0:T(8,128)S(1)} %get-tuple-element.91), channel_id=1, source_target_pairs={{0,1},{2,3},{7,6},{5,4},{8,9},{10,11},{15,14},{13,12},{16,17},{18,... | collective-permute-start | bytes 368648 | tf_op jit(solution)/shard_map/ppermute | solution.py:501
  26.0 6.2 %collective-permute-start.6 = (f32[12,16,128]{2,1,0:T(8,128)S(1)}, f32[12,16,128]{2,1,0:T(8,128)S(1)}, u32[]{:S(2)}, u32[]{:S(2)}) collective-permute-start(f32[12,16,128]{2,1,0:T(8,128)S(1)} %get-tuple-element.97), channel_id=1, source_target_pairs={{1,2},{3,7},{6,5},{4,8},{9,10},{11,15},{14,13},{12,16},{17,18},{19... | collective-permute-start | bytes 294920 | tf_op jit(solution)/shard_map/ppermute | solution.py:500
  34.2 3.1 %collective-permute-start.7 = (f32[15,16,128]{2,1,0:T(8,128)S(1)}, f32[15,16,128]{2,1,0:T(8,128)S(1)}, u32[]{:S(2)}, u32[]{:S(2)}) collective-permute-start(f32[15,16,128]{2,1,0:T(8,128)S(1)} %get-tuple-element.103), channel_id=1, source_target_pairs={{0,1},{2,3},{7,6},{5,4},{8,9},{10,11},{15,14},{13,12},{16,17},{18,... | collective-permute-start | bytes 368648 | tf_op jit(solution)/shard_map/ppermute | solution.py:501
  35.4 6.2 %collective-permute-start.8 = (f32[12,16,128]{2,1,0:T(8,128)S(1)}, f32[12,16,128]{2,1,0:T(8,128)S(1)}, u32[]{:S(2)}, u32[]{:S(2)}) collective-permute-start(f32[12,16,128]{2,1,0:T(8,128)S(1)} %get-tuple-element.109), channel_id=1, source_target_pairs={{1,2},{3,7},{6,5},{4,8},{9,10},{11,15},{14,13},{12,16},{17,18},{19... | collective-permute-start | bytes 294920 | tf_op jit(solution)/shard_map/ppermute | solution.py:500
  43.6 3.3 %collective-permute-start.9 = (f32[15,16,128]{2,1,0:T(8,128)S(1)}, f32[15,16,128]{2,1,0:T(8,128)S(1)}, u32[]{:S(2)}, u32[]{:S(2)}) collective-permute-start(f32[15,16,128]{2,1,0:T(8,128)S(1)} %get-tuple-element.115), channel_id=1, source_target_pairs={{0,1},{2,3},{7,6},{5,4},{8,9},{10,11},{15,14},{13,12},{16,17},{18,... | collective-permute-start | bytes 368648 | tf_op jit(solution)/shard_map/ppermute | solution.py:501
  44.8 6.2 %collective-permute-start.10 = (f32[12,16,128]{2,1,0:T(8,128)S(1)}, f32[12,16,128]{2,1,0:T(8,128)S(1)}, u32[]{:S(2)}, u32[]{:S(2)}) collective-permute-start(f32[12,16,128]{2,1,0:T(8,128)S(1)} %get-tuple-element.121), channel_id=1, source_target_pairs={{1,2},{3,7},{6,5},{4,8},{9,10},{11,15},{14,13},{12,16},{17,18},{19... | collective-permute-start | bytes 294920 | tf_op jit(solution)/shard_map/ppermute | solution.py:500
  52.7 3.8 %collective-permute-start.12 = (f32[16,16,128]{2,1,0:T(8,128)S(1)}, f32[16,16,128]{2,1,0:T(8,128)S(1)}, u32[]{:S(2)}, u32[]{:S(2)}) collective-permute-start(f32[16,16,128]{2,1,0:T(8,128)S(1)} %get-tuple-element.122.refs_0_), channel_id=1, source_target_pairs={{2,0},{3,1},{0,2},{1,3},{6,4},{7,5},{4,6},{5,7},{10,8},{11,9},{8,1... | collective-permute-start | bytes 393224 | tf_op jit(solution)/shard_map/ppermute | solution.py:394
  52.7 6.2 %collective-permute-start.11 = (f32[16,16,128]{2,1,0:T(8,128)S(1)}, f32[16,16,128]{2,1,0:T(8,128)S(1)}, u32[]{:S(2)}, u32[]{:S(2)}) collective-permute-start(f32[16,16,128]{2,1,0:T(8,128)S(1)} %get-tuple-element.122.refs_0_), channel_id=1, source_target_pairs={{0,1},{1,0},{2,3},{3,2},{4,5},{5,4},{6,7},{7,6},{8,9},{9,8},{10,11... | collective-permute-start | bytes 393224 | tf_op jit(solution)/shard_map/ppermute | solution.py:398
  56.5 3.3 %collective-permute-start.13 = (f32[16,16,128]{2,1,0:T(8,128)S(1)}, f32[16,16,128]{2,1,0:T(8,128)S(1)}, u32[]{:S(2)}, u32[]{:S(2)}) collective-permute-start(f32[16,16,128]{2,1,0:T(8,128)S(1)} %collective-permute-done.12.refs_2_), channel_id=1, source_target_pairs={{0,1},{1,0},{2,3},{3,2},{4,5},{5,4},{6,7},{7,6},{8,9},{9,8},{10,11... | collective-permute-start | bytes 393224 | tf_op jit(solution)/shard_map/ppermute | solution.py:398

commit v10 on v8

--- a/solution.py
+++ b/solution.py
@@ -82,12 +82,13 @@
 def put_far(ob, steps, even, u, r, pay):
     h = HB * steps
     pay[: 2 * HB] = u[pl.ds(jnp.where(even, h, h + ob - 2 * HB), 2 * HB)]
-    pay[2 * HB : 3 * HB] = r[pl.ds(jnp.where(even, h, h + ob - HB), HB)]
+    if pay.shape[0] - sent_blocks(steps) > 2 * HB:
+        pay[2 * HB : 3 * HB] = r[pl.ds(jnp.where(even, h, h + ob - HB), HB)]
 
 
 def put_far_ahead(ob, steps, even, u, pay):
     h, n = HB * steps, sent_blocks(steps)
-    pay[3 * HB :] = u[pl.ds(jnp.where(even, h + HB, h + ob - HB - n), n)]
+    pay[pay.shape[0] - n :] = u[pl.ds(jnp.where(even, h + HB, h + ob - HB - n), n)]
 
 
 def take_far(ob, steps, even, got, u, r, now, later):
@@ -97,10 +98,11 @@
     now[pl.ds(at, 2 * HB), :16] = high
     now[pl.ds(at, 2 * HB), 16:] = low
     at = jnp.where(even, h - HB, h + ob)
-    u[pl.ds(at, HB)] = got[pl.ds(jnp.where(even, HB, 0), HB)]
-    r[pl.ds(at, HB)] = got[2 * HB : 3 * HB]
+    nearest = got[pl.ds(jnp.where(even, HB, 0), HB)]
+    u[pl.ds(at, HB)] = nearest
+    r[pl.ds(at, HB)] = got[2 * HB : 3 * HB] if got.shape[0] - n > 2 * HB else nearest * THETA
     if n:
-        ahead = got[3 * HB :]
+        ahead = got[got.shape[0] - n :]
         at = jnp.where(even, h - HB - n, h + ob + HB)
         u[pl.ds(at, n)] = ahead
         r[pl.ds(at, n)] = ahead * THETA
@@ -127,8 +129,23 @@
     return jnp.where(backwards == 1, folds - 1 - fold, fold)
 
 
-def align_kernel(ob, folds, facts, *refs):
-    sources, outs = refs[:2], refs[2:]
+def align_kernel(ob, folds, lend, width, facts, indices, blocks, *refs):
+    sources, outs, (border, sem) = refs[:2], refs[2:-2], refs[-2:]
+    own = indices.shape[1]
+    size = blocks.shape[0] // own
+    edge = (facts[0] == 0) | (facts[0] == folds - 1)
+    first = jnp.where(facts[0] == 0, 0, own - lend)
+
+    def copies():
+        for i in range(lend):
+            row = blocks.at[pl.ds(pl.multiple_of((first + i) * size, size), size)]
+            yield pltpu.make_async_copy(row, border.at[i * size : (i + 1) * size], sem.at[i])
+
+    @pl.when(edge)
+    def _():
+        for copy in copies():
+            copy.start()
+
     capacity = sources[0].shape[-1]
     lane = lax.broadcasted_iota(jnp.int32, (16, 128), 1)
     spans = []
@@ -160,30 +177,25 @@
 
         lax.fori_loop(0, ob, block, 0, unroll=4)
 
-
-def first_kernel(folds, lend, width, counts, columns, initial, right_side, blocks, facts, held, stacked, border, live, sem):
-    own = columns.shape[1]
-    size = blocks.shape[0] // own
+    @pl.when(edge)
+    def _():
+        place = lax.broadcasted_iota(jnp.int32, (8, 128), 1)
+        lines = jnp.zeros((8, 128), jnp.int32)
+        for i in range(lend):
+            for k in range(width):
+                lines = jnp.where(place == i * width + k, indices[k, first + i], lines)
+        border[lend * size :] = lines.astype(F32)
+        for copy in copies():
+            copy.wait()
+
+
+def first_kernel(folds, counts, columns, initial, right_side, facts, held, stacked, live, sem):
     fold = lax.axis_index("fold")
     backwards = lax.rem(lax.axis_index("group"), 2)
     part = part_of(fold, folds, backwards)
-    edge = (part == 0) | (part == folds - 1)
-    first = jnp.where(part == 0, 0, own - lend)
     small = [pltpu.make_async_copy(columns, held, sem.at[0]), pltpu.make_async_copy(counts, live, sem.at[1])]
     pair = [pltpu.make_async_copy(array, stacked.at[i], sem.at[2 + i]) for i, array in enumerate((initial, right_side))]
-    rows = []
-    for i in range(lend):
-        row = blocks.at[pl.ds(pl.multiple_of((first + i) * size, size), size)]
-        rows.append(pltpu.make_async_copy(row, border.at[i * size : (i + 1) * size], sem.at[4 + i]))
-    for copy in small:
-        copy.start()
-
-    @pl.when(edge)
-    def _():
-        for copy in rows:
-            copy.start()
-
-    for copy in pair:
+    for copy in pair + small:
         copy.start()
     for copy in small:
         copy.wait()
@@ -191,18 +203,6 @@
         facts[i] = fact
     for i in range(folds):
         facts[COUNTS + i] = live[0, i]
-
-    @pl.when(edge)
-    def _():
-        lane = lax.broadcasted_iota(jnp.int32, (8, 128), 1)
-        indices = jnp.zeros((8, 128), jnp.int32)
-        for i in range(lend):
-            for k in range(width):
-                indices = jnp.where(lane == i * width + k, held[k, first + i], indices)
-        border[lend * size :] = indices.astype(F32)
-        for copy in rows:
-            copy.wait()
-
     for copy in pair:
         copy.wait()
 
@@ -215,18 +215,19 @@
         out[a, k * side : (k + 1) * side, side:] = low.T
 
 
-def prepare_kernel(ob, halo, width, facts, columns, blocks, token, out, offsets, raw, sem):
+def prepare_kernel(ob, halo, lend, width, facts, columns, blocks, token, out, offsets, raw, sem):
     del token
-    rows, size = raw.shape[0], raw.shape[1]
+    used, size = raw.shape[0], raw.shape[1]
     own = blocks.shape[0] // size
     first = facts[0] * ob - halo
-
-    def copy(a):
-        i = pl.multiple_of(jnp.clip(first + a, 0, own - 1) * size, size)
-        return pltpu.make_async_copy(blocks.at[pl.ds(i, size)], raw.at[a], sem.at[a])
-
-    for a in range(rows):
-        copy(a).start()
+    start = jnp.where(facts[1] == 0, halo - lend, 0)
+
+    def copy(n):
+        i = pl.multiple_of(jnp.clip(first + start + n, 0, own - 1) * size, size)
+        return pltpu.make_async_copy(blocks.at[pl.ds(i, size)], raw.at[n], sem.at[n])
+
+    for n in range(used):
+        copy(n).start()
 
     def indices(a, carry):
         i = first + a
@@ -234,17 +235,17 @@
             offsets[a * width + k] = columns[k, jnp.clip(i, 0, own - 1)] - HB - i
         return carry
 
-    lax.fori_loop(0, rows, indices, 0)
-    group = 4 if rows % 4 == 0 else 2
+    lax.fori_loop(0, ob + 2 * halo, indices, 0)
+    group = max(n for n in (1, 2, 3, 4, 5) if used % n == 0)
 
     def several(g, carry):
         for s in range(group):
-            a = g * group + s
-            copy(a).wait()
-            put_row(out, a, raw.at[a])
+            n = g * group + s
+            copy(n).wait()
+            put_row(out, start + n, raw.at[n])
         return carry
 
-    lax.fori_loop(0, rows // group, several, 0)
+    lax.fori_loop(0, used // group, several, 0)
 
 
 def border_kernel(ob, folds, halo, lend, width, facts, prepared, raw, before, out, offsets, vector, scalars, sem):
@@ -410,7 +411,11 @@
 
 
     payload_a = jax.ShapeDtypeStruct((2 * HB * steps - HB, vectors, side), F32)
-    payload_b = jax.ShapeDtypeStruct((3 * HB + sent_blocks(steps), vectors, side), F32)
+
+    def payload_b(done):
+        blocks = (2 if done and pairs[done - 1][0] == 0.0 else 3) * HB + sent_blocks(steps)
+        return jax.ShapeDtypeStruct((blocks, vectors, side), F32)
+
 
     line = [g * folds + (folds - 1 - p if g % 2 else p) for g in range(groups) for p in range(folds)]
 
@@ -424,38 +429,40 @@
         return pltpu.with_memory_space_constraint(array, space)
 
     flat = fixed(blocks.reshape(own * size, side))
-    facts, indices, stacked, border = pl.pallas_call(
-        functools.partial(first_kernel, folds, lend, width),
+    facts, indices, stacked = pl.pallas_call(
+        functools.partial(first_kernel, folds),
         out_shape=(
             pltpu.SMEM((COUNTS + folds,), jnp.int32),
             pltpu.SMEM((width, own), jnp.int32),
             pltpu.VMEM((2, vectors, capacity), F32),
-            pltpu.VMEM((lend * size + 8, side), F32),
         ),
-        in_specs=[HBM] * 5,
-        out_specs=(SMEM, SMEM, VMEM, VMEM),
-        scratch_shapes=[pltpu.SMEM((1, folds), jnp.int32), pltpu.SemaphoreType.DMA((4 + lend,))],
+        in_specs=[HBM] * 4,
+        out_specs=(SMEM, SMEM, VMEM),
+        scratch_shapes=[pltpu.SMEM((1, folds), jnp.int32), pltpu.SemaphoreType.DMA((4,))],
         compiler_params=params(),
-    )(fixed(counts), fixed(columns.T), fixed(initial), fixed(right_side), flat)
+    )(fixed(counts), fixed(columns.T), fixed(initial), fixed(right_side))
     facts, indices = fixed(facts, pltpu.SMEM), fixed(indices, pltpu.SMEM)
+    mate = other_core(stacked, folds)
+
+    rows_of = jax.ShapeDtypeStruct((2, ob, vectors, side), F32)
+    *partial, border = pl.pallas_call(
+        functools.partial(align_kernel, ob, folds, lend, width),
+        out_shape=(rows_of,) * (folds // 2) + (pltpu.VMEM((lend * size + 8, side), F32),),
+        in_specs=[SMEM, SMEM, HBM, VMEM, VMEM],
+        out_specs=(VMEM,) * (1 + folds // 2),
+        scratch_shapes=[pltpu.SemaphoreType.DMA((lend,))],
+        compiler_params=params(),
+    )(facts, indices, flat, fixed(stacked, pltpu.VMEM), fixed(mate, pltpu.VMEM))
+    sent = [over_chips(partial[d], folds // 2 - d, folds) for d in range(1, folds // 2)]
     border = lax.ppermute(border, AXES, swap_border)
-    mate = other_core(stacked, folds)
-    rows_of = jax.ShapeDtypeStruct((2, ob, vectors, side), F32)
-    partial = pl.pallas_call(
-        functools.partial(align_kernel, ob, folds),
-        out_shape=(rows_of,) * (folds // 2),
-        in_specs=[SMEM, VMEM, VMEM],
-        out_specs=(VMEM,) * (folds // 2),
-        compiler_params=params(),
-    )(facts, fixed(stacked, pltpu.VMEM), fixed(mate, pltpu.VMEM))
-    sent = [over_chips(partial[d], folds // 2 - d, folds) for d in range(1, folds // 2)]
-
+
+    used = ob + halo + lend
     operator, offsets = pl.pallas_call(
-        functools.partial(prepare_kernel, ob, halo, width),
+        functools.partial(prepare_kernel, ob, halo, lend, width),
         out_shape=(operator_shape, pltpu.SMEM((rows * width,), jnp.int32)),
         in_specs=[SMEM, SMEM, HBM, pl.BlockSpec(memory_space=pl.ANY)],
         out_specs=(VMEM, SMEM),
-        scratch_shapes=[pltpu.VMEM((rows, size, side), F32), pltpu.SemaphoreType.DMA((rows,))],
+        scratch_shapes=[pltpu.VMEM((used, size, side), F32), pltpu.SemaphoreType.DMA((used,))],
         compiler_params=params(32),
         cost_estimate=pl.CostEstimate(flops=10**7, bytes_accessed=2 * rows * size * side * 4, transcendentals=0),
     )(facts, indices, flat, partial[0])
@@ -465,7 +472,7 @@
     state = (pltpu.VMEM((extent, vectors, side), F32),) * 3 + (pltpu.VMEM((extent, 2 * vectors, side), BF16),) * 2
     *held, pay_a, pay_b = pl.pallas_call(
         functools.partial(begin_kernel, ob, steps, pairs[0]),
-        out_shape=(*state, payload_a, payload_b),
+        out_shape=(*state, payload_a, payload_b(0)),
         in_specs=[SMEM, SMEM] + [VMEM] * (1 + folds // 2),
         out_specs=(VMEM,) * 7,
         compiler_params=params(),
@@ -505,7 +512,7 @@
             lent = fixed(lent, pltpu.SMEM)
         if done + steps < APPLIES:
             held, (pay_a, pay_b) = part_of_phase(
-                outer_kernel, operator, [offsets, lent], held, got_b, (payload_a, payload_b)
+                outer_kernel, operator, [offsets, lent], held, got_b, (payload_a, payload_b(done + steps))
             )
         else:
             result = jax.ShapeDtypeStruct((ob, vectors, side), F32)

time: 62.1 us -> 61 us (0.982)
  waiting for transfers between devices: 13.7 us -> 12.2 us
  starting transfers between devices: 22.1 us -> 23.2 us
    ppermute x2, starting transfers between devices: 0.82 us -> 3.74 us  [over_chips(): lax.ppermute(array, 'fold', [((i + 2 * d) % folds, i) for i in range(fold...]
    ppermute x3, starting transfers between devices: 7.22 us -> 4.94 us  [other_core(): return lax.ppermute(array, 'fold', [(i, i ^ 1) for i in range(folds)])]
    ppermute x2, waiting for transfers between devices: 4.09 us -> 3.11 us  [over_chips(): lax.ppermute(array, 'fold', [((i + 2 * d) % folds, i) for i in range(fold...]
  transfers between devices with their start and end apart: 14 -> 14, of which waited for: 8 -> 8; matrix products, arithmetic and copies ran while one was open for 0% -> 0% of each run, Pallas kernels for 26% -> 23%
where the time goes in v10:
time: 61 us; the launch traced here: 60.8 us
  Pallas kernels  25.3 us (41%)
  starting transfers between devices  23.2 us (38%)
  waiting for transfers between devices  12.2 us (20%)
    pallas_call x8, Pallas kernels, part_of_phase(): pl.pallas_call(functools.partial(kernel, ob, folds, steps, done == 0, don...  16.8 us
    ppermute x4, starting transfers between devices, on_device(): got_b = lax.ppermute(pay_b, AXES, swap_b)  8.48 us
    ppermute x4, waiting for transfers between devices, on_device(): got_b = lax.ppermute(pay_b, AXES, swap_b)  6.52 us
    ppermute x4, starting transfers between devices, on_device(): got_a = lax.ppermute(pay_a, AXES, swap_a)  5.31 us
    ppermute x3, starting transfers between devices, other_core(): return lax.ppermute(array, 'fold', [(i, i ^ 1) for i in range(folds)])  4.94 us
    pallas_call x1, Pallas kernels, on_device(): pl.pallas_call(functools.partial(prepare_kernel, ob, halo, lend, width),...  4.79 us
    ppermute x2, starting transfers between devices, over_chips(): lax.ppermute(array, 'fold', [((i + 2 * d) % folds, i) for i in range(fold...  3.74 us
    ppermute x2, waiting for transfers between devices, over_chips(): lax.ppermute(array, 'fold', [((i + 2 * d) % folds, i) for i in range(fold...  3.11 us
  transfers between devices with their start and end apart: 14, of which 8 were waited for; matrix products, arithmetic and copies ran while one was open for 0% of the time, Pallas kernels for 23%

profile of v10, /device:TPU:9, one launch (start us, length us, event | category | flops | bytes accessed | tf_op | source)
XLA Modules:
  0.0 60.8 jit_solution(335059264303075494)
XLA Ops:
  0.0 1.1 %shard_map.55 = (s32[8]{0:T(128)S(4)}, s32[5,64]{1,0:T(8,128)S(4)}, f32[2,16,4096]{2,1,0:T(8,128)S(1)}) custom-call(s32[1,4]{1,0:T(1,128)} %counts.1, s32[5,64]{1,0:T(8,128)} %bitcast.4, f32[16,4096]{1,0:T(8,128)} %initial.1, f32[16,4096]{1,0:T(8,128)} %right_side.1), custom_call_target="tpu_custom_call" | custom-call | tf_op jit(solution)/shard_map/pallas_call | solution.py:432
  1.1 0.7 %collective-permute-start = (f32[2,16,4096]{2,1,0:T(8,128)S(1)}, f32[2,16,4096]{2,1,0:T(8,128)S(1)}, u32[]{:S(2)}, u32[]{:S(2)}) collective-permute-start(f32[2,16,4096]{2,1,0:T(8,128)S(1)} %get-tuple-element.66.refs_0_), channel_id=1, source_target_pairs={{0,1},{1,0},{2,3},{3,2},{4,5},{5,4},{6,7},{7,6},{8,9},{9,8},{10,11... | collective-permute-start | bytes 1572872 | tf_op jit(solution)/shard_map/ppermute | solution.py:395
  1.8 1.5 %collective-permute-done.refs_1_ = f32[2,16,4096]{2,1,0:T(8,128)S(1)} collective-permute-done((f32[2,16,4096]{2,1,0:T(8,128)S(1)}, f32[2,16,4096]{2,1,0:T(8,128)S(1)}, u32[]{:S(2)}, u32[]{:S(2)}) %collective-permute-start) | collective-permute-done | bytes 524320 | tf_op jit(solution)/shard_map/ppermute | solution.py:395
  3.3 1.2 %shard_map.56 = (f32[2,16,16,128]{3,2,1,0:T(8,128)S(1)}, f32[2,16,16,128]{3,2,1,0:T(8,128)S(1)}, f32[1928,128]{1,0:T(8,128)S(1)}) custom-call(s32[8]{0:T(128)S(4)} %get-tuple-element.64.facts, s32[5,64]{1,0:T(8,128)S(4)} %get-tuple-element.65.indices.columns, f32[40960,128]{1,0:T(8,128)} %bitcast.2, f32[2,16,4096]{2,1,0:T(8,128)S(1)} %get-tuple-element.66.refs_0_, ...), custom_call_target="tpu_custom_call" | custom-call | tf_op jit(solution)/shard_map/pallas_call | solution.py:448
  4.5 0.7 %collective-permute-start.1 = (f32[1928,128]{1,0:T(8,128)S(1)}, f32[1928,128]{1,0:T(8,128)S(1)}, u32[]{:S(2)}, u32[]{:S(2)}) collective-permute-start(f32[1928,128]{1,0:T(8,128)S(1)} %get-tuple-element.70), channel_id=1, source_target_pairs={{3,7},{4,8},{11,15},{12,16},{19,23},{20,24},{27,31},{7,3},{8,4},{1... | collective-permute-start | bytes 2961416 | tf_op jit(solution)/shard_map/ppermute | solution.py:457
  5.3 3.7 %collective-permute-start.2 = (f32[2,16,16,128]{3,2,1,0:T(8,128)S(1)}, f32[2,16,16,128]{3,2,1,0:T(8,128)S(1)}, u32[]{:S(2)}, u32[]{:S(2)}) collective-permute-start(f32[2,16,16,128]{3,2,1,0:T(8,128)S(1)} %get-tuple-element.71), channel_id=1, source_target_pairs={{2,0},{3,1},{0,2},{1,3},{6,4},{7,5},{4,6},{5,7},{10,8},{11,9},{8,1... | collective-permute-start | bytes 786440 | tf_op jit(solution)/shard_map/ppermute | solution.py:391
  9.0 4.8 %shard_map.57 = (bf16[28,640,256]{2,1,0:T(8,128)(2,1)S(1)}, s32[140]{0:T(256)S(4)}) custom-call(s32[8]{0:T(128)S(4)} %get-tuple-element.64.facts, s32[5,64]{1,0:T(8,128)S(4)} %get-tuple-element.65.indices.columns, f32[40960,128]{1,0:T(8,128)} %bitcast.3, f32[2,16,16,128]{3,2,1,0:T(8,128)S(1)} %get-tuple-element.67.token.refs_0_), custom_call_target="tpu_custom_call" | custom-call | flops 10000000 | bytes 18350080 | tf_op jit(solution)/shard_map/pallas_call | solution.py:460
  13.8 0.8 %collective-permute-done.2.refs_1_ = f32[2,16,16,128]{3,2,1,0:T(8,128)S(1)} collective-permute-done((f32[2,16,16,128]{3,2,1,0:T(8,128)S(1)}, f32[2,16,16,128]{3,2,1,0:T(8,128)S(1)}, u32[]{:S(2)}, u32[]{:S(2)}) %collective-permute-start.2) | collective-permute-done | bytes 262176 | tf_op jit(solution)/shard_map/ppermute | solution.py:391
  14.6 0.3 shard_map.58
  14.9 1.7 %collective-permute-start.3 = (f32[15,16,128]{2,1,0:T(8,128)S(1)}, f32[15,16,128]{2,1,0:T(8,128)S(1)}, u32[]{:S(2)}, u32[]{:S(2)}) collective-permute-start(f32[15,16,128]{2,1,0:T(8,128)S(1)} %get-tuple-element.77), channel_id=1, source_target_pairs={{0,1},{2,3},{7,6},{5,4},{8,9},{10,11},{15,14},{13,12},{16,17},{18,... | collective-permute-start | bytes 368648 | tf_op jit(solution)/shard_map/ppermute | solution.py:496
  16.6 2.6 %collective-permute-start.4 = (f32[12,16,128]{2,1,0:T(8,128)S(1)}, f32[12,16,128]{2,1,0:T(8,128)S(1)}, u32[]{:S(2)}, u32[]{:S(2)}) collective-permute-start(f32[12,16,128]{2,1,0:T(8,128)S(1)} %get-tuple-element.85), channel_id=1, source_target_pairs={{1,2},{3,7},{6,5},{4,8},{9,10},{11,15},{14,13},{12,16},{17,18},{19... | collective-permute-start | bytes 294920 | tf_op jit(solution)/shard_map/ppermute | solution.py:495
  19.2 0.0 collective-permute-done.3.refs_5_
  19.2 2.3 %shard_map.59 = (f32[34,16,128]{2,1,0:T(8,128)S(1)}, f32[34,16,128]{2,1,0:T(8,128)S(1)}, f32[34,16,128]{2,1,0:T(8,128)S(1)}, bf16[34,32,128]{2,1,0:T(8,128)(2,1)S(1)}, bf16[34,32,128]{2,1,0:T(8,128)(2,1)S(1)}) custom-call(s32[8]{0:T(128)S(4)} %get-tuple-element.64.facts, ...), custom_call_target="tpu_custom_call", output_to_operand_aliasing={{0}: (3, {}), {1}: (4, {}), {2}: (5, {}), {3}: (6, {}), {4}... | custom-call | tf_op jit(solution)/shard_map/pallas_call | solution.py:484
  21.5 0.0 collective-permute-done.1.raw
  21.6 1.3 %collective-permute-done.4.refs_5_ = f32[12,16,128]{2,1,0:T(8,128)S(1)} collective-permute-done((f32[12,16,128]{2,1,0:T(8,128)S(1)}, f32[12,16,128]{2,1,0:T(8,128)S(1)}, u32[]{:S(2)}, u32[]{:S(2)}) %collective-permute-start.4) | collective-permute-done | bytes 98336 | tf_op jit(solution)/shard_map/ppermute | solution.py:495
  22.8 2.0 %shard_map.61 = (f32[34,16,128]{2,1,0:T(8,128)S(1)}, f32[34,16,128]{2,1,0:T(8,128)S(1)}, f32[34,16,128]{2,1,0:T(8,128)S(1)}, bf16[34,32,128]{2,1,0:T(8,128)(2,1)...) custom-call(s32[8]{0:T(128)S(4)} %get-tuple-element.64.facts, ...), custom_call_target="tpu_custom_call", output_to_operand_aliasing={{0}: (4, {}), {1}: (5, {}), {2}: (6, {}), {3}: (7, {}), {4}... | custom-call | tf_op jit(solution)/shard_map/pallas_call | solution.py:484
  24.8 1.2 %collective-permute-start.5 = (f32[15,16,128]{2,1,0:T(8,128)S(1)}, f32[15,16,128]{2,1,0:T(8,128)S(1)}, u32[]{:S(2)}, u32[]{:S(2)}) collective-permute-start(f32[15,16,128]{2,1,0:T(8,128)S(1)} %get-tuple-element.91), channel_id=1, source_target_pairs={{0,1},{2,3},{7,6},{5,4},{8,9},{10,11},{15,14},{13,12},{16,17},{18,... | collective-permute-start | bytes 368648 | tf_op jit(solution)/shard_map/ppermute | solution.py:496
  26.0 1.9 %collective-permute-start.6 = (f32[12,16,128]{2,1,0:T(8,128)S(1)}, f32[12,16,128]{2,1,0:T(8,128)S(1)}, u32[]{:S(2)}, u32[]{:S(2)}) collective-permute-start(f32[12,16,128]{2,1,0:T(8,128)S(1)} %get-tuple-element.97), channel_id=1, source_target_pairs={{1,2},{3,7},{6,5},{4,8},{9,10},{11,15},{14,13},{12,16},{17,18},{19... | collective-permute-start | bytes 294920 | tf_op jit(solution)/shard_map/ppermute | solution.py:495
  27.9 0.0 collective-permute-done.5.refs_5_
  27.9 2.3 %shard_map.62 = (f32[34,16,128]{2,1,0:T(8,128)S(1)}, f32[34,16,128]{2,1,0:T(8,128)S(1)}, f32[34,16,128]{2,1,0:T(8,128)S(1)}, bf16[34,32,128]{2,1,0:T(8,128)(2,1)S(1)}, bf16[34,32,128]{2,1,0:T(8,128)(2,1)S(1)}) custom-call(s32[8]{0:T(128)S(4)} %get-tuple-element.64.facts, ...), custom_call_target="tpu_custom_call", output_to_operand_aliasing={{0}: (3, {}), {1}: (4, {}), {2}: (5, {}), {3}: (6, {}), {4}... | custom-call | tf_op jit(solution)/shard_map/pallas_call | solution.py:484
  30.2 2.0 %collective-permute-done.6.refs_5_ = f32[12,16,128]{2,1,0:T(8,128)S(1)} collective-permute-done((f32[12,16,128]{2,1,0:T(8,128)S(1)}, f32[12,16,128]{2,1,0:T(8,128)S(1)}, u32[]{:S(2)}, u32[]{:S(2)}) %collective-permute-start.6) | collective-permute-done | bytes 98336 | tf_op jit(solution)/shard_map/ppermute | solution.py:495
  32.2 2.0 %shard_map.63 = (f32[34,16,128]{2,1,0:T(8,128)S(1)}, f32[34,16,128]{2,1,0:T(8,128)S(1)}, f32[34,16,128]{2,1,0:T(8,128)S(1)}, bf16[34,32,128]{2,1,0:T(8,128)(2,1)...) custom-call(s32[8]{0:T(128)S(4)} %get-tuple-element.64.facts, ...), custom_call_target="tpu_custom_call", output_to_operand_aliasing={{0}: (4, {}), {1}: (5, {}), {2}: (6, {}), {3}: (7, {}), {4}... | custom-call | tf_op jit(solution)/shard_map/pallas_call | solution.py:484
  34.2 1.2 %collective-permute-start.7 = (f32[15,16,128]{2,1,0:T(8,128)S(1)}, f32[15,16,128]{2,1,0:T(8,128)S(1)}, u32[]{:S(2)}, u32[]{:S(2)}) collective-permute-start(f32[15,16,128]{2,1,0:T(8,128)S(1)} %get-tuple-element.103), channel_id=1, source_target_pairs={{0,1},{2,3},{7,6},{5,4},{8,9},{10,11},{15,14},{13,12},{16,17},{18,... | collective-permute-start | bytes 368648 | tf_op jit(solution)/shard_map/ppermute | solution.py:496
  35.4 1.9 %collective-permute-start.8 = (f32[12,16,128]{2,1,0:T(8,128)S(1)}, f32[12,16,128]{2,1,0:T(8,128)S(1)}, u32[]{:S(2)}, u32[]{:S(2)}) collective-permute-start(f32[12,16,128]{2,1,0:T(8,128)S(1)} %get-tuple-element.109), channel_id=1, source_target_pairs={{1,2},{3,7},{6,5},{4,8},{9,10},{11,15},{14,13},{12,16},{17,18},{19... | collective-permute-start | bytes 294920 | tf_op jit(solution)/shard_map/ppermute | solution.py:495
  37.3 0.0 collective-permute-done.7.refs_5_
  37.3 2.3 %shard_map.64 = (f32[34,16,128]{2,1,0:T(8,128)S(1)}, f32[34,16,128]{2,1,0:T(8,128)S(1)}, f32[34,16,128]{2,1,0:T(8,128)S(1)}, bf16[34,32,128]{2,1,0:T(8,128)(2,1)S(1)}, bf16[34,32,128]{2,1,0:T(8,128)(2,1)S(1)}) custom-call(s32[8]{0:T(128)S(4)} %get-tuple-element.64.facts, ...), custom_call_target="tpu_custom_call", output_to_operand_aliasing={{0}: (3, {}), {1}: (4, {}), {2}: (5, {}), {3}: (6, {}), {4}... | custom-call | tf_op jit(solution)/shard_map/pallas_call | solution.py:484
  39.6 2.0 %collective-permute-done.8.refs_5_ = f32[12,16,128]{2,1,0:T(8,128)S(1)} collective-permute-done((f32[12,16,128]{2,1,0:T(8,128)S(1)}, f32[12,16,128]{2,1,0:T(8,128)S(1)}, u32[]{:S(2)}, u32[]{:S(2)}) %collective-permute-start.8) | collective-permute-done | bytes 98336 | tf_op jit(solution)/shard_map/ppermute | solution.py:495
  41.6 2.0 %shard_map.65 = (f32[34,16,128]{2,1,0:T(8,128)S(1)}, f32[34,16,128]{2,1,0:T(8,128)S(1)}, f32[34,16,128]{2,1,0:T(8,128)S(1)}, bf16[34,32,128]{2,1,0:T(8,128)(2,1)...) custom-call(s32[8]{0:T(128)S(4)} %get-tuple-element.64.facts, ...), custom_call_target="tpu_custom_call", output_to_operand_aliasing={{0}: (4, {}), {1}: (5, {}), {2}: (6, {}), {3}: (7, {}), {4}... | custom-call | tf_op jit(solution)/shard_map/pallas_call | solution.py:484
  43.6 1.2 %collective-permute-start.9 = (f32[15,16,128]{2,1,0:T(8,128)S(1)}, f32[15,16,128]{2,1,0:T(8,128)S(1)}, u32[]{:S(2)}, u32[]{:S(2)}) collective-permute-start(f32[15,16,128]{2,1,0:T(8,128)S(1)} %get-tuple-element.115), channel_id=1, source_target_pairs={{0,1},{2,3},{7,6},{5,4},{8,9},{10,11},{15,14},{13,12},{16,17},{18,... | collective-permute-start | bytes 368648 | tf_op jit(solution)/shard_map/ppermute | solution.py:496
  44.8 2.1 %collective-permute-start.10 = (f32[9,16,128]{2,1,0:T(8,128)S(1)}, f32[9,16,128]{2,1,0:T(8,128)S(1)}, u32[]{:S(2)}, u32[]{:S(2)}) collective-permute-start(f32[9,16,128]{2,1,0:T(8,128)S(1)} %get-tuple-element.121), channel_id=1, source_target_pairs={{1,2},{3,7},{6,5},{4,8},{9,10},{11,15},{14,13},{12,16},{17,18},{19... | collective-permute-start | bytes 221192 | tf_op jit(solution)/shard_map/ppermute | solution.py:495
  46.9 0.0 collective-permute-done.9.refs_5_
  46.9 2.3 %shard_map.66 = (f32[34,16,128]{2,1,0:T(8,128)S(1)}, f32[34,16,128]{2,1,0:T(8,128)S(1)}, f32[34,16,128]{2,1,0:T(8,128)S(1)}, bf16[34,32,128]{2,1,0:T(8,128)(2,1)S(1)}, bf16[34,32,128]{2,1,0:T(8,128)(2,1)S(1)}) custom-call(s32[8]{0:T(128)S(4)} %get-tuple-element.64.facts, ...), custom_call_target="tpu_custom_call", output_to_operand_aliasing={{0}: (3, {}), {1}: (4, {}), {2}: (5, {}), {3}: (6, {}), {4}... | custom-call | tf_op jit(solution)/shard_map/pallas_call | solution.py:484
  49.2 1.3 %collective-permute-done.10.refs_5_ = f32[9,16,128]{2,1,0:T(8,128)S(1)} collective-permute-done((f32[9,16,128]{2,1,0:T(8,128)S(1)}, f32[9,16,128]{2,1,0:T(8,128)S(1)}, u32[]{:S(2)}, u32[]{:S(2)}) %collective-permute-start.10) | collective-permute-done | bytes 73760 | tf_op jit(solution)/shard_map/ppermute | solution.py:495
  50.5 1.7 %shard_map.67 = (f32[34,16,128]{2,1,0:T(8,128)S(1)}, f32[34,16,128]{2,1,0:T(8,128)S(1)}, f32[34,16,128]{2,1,0:T(8,128)S(1)}, bf16[34,32,128]{2,1,0:T(8,128)(2,1)...) custom-call(s32[8]{0:T(128)S(4)} %get-tuple-element.64.facts, ...), custom_call_target="tpu_custom_call", output_to_operand_aliasing={{0}: (4, {}), {1}: (5, {}), {2}: (6, {}), {3}: (7, {}), {4}... | custom-call | tf_op jit(solution)/shard_map/pallas_call | solution.py:484
  52.2 0.0 collective-permute-start.12
  52.2 1.6 %collective-permute-start.11 = (f32[16,16,128]{2,1,0:T(8,128)S(1)}, f32[16,16,128]{2,1,0:T(8,128)S(1)}, u32[]{:S(2)}, u32[]{:S(2)}) collective-permute-start(f32[16,16,128]{2,1,0:T(8,128)S(1)} %get-tuple-element.122.refs_0_), channel_id=1, source_target_pairs={{0,1},{1,0},{2,3},{3,2},{4,5},{5,4},{6,7},{7,6},{8,9},{9,8},{10,11... | collective-permute-start | bytes 393224 | tf_op jit(solution)/shard_map/ppermute | solution.py:395
  53.7 2.3 %collective-permute-done.12.refs_2_ = f32[16,16,128]{2,1,0:T(8,128)S(1)} collective-permute-done((f32[16,16,128]{2,1,0:T(8,128)S(1)}, f32[16,16,128]{2,1,0:T(8,128)S(1)}, u32[]{:S(2)}, u32[]{:S(2)}) %collective-permute-start.12) | collective-permute-done | bytes 131104 | tf_op jit(solution)/shard_map/ppermute | solution.py:391
  56.0 2.6 %collective-permute-start.13 = (f32[16,16,128]{2,1,0:T(8,128)S(1)}, f32[16,16,128]{2,1,0:T(8,128)S(1)}, u32[]{:S(2)}, u32[]{:S(2)}) collective-permute-start(f32[16,16,128]{2,1,0:T(8,128)S(1)} %collective-permute-done.12.refs_2_), channel_id=1, source_target_pairs={{0,1},{1,0},{2,3},{3,2},{4,5},{5,4},{6,7},{7,6},{8,9},{9,8},{10,11... | collective-permute-start | bytes 393224 | tf_op jit(solution)/shard_map/ppermute | solution.py:395
  58.6 0.0 collective-permute-done.11.refs_1_
  58.6 1.0 %collective-permute-done.13.refs_3_ = f32[16,16,128]{2,1,0:T(8,128)S(1)} collective-permute-done((f32[16,16,128]{2,1,0:T(8,128)S(1)}, f32[16,16,128]{2,1,0:T(8,128)S(1)}, u32[]{:S(2)}, u32[]{:S(2)}) %collective-permute-start.13) | collective-permute-done | bytes 131104 | tf_op jit(solution)/shard_map/ppermute | solution.py:395
  59.6 1.2 %shard_map.68 = f32[16,4096]{1,0:T(8,128)} custom-call(s32[8]{0:T(128)S(4)} %get-tuple-element.64.facts, f32[16,16,128]{2,1,0:T(8,128)S(1)} %get-tuple-element.122.refs_0_, f32[16,16,128]{2,1,0:T(8,128)S(1)} %collective-permute-done.11.refs_1_, f32[16,16,128]{2,1,0:T(8,128)S(1)} %collective-permute-done.12.refs_2_, ...), custom_call_target="tpu_custom_call" | custom-call | tf_op jit(solution)/shard_map/pallas_call | solution.py:528
  (1 shorter events, 0.0 us)
Async XLA Ops:
  1.1 2.3 %collective-permute-start = (f32[2,16,4096]{2,1,0:T(8,128)S(1)}, f32[2,16,4096]{2,1,0:T(8,128)S(1)}, u32[]{:S(2)}, u32[]{:S(2)}) collective-permute-start(f32[2,16,4096]{2,1,0:T(8,128)S(1)} %get-tuple-element.66.refs_0_), channel_id=1, source_target_pairs={{0,1},{1,0},{2,3},{3,2},{4,5},{5,4},{6,7},{7,6},{8,9},{9,8},{10,11... | collective-permute-start | bytes 1572872 | tf_op jit(solution)/shard_map/ppermute | solution.py:395
  4.5 17.0 %collective-permute-start.1 = (f32[1928,128]{1,0:T(8,128)S(1)}, f32[1928,128]{1,0:T(8,128)S(1)}, u32[]{:S(2)}, u32[]{:S(2)}) collective-permute-start(f32[1928,128]{1,0:T(8,128)S(1)} %get-tuple-element.70), channel_id=1, source_target_pairs={{3,7},{4,8},{11,15},{12,16},{19,23},{20,24},{27,31},{7,3},{8,4},{1... | collective-permute-start | bytes 2961416 | tf_op jit(solution)/shard_map/ppermute | solution.py:457
  5.3 9.4 %collective-permute-start.2 = (f32[2,16,16,128]{3,2,1,0:T(8,128)S(1)}, f32[2,16,16,128]{3,2,1,0:T(8,128)S(1)}, u32[]{:S(2)}, u32[]{:S(2)}) collective-permute-start(f32[2,16,16,128]{3,2,1,0:T(8,128)S(1)} %get-tuple-element.71), channel_id=1, source_target_pairs={{2,0},{3,1},{0,2},{1,3},{6,4},{7,5},{4,6},{5,7},{10,8},{11,9},{8,1... | collective-permute-start | bytes 786440 | tf_op jit(solution)/shard_map/ppermute | solution.py:391
  14.9 4.3 %collective-permute-start.3 = (f32[15,16,128]{2,1,0:T(8,128)S(1)}, f32[15,16,128]{2,1,0:T(8,128)S(1)}, u32[]{:S(2)}, u32[]{:S(2)}) collective-permute-start(f32[15,16,128]{2,1,0:T(8,128)S(1)} %get-tuple-element.77), channel_id=1, source_target_pairs={{0,1},{2,3},{7,6},{5,4},{8,9},{10,11},{15,14},{13,12},{16,17},{18,... | collective-permute-start | bytes 368648 | tf_op jit(solution)/shard_map/ppermute | solution.py:496
  16.6 6.2 %collective-permute-start.4 = (f32[12,16,128]{2,1,0:T(8,128)S(1)}, f32[12,16,128]{2,1,0:T(8,128)S(1)}, u32[]{:S(2)}, u32[]{:S(2)}) collective-permute-start(f32[12,16,128]{2,1,0:T(8,128)S(1)} %get-tuple-element.85), channel_id=1, source_target_pairs={{1,2},{3,7},{6,5},{4,8},{9,10},{11,15},{14,13},{12,16},{17,18},{19... | collective-permute-start | bytes 294920 | tf_op jit(solution)/shard_map/ppermute | solution.py:495
  24.8 3.1 %collective-permute-start.5 = (f32[15,16,128]{2,1,0:T(8,128)S(1)}, f32[15,16,128]{2,1,0:T(8,128)S(1)}, u32[]{:S(2)}, u32[]{:S(2)}) collective-permute-start(f32[15,16,128]{2,1,0:T(8,128)S(1)} %get-tuple-element.91), channel_id=1, source_target_pairs={{0,1},{2,3},{7,6},{5,4},{8,9},{10,11},{15,14},{13,12},{16,17},{18,... | collective-permute-start | bytes 368648 | tf_op jit(solution)/shard_map/ppermute | solution.py:496
  26.0 6.2 %collective-permute-start.6 = (f32[12,16,128]{2,1,0:T(8,128)S(1)}, f32[12,16,128]{2,1,0:T(8,128)S(1)}, u32[]{:S(2)}, u32[]{:S(2)}) collective-permute-start(f32[12,16,128]{2,1,0:T(8,128)S(1)} %get-tuple-element.97), channel_id=1, source_target_pairs={{1,2},{3,7},{6,5},{4,8},{9,10},{11,15},{14,13},{12,16},{17,18},{19... | collective-permute-start | bytes 294920 | tf_op jit(solution)/shard_map/ppermute | solution.py:495
  34.2 3.1 %collective-permute-start.7 = (f32[15,16,128]{2,1,0:T(8,128)S(1)}, f32[15,16,128]{2,1,0:T(8,128)S(1)}, u32[]{:S(2)}, u32[]{:S(2)}) collective-permute-start(f32[15,16,128]{2,1,0:T(8,128)S(1)} %get-tuple-element.103), channel_id=1, source_target_pairs={{0,1},{2,3},{7,6},{5,4},{8,9},{10,11},{15,14},{13,12},{16,17},{18,... | collective-permute-start | bytes 368648 | tf_op jit(solution)/shard_map/ppermute | solution.py:496
  35.4 6.2 %collective-permute-start.8 = (f32[12,16,128]{2,1,0:T(8,128)S(1)}, f32[12,16,128]{2,1,0:T(8,128)S(1)}, u32[]{:S(2)}, u32[]{:S(2)}) collective-permute-start(f32[12,16,128]{2,1,0:T(8,128)S(1)} %get-tuple-element.109), channel_id=1, source_target_pairs={{1,2},{3,7},{6,5},{4,8},{9,10},{11,15},{14,13},{12,16},{17,18},{19... | collective-permute-start | bytes 294920 | tf_op jit(solution)/shard_map/ppermute | solution.py:495
  43.6 3.3 %collective-permute-start.9 = (f32[15,16,128]{2,1,0:T(8,128)S(1)}, f32[15,16,128]{2,1,0:T(8,128)S(1)}, u32[]{:S(2)}, u32[]{:S(2)}) collective-permute-start(f32[15,16,128]{2,1,0:T(8,128)S(1)} %get-tuple-element.115), channel_id=1, source_target_pairs={{0,1},{2,3},{7,6},{5,4},{8,9},{10,11},{15,14},{13,12},{16,17},{18,... | collective-permute-start | bytes 368648 | tf_op jit(solution)/shard_map/ppermute | solution.py:496
  44.8 5.7 %collective-permute-start.10 = (f32[9,16,128]{2,1,0:T(8,128)S(1)}, f32[9,16,128]{2,1,0:T(8,128)S(1)}, u32[]{:S(2)}, u32[]{:S(2)}) collective-permute-start(f32[9,16,128]{2,1,0:T(8,128)S(1)} %get-tuple-element.121), channel_id=1, source_target_pairs={{1,2},{3,7},{6,5},{4,8},{9,10},{11,15},{14,13},{12,16},{17,18},{19... | collective-permute-start | bytes 221192 | tf_op jit(solution)/shard_map/ppermute | solution.py:495
  52.2 3.8 %collective-permute-start.12 = (f32[16,16,128]{2,1,0:T(8,128)S(1)}, f32[16,16,128]{2,1,0:T(8,128)S(1)}, u32[]{:S(2)}, u32[]{:S(2)}) collective-permute-start(f32[16,16,128]{2,1,0:T(8,128)S(1)} %get-tuple-element.122.refs_0_), channel_id=1, source_target_pairs={{2,0},{3,1},{0,2},{1,3},{6,4},{7,5},{4,6},{5,7},{10,8},{11,9},{8,1... | collective-permute-start | bytes 393224 | tf_op jit(solution)/shard_map/ppermute | solution.py:391
  52.2 6.5 %collective-permute-start.11 = (f32[16,16,128]{2,1,0:T(8,128)S(1)}, f32[16,16,128]{2,1,0:T(8,128)S(1)}, u32[]{:S(2)}, u32[]{:S(2)}) collective-permute-start(f32[16,16,128]{2,1,0:T(8,128)S(1)} %get-tuple-element.122.refs_0_), channel_id=1, source_target_pairs={{0,1},{1,0},{2,3},{3,2},{4,5},{5,4},{6,7},{7,6},{8,9},{9,8},{10,11... | collective-permute-start | bytes 393224 | tf_op jit(solution)/shard_map/ppermute | solution.py:395
  56.0 3.6 %collective-permute-start.13 = (f32[16,16,128]{2,1,0:T(8,128)S(1)}, f32[16,16,128]{2,1,0:T(8,128)S(1)}, u32[]{:S(2)}, u32[]{:S(2)}) collective-permute-start(f32[16,16,128]{2,1,0:T(8,128)S(1)} %collective-permute-done.12.refs_2_), channel_id=1, source_target_pairs={{0,1},{1,0},{2,3},{3,2},{4,5},{5,4},{6,7},{7,6},{8,9},{9,8},{10,11... | collective-permute-start | bytes 393224 | tf_op jit(solution)/shard_map/ppermute | solution.py:395

commit v11 on v10

--- a/solution.py
+++ b/solution.py
@@ -55,21 +55,27 @@
     return jnp.where(lane < 128 - shift, first, second)
 
 
+def choose(even, left, right):
+    if isinstance(even, bool):
+        return left if even else right
+    return jnp.where(even, left, right)
+
+
 def put_near(ob, steps, even, u, r, pay):
     h = HB * steps
     inner = h - HB
-    pay[:h] = u[pl.ds(jnp.where(even, ob, h), h)]
+    pay[:h] = u[pl.ds(choose(even, ob, h), h)]
     if inner:
-        pay[h:] = r[pl.ds(jnp.where(even, h + ob - inner, h), inner)]
+        pay[h:] = r[pl.ds(choose(even, h + ob - inner, h), inner)]
 
 
 def take_near(ob, steps, even, got, u, r, now):
     h = HB * steps
     inner = h - HB
-    at = jnp.where(even, h + ob, 0)
+    at = choose(even, h + ob, 0)
     u[pl.ds(at, h)] = got[:h]
     if inner:
-        r[pl.ds(jnp.where(even, h + ob, HB), inner)] = got[h:]
+        r[pl.ds(choose(even, h + ob, HB), inner)] = got[h:]
     high, low = split(got[:h])
     now[pl.ds(at, h), :16] = high
     now[pl.ds(at, h), 16:] = low
@@ -81,29 +87,29 @@
 
 def put_far(ob, steps, even, u, r, pay):
     h = HB * steps
-    pay[: 2 * HB] = u[pl.ds(jnp.where(even, h, h + ob - 2 * HB), 2 * HB)]
+    pay[: 2 * HB] = u[pl.ds(choose(even, h, h + ob - 2 * HB), 2 * HB)]
     if pay.shape[0] - sent_blocks(steps) > 2 * HB:
-        pay[2 * HB : 3 * HB] = r[pl.ds(jnp.where(even, h, h + ob - HB), HB)]
+        pay[2 * HB : 3 * HB] = r[pl.ds(choose(even, h, h + ob - HB), HB)]
 
 
 def put_far_ahead(ob, steps, even, u, pay):
     h, n = HB * steps, sent_blocks(steps)
-    pay[pay.shape[0] - n :] = u[pl.ds(jnp.where(even, h + HB, h + ob - HB - n), n)]
+    pay[pay.shape[0] - n :] = u[pl.ds(choose(even, h + HB, h + ob - HB - n), n)]
 
 
 def take_far(ob, steps, even, got, u, r, now, later):
     h, n = HB * steps, sent_blocks(steps)
     high, low = split(got[: 2 * HB])
-    at = jnp.where(even, h - 2 * HB, h + ob)
+    at = choose(even, h - 2 * HB, h + ob)
     now[pl.ds(at, 2 * HB), :16] = high
     now[pl.ds(at, 2 * HB), 16:] = low
-    at = jnp.where(even, h - HB, h + ob)
-    nearest = got[pl.ds(jnp.where(even, HB, 0), HB)]
+    at = choose(even, h - HB, h + ob)
+    nearest = got[pl.ds(choose(even, HB, 0), HB)]
     u[pl.ds(at, HB)] = nearest
     r[pl.ds(at, HB)] = got[2 * HB : 3 * HB] if got.shape[0] - n > 2 * HB else nearest * THETA
     if n:
         ahead = got[got.shape[0] - n :]
-        at = jnp.where(even, h - HB - n, h + ob + HB)
+        at = choose(even, h - HB - n, h + ob + HB)
         u[pl.ds(at, n)] = ahead
         r[pl.ds(at, n)] = ahead * THETA
         high, low = split(ahead)
@@ -277,7 +283,18 @@
     def row(n, carry):
         e = starts + n
         a = e - HB
-        left = jnp.concatenate([now[e + offset(a, k)] for k in range(width)], axis=1)
+        if isinstance(starts, int):
+            near = [now[e + j] for j in range(-HB, HB + 1)]
+            parts = []
+            for k in range(width):
+                place = offset(a, k)
+                part = near[0]
+                for j in range(1, 2 * HB + 1):
+                    part = jnp.where(place == j - HB, near[j], part)
+                parts.append(part)
+            left = jnp.concatenate(parts, axis=1)
+        else:
+            left = jnp.concatenate([now[e + offset(a, k)] for k in range(width)], axis=1)
         product = jnp.dot(left, operator[a], preferred_element_type=F32)
         product = product[:16] + product[16:]
         resid = r[e] - (product[:, :128] + product[:, 128:])
@@ -293,7 +310,11 @@
             later[e, 16:] = low
         return carry
 
-    lax.fori_loop(0, count, row, 0, unroll=True)
+    if isinstance(starts, int):
+        for n in range(count):
+            row(n, 0)
+    else:
+        lax.fori_loop(0, count, row, 0, unroll=True)
 
 
 def look_up(offsets, width):
@@ -302,7 +323,7 @@
 
 def ahead(ob, steps, even, first, pair, offset, operator, x, u, r, pieces):
     h, n = HB * steps, sent_blocks(steps)
-    starts = jnp.where(even, h + HB, h + ob - HB - n)
+    starts = choose(even, h + HB, h + ob - HB - n)
     apply_rows(0, steps, starts, n, first, False, pair, offset, operator, x, u, r, pieces)
 
 
@@ -317,12 +338,16 @@
     high, low = split(total[0])
     pieces[0][h : h + ob, :16] = high
     pieces[0][h : h + ob, 16:] = low
-    even = facts[1] == 0
-    put_near(ob, steps, even, u, r, pay_a)
-    put_far(ob, steps, even, u, r, pay_b)
-    if sent_blocks(steps):
-        ahead(ob, steps, even, True, pair, look_up(offsets, operator.shape[1] // 128), operator, x, u, r, pieces)
-        put_far_ahead(ob, steps, even, u, pay_b)
+    for left in (True, False):
+
+        @pl.when((facts[1] == 0) == left)
+        def _():
+            put_near(ob, steps, left, u, r, pay_a)
+            put_far(ob, steps, left, u, r, pay_b)
+            if sent_blocks(steps):
+                offset = look_up(offsets, operator.shape[1] // 128)
+                ahead(ob, steps, left, True, pair, offset, operator, x, u, r, pieces)
+                put_far_ahead(ob, steps, left, u, pay_b)
 
 
 def inner_kernel(ob, folds, steps, first, last, pairs, facts, offsets, operator, *refs):
@@ -331,11 +356,15 @@
     even = facts[1] == 0
     offset = look_up(offsets, operator.shape[1] // 128)
     take_near(ob, steps, even, got_a, u, r, pieces[0])
-    for t in range(steps):
-        done = HB + (HB * t if t else sent_blocks(steps))
-        starts = jnp.where(even, h + done, HB + HB * t)
-        count = ob + h - HB - HB * t - done
-        apply_rows(t, steps, starts, count, first, last, pairs[t], offset, operator, x, u, r, pieces)
+    for left in (True, False):
+
+        @pl.when(even == left)
+        def _():
+            for t in range(steps):
+                done = HB + (HB * t if t else sent_blocks(steps))
+                starts = h + done if left else HB + HB * t
+                count = ob + h - HB - HB * t - done
+                apply_rows(t, steps, starts, count, first, last, pairs[t], offset, operator, x, u, r, pieces)
 
 
 def outer_kernel(ob, folds, steps, first, last, pairs, facts, offsets, lent, operator, *refs):
@@ -349,23 +378,28 @@
     take_far(ob, steps, even, got_b, u, r, *pieces)
 
     def offset(a, k):
-        i = a - jnp.where(even, inner - lend, inner + ob)
-        outside = edge & (i >= 0) & (i < lend)
-        return jnp.where(outside, lent[jnp.clip(i, 0, lend - 1) * width + k], offsets[a * width + k])
-
-    for t in range(steps):
-        count = h if t else 2 * HB
-        starts = jnp.where(even, HB + HB * t + h - count if not t else HB + HB * t, h + ob - HB - HB * t)
-        apply_rows(t, steps, starts, count, first, last, pairs[t], offset, operator, x, u, r, pieces)
-    if last:
-        outs[0][...] = x[h : h + ob]
-        return
-    put_near(ob, steps, even, u, r, outs[0])
-    put_far(ob, steps, even, u, r, outs[1])
-    if sent_blocks(steps):
-        pieces = pieces[::-1] if steps % 2 else pieces
-        ahead(ob, steps, even, False, pairs[steps], look_up(offsets, width), operator, x, u, r, pieces)
-        put_far_ahead(ob, steps, even, u, outs[1])
+        i = a - choose(left, inner - lend, inner + ob)
+        if not 0 <= i < lend:
+            return offsets[a * width + k]
+        return jnp.where(edge, lent[i * width + k], offsets[a * width + k])
+
+    for left in (True, False):
+
+        @pl.when(even == left)
+        def _():
+            for t in range(steps):
+                count = h if t else 2 * HB
+                starts = (HB + HB * t if t else h - HB) if left else h + ob - HB - HB * t
+                apply_rows(t, steps, starts, count, first, last, pairs[t], offset, operator, x, u, r, pieces)
+            if last:
+                outs[0][...] = x[h : h + ob]
+                return
+            put_near(ob, steps, left, u, r, outs[0])
+            put_far(ob, steps, left, u, r, outs[1])
+            if sent_blocks(steps):
+                turned = pieces[::-1] if steps % 2 else pieces
+                ahead(ob, steps, left, False, pairs[steps], look_up(offsets, width), operator, x, u, r, turned)
+                put_far_ahead(ob, steps, left, u, outs[1])
 
 
 def finish_kernel(ob, keys, facts, *refs):

time: 61 us -> 60 us (0.984)
  Pallas kernels: 25.3 us -> 23.2 us
    pallas_call x8, Pallas kernels: 16.8 us -> 14.6 us  [part_of_phase(): pl.pallas_call(functools.partial(kernel, ob, folds, steps, done == 0, don...]
    ppermute x4, waiting for transfers between devices: 6.52 us -> 7.29 us  [on_device(): got_b = lax.ppermute(pay_b, AXES, swap_b)]
where the time goes in v11:
time: 60 us; the launch traced here: 59.8 us
  starting transfers between devices  23.6 us (39%)
  Pallas kernels  23.2 us (39%)
  waiting for transfers between devices  12.8 us (21%)
    pallas_call x8, Pallas kernels, part_of_phase(): pl.pallas_call(functools.partial(kernel, ob, folds, steps, done == 0, don...  14.6 us
    ppermute x4, starting transfers between devices, on_device(): got_b = lax.ppermute(pay_b, AXES, swap_b)  8.29 us
    ppermute x4, waiting for transfers between devices, on_device(): got_b = lax.ppermute(pay_b, AXES, swap_b)  7.29 us
    ppermute x4, starting transfers between devices, on_device(): got_a = lax.ppermute(pay_a, AXES, swap_a)  5.76 us
    ppermute x3, starting transfers between devices, other_core(): return lax.ppermute(array, 'fold', [(i, i ^ 1) for i in range(folds)])  5.09 us
    pallas_call x1, Pallas kernels, on_device(): pl.pallas_call(functools.partial(prepare_kernel, ob, halo, lend, width),...  4.79 us
    ppermute x2, starting transfers between devices, over_chips(): lax.ppermute(array, 'fold', [((i + 2 * d) % folds, i) for i in range(fold...  3.74 us
    ppermute x2, waiting for transfers between devices, over_chips(): lax.ppermute(array, 'fold', [((i + 2 * d) % folds, i) for i in range(fold...  3.02 us
  transfers between devices with their start and end apart: 14, of which 8 were waited for; matrix products, arithmetic and copies ran while one was open for 0% of the time, Pallas kernels for 23%

profile of v11, /device:TPU:9, one launch (start us, length us, event | category | flops | bytes accessed | tf_op | source)
XLA Modules:
  0.0 59.8 jit_solution(11933719713926273344)
XLA Ops:
  0.0 1.1 %shard_map.55 = (s32[8]{0:T(128)S(4)}, s32[5,64]{1,0:T(8,128)S(4)}, f32[2,16,4096]{2,1,0:T(8,128)S(1)}) custom-call(s32[1,4]{1,0:T(1,128)} %counts.1, s32[5,64]{1,0:T(8,128)} %bitcast.4, f32[16,4096]{1,0:T(8,128)} %initial.1, f32[16,4096]{1,0:T(8,128)} %right_side.1), custom_call_target="tpu_custom_call" | custom-call | tf_op jit(solution)/shard_map/pallas_call | solution.py:466
  1.1 0.7 %collective-permute-start = (f32[2,16,4096]{2,1,0:T(8,128)S(1)}, f32[2,16,4096]{2,1,0:T(8,128)S(1)}, u32[]{:S(2)}, u32[]{:S(2)}) collective-permute-start(f32[2,16,4096]{2,1,0:T(8,128)S(1)} %get-tuple-element.66.refs_0_), channel_id=1, source_target_pairs={{0,1},{1,0},{2,3},{3,2},{4,5},{5,4},{6,7},{7,6},{8,9},{9,8},{10,11... | collective-permute-start | bytes 1572872 | tf_op jit(solution)/shard_map/ppermute | solution.py:429
  1.8 1.5 %collective-permute-done.refs_1_ = f32[2,16,4096]{2,1,0:T(8,128)S(1)} collective-permute-done((f32[2,16,4096]{2,1,0:T(8,128)S(1)}, f32[2,16,4096]{2,1,0:T(8,128)S(1)}, u32[]{:S(2)}, u32[]{:S(2)}) %collective-permute-start) | collective-permute-done | bytes 524320 | tf_op jit(solution)/shard_map/ppermute | solution.py:429
  3.3 1.2 %shard_map.56 = (f32[2,16,16,128]{3,2,1,0:T(8,128)S(1)}, f32[2,16,16,128]{3,2,1,0:T(8,128)S(1)}, f32[1928,128]{1,0:T(8,128)S(1)}) custom-call(s32[8]{0:T(128)S(4)} %get-tuple-element.64.facts, s32[5,64]{1,0:T(8,128)S(4)} %get-tuple-element.65.indices.columns, f32[40960,128]{1,0:T(8,128)} %bitcast.2, f32[2,16,4096]{2,1,0:T(8,128)S(1)} %get-tuple-element.66.refs_0_, ...), custom_call_target="tpu_custom_call" | custom-call | tf_op jit(solution)/shard_map/pallas_call | solution.py:482
  4.5 0.7 %collective-permute-start.1 = (f32[1928,128]{1,0:T(8,128)S(1)}, f32[1928,128]{1,0:T(8,128)S(1)}, u32[]{:S(2)}, u32[]{:S(2)}) collective-permute-start(f32[1928,128]{1,0:T(8,128)S(1)} %get-tuple-element.70), channel_id=1, source_target_pairs={{3,7},{4,8},{11,15},{12,16},{19,23},{20,24},{27,31},{7,3},{8,4},{1... | collective-permute-start | bytes 2961416 | tf_op jit(solution)/shard_map/ppermute | solution.py:491
  5.3 3.7 %collective-permute-start.2 = (f32[2,16,16,128]{3,2,1,0:T(8,128)S(1)}, f32[2,16,16,128]{3,2,1,0:T(8,128)S(1)}, u32[]{:S(2)}, u32[]{:S(2)}) collective-permute-start(f32[2,16,16,128]{3,2,1,0:T(8,128)S(1)} %get-tuple-element.71), channel_id=1, source_target_pairs={{2,0},{3,1},{0,2},{1,3},{6,4},{7,5},{4,6},{5,7},{10,8},{11,9},{8,1... | collective-permute-start | bytes 786440 | tf_op jit(solution)/shard_map/ppermute | solution.py:425
  9.0 4.8 %shard_map.57 = (bf16[28,640,256]{2,1,0:T(8,128)(2,1)S(1)}, s32[140]{0:T(256)S(4)}) custom-call(s32[8]{0:T(128)S(4)} %get-tuple-element.64.facts, s32[5,64]{1,0:T(8,128)S(4)} %get-tuple-element.65.indices.columns, f32[40960,128]{1,0:T(8,128)} %bitcast.3, f32[2,16,16,128]{3,2,1,0:T(8,128)S(1)} %get-tuple-element.67.token.refs_0_), custom_call_target="tpu_custom_call" | custom-call | flops 10000000 | bytes 18350080 | tf_op jit(solution)/shard_map/pallas_call | solution.py:494
  13.8 0.8 %collective-permute-done.2.refs_1_ = f32[2,16,16,128]{3,2,1,0:T(8,128)S(1)} collective-permute-done((f32[2,16,16,128]{3,2,1,0:T(8,128)S(1)}, f32[2,16,16,128]{3,2,1,0:T(8,128)S(1)}, u32[]{:S(2)}, u32[]{:S(2)}) %collective-permute-start.2) | collective-permute-done | bytes 262176 | tf_op jit(solution)/shard_map/ppermute | solution.py:425
  14.6 0.3 shard_map.58
  15.0 1.7 %collective-permute-start.3 = (f32[15,16,128]{2,1,0:T(8,128)S(1)}, f32[15,16,128]{2,1,0:T(8,128)S(1)}, u32[]{:S(2)}, u32[]{:S(2)}) collective-permute-start(f32[15,16,128]{2,1,0:T(8,128)S(1)} %get-tuple-element.77), channel_id=1, source_target_pairs={{0,1},{2,3},{7,6},{5,4},{8,9},{10,11},{15,14},{13,12},{16,17},{18,... | collective-permute-start | bytes 368648 | tf_op jit(solution)/shard_map/ppermute | solution.py:530
  16.7 2.6 %collective-permute-start.4 = (f32[12,16,128]{2,1,0:T(8,128)S(1)}, f32[12,16,128]{2,1,0:T(8,128)S(1)}, u32[]{:S(2)}, u32[]{:S(2)}) collective-permute-start(f32[12,16,128]{2,1,0:T(8,128)S(1)} %get-tuple-element.85), channel_id=1, source_target_pairs={{1,2},{3,7},{6,5},{4,8},{9,10},{11,15},{14,13},{12,16},{17,18},{19... | collective-permute-start | bytes 294920 | tf_op jit(solution)/shard_map/ppermute | solution.py:529
  19.2 0.0 collective-permute-done.3.refs_5_
  19.3 2.1 %shard_map.59 = (f32[34,16,128]{2,1,0:T(8,128)S(1)}, f32[34,16,128]{2,1,0:T(8,128)S(1)}, f32[34,16,128]{2,1,0:T(8,128)S(1)}, bf16[34,32,128]{2,1,0:T(8,128)(2,1)S(1)}, bf16[34,32,128]{2,1,0:T(8,128)(2,1)S(1)}) custom-call(s32[8]{0:T(128)S(4)} %get-tuple-element.64.facts, ...), custom_call_target="tpu_custom_call", output_to_operand_aliasing={{0}: (3, {}), {1}: (4, {}), {2}: (5, {}), {3}: (6, {}), {4}... | custom-call | tf_op jit(solution)/shard_map/pallas_call | solution.py:518
  21.3 0.0 collective-permute-done.1.raw
  21.3 1.5 %collective-permute-done.4.refs_5_ = f32[12,16,128]{2,1,0:T(8,128)S(1)} collective-permute-done((f32[12,16,128]{2,1,0:T(8,128)S(1)}, f32[12,16,128]{2,1,0:T(8,128)S(1)}, u32[]{:S(2)}, u32[]{:S(2)}) %collective-permute-start.4) | collective-permute-done | bytes 98336 | tf_op jit(solution)/shard_map/ppermute | solution.py:529
  22.9 1.6 %shard_map.61 = (f32[34,16,128]{2,1,0:T(8,128)S(1)}, f32[34,16,128]{2,1,0:T(8,128)S(1)}, f32[34,16,128]{2,1,0:T(8,128)S(1)}, bf16[34,32,128]{2,1,0:T(8,128)(2,1)...) custom-call(s32[8]{0:T(128)S(4)} %get-tuple-element.64.facts, ...), custom_call_target="tpu_custom_call", output_to_operand_aliasing={{0}: (4, {}), {1}: (5, {}), {2}: (6, {}), {3}: (7, {}), {4}... | custom-call | tf_op jit(solution)/shard_map/pallas_call | solution.py:518
  24.4 1.3 %collective-permute-start.5 = (f32[15,16,128]{2,1,0:T(8,128)S(1)}, f32[15,16,128]{2,1,0:T(8,128)S(1)}, u32[]{:S(2)}, u32[]{:S(2)}) collective-permute-start(f32[15,16,128]{2,1,0:T(8,128)S(1)} %get-tuple-element.91), channel_id=1, source_target_pairs={{0,1},{2,3},{7,6},{5,4},{8,9},{10,11},{15,14},{13,12},{16,17},{18,... | collective-permute-start | bytes 368648 | tf_op jit(solution)/shard_map/ppermute | solution.py:530
  25.8 1.9 %collective-permute-start.6 = (f32[12,16,128]{2,1,0:T(8,128)S(1)}, f32[12,16,128]{2,1,0:T(8,128)S(1)}, u32[]{:S(2)}, u32[]{:S(2)}) collective-permute-start(f32[12,16,128]{2,1,0:T(8,128)S(1)} %get-tuple-element.97), channel_id=1, source_target_pairs={{1,2},{3,7},{6,5},{4,8},{9,10},{11,15},{14,13},{12,16},{17,18},{19... | collective-permute-start | bytes 294920 | tf_op jit(solution)/shard_map/ppermute | solution.py:529
  27.7 0.0 collective-permute-done.5.refs_5_
  27.7 2.2 %shard_map.62 = (f32[34,16,128]{2,1,0:T(8,128)S(1)}, f32[34,16,128]{2,1,0:T(8,128)S(1)}, f32[34,16,128]{2,1,0:T(8,128)S(1)}, bf16[34,32,128]{2,1,0:T(8,128)(2,1)S(1)}, bf16[34,32,128]{2,1,0:T(8,128)(2,1)S(1)}) custom-call(s32[8]{0:T(128)S(4)} %get-tuple-element.64.facts, ...), custom_call_target="tpu_custom_call", output_to_operand_aliasing={{0}: (3, {}), {1}: (4, {}), {2}: (5, {}), {3}: (6, {}), {4}... | custom-call | tf_op jit(solution)/shard_map/pallas_call | solution.py:518
  29.9 2.1 %collective-permute-done.6.refs_5_ = f32[12,16,128]{2,1,0:T(8,128)S(1)} collective-permute-done((f32[12,16,128]{2,1,0:T(8,128)S(1)}, f32[12,16,128]{2,1,0:T(8,128)S(1)}, u32[]{:S(2)}, u32[]{:S(2)}) %collective-permute-start.6) | collective-permute-done | bytes 98336 | tf_op jit(solution)/shard_map/ppermute | solution.py:529
  32.0 1.5 %shard_map.63 = (f32[34,16,128]{2,1,0:T(8,128)S(1)}, f32[34,16,128]{2,1,0:T(8,128)S(1)}, f32[34,16,128]{2,1,0:T(8,128)S(1)}, bf16[34,32,128]{2,1,0:T(8,128)(2,1)...) custom-call(s32[8]{0:T(128)S(4)} %get-tuple-element.64.facts, ...), custom_call_target="tpu_custom_call", output_to_operand_aliasing={{0}: (4, {}), {1}: (5, {}), {2}: (6, {}), {3}: (7, {}), {4}... | custom-call | tf_op jit(solution)/shard_map/pallas_call | solution.py:518
  33.6 1.4 %collective-permute-start.7 = (f32[15,16,128]{2,1,0:T(8,128)S(1)}, f32[15,16,128]{2,1,0:T(8,128)S(1)}, u32[]{:S(2)}, u32[]{:S(2)}) collective-permute-start(f32[15,16,128]{2,1,0:T(8,128)S(1)} %get-tuple-element.103), channel_id=1, source_target_pairs={{0,1},{2,3},{7,6},{5,4},{8,9},{10,11},{15,14},{13,12},{16,17},{18,... | collective-permute-start | bytes 368648 | tf_op jit(solution)/shard_map/ppermute | solution.py:530
  34.9 1.9 %collective-permute-start.8 = (f32[12,16,128]{2,1,0:T(8,128)S(1)}, f32[12,16,128]{2,1,0:T(8,128)S(1)}, u32[]{:S(2)}, u32[]{:S(2)}) collective-permute-start(f32[12,16,128]{2,1,0:T(8,128)S(1)} %get-tuple-element.109), channel_id=1, source_target_pairs={{1,2},{3,7},{6,5},{4,8},{9,10},{11,15},{14,13},{12,16},{17,18},{19... | collective-permute-start | bytes 294920 | tf_op jit(solution)/shard_map/ppermute | solution.py:529
  36.8 0.0 collective-permute-done.7.refs_5_
  36.8 2.1 %shard_map.64 = (f32[34,16,128]{2,1,0:T(8,128)S(1)}, f32[34,16,128]{2,1,0:T(8,128)S(1)}, f32[34,16,128]{2,1,0:T(8,128)S(1)}, bf16[34,32,128]{2,1,0:T(8,128)(2,1)S(1)}, bf16[34,32,128]{2,1,0:T(8,128)(2,1)S(1)}) custom-call(s32[8]{0:T(128)S(4)} %get-tuple-element.64.facts, ...), custom_call_target="tpu_custom_call", output_to_operand_aliasing={{0}: (3, {}), {1}: (4, {}), {2}: (5, {}), {3}: (6, {}), {4}... | custom-call | tf_op jit(solution)/shard_map/pallas_call | solution.py:518
  38.9 2.2 %collective-permute-done.8.refs_5_ = f32[12,16,128]{2,1,0:T(8,128)S(1)} collective-permute-done((f32[12,16,128]{2,1,0:T(8,128)S(1)}, f32[12,16,128]{2,1,0:T(8,128)S(1)}, u32[]{:S(2)}, u32[]{:S(2)}) %collective-permute-start.8) | collective-permute-done | bytes 98336 | tf_op jit(solution)/shard_map/ppermute | solution.py:529
  41.1 1.5 %shard_map.65 = (f32[34,16,128]{2,1,0:T(8,128)S(1)}, f32[34,16,128]{2,1,0:T(8,128)S(1)}, f32[34,16,128]{2,1,0:T(8,128)S(1)}, bf16[34,32,128]{2,1,0:T(8,128)(2,1)...) custom-call(s32[8]{0:T(128)S(4)} %get-tuple-element.64.facts, ...), custom_call_target="tpu_custom_call", output_to_operand_aliasing={{0}: (4, {}), {1}: (5, {}), {2}: (6, {}), {3}: (7, {}), {4}... | custom-call | tf_op jit(solution)/shard_map/pallas_call | solution.py:518
  42.6 1.4 %collective-permute-start.9 = (f32[15,16,128]{2,1,0:T(8,128)S(1)}, f32[15,16,128]{2,1,0:T(8,128)S(1)}, u32[]{:S(2)}, u32[]{:S(2)}) collective-permute-start(f32[15,16,128]{2,1,0:T(8,128)S(1)} %get-tuple-element.115), channel_id=1, source_target_pairs={{0,1},{2,3},{7,6},{5,4},{8,9},{10,11},{15,14},{13,12},{16,17},{18,... | collective-permute-start | bytes 368648 | tf_op jit(solution)/shard_map/ppermute | solution.py:530
  44.0 1.9 %collective-permute-start.10 = (f32[9,16,128]{2,1,0:T(8,128)S(1)}, f32[9,16,128]{2,1,0:T(8,128)S(1)}, u32[]{:S(2)}, u32[]{:S(2)}) collective-permute-start(f32[9,16,128]{2,1,0:T(8,128)S(1)} %get-tuple-element.121), channel_id=1, source_target_pairs={{1,2},{3,7},{6,5},{4,8},{9,10},{11,15},{14,13},{12,16},{17,18},{19... | collective-permute-start | bytes 221192 | tf_op jit(solution)/shard_map/ppermute | solution.py:529
  45.9 0.0 collective-permute-done.9.refs_5_
  45.9 2.3 %shard_map.66 = (f32[34,16,128]{2,1,0:T(8,128)S(1)}, f32[34,16,128]{2,1,0:T(8,128)S(1)}, f32[34,16,128]{2,1,0:T(8,128)S(1)}, bf16[34,32,128]{2,1,0:T(8,128)(2,1)S(1)}, bf16[34,32,128]{2,1,0:T(8,128)(2,1)S(1)}) custom-call(s32[8]{0:T(128)S(4)} %get-tuple-element.64.facts, ...), custom_call_target="tpu_custom_call", output_to_operand_aliasing={{0}: (3, {}), {1}: (4, {}), {2}: (5, {}), {3}: (6, {}), {4}... | custom-call | tf_op jit(solution)/shard_map/pallas_call | solution.py:518
  48.2 1.5 %collective-permute-done.10.refs_5_ = f32[9,16,128]{2,1,0:T(8,128)S(1)} collective-permute-done((f32[9,16,128]{2,1,0:T(8,128)S(1)}, f32[9,16,128]{2,1,0:T(8,128)S(1)}, u32[]{:S(2)}, u32[]{:S(2)}) %collective-permute-start.10) | collective-permute-done | bytes 73760 | tf_op jit(solution)/shard_map/ppermute | solution.py:529
  49.7 1.4 %shard_map.67 = (f32[34,16,128]{2,1,0:T(8,128)S(1)}, f32[34,16,128]{2,1,0:T(8,128)S(1)}, f32[34,16,128]{2,1,0:T(8,128)S(1)}, bf16[34,32,128]{2,1,0:T(8,128)(2,1)...) custom-call(s32[8]{0:T(128)S(4)} %get-tuple-element.64.facts, ...), custom_call_target="tpu_custom_call", output_to_operand_aliasing={{0}: (4, {}), {1}: (5, {}), {2}: (6, {}), {3}: (7, {}), {4}... | custom-call | tf_op jit(solution)/shard_map/pallas_call | solution.py:518
  51.1 0.0 collective-permute-start.12
  51.1 1.6 %collective-permute-start.11 = (f32[16,16,128]{2,1,0:T(8,128)S(1)}, f32[16,16,128]{2,1,0:T(8,128)S(1)}, u32[]{:S(2)}, u32[]{:S(2)}) collective-permute-start(f32[16,16,128]{2,1,0:T(8,128)S(1)} %get-tuple-element.122.refs_0_), channel_id=1, source_target_pairs={{0,1},{1,0},{2,3},{3,2},{4,5},{5,4},{6,7},{7,6},{8,9},{9,8},{10,11... | collective-permute-start | bytes 393224 | tf_op jit(solution)/shard_map/ppermute | solution.py:429
  52.7 2.2 %collective-permute-done.12.refs_2_ = f32[16,16,128]{2,1,0:T(8,128)S(1)} collective-permute-done((f32[16,16,128]{2,1,0:T(8,128)S(1)}, f32[16,16,128]{2,1,0:T(8,128)S(1)}, u32[]{:S(2)}, u32[]{:S(2)}) %collective-permute-start.12) | collective-permute-done | bytes 131104 | tf_op jit(solution)/shard_map/ppermute | solution.py:425
  54.9 2.7 %collective-permute-start.13 = (f32[16,16,128]{2,1,0:T(8,128)S(1)}, f32[16,16,128]{2,1,0:T(8,128)S(1)}, u32[]{:S(2)}, u32[]{:S(2)}) collective-permute-start(f32[16,16,128]{2,1,0:T(8,128)S(1)} %collective-permute-done.12.refs_2_), channel_id=1, source_target_pairs={{0,1},{1,0},{2,3},{3,2},{4,5},{5,4},{6,7},{7,6},{8,9},{9,8},{10,11... | collective-permute-start | bytes 393224 | tf_op jit(solution)/shard_map/ppermute | solution.py:429
  57.6 0.0 collective-permute-done.11.refs_1_
  57.6 1.0 %collective-permute-done.13.refs_3_ = f32[16,16,128]{2,1,0:T(8,128)S(1)} collective-permute-done((f32[16,16,128]{2,1,0:T(8,128)S(1)}, f32[16,16,128]{2,1,0:T(8,128)S(1)}, u32[]{:S(2)}, u32[]{:S(2)}) %collective-permute-start.13) | collective-permute-done | bytes 131104 | tf_op jit(solution)/shard_map/ppermute | solution.py:429
  58.6 1.2 %shard_map.68 = f32[16,4096]{1,0:T(8,128)} custom-call(s32[8]{0:T(128)S(4)} %get-tuple-element.64.facts, f32[16,16,128]{2,1,0:T(8,128)S(1)} %get-tuple-element.122.refs_0_, f32[16,16,128]{2,1,0:T(8,128)S(1)} %collective-permute-done.11.refs_1_, f32[16,16,128]{2,1,0:T(8,128)S(1)} %collective-permute-done.12.refs_2_, ...), custom_call_target="tpu_custom_call" | custom-call | tf_op jit(solution)/shard_map/pallas_call | solution.py:562
  (1 shorter events, 0.0 us)
Async XLA Ops:
  1.1 2.3 %collective-permute-start = (f32[2,16,4096]{2,1,0:T(8,128)S(1)}, f32[2,16,4096]{2,1,0:T(8,128)S(1)}, u32[]{:S(2)}, u32[]{:S(2)}) collective-permute-start(f32[2,16,4096]{2,1,0:T(8,128)S(1)} %get-tuple-element.66.refs_0_), channel_id=1, source_target_pairs={{0,1},{1,0},{2,3},{3,2},{4,5},{5,4},{6,7},{7,6},{8,9},{9,8},{10,11... | collective-permute-start | bytes 1572872 | tf_op jit(solution)/shard_map/ppermute | solution.py:429
  4.5 16.8 %collective-permute-start.1 = (f32[1928,128]{1,0:T(8,128)S(1)}, f32[1928,128]{1,0:T(8,128)S(1)}, u32[]{:S(2)}, u32[]{:S(2)}) collective-permute-start(f32[1928,128]{1,0:T(8,128)S(1)} %get-tuple-element.70), channel_id=1, source_target_pairs={{3,7},{4,8},{11,15},{12,16},{19,23},{20,24},{27,31},{7,3},{8,4},{1... | collective-permute-start | bytes 2961416 | tf_op jit(solution)/shard_map/ppermute | solution.py:491
  5.3 9.4 %collective-permute-start.2 = (f32[2,16,16,128]{3,2,1,0:T(8,128)S(1)}, f32[2,16,16,128]{3,2,1,0:T(8,128)S(1)}, u32[]{:S(2)}, u32[]{:S(2)}) collective-permute-start(f32[2,16,16,128]{3,2,1,0:T(8,128)S(1)} %get-tuple-element.71), channel_id=1, source_target_pairs={{2,0},{3,1},{0,2},{1,3},{6,4},{7,5},{4,6},{5,7},{10,8},{11,9},{8,1... | collective-permute-start | bytes 786440 | tf_op jit(solution)/shard_map/ppermute | solution.py:425
  15.0 4.3 %collective-permute-start.3 = (f32[15,16,128]{2,1,0:T(8,128)S(1)}, f32[15,16,128]{2,1,0:T(8,128)S(1)}, u32[]{:S(2)}, u32[]{:S(2)}) collective-permute-start(f32[15,16,128]{2,1,0:T(8,128)S(1)} %get-tuple-element.77), channel_id=1, source_target_pairs={{0,1},{2,3},{7,6},{5,4},{8,9},{10,11},{15,14},{13,12},{16,17},{18,... | collective-permute-start | bytes 368648 | tf_op jit(solution)/shard_map/ppermute | solution.py:530
  16.7 6.2 %collective-permute-start.4 = (f32[12,16,128]{2,1,0:T(8,128)S(1)}, f32[12,16,128]{2,1,0:T(8,128)S(1)}, u32[]{:S(2)}, u32[]{:S(2)}) collective-permute-start(f32[12,16,128]{2,1,0:T(8,128)S(1)} %get-tuple-element.85), channel_id=1, source_target_pairs={{1,2},{3,7},{6,5},{4,8},{9,10},{11,15},{14,13},{12,16},{17,18},{19... | collective-permute-start | bytes 294920 | tf_op jit(solution)/shard_map/ppermute | solution.py:529
  24.4 3.3 %collective-permute-start.5 = (f32[15,16,128]{2,1,0:T(8,128)S(1)}, f32[15,16,128]{2,1,0:T(8,128)S(1)}, u32[]{:S(2)}, u32[]{:S(2)}) collective-permute-start(f32[15,16,128]{2,1,0:T(8,128)S(1)} %get-tuple-element.91), channel_id=1, source_target_pairs={{0,1},{2,3},{7,6},{5,4},{8,9},{10,11},{15,14},{13,12},{16,17},{18,... | collective-permute-start | bytes 368648 | tf_op jit(solution)/shard_map/ppermute | solution.py:530
  25.8 6.2 %collective-permute-start.6 = (f32[12,16,128]{2,1,0:T(8,128)S(1)}, f32[12,16,128]{2,1,0:T(8,128)S(1)}, u32[]{:S(2)}, u32[]{:S(2)}) collective-permute-start(f32[12,16,128]{2,1,0:T(8,128)S(1)} %get-tuple-element.97), channel_id=1, source_target_pairs={{1,2},{3,7},{6,5},{4,8},{9,10},{11,15},{14,13},{12,16},{17,18},{19... | collective-permute-start | bytes 294920 | tf_op jit(solution)/shard_map/ppermute | solution.py:529
  33.6 3.3 %collective-permute-start.7 = (f32[15,16,128]{2,1,0:T(8,128)S(1)}, f32[15,16,128]{2,1,0:T(8,128)S(1)}, u32[]{:S(2)}, u32[]{:S(2)}) collective-permute-start(f32[15,16,128]{2,1,0:T(8,128)S(1)} %get-tuple-element.103), channel_id=1, source_target_pairs={{0,1},{2,3},{7,6},{5,4},{8,9},{10,11},{15,14},{13,12},{16,17},{18,... | collective-permute-start | bytes 368648 | tf_op jit(solution)/shard_map/ppermute | solution.py:530
  34.9 6.2 %collective-permute-start.8 = (f32[12,16,128]{2,1,0:T(8,128)S(1)}, f32[12,16,128]{2,1,0:T(8,128)S(1)}, u32[]{:S(2)}, u32[]{:S(2)}) collective-permute-start(f32[12,16,128]{2,1,0:T(8,128)S(1)} %get-tuple-element.109), channel_id=1, source_target_pairs={{1,2},{3,7},{6,5},{4,8},{9,10},{11,15},{14,13},{12,16},{17,18},{19... | collective-permute-start | bytes 294920 | tf_op jit(solution)/shard_map/ppermute | solution.py:529
  42.6 3.3 %collective-permute-start.9 = (f32[15,16,128]{2,1,0:T(8,128)S(1)}, f32[15,16,128]{2,1,0:T(8,128)S(1)}, u32[]{:S(2)}, u32[]{:S(2)}) collective-permute-start(f32[15,16,128]{2,1,0:T(8,128)S(1)} %get-tuple-element.115), channel_id=1, source_target_pairs={{0,1},{2,3},{7,6},{5,4},{8,9},{10,11},{15,14},{13,12},{16,17},{18,... | collective-permute-start | bytes 368648 | tf_op jit(solution)/shard_map/ppermute | solution.py:530
  44.0 5.7 %collective-permute-start.10 = (f32[9,16,128]{2,1,0:T(8,128)S(1)}, f32[9,16,128]{2,1,0:T(8,128)S(1)}, u32[]{:S(2)}, u32[]{:S(2)}) collective-permute-start(f32[9,16,128]{2,1,0:T(8,128)S(1)} %get-tuple-element.121), channel_id=1, source_target_pairs={{1,2},{3,7},{6,5},{4,8},{9,10},{11,15},{14,13},{12,16},{17,18},{19... | collective-permute-start | bytes 221192 | tf_op jit(solution)/shard_map/ppermute | solution.py:529
  51.1 3.8 %collective-permute-start.12 = (f32[16,16,128]{2,1,0:T(8,128)S(1)}, f32[16,16,128]{2,1,0:T(8,128)S(1)}, u32[]{:S(2)}, u32[]{:S(2)}) collective-permute-start(f32[16,16,128]{2,1,0:T(8,128)S(1)} %get-tuple-element.122.refs_0_), channel_id=1, source_target_pairs={{2,0},{3,1},{0,2},{1,3},{6,4},{7,5},{4,6},{5,7},{10,8},{11,9},{8,1... | collective-permute-start | bytes 393224 | tf_op jit(solution)/shard_map/ppermute | solution.py:425
  51.1 6.5 %collective-permute-start.11 = (f32[16,16,128]{2,1,0:T(8,128)S(1)}, f32[16,16,128]{2,1,0:T(8,128)S(1)}, u32[]{:S(2)}, u32[]{:S(2)}) collective-permute-start(f32[16,16,128]{2,1,0:T(8,128)S(1)} %get-tuple-element.122.refs_0_), channel_id=1, source_target_pairs={{0,1},{1,0},{2,3},{3,2},{4,5},{5,4},{6,7},{7,6},{8,9},{9,8},{10,11... | collective-permute-start | bytes 393224 | tf_op jit(solution)/shard_map/ppermute | solution.py:429
  54.9 3.7 %collective-permute-start.13 = (f32[16,16,128]{2,1,0:T(8,128)S(1)}, f32[16,16,128]{2,1,0:T(8,128)S(1)}, u32[]{:S(2)}, u32[]{:S(2)}) collective-permute-start(f32[16,16,128]{2,1,0:T(8,128)S(1)} %collective-permute-done.12.refs_2_), channel_id=1, source_target_pairs={{0,1},{1,0},{2,3},{3,2},{4,5},{5,4},{6,7},{7,6},{8,9},{9,8},{10,11... | collective-permute-start | bytes 393224 | tf_op jit(solution)/shard_map/ppermute | solution.py:429

commit v12 on v11

--- a/solution.py
+++ b/solution.py
@@ -135,30 +135,14 @@
     return jnp.where(backwards == 1, folds - 1 - fold, fold)
 
 
-def align_kernel(ob, folds, lend, width, facts, indices, blocks, *refs):
-    sources, outs, (border, sem) = refs[:2], refs[2:-2], refs[-2:]
-    own = indices.shape[1]
-    size = blocks.shape[0] // own
-    edge = (facts[0] == 0) | (facts[0] == folds - 1)
-    first = jnp.where(facts[0] == 0, 0, own - lend)
-
-    def copies():
-        for i in range(lend):
-            row = blocks.at[pl.ds(pl.multiple_of((first + i) * size, size), size)]
-            yield pltpu.make_async_copy(row, border.at[i * size : (i + 1) * size], sem.at[i])
-
-    @pl.when(edge)
-    def _():
-        for copy in copies():
-            copy.start()
-
+def rows_of_parts(ob, folds, facts, sources, outs):
     capacity = sources[0].shape[-1]
     lane = lax.broadcasted_iota(jnp.int32, (16, 128), 1)
     spans = []
     for c in (False, True):
         owner = holder(facts[2], folds, 0, c)
         spans.append((begin_of(facts, folds, owner), facts[COUNTS + owner]))
-    for d, out in enumerate(outs):
+    for d, out in outs:
         base = part_of(holder(facts[2], folds, d, False), folds, facts[3]) * (ob * 128)
 
         def block(e, carry, out=out, base=base):
@@ -181,27 +165,40 @@
             out[1, e] = totals[1]
             return carry
 
-        lax.fori_loop(0, ob, block, 0, unroll=4)
-
-    @pl.when(edge)
-    def _():
-        place = lax.broadcasted_iota(jnp.int32, (8, 128), 1)
-        lines = jnp.zeros((8, 128), jnp.int32)
-        for i in range(lend):
-            for k in range(width):
-                lines = jnp.where(place == i * width + k, indices[k, first + i], lines)
-        border[lend * size :] = lines.astype(F32)
-        for copy in copies():
-            copy.wait()
-
-
-def first_kernel(folds, counts, columns, initial, right_side, facts, held, stacked, live, sem):
+        lax.fori_loop(0, ob, block, 0, unroll=True)
+
+
+def align_kernel(ob, folds, facts, first, second, *outs):
+    rows_of_parts(ob, folds, facts, (first, second), list(enumerate(outs, 1)))
+
+
+def own_rows_kernel(ob, folds, facts, first, second, out):
+    rows_of_parts(ob, folds, facts, (first, second), [(0, out)])
+
+
+def first_kernel(folds, lend, width, counts, columns, initial, right_side, blocks, facts, held, stacked, border, live, sem):
+    own = columns.shape[1]
+    size = blocks.shape[0] // own
     fold = lax.axis_index("fold")
     backwards = lax.rem(lax.axis_index("group"), 2)
     part = part_of(fold, folds, backwards)
+    edge = (part == 0) | (part == folds - 1)
+    first = jnp.where(part == 0, 0, own - lend)
     small = [pltpu.make_async_copy(columns, held, sem.at[0]), pltpu.make_async_copy(counts, live, sem.at[1])]
     pair = [pltpu.make_async_copy(array, stacked.at[i], sem.at[2 + i]) for i, array in enumerate((initial, right_side))]
-    for copy in pair + small:
+    rows = []
+    for i in range(lend):
+        row = blocks.at[pl.ds(pl.multiple_of((first + i) * size, size), size)]
+        rows.append(pltpu.make_async_copy(row, border.at[i * size : (i + 1) * size], sem.at[4 + i]))
+    for copy in small:
+        copy.start()
+
+    @pl.when(edge)
+    def _():
+        for copy in rows:
+            copy.start()
+
+    for copy in pair:
         copy.start()
     for copy in small:
         copy.wait()
@@ -209,8 +206,24 @@
         facts[i] = fact
     for i in range(folds):
         facts[COUNTS + i] = live[0, i]
+
+    @pl.when(edge)
+    def _():
+        lane = lax.broadcasted_iota(jnp.int32, (8, 128), 1)
+        indices = jnp.zeros((8, 128), jnp.int32)
+        for i in range(lend):
+            for k in range(width):
+                indices = jnp.where(lane == i * width + k, held[k, first + i], indices)
+        border[lend * size :] = indices.astype(F32)
+        for copy in rows:
+            copy.wait()
+
     for copy in pair:
         copy.wait()
+
+
+def gate_kernel(*refs):
+    del refs
 
 
 def put_row(out, a, raw):
@@ -418,7 +431,7 @@
         out[:, pl.ds(pl.multiple_of(b * 128, 128), 128)] = piece
         return carry
 
-    lax.fori_loop(0, out.shape[1] // 128, block, 0, unroll=8)
+    lax.fori_loop(0, out.shape[1] // 128, block, 0, unroll=True)
 
 
 def over_chips(array, d, folds):
@@ -463,31 +476,40 @@
         return pltpu.with_memory_space_constraint(array, space)
 
     flat = fixed(blocks.reshape(own * size, side))
-    facts, indices, stacked = pl.pallas_call(
-        functools.partial(first_kernel, folds),
+    facts, indices, stacked, border = pl.pallas_call(
+        functools.partial(first_kernel, folds, lend, width),
         out_shape=(
             pltpu.SMEM((COUNTS + folds,), jnp.int32),
             pltpu.SMEM((width, own), jnp.int32),
             pltpu.VMEM((2, vectors, capacity), F32),
+            pltpu.VMEM((lend * size + 8, side), F32),
         ),
-        in_specs=[HBM] * 4,
-        out_specs=(SMEM, SMEM, VMEM),
-        scratch_shapes=[pltpu.SMEM((1, folds), jnp.int32), pltpu.SemaphoreType.DMA((4,))],
+        in_specs=[HBM] * 5,
+        out_specs=(SMEM, SMEM, VMEM, VMEM),
+        scratch_shapes=[pltpu.SMEM((1, folds), jnp.int32), pltpu.SemaphoreType.DMA((4 + lend,))],
         compiler_params=params(),
-    )(fixed(counts), fixed(columns.T), fixed(initial), fixed(right_side))
+    )(fixed(counts), fixed(columns.T), fixed(initial), fixed(right_side), flat)
     facts, indices = fixed(facts, pltpu.SMEM), fixed(indices, pltpu.SMEM)
     mate = other_core(stacked, folds)
 
     rows_of = jax.ShapeDtypeStruct((2, ob, vectors, side), F32)
-    *partial, border = pl.pallas_call(
-        functools.partial(align_kernel, ob, folds, lend, width),
-        out_shape=(rows_of,) * (folds // 2) + (pltpu.VMEM((lend * size + 8, side), F32),),
-        in_specs=[SMEM, SMEM, HBM, VMEM, VMEM],
-        out_specs=(VMEM,) * (1 + folds // 2),
-        scratch_shapes=[pltpu.SemaphoreType.DMA((lend,))],
+    slots = [fixed(stacked, pltpu.VMEM), fixed(mate, pltpu.VMEM)]
+    partial = pl.pallas_call(
+        functools.partial(align_kernel, ob, folds),
+        out_shape=(rows_of,) * (folds // 2 - 1),
+        in_specs=[SMEM, VMEM, VMEM],
+        out_specs=(VMEM,) * (folds // 2 - 1),
         compiler_params=params(),
-    )(facts, indices, flat, fixed(stacked, pltpu.VMEM), fixed(mate, pltpu.VMEM))
-    sent = [over_chips(partial[d], folds // 2 - d, folds) for d in range(1, folds // 2)]
+    )(facts, *slots)
+    sent = [over_chips(array, folds // 2 - d, folds) for d, array in enumerate(partial, 1)]
+    border = pl.pallas_call(
+        gate_kernel,
+        out_shape=pltpu.VMEM(border.shape, F32),
+        in_specs=[VMEM, pl.BlockSpec(memory_space=pl.ANY)],
+        out_specs=VMEM,
+        input_output_aliases={0: 0},
+        compiler_params=params(),
+    )(fixed(border, pltpu.VMEM), partial[0])
     border = lax.ppermute(border, AXES, swap_border)
 
     used = ob + halo + lend
@@ -500,6 +522,13 @@
         compiler_params=params(32),
         cost_estimate=pl.CostEstimate(flops=10**7, bytes_accessed=2 * rows * size * side * 4, transcendentals=0),
     )(facts, indices, flat, partial[0])
+    mine = pl.pallas_call(
+        functools.partial(own_rows_kernel, ob, folds),
+        out_shape=rows_of,
+        in_specs=[SMEM, VMEM, VMEM],
+        out_specs=VMEM,
+        compiler_params=params(),
+    )(facts, *slots)
     offsets = fixed(offsets, pltpu.SMEM)
 
     extent = ob + 2 * HB * steps
@@ -510,7 +539,7 @@
         in_specs=[SMEM, SMEM] + [VMEM] * (1 + folds // 2),
         out_specs=(VMEM,) * 7,
         compiler_params=params(),
-    )(facts, offsets, fixed(operator, pltpu.VMEM), partial[0], *sent)
+    )(facts, offsets, fixed(operator, pltpu.VMEM), mine, *sent)
 
     def part_of_phase(kernel, operator, indices, held, got, outs):
         held = [pltpu.with_memory_space_constraint(array, pltpu.VMEM) for array in held]

time: 60 us -> 59 us (0.983)
  Pallas kernels: 23.2 us -> 22.5 us
    pallas_call x2 -> x4, Pallas kernels: 2.25 us -> 1.78 us  [the longest x1 1.09 us: on_device(): pl.pallas_call(functools.partial(first_kernel, folds, lend, width), out_s...]
  transfers between devices with their start and end apart: 14 -> 14, of which waited for: 8 -> 8; matrix products, arithmetic and copies ran while one was open for 0% -> 0% of each run, Pallas kernels for 23% -> 24%
where the time goes in v12:
time: 59 us; the launch traced here: 58.7 us
  starting transfers between devices  23.7 us (40%)
  Pallas kernels  22.5 us (38%)
  waiting for transfers between devices  12.4 us (21%)
    pallas_call x8, Pallas kernels, part_of_phase(): pl.pallas_call(functools.partial(kernel, ob, folds, steps, done == 0, don...  14.6 us
    ppermute x4, starting transfers between devices, on_device(): got_b = lax.ppermute(pay_b, AXES, swap_b)  8.69 us
    ppermute x4, waiting for transfers between devices, on_device(): got_b = lax.ppermute(pay_b, AXES, swap_b)  6.89 us
    ppermute x4, starting transfers between devices, on_device(): got_a = lax.ppermute(pay_a, AXES, swap_a)  5.46 us
    ppermute x3, starting transfers between devices, other_core(): return lax.ppermute(array, 'fold', [(i, i ^ 1) for i in range(folds)])  5.39 us
    pallas_call x1, Pallas kernels, on_device(): pl.pallas_call(functools.partial(prepare_kernel, ob, halo, lend, width),...  4.8 us
    ppermute x2, starting transfers between devices, over_chips(): lax.ppermute(array, 'fold', [((i + 2 * d) % folds, i) for i in range(fold...  3.42 us
    ppermute x2, waiting for transfers between devices, over_chips(): lax.ppermute(array, 'fold', [((i + 2 * d) % folds, i) for i in range(fold...  2.95 us
  transfers between devices with their start and end apart: 14, of which 8 were waited for; matrix products, arithmetic and copies ran while one was open for 0% of the time, Pallas kernels for 24%

profile of v12, /device:TPU:9, one launch (start us, length us, event | category | flops | bytes accessed | tf_op | source)
XLA Modules:
  0.0 58.7 jit_solution(6472453288358248781)
XLA Ops:
  0.0 1.1 %shard_map.55 = (s32[8]{0:T(128)S(4)}, s32[5,64]{1,0:T(8,128)S(4)}, f32[2,16,4096]{2,1,0:T(8,128)S(1)}, f32[1928,128]{1,0:T(8,128)S(1)}) custom-call(s32[1,4]{1,0:T(1,128)} %counts.1, s32[5,64]{1,0:T(8,128)} %bitcast.4, f32[16,4096]{1,0:T(8,128)} %initial.1, f32[16,4096]{1,0:T(8,128)} %right_side.1, f32[40960,128]{1,0:T(8,128)} %bitcast.2), custom_call_target="tpu_custom_call" | custom-call | tf_op jit(solution)/shard_map/pallas_call | solution.py:479
  1.1 1.0 %collective-permute-start = (f32[2,16,4096]{2,1,0:T(8,128)S(1)}, f32[2,16,4096]{2,1,0:T(8,128)S(1)}, u32[]{:S(2)}, u32[]{:S(2)}) collective-permute-start(f32[2,16,4096]{2,1,0:T(8,128)S(1)} %get-tuple-element.64.first), channel_id=1, source_target_pairs={{0,1},{1,0},{2,3},{3,2},{4,5},{5,4},{6,7},{7,6},{8,9},{9,8},{10,11... | collective-permute-start | bytes 1572872 | tf_op jit(solution)/shard_map/ppermute | solution.py:442
  2.1 1.5 %collective-permute-done.second = f32[2,16,4096]{2,1,0:T(8,128)S(1)} collective-permute-done((f32[2,16,4096]{2,1,0:T(8,128)S(1)}, f32[2,16,4096]{2,1,0:T(8,128)S(1)}, u32[]{:S(2)}, u32[]{:S(2)}) %collective-permute-start) | collective-permute-done | bytes 524320 | tf_op jit(solution)/shard_map/ppermute | solution.py:442
  3.7 0.3 shard_map.56.token.refs_1_
  4.0 0.7 %collective-permute-start.1 = (f32[1928,128]{1,0:T(8,128)S(1)}, f32[1928,128]{1,0:T(8,128)S(1)}, u32[]{:S(2)}, u32[]{:S(2)}) collective-permute-start(f32[1928,128]{1,0:T(8,128)S(1)} %shard_map.58), channel_id=1, source_target_pairs={{3,7},{4,8},{11,15},{12,16},{19,23},{20,24},{27,31},{7,3},{8,4},{1... | collective-permute-start | bytes 2961416 | tf_op jit(solution)/shard_map/ppermute | solution.py:513
  4.8 3.4 %collective-permute-start.2 = (f32[2,16,16,128]{3,2,1,0:T(8,128)S(1)}, f32[2,16,16,128]{3,2,1,0:T(8,128)S(1)}, u32[]{:S(2)}, u32[]{:S(2)}) collective-permute-start(f32[2,16,16,128]{3,2,1,0:T(8,128)S(1)} %shard_map.56.token.refs_1_), channel_id=1, source_target_pairs={{2,0},{3,1},{0,2},{1,3},{6,4},{7,5},{4,6},{5,7},{10,8},{11,9},{8,1... | collective-permute-start | bytes 786440 | tf_op jit(solution)/shard_map/ppermute | solution.py:438
  8.2 0.3 shard_map.59.refs_0_
  8.5 4.8 %shard_map.57 = (bf16[28,640,256]{2,1,0:T(8,128)(2,1)S(1)}, s32[140]{0:T(256)S(4)}) custom-call(s32[8]{0:T(128)S(4)} %get-tuple-element.62.facts, s32[5,64]{1,0:T(8,128)S(4)} %get-tuple-element.63.columns, f32[40960,128]{1,0:T(8,128)} %bitcast.3, f32[2,16,16,128]{3,2,1,0:T(8,128)S(1)} %shard_map.56.token.refs_1_), custom_call_target="tpu_custom_call" | custom-call | flops 10000000 | bytes 18350080 | tf_op jit(solution)/shard_map/pallas_call | solution.py:516
  13.3 0.8 %collective-permute-done.2.refs_1_ = f32[2,16,16,128]{3,2,1,0:T(8,128)S(1)} collective-permute-done((f32[2,16,16,128]{3,2,1,0:T(8,128)S(1)}, f32[2,16,16,128]{3,2,1,0:T(8,128)S(1)}, u32[]{:S(2)}, u32[]{:S(2)}) %collective-permute-start.2) | collective-permute-done | bytes 262176 | tf_op jit(solution)/shard_map/ppermute | solution.py:438
  14.1 0.3 shard_map.60
  14.4 1.4 %collective-permute-start.3 = (f32[15,16,128]{2,1,0:T(8,128)S(1)}, f32[15,16,128]{2,1,0:T(8,128)S(1)}, u32[]{:S(2)}, u32[]{:S(2)}) collective-permute-start(f32[15,16,128]{2,1,0:T(8,128)S(1)} %get-tuple-element.73), channel_id=1, source_target_pairs={{0,1},{2,3},{7,6},{5,4},{8,9},{10,11},{15,14},{13,12},{16,17},{18,... | collective-permute-start | bytes 368648 | tf_op jit(solution)/shard_map/ppermute | solution.py:559
  15.8 3.0 %collective-permute-start.4 = (f32[12,16,128]{2,1,0:T(8,128)S(1)}, f32[12,16,128]{2,1,0:T(8,128)S(1)}, u32[]{:S(2)}, u32[]{:S(2)}) collective-permute-start(f32[12,16,128]{2,1,0:T(8,128)S(1)} %get-tuple-element.81), channel_id=1, source_target_pairs={{1,2},{3,7},{6,5},{4,8},{9,10},{11,15},{14,13},{12,16},{17,18},{19... | collective-permute-start | bytes 294920 | tf_op jit(solution)/shard_map/ppermute | solution.py:558
  18.8 0.0 collective-permute-done.3.refs_5_
  18.8 2.1 %shard_map.61 = (f32[34,16,128]{2,1,0:T(8,128)S(1)}, f32[34,16,128]{2,1,0:T(8,128)S(1)}, f32[34,16,128]{2,1,0:T(8,128)S(1)}, bf16[34,32,128]{2,1,0:T(8,128)(2,1)S(1)}, bf16[34,32,128]{2,1,0:T(8,128)(2,1)S(1)}) custom-call(s32[8]{0:T(128)S(4)} %get-tuple-element.62.facts, ...), custom_call_target="tpu_custom_call", output_to_operand_aliasing={{0}: (3, {}), {1}: (4, {}), {2}: (5, {}), {3}: (6, {}), {4}... | custom-call | tf_op jit(solution)/shard_map/pallas_call | solution.py:547
  20.9 0.0 collective-permute-done.1.raw
  20.9 1.1 %collective-permute-done.4.refs_5_ = f32[12,16,128]{2,1,0:T(8,128)S(1)} collective-permute-done((f32[12,16,128]{2,1,0:T(8,128)S(1)}, f32[12,16,128]{2,1,0:T(8,128)S(1)}, u32[]{:S(2)}, u32[]{:S(2)}) %collective-permute-start.4) | collective-permute-done | bytes 98336 | tf_op jit(solution)/shard_map/ppermute | solution.py:558
  22.1 1.6 %shard_map.63 = (f32[34,16,128]{2,1,0:T(8,128)S(1)}, f32[34,16,128]{2,1,0:T(8,128)S(1)}, f32[34,16,128]{2,1,0:T(8,128)S(1)}, bf16[34,32,128]{2,1,0:T(8,128)(2,1)...) custom-call(s32[8]{0:T(128)S(4)} %get-tuple-element.62.facts, ...), custom_call_target="tpu_custom_call", output_to_operand_aliasing={{0}: (4, {}), {1}: (5, {}), {2}: (6, {}), {3}: (7, {}), {4}... | custom-call | tf_op jit(solution)/shard_map/pallas_call | solution.py:547
  23.6 1.3 %collective-permute-start.5 = (f32[15,16,128]{2,1,0:T(8,128)S(1)}, f32[15,16,128]{2,1,0:T(8,128)S(1)}, u32[]{:S(2)}, u32[]{:S(2)}) collective-permute-start(f32[15,16,128]{2,1,0:T(8,128)S(1)} %get-tuple-element.87), channel_id=1, source_target_pairs={{0,1},{2,3},{7,6},{5,4},{8,9},{10,11},{15,14},{13,12},{16,17},{18,... | collective-permute-start | bytes 368648 | tf_op jit(solution)/shard_map/ppermute | solution.py:559
  24.9 1.9 %collective-permute-start.6 = (f32[12,16,128]{2,1,0:T(8,128)S(1)}, f32[12,16,128]{2,1,0:T(8,128)S(1)}, u32[]{:S(2)}, u32[]{:S(2)}) collective-permute-start(f32[12,16,128]{2,1,0:T(8,128)S(1)} %get-tuple-element.93), channel_id=1, source_target_pairs={{1,2},{3,7},{6,5},{4,8},{9,10},{11,15},{14,13},{12,16},{17,18},{19... | collective-permute-start | bytes 294920 | tf_op jit(solution)/shard_map/ppermute | solution.py:558
  26.9 0.0 collective-permute-done.5.refs_5_
  26.9 2.2 %shard_map.64 = (f32[34,16,128]{2,1,0:T(8,128)S(1)}, f32[34,16,128]{2,1,0:T(8,128)S(1)}, f32[34,16,128]{2,1,0:T(8,128)S(1)}, bf16[34,32,128]{2,1,0:T(8,128)(2,1)S(1)}, bf16[34,32,128]{2,1,0:T(8,128)(2,1)S(1)}) custom-call(s32[8]{0:T(128)S(4)} %get-tuple-element.62.facts, ...), custom_call_target="tpu_custom_call", output_to_operand_aliasing={{0}: (3, {}), {1}: (4, {}), {2}: (5, {}), {3}: (6, {}), {4}... | custom-call | tf_op jit(solution)/shard_map/pallas_call | solution.py:547
  29.1 2.1 %collective-permute-done.6.refs_5_ = f32[12,16,128]{2,1,0:T(8,128)S(1)} collective-permute-done((f32[12,16,128]{2,1,0:T(8,128)S(1)}, f32[12,16,128]{2,1,0:T(8,128)S(1)}, u32[]{:S(2)}, u32[]{:S(2)}) %collective-permute-start.6) | collective-permute-done | bytes 98336 | tf_op jit(solution)/shard_map/ppermute | solution.py:558
  31.2 1.5 %shard_map.65 = (f32[34,16,128]{2,1,0:T(8,128)S(1)}, f32[34,16,128]{2,1,0:T(8,128)S(1)}, f32[34,16,128]{2,1,0:T(8,128)S(1)}, bf16[34,32,128]{2,1,0:T(8,128)(2,1)...) custom-call(s32[8]{0:T(128)S(4)} %get-tuple-element.62.facts, ...), custom_call_target="tpu_custom_call", output_to_operand_aliasing={{0}: (4, {}), {1}: (5, {}), {2}: (6, {}), {3}: (7, {}), {4}... | custom-call | tf_op jit(solution)/shard_map/pallas_call | solution.py:547
  32.7 1.4 %collective-permute-start.7 = (f32[15,16,128]{2,1,0:T(8,128)S(1)}, f32[15,16,128]{2,1,0:T(8,128)S(1)}, u32[]{:S(2)}, u32[]{:S(2)}) collective-permute-start(f32[15,16,128]{2,1,0:T(8,128)S(1)} %get-tuple-element.99), channel_id=1, source_target_pairs={{0,1},{2,3},{7,6},{5,4},{8,9},{10,11},{15,14},{13,12},{16,17},{18,... | collective-permute-start | bytes 368648 | tf_op jit(solution)/shard_map/ppermute | solution.py:559
  34.1 1.9 %collective-permute-start.8 = (f32[12,16,128]{2,1,0:T(8,128)S(1)}, f32[12,16,128]{2,1,0:T(8,128)S(1)}, u32[]{:S(2)}, u32[]{:S(2)}) collective-permute-start(f32[12,16,128]{2,1,0:T(8,128)S(1)} %get-tuple-element.105), channel_id=1, source_target_pairs={{1,2},{3,7},{6,5},{4,8},{9,10},{11,15},{14,13},{12,16},{17,18},{19... | collective-permute-start | bytes 294920 | tf_op jit(solution)/shard_map/ppermute | solution.py:558
  36.0 0.0 collective-permute-done.7.refs_5_
  36.0 2.1 %shard_map.66 = (f32[34,16,128]{2,1,0:T(8,128)S(1)}, f32[34,16,128]{2,1,0:T(8,128)S(1)}, f32[34,16,128]{2,1,0:T(8,128)S(1)}, bf16[34,32,128]{2,1,0:T(8,128)(2,1)S(1)}, bf16[34,32,128]{2,1,0:T(8,128)(2,1)S(1)}) custom-call(s32[8]{0:T(128)S(4)} %get-tuple-element.62.facts, ...), custom_call_target="tpu_custom_call", output_to_operand_aliasing={{0}: (3, {}), {1}: (4, {}), {2}: (5, {}), {3}: (6, {}), {4}... | custom-call | tf_op jit(solution)/shard_map/pallas_call | solution.py:547
  38.0 2.2 %collective-permute-done.8.refs_5_ = f32[12,16,128]{2,1,0:T(8,128)S(1)} collective-permute-done((f32[12,16,128]{2,1,0:T(8,128)S(1)}, f32[12,16,128]{2,1,0:T(8,128)S(1)}, u32[]{:S(2)}, u32[]{:S(2)}) %collective-permute-start.8) | collective-permute-done | bytes 98336 | tf_op jit(solution)/shard_map/ppermute | solution.py:558
  40.3 1.5 %shard_map.67 = (f32[34,16,128]{2,1,0:T(8,128)S(1)}, f32[34,16,128]{2,1,0:T(8,128)S(1)}, f32[34,16,128]{2,1,0:T(8,128)S(1)}, bf16[34,32,128]{2,1,0:T(8,128)(2,1)...) custom-call(s32[8]{0:T(128)S(4)} %get-tuple-element.62.facts, ...), custom_call_target="tpu_custom_call", output_to_operand_aliasing={{0}: (4, {}), {1}: (5, {}), {2}: (6, {}), {3}: (7, {}), {4}... | custom-call | tf_op jit(solution)/shard_map/pallas_call | solution.py:547
  41.8 1.4 %collective-permute-start.9 = (f32[15,16,128]{2,1,0:T(8,128)S(1)}, f32[15,16,128]{2,1,0:T(8,128)S(1)}, u32[]{:S(2)}, u32[]{:S(2)}) collective-permute-start(f32[15,16,128]{2,1,0:T(8,128)S(1)} %get-tuple-element.111), channel_id=1, source_target_pairs={{0,1},{2,3},{7,6},{5,4},{8,9},{10,11},{15,14},{13,12},{16,17},{18,... | collective-permute-start | bytes 368648 | tf_op jit(solution)/shard_map/ppermute | solution.py:559
  43.2 1.9 %collective-permute-start.10 = (f32[9,16,128]{2,1,0:T(8,128)S(1)}, f32[9,16,128]{2,1,0:T(8,128)S(1)}, u32[]{:S(2)}, u32[]{:S(2)}) collective-permute-start(f32[9,16,128]{2,1,0:T(8,128)S(1)} %get-tuple-element.117), channel_id=1, source_target_pairs={{1,2},{3,7},{6,5},{4,8},{9,10},{11,15},{14,13},{12,16},{17,18},{19... | collective-permute-start | bytes 221192 | tf_op jit(solution)/shard_map/ppermute | solution.py:558
  45.1 0.0 collective-permute-done.9.refs_5_
  45.1 2.3 %shard_map.68 = (f32[34,16,128]{2,1,0:T(8,128)S(1)}, f32[34,16,128]{2,1,0:T(8,128)S(1)}, f32[34,16,128]{2,1,0:T(8,128)S(1)}, bf16[34,32,128]{2,1,0:T(8,128)(2,1)S(1)}, bf16[34,32,128]{2,1,0:T(8,128)(2,1)S(1)}) custom-call(s32[8]{0:T(128)S(4)} %get-tuple-element.62.facts, ...), custom_call_target="tpu_custom_call", output_to_operand_aliasing={{0}: (3, {}), {1}: (4, {}), {2}: (5, {}), {3}: (6, {}), {4}... | custom-call | tf_op jit(solution)/shard_map/pallas_call | solution.py:547
  47.4 1.5 %collective-permute-done.10.refs_5_ = f32[9,16,128]{2,1,0:T(8,128)S(1)} collective-permute-done((f32[9,16,128]{2,1,0:T(8,128)S(1)}, f32[9,16,128]{2,1,0:T(8,128)S(1)}, u32[]{:S(2)}, u32[]{:S(2)}) %collective-permute-start.10) | collective-permute-done | bytes 73760 | tf_op jit(solution)/shard_map/ppermute | solution.py:558
  48.8 1.4 %shard_map.69 = (f32[34,16,128]{2,1,0:T(8,128)S(1)}, f32[34,16,128]{2,1,0:T(8,128)S(1)}, f32[34,16,128]{2,1,0:T(8,128)S(1)}, bf16[34,32,128]{2,1,0:T(8,128)(2,1)...) custom-call(s32[8]{0:T(128)S(4)} %get-tuple-element.62.facts, ...), custom_call_target="tpu_custom_call", output_to_operand_aliasing={{0}: (4, {}), {1}: (5, {}), {2}: (6, {}), {3}: (7, {}), {4}... | custom-call | tf_op jit(solution)/shard_map/pallas_call | solution.py:547
  50.2 0.0 collective-permute-start.12
  50.3 1.6 %collective-permute-start.11 = (f32[16,16,128]{2,1,0:T(8,128)S(1)}, f32[16,16,128]{2,1,0:T(8,128)S(1)}, u32[]{:S(2)}, u32[]{:S(2)}) collective-permute-start(f32[16,16,128]{2,1,0:T(8,128)S(1)} %get-tuple-element.118.refs_0_), channel_id=1, source_target_pairs={{0,1},{1,0},{2,3},{3,2},{4,5},{5,4},{6,7},{7,6},{8,9},{9,8},{10,11... | collective-permute-start | bytes 393224 | tf_op jit(solution)/shard_map/ppermute | solution.py:442
  51.9 2.2 %collective-permute-done.12.refs_2_ = f32[16,16,128]{2,1,0:T(8,128)S(1)} collective-permute-done((f32[16,16,128]{2,1,0:T(8,128)S(1)}, f32[16,16,128]{2,1,0:T(8,128)S(1)}, u32[]{:S(2)}, u32[]{:S(2)}) %collective-permute-start.12) | collective-permute-done | bytes 131104 | tf_op jit(solution)/shard_map/ppermute | solution.py:438
  54.1 2.7 %collective-permute-start.13 = (f32[16,16,128]{2,1,0:T(8,128)S(1)}, f32[16,16,128]{2,1,0:T(8,128)S(1)}, u32[]{:S(2)}, u32[]{:S(2)}) collective-permute-start(f32[16,16,128]{2,1,0:T(8,128)S(1)} %collective-permute-done.12.refs_2_), channel_id=1, source_target_pairs={{0,1},{1,0},{2,3},{3,2},{4,5},{5,4},{6,7},{7,6},{8,9},{9,8},{10,11... | collective-permute-start | bytes 393224 | tf_op jit(solution)/shard_map/ppermute | solution.py:442
  56.8 0.0 collective-permute-done.11.refs_1_
  56.8 1.0 %collective-permute-done.13.refs_3_ = f32[16,16,128]{2,1,0:T(8,128)S(1)} collective-permute-done((f32[16,16,128]{2,1,0:T(8,128)S(1)}, f32[16,16,128]{2,1,0:T(8,128)S(1)}, u32[]{:S(2)}, u32[]{:S(2)}) %collective-permute-start.13) | collective-permute-done | bytes 131104 | tf_op jit(solution)/shard_map/ppermute | solution.py:442
  57.8 0.9 %shard_map.70 = f32[16,4096]{1,0:T(8,128)} custom-call(s32[8]{0:T(128)S(4)} %get-tuple-element.62.facts, f32[16,16,128]{2,1,0:T(8,128)S(1)} %get-tuple-element.118.refs_0_, f32[16,16,128]{2,1,0:T(8,128)S(1)} %collective-permute-done.11.refs_1_, f32[16,16,128]{2,1,0:T(8,128)S(1)} %collective-permute-done.12.refs_2_, ...), custom_call_target="tpu_custom_call" | custom-call | tf_op jit(solution)/shard_map/pallas_call | solution.py:591
  (2 shorter events, 0.0 us)
Async XLA Ops:
  1.1 2.6 %collective-permute-start = (f32[2,16,4096]{2,1,0:T(8,128)S(1)}, f32[2,16,4096]{2,1,0:T(8,128)S(1)}, u32[]{:S(2)}, u32[]{:S(2)}) collective-permute-start(f32[2,16,4096]{2,1,0:T(8,128)S(1)} %get-tuple-element.64.first), channel_id=1, source_target_pairs={{0,1},{1,0},{2,3},{3,2},{4,5},{5,4},{6,7},{7,6},{8,9},{9,8},{10,11... | collective-permute-start | bytes 1572872 | tf_op jit(solution)/shard_map/ppermute | solution.py:442
  4.0 16.8 %collective-permute-start.1 = (f32[1928,128]{1,0:T(8,128)S(1)}, f32[1928,128]{1,0:T(8,128)S(1)}, u32[]{:S(2)}, u32[]{:S(2)}) collective-permute-start(f32[1928,128]{1,0:T(8,128)S(1)} %shard_map.58), channel_id=1, source_target_pairs={{3,7},{4,8},{11,15},{12,16},{19,23},{20,24},{27,31},{7,3},{8,4},{1... | collective-permute-start | bytes 2961416 | tf_op jit(solution)/shard_map/ppermute | solution.py:513
  4.8 9.3 %collective-permute-start.2 = (f32[2,16,16,128]{3,2,1,0:T(8,128)S(1)}, f32[2,16,16,128]{3,2,1,0:T(8,128)S(1)}, u32[]{:S(2)}, u32[]{:S(2)}) collective-permute-start(f32[2,16,16,128]{3,2,1,0:T(8,128)S(1)} %shard_map.56.token.refs_1_), channel_id=1, source_target_pairs={{2,0},{3,1},{0,2},{1,3},{6,4},{7,5},{4,6},{5,7},{10,8},{11,9},{8,1... | collective-permute-start | bytes 786440 | tf_op jit(solution)/shard_map/ppermute | solution.py:438
  14.4 4.4 %collective-permute-start.3 = (f32[15,16,128]{2,1,0:T(8,128)S(1)}, f32[15,16,128]{2,1,0:T(8,128)S(1)}, u32[]{:S(2)}, u32[]{:S(2)}) collective-permute-start(f32[15,16,128]{2,1,0:T(8,128)S(1)} %get-tuple-element.73), channel_id=1, source_target_pairs={{0,1},{2,3},{7,6},{5,4},{8,9},{10,11},{15,14},{13,12},{16,17},{18,... | collective-permute-start | bytes 368648 | tf_op jit(solution)/shard_map/ppermute | solution.py:559
  15.8 6.2 %collective-permute-start.4 = (f32[12,16,128]{2,1,0:T(8,128)S(1)}, f32[12,16,128]{2,1,0:T(8,128)S(1)}, u32[]{:S(2)}, u32[]{:S(2)}) collective-permute-start(f32[12,16,128]{2,1,0:T(8,128)S(1)} %get-tuple-element.81), channel_id=1, source_target_pairs={{1,2},{3,7},{6,5},{4,8},{9,10},{11,15},{14,13},{12,16},{17,18},{19... | collective-permute-start | bytes 294920 | tf_op jit(solution)/shard_map/ppermute | solution.py:558
  23.6 3.3 %collective-permute-start.5 = (f32[15,16,128]{2,1,0:T(8,128)S(1)}, f32[15,16,128]{2,1,0:T(8,128)S(1)}, u32[]{:S(2)}, u32[]{:S(2)}) collective-permute-start(f32[15,16,128]{2,1,0:T(8,128)S(1)} %get-tuple-element.87), channel_id=1, source_target_pairs={{0,1},{2,3},{7,6},{5,4},{8,9},{10,11},{15,14},{13,12},{16,17},{18,... | collective-permute-start | bytes 368648 | tf_op jit(solution)/shard_map/ppermute | solution.py:559
  24.9 6.2 %collective-permute-start.6 = (f32[12,16,128]{2,1,0:T(8,128)S(1)}, f32[12,16,128]{2,1,0:T(8,128)S(1)}, u32[]{:S(2)}, u32[]{:S(2)}) collective-permute-start(f32[12,16,128]{2,1,0:T(8,128)S(1)} %get-tuple-element.93), channel_id=1, source_target_pairs={{1,2},{3,7},{6,5},{4,8},{9,10},{11,15},{14,13},{12,16},{17,18},{19... | collective-permute-start | bytes 294920 | tf_op jit(solution)/shard_map/ppermute | solution.py:558
  32.7 3.3 %collective-permute-start.7 = (f32[15,16,128]{2,1,0:T(8,128)S(1)}, f32[15,16,128]{2,1,0:T(8,128)S(1)}, u32[]{:S(2)}, u32[]{:S(2)}) collective-permute-start(f32[15,16,128]{2,1,0:T(8,128)S(1)} %get-tuple-element.99), channel_id=1, source_target_pairs={{0,1},{2,3},{7,6},{5,4},{8,9},{10,11},{15,14},{13,12},{16,17},{18,... | collective-permute-start | bytes 368648 | tf_op jit(solution)/shard_map/ppermute | solution.py:559
  34.1 6.2 %collective-permute-start.8 = (f32[12,16,128]{2,1,0:T(8,128)S(1)}, f32[12,16,128]{2,1,0:T(8,128)S(1)}, u32[]{:S(2)}, u32[]{:S(2)}) collective-permute-start(f32[12,16,128]{2,1,0:T(8,128)S(1)} %get-tuple-element.105), channel_id=1, source_target_pairs={{1,2},{3,7},{6,5},{4,8},{9,10},{11,15},{14,13},{12,16},{17,18},{19... | collective-permute-start | bytes 294920 | tf_op jit(solution)/shard_map/ppermute | solution.py:558
  41.8 3.3 %collective-permute-start.9 = (f32[15,16,128]{2,1,0:T(8,128)S(1)}, f32[15,16,128]{2,1,0:T(8,128)S(1)}, u32[]{:S(2)}, u32[]{:S(2)}) collective-permute-start(f32[15,16,128]{2,1,0:T(8,128)S(1)} %get-tuple-element.111), channel_id=1, source_target_pairs={{0,1},{2,3},{7,6},{5,4},{8,9},{10,11},{15,14},{13,12},{16,17},{18,... | collective-permute-start | bytes 368648 | tf_op jit(solution)/shard_map/ppermute | solution.py:559
  43.2 5.7 %collective-permute-start.10 = (f32[9,16,128]{2,1,0:T(8,128)S(1)}, f32[9,16,128]{2,1,0:T(8,128)S(1)}, u32[]{:S(2)}, u32[]{:S(2)}) collective-permute-start(f32[9,16,128]{2,1,0:T(8,128)S(1)} %get-tuple-element.117), channel_id=1, source_target_pairs={{1,2},{3,7},{6,5},{4,8},{9,10},{11,15},{14,13},{12,16},{17,18},{19... | collective-permute-start | bytes 221192 | tf_op jit(solution)/shard_map/ppermute | solution.py:558
  50.2 3.8 %collective-permute-start.12 = (f32[16,16,128]{2,1,0:T(8,128)S(1)}, f32[16,16,128]{2,1,0:T(8,128)S(1)}, u32[]{:S(2)}, u32[]{:S(2)}) collective-permute-start(f32[16,16,128]{2,1,0:T(8,128)S(1)} %get-tuple-element.118.refs_0_), channel_id=1, source_target_pairs={{2,0},{3,1},{0,2},{1,3},{6,4},{7,5},{4,6},{5,7},{10,8},{11,9},{8,1... | collective-permute-start | bytes 393224 | tf_op jit(solution)/shard_map/ppermute | solution.py:438
  50.3 6.5 %collective-permute-start.11 = (f32[16,16,128]{2,1,0:T(8,128)S(1)}, f32[16,16,128]{2,1,0:T(8,128)S(1)}, u32[]{:S(2)}, u32[]{:S(2)}) collective-permute-start(f32[16,16,128]{2,1,0:T(8,128)S(1)} %get-tuple-element.118.refs_0_), channel_id=1, source_target_pairs={{0,1},{1,0},{2,3},{3,2},{4,5},{5,4},{6,7},{7,6},{8,9},{9,8},{10,11... | collective-permute-start | bytes 393224 | tf_op jit(solution)/shard_map/ppermute | solution.py:442
  54.1 3.7 %collective-permute-start.13 = (f32[16,16,128]{2,1,0:T(8,128)S(1)}, f32[16,16,128]{2,1,0:T(8,128)S(1)}, u32[]{:S(2)}, u32[]{:S(2)}) collective-permute-start(f32[16,16,128]{2,1,0:T(8,128)S(1)} %collective-permute-done.12.refs_2_), channel_id=1, source_target_pairs={{0,1},{1,0},{2,3},{3,2},{4,5},{5,4},{6,7},{7,6},{8,9},{9,8},{10,11... | collective-permute-start | bytes 393224 | tf_op jit(solution)/shard_map/ppermute | solution.py:442

commit v13 on v12

--- a/solution.py
+++ b/solution.py
@@ -176,29 +176,13 @@
     rows_of_parts(ob, folds, facts, (first, second), [(0, out)])
 
 
-def first_kernel(folds, lend, width, counts, columns, initial, right_side, blocks, facts, held, stacked, border, live, sem):
-    own = columns.shape[1]
-    size = blocks.shape[0] // own
+def first_kernel(folds, counts, columns, initial, right_side, facts, held, stacked, live, sem):
     fold = lax.axis_index("fold")
     backwards = lax.rem(lax.axis_index("group"), 2)
     part = part_of(fold, folds, backwards)
-    edge = (part == 0) | (part == folds - 1)
-    first = jnp.where(part == 0, 0, own - lend)
     small = [pltpu.make_async_copy(columns, held, sem.at[0]), pltpu.make_async_copy(counts, live, sem.at[1])]
     pair = [pltpu.make_async_copy(array, stacked.at[i], sem.at[2 + i]) for i, array in enumerate((initial, right_side))]
-    rows = []
-    for i in range(lend):
-        row = blocks.at[pl.ds(pl.multiple_of((first + i) * size, size), size)]
-        rows.append(pltpu.make_async_copy(row, border.at[i * size : (i + 1) * size], sem.at[4 + i]))
-    for copy in small:
-        copy.start()
-
-    @pl.when(edge)
-    def _():
-        for copy in rows:
-            copy.start()
-
-    for copy in pair:
+    for copy in pair + small:
         copy.start()
     for copy in small:
         copy.wait()
@@ -206,9 +190,25 @@
         facts[i] = fact
     for i in range(folds):
         facts[COUNTS + i] = live[0, i]
-
-    @pl.when(edge)
+    for copy in pair:
+        copy.wait()
+
+
+def outward_kernel(folds, lend, width, facts, held, blocks, before, border, sem):
+    del before
+    own = held.shape[1]
+    size = blocks.shape[0] // own
+    part = facts[0]
+    first = jnp.where(part == 0, 0, own - lend)
+
+    @pl.when((part == 0) | (part == folds - 1))
     def _():
+        rows = []
+        for i in range(lend):
+            row = blocks.at[pl.ds(pl.multiple_of((first + i) * size, size), size)]
+            rows.append(pltpu.make_async_copy(row, border.at[i * size : (i + 1) * size], sem.at[i]))
+        for copy in rows:
+            copy.start()
         lane = lax.broadcasted_iota(jnp.int32, (8, 128), 1)
         indices = jnp.zeros((8, 128), jnp.int32)
         for i in range(lend):
@@ -217,9 +217,6 @@
         border[lend * size :] = indices.astype(F32)
         for copy in rows:
             copy.wait()
-
-    for copy in pair:
-        copy.wait()
 
 
 def gate_kernel(*refs):
@@ -290,6 +287,7 @@
 def apply_rows(t, steps, starts, count, first, last, pair, offset, operator, x, u, r, pieces):
     now, later = pieces[t % 2], pieces[(t + 1) % 2]
     width = operator.shape[1] // 128
+    home = HB * steps
     old, new = pair
     final = last and t == steps - 1
 
@@ -313,8 +311,9 @@
         resid = r[e] - (product[:, :128] + product[:, 128:])
         before = u[e]
         update = new * resid if old == 0.0 else old * before + new * resid
-        total = before if first and t == 0 else x[e] + before
-        x[e] = total + update if final else total
+        if not isinstance(starts, int) or home <= e < x.shape[0] - home:
+            total = before if first and t == 0 else x[e] + before
+            x[e] = total + update if final else total
         if not final:
             r[e] = resid
             u[e] = update
@@ -476,21 +475,28 @@
         return pltpu.with_memory_space_constraint(array, space)
 
     flat = fixed(blocks.reshape(own * size, side))
-    facts, indices, stacked, border = pl.pallas_call(
-        functools.partial(first_kernel, folds, lend, width),
+    facts, indices, stacked = pl.pallas_call(
+        functools.partial(first_kernel, folds),
         out_shape=(
             pltpu.SMEM((COUNTS + folds,), jnp.int32),
             pltpu.SMEM((width, own), jnp.int32),
             pltpu.VMEM((2, vectors, capacity), F32),
-            pltpu.VMEM((lend * size + 8, side), F32),
         ),
-        in_specs=[HBM] * 5,
-        out_specs=(SMEM, SMEM, VMEM, VMEM),
-        scratch_shapes=[pltpu.SMEM((1, folds), jnp.int32), pltpu.SemaphoreType.DMA((4 + lend,))],
+        in_specs=[HBM] * 4,
+        out_specs=(SMEM, SMEM, VMEM),
+        scratch_shapes=[pltpu.SMEM((1, folds), jnp.int32), pltpu.SemaphoreType.DMA((4,))],
         compiler_params=params(),
-    )(fixed(counts), fixed(columns.T), fixed(initial), fixed(right_side), flat)
+    )(fixed(counts), fixed(columns.T), fixed(initial), fixed(right_side))
     facts, indices = fixed(facts, pltpu.SMEM), fixed(indices, pltpu.SMEM)
     mate = other_core(stacked, folds)
+    border = pl.pallas_call(
+        functools.partial(outward_kernel, folds, lend, width),
+        out_shape=pltpu.VMEM((lend * size + 8, side), F32),
+        in_specs=[SMEM, SMEM, HBM, pl.BlockSpec(memory_space=pl.ANY)],
+        out_specs=VMEM,
+        scratch_shapes=[pltpu.SemaphoreType.DMA((lend,))],
+        compiler_params=params(),
+    )(facts, indices, flat, stacked)
 
     rows_of = jax.ShapeDtypeStruct((2, ob, vectors, side), F32)
     slots = [fixed(stacked, pltpu.VMEM), fixed(mate, pltpu.VMEM)]

time: 59 us -> 58.9 us (level)
  no operation moved by 1% of the time
where the time goes in v13:
time: 58.9 us; the launch traced here: 58.7 us
  starting transfers between devices  23.5 us (40%)
  Pallas kernels  22.5 us (38%)
  waiting for transfers between devices  12.5 us (21%)
    pallas_call x8, Pallas kernels, part_of_phase(): pl.pallas_call(functools.partial(kernel, ob, folds, steps, done == 0, don...  14.6 us
    ppermute x4, starting transfers between devices, on_device(): got_b = lax.ppermute(pay_b, AXES, swap_b)  8.29 us
    ppermute x4, waiting for transfers between devices, on_device(): got_b = lax.ppermute(pay_b, AXES, swap_b)  7.29 us
    ppermute x4, starting transfers between devices, on_device(): got_a = lax.ppermute(pay_a, AXES, swap_a)  5.8 us
    ppermute x3, starting transfers between devices, other_core(): return lax.ppermute(array, 'fold', [(i, i ^ 1) for i in range(folds)])  4.95 us
    pallas_call x1, Pallas kernels, on_device(): pl.pallas_call(functools.partial(prepare_kernel, ob, halo, lend, width),...  4.8 us
    ppermute x2, starting transfers between devices, over_chips(): lax.ppermute(array, 'fold', [((i + 2 * d) % folds, i) for i in range(fold...  3.77 us
    ppermute x2, waiting for transfers between devices, over_chips(): lax.ppermute(array, 'fold', [((i + 2 * d) % folds, i) for i in range(fold...  2.72 us
  transfers between devices with their start and end apart: 14, of which 8 were waited for; matrix products, arithmetic and copies ran while one was open for 0% of the time, Pallas kernels for 24%

profile of v13, /device:TPU:9, one launch (start us, length us, event | category | flops | bytes accessed | tf_op | source)
XLA Modules:
  0.0 58.7 jit_solution(11802760360936468065)
XLA Ops:
  0.0 1.1 %shard_map.55 = (s32[8]{0:T(128)S(4)}, s32[5,64]{1,0:T(8,128)S(4)}, f32[2,16,4096]{2,1,0:T(8,128)S(1)}) custom-call(s32[1,4]{1,0:T(1,128)} %counts.1, s32[5,64]{1,0:T(8,128)} %bitcast.4, f32[16,4096]{1,0:T(8,128)} %initial.1, f32[16,4096]{1,0:T(8,128)} %right_side.1), custom_call_target="tpu_custom_call" | custom-call | tf_op jit(solution)/shard_map/pallas_call | solution.py:478
  1.1 0.7 %collective-permute-start = (f32[2,16,4096]{2,1,0:T(8,128)S(1)}, f32[2,16,4096]{2,1,0:T(8,128)S(1)}, u32[]{:S(2)}, u32[]{:S(2)}) collective-permute-start(f32[2,16,4096]{2,1,0:T(8,128)S(1)} %get-tuple-element.63.first.before), channel_id=1, source_target_pairs={{0,1},{1,0},{2,3},{3,2},{4,5},{5,4},{6,7},{7,6},{8,9},{9,8},{10,11... | collective-permute-start | bytes 1572872 | tf_op jit(solution)/shard_map/ppermute | solution.py:441
  1.8 1.5 %collective-permute-done.second = f32[2,16,4096]{2,1,0:T(8,128)S(1)} collective-permute-done((f32[2,16,4096]{2,1,0:T(8,128)S(1)}, f32[2,16,4096]{2,1,0:T(8,128)S(1)}, u32[]{:S(2)}, u32[]{:S(2)}) %collective-permute-start) | collective-permute-done | bytes 524320 | tf_op jit(solution)/shard_map/ppermute | solution.py:441
  3.3 0.3 shard_map.56.token.refs_1_
  3.7 0.7 %collective-permute-start.1 = (f32[1928,128]{1,0:T(8,128)S(1)}, f32[1928,128]{1,0:T(8,128)S(1)}, u32[]{:S(2)}, u32[]{:S(2)}) collective-permute-start(f32[1928,128]{1,0:T(8,128)S(1)} %shard_map.59), channel_id=1, source_target_pairs={{3,7},{4,8},{11,15},{12,16},{19,23},{20,24},{27,31},{7,3},{8,4},{1... | collective-permute-start | bytes 2961416 | tf_op jit(solution)/shard_map/ppermute | solution.py:519
  4.4 3.7 %collective-permute-start.2 = (f32[2,16,16,128]{3,2,1,0:T(8,128)S(1)}, f32[2,16,16,128]{3,2,1,0:T(8,128)S(1)}, u32[]{:S(2)}, u32[]{:S(2)}) collective-permute-start(f32[2,16,16,128]{3,2,1,0:T(8,128)S(1)} %shard_map.56.token.refs_1_), channel_id=1, source_target_pairs={{2,0},{3,1},{0,2},{1,3},{6,4},{7,5},{4,6},{5,7},{10,8},{11,9},{8,1... | collective-permute-start | bytes 786440 | tf_op jit(solution)/shard_map/ppermute | solution.py:437
  8.1 0.3 shard_map.60.refs_0_
  8.5 4.8 %shard_map.57 = (bf16[28,640,256]{2,1,0:T(8,128)(2,1)S(1)}, s32[140]{0:T(256)S(4)}) custom-call(s32[8]{0:T(128)S(4)} %get-tuple-element.61.facts, s32[5,64]{1,0:T(8,128)S(4)} %get-tuple-element.62.columns.held, f32[40960,128]{1,0:T(8,128)} %bitcast.3, f32[2,16,16,128]{3,2,1,0:T(8,128)S(1)} %shard_map.56.token.refs_1_), custom_call_target="tpu_custom_call" | custom-call | flops 10000000 | bytes 18350080 | tf_op jit(solution)/shard_map/pallas_call | solution.py:522
  13.3 0.5 collective-permute-done.2.refs_1_
  13.8 0.3 shard_map.61
  14.1 1.7 %collective-permute-start.3 = (f32[15,16,128]{2,1,0:T(8,128)S(1)}, f32[15,16,128]{2,1,0:T(8,128)S(1)}, u32[]{:S(2)}, u32[]{:S(2)}) collective-permute-start(f32[15,16,128]{2,1,0:T(8,128)S(1)} %get-tuple-element.71), channel_id=1, source_target_pairs={{0,1},{2,3},{7,6},{5,4},{8,9},{10,11},{15,14},{13,12},{16,17},{18,... | collective-permute-start | bytes 368648 | tf_op jit(solution)/shard_map/ppermute | solution.py:565
  15.8 2.6 %collective-permute-start.4 = (f32[12,16,128]{2,1,0:T(8,128)S(1)}, f32[12,16,128]{2,1,0:T(8,128)S(1)}, u32[]{:S(2)}, u32[]{:S(2)}) collective-permute-start(f32[12,16,128]{2,1,0:T(8,128)S(1)} %get-tuple-element.79), channel_id=1, source_target_pairs={{1,2},{3,7},{6,5},{4,8},{9,10},{11,15},{14,13},{12,16},{17,18},{19... | collective-permute-start | bytes 294920 | tf_op jit(solution)/shard_map/ppermute | solution.py:564
  18.4 0.0 collective-permute-done.3.refs_5_
  18.4 2.0 %shard_map.62 = (f32[34,16,128]{2,1,0:T(8,128)S(1)}, f32[34,16,128]{2,1,0:T(8,128)S(1)}, f32[34,16,128]{2,1,0:T(8,128)S(1)}, bf16[34,32,128]{2,1,0:T(8,128)(2,1)S(1)}, bf16[34,32,128]{2,1,0:T(8,128)(2,1)S(1)}) custom-call(s32[8]{0:T(128)S(4)} %get-tuple-element.61.facts, ...), custom_call_target="tpu_custom_call", output_to_operand_aliasing={{0}: (3, {}), {1}: (4, {}), {2}: (5, {}), {3}: (6, {}), {4}... | custom-call | tf_op jit(solution)/shard_map/pallas_call | solution.py:553
  20.4 0.0 collective-permute-done.1.raw
  20.5 1.5 %collective-permute-done.4.refs_5_ = f32[12,16,128]{2,1,0:T(8,128)S(1)} collective-permute-done((f32[12,16,128]{2,1,0:T(8,128)S(1)}, f32[12,16,128]{2,1,0:T(8,128)S(1)}, u32[]{:S(2)}, u32[]{:S(2)}) %collective-permute-start.4) | collective-permute-done | bytes 98336 | tf_op jit(solution)/shard_map/ppermute | solution.py:564
  22.0 1.5 %shard_map.64 = (f32[34,16,128]{2,1,0:T(8,128)S(1)}, f32[34,16,128]{2,1,0:T(8,128)S(1)}, f32[34,16,128]{2,1,0:T(8,128)S(1)}, bf16[34,32,128]{2,1,0:T(8,128)(2,1)...) custom-call(s32[8]{0:T(128)S(4)} %get-tuple-element.61.facts, ...), custom_call_target="tpu_custom_call", output_to_operand_aliasing={{0}: (4, {}), {1}: (5, {}), {2}: (6, {}), {3}: (7, {}), {4}... | custom-call | tf_op jit(solution)/shard_map/pallas_call | solution.py:553
  23.5 1.4 %collective-permute-start.5 = (f32[15,16,128]{2,1,0:T(8,128)S(1)}, f32[15,16,128]{2,1,0:T(8,128)S(1)}, u32[]{:S(2)}, u32[]{:S(2)}) collective-permute-start(f32[15,16,128]{2,1,0:T(8,128)S(1)} %get-tuple-element.85), channel_id=1, source_target_pairs={{0,1},{2,3},{7,6},{5,4},{8,9},{10,11},{15,14},{13,12},{16,17},{18,... | collective-permute-start | bytes 368648 | tf_op jit(solution)/shard_map/ppermute | solution.py:565
  24.9 1.9 %collective-permute-start.6 = (f32[12,16,128]{2,1,0:T(8,128)S(1)}, f32[12,16,128]{2,1,0:T(8,128)S(1)}, u32[]{:S(2)}, u32[]{:S(2)}) collective-permute-start(f32[12,16,128]{2,1,0:T(8,128)S(1)} %get-tuple-element.91), channel_id=1, source_target_pairs={{1,2},{3,7},{6,5},{4,8},{9,10},{11,15},{14,13},{12,16},{17,18},{19... | collective-permute-start | bytes 294920 | tf_op jit(solution)/shard_map/ppermute | solution.py:564
  26.8 0.0 collective-permute-done.5.refs_5_
  26.8 2.2 %shard_map.65 = (f32[34,16,128]{2,1,0:T(8,128)S(1)}, f32[34,16,128]{2,1,0:T(8,128)S(1)}, f32[34,16,128]{2,1,0:T(8,128)S(1)}, bf16[34,32,128]{2,1,0:T(8,128)(2,1)S(1)}, bf16[34,32,128]{2,1,0:T(8,128)(2,1)S(1)}) custom-call(s32[8]{0:T(128)S(4)} %get-tuple-element.61.facts, ...), custom_call_target="tpu_custom_call", output_to_operand_aliasing={{0}: (3, {}), {1}: (4, {}), {2}: (5, {}), {3}: (6, {}), {4}... | custom-call | tf_op jit(solution)/shard_map/pallas_call | solution.py:553
  29.1 2.1 %collective-permute-done.6.refs_5_ = f32[12,16,128]{2,1,0:T(8,128)S(1)} collective-permute-done((f32[12,16,128]{2,1,0:T(8,128)S(1)}, f32[12,16,128]{2,1,0:T(8,128)S(1)}, u32[]{:S(2)}, u32[]{:S(2)}) %collective-permute-start.6) | collective-permute-done | bytes 98336 | tf_op jit(solution)/shard_map/ppermute | solution.py:564
  31.1 1.5 %shard_map.66 = (f32[34,16,128]{2,1,0:T(8,128)S(1)}, f32[34,16,128]{2,1,0:T(8,128)S(1)}, f32[34,16,128]{2,1,0:T(8,128)S(1)}, bf16[34,32,128]{2,1,0:T(8,128)(2,1)...) custom-call(s32[8]{0:T(128)S(4)} %get-tuple-element.61.facts, ...), custom_call_target="tpu_custom_call", output_to_operand_aliasing={{0}: (4, {}), {1}: (5, {}), {2}: (6, {}), {3}: (7, {}), {4}... | custom-call | tf_op jit(solution)/shard_map/pallas_call | solution.py:553
  32.7 1.4 %collective-permute-start.7 = (f32[15,16,128]{2,1,0:T(8,128)S(1)}, f32[15,16,128]{2,1,0:T(8,128)S(1)}, u32[]{:S(2)}, u32[]{:S(2)}) collective-permute-start(f32[15,16,128]{2,1,0:T(8,128)S(1)} %get-tuple-element.97), channel_id=1, source_target_pairs={{0,1},{2,3},{7,6},{5,4},{8,9},{10,11},{15,14},{13,12},{16,17},{18,... | collective-permute-start | bytes 368648 | tf_op jit(solution)/shard_map/ppermute | solution.py:565
  34.0 1.9 %collective-permute-start.8 = (f32[12,16,128]{2,1,0:T(8,128)S(1)}, f32[12,16,128]{2,1,0:T(8,128)S(1)}, u32[]{:S(2)}, u32[]{:S(2)}) collective-permute-start(f32[12,16,128]{2,1,0:T(8,128)S(1)} %get-tuple-element.103), channel_id=1, source_target_pairs={{1,2},{3,7},{6,5},{4,8},{9,10},{11,15},{14,13},{12,16},{17,18},{19... | collective-permute-start | bytes 294920 | tf_op jit(solution)/shard_map/ppermute | solution.py:564
  35.9 0.0 collective-permute-done.7.refs_5_
  35.9 2.1 %shard_map.67 = (f32[34,16,128]{2,1,0:T(8,128)S(1)}, f32[34,16,128]{2,1,0:T(8,128)S(1)}, f32[34,16,128]{2,1,0:T(8,128)S(1)}, bf16[34,32,128]{2,1,0:T(8,128)(2,1)S(1)}, bf16[34,32,128]{2,1,0:T(8,128)(2,1)S(1)}) custom-call(s32[8]{0:T(128)S(4)} %get-tuple-element.61.facts, ...), custom_call_target="tpu_custom_call", output_to_operand_aliasing={{0}: (3, {}), {1}: (4, {}), {2}: (5, {}), {3}: (6, {}), {4}... | custom-call | tf_op jit(solution)/shard_map/pallas_call | solution.py:553
  38.0 2.2 %collective-permute-done.8.refs_5_ = f32[12,16,128]{2,1,0:T(8,128)S(1)} collective-permute-done((f32[12,16,128]{2,1,0:T(8,128)S(1)}, f32[12,16,128]{2,1,0:T(8,128)S(1)}, u32[]{:S(2)}, u32[]{:S(2)}) %collective-permute-start.8) | collective-permute-done | bytes 98336 | tf_op jit(solution)/shard_map/ppermute | solution.py:564
  40.2 1.5 %shard_map.68 = (f32[34,16,128]{2,1,0:T(8,128)S(1)}, f32[34,16,128]{2,1,0:T(8,128)S(1)}, f32[34,16,128]{2,1,0:T(8,128)S(1)}, bf16[34,32,128]{2,1,0:T(8,128)(2,1)...) custom-call(s32[8]{0:T(128)S(4)} %get-tuple-element.61.facts, ...), custom_call_target="tpu_custom_call", output_to_operand_aliasing={{0}: (4, {}), {1}: (5, {}), {2}: (6, {}), {3}: (7, {}), {4}... | custom-call | tf_op jit(solution)/shard_map/pallas_call | solution.py:553
  41.7 1.4 %collective-permute-start.9 = (f32[15,16,128]{2,1,0:T(8,128)S(1)}, f32[15,16,128]{2,1,0:T(8,128)S(1)}, u32[]{:S(2)}, u32[]{:S(2)}) collective-permute-start(f32[15,16,128]{2,1,0:T(8,128)S(1)} %get-tuple-element.109), channel_id=1, source_target_pairs={{0,1},{2,3},{7,6},{5,4},{8,9},{10,11},{15,14},{13,12},{16,17},{18,... | collective-permute-start | bytes 368648 | tf_op jit(solution)/shard_map/ppermute | solution.py:565
  43.1 1.9 %collective-permute-start.10 = (f32[9,16,128]{2,1,0:T(8,128)S(1)}, f32[9,16,128]{2,1,0:T(8,128)S(1)}, u32[]{:S(2)}, u32[]{:S(2)}) collective-permute-start(f32[9,16,128]{2,1,0:T(8,128)S(1)} %get-tuple-element.115), channel_id=1, source_target_pairs={{1,2},{3,7},{6,5},{4,8},{9,10},{11,15},{14,13},{12,16},{17,18},{19... | collective-permute-start | bytes 221192 | tf_op jit(solution)/shard_map/ppermute | solution.py:564
  45.0 0.0 collective-permute-done.9.refs_5_
  45.1 2.3 %shard_map.69 = (f32[34,16,128]{2,1,0:T(8,128)S(1)}, f32[34,16,128]{2,1,0:T(8,128)S(1)}, f32[34,16,128]{2,1,0:T(8,128)S(1)}, bf16[34,32,128]{2,1,0:T(8,128)(2,1)S(1)}, bf16[34,32,128]{2,1,0:T(8,128)(2,1)S(1)}) custom-call(s32[8]{0:T(128)S(4)} %get-tuple-element.61.facts, ...), custom_call_target="tpu_custom_call", output_to_operand_aliasing={{0}: (3, {}), {1}: (4, {}), {2}: (5, {}), {3}: (6, {}), {4}... | custom-call | tf_op jit(solution)/shard_map/pallas_call | solution.py:553
  47.3 1.5 %collective-permute-done.10.refs_5_ = f32[9,16,128]{2,1,0:T(8,128)S(1)} collective-permute-done((f32[9,16,128]{2,1,0:T(8,128)S(1)}, f32[9,16,128]{2,1,0:T(8,128)S(1)}, u32[]{:S(2)}, u32[]{:S(2)}) %collective-permute-start.10) | collective-permute-done | bytes 73760 | tf_op jit(solution)/shard_map/ppermute | solution.py:564
  48.8 1.4 %shard_map.70 = (f32[34,16,128]{2,1,0:T(8,128)S(1)}, f32[34,16,128]{2,1,0:T(8,128)S(1)}, f32[34,16,128]{2,1,0:T(8,128)S(1)}, bf16[34,32,128]{2,1,0:T(8,128)(2,1)...) custom-call(s32[8]{0:T(128)S(4)} %get-tuple-element.61.facts, ...), custom_call_target="tpu_custom_call", output_to_operand_aliasing={{0}: (4, {}), {1}: (5, {}), {2}: (6, {}), {3}: (7, {}), {4}... | custom-call | tf_op jit(solution)/shard_map/pallas_call | solution.py:553
  50.2 0.1 collective-permute-start.12
  50.3 1.6 %collective-permute-start.11 = (f32[16,16,128]{2,1,0:T(8,128)S(1)}, f32[16,16,128]{2,1,0:T(8,128)S(1)}, u32[]{:S(2)}, u32[]{:S(2)}) collective-permute-start(f32[16,16,128]{2,1,0:T(8,128)S(1)} %get-tuple-element.116.refs_0_), channel_id=1, source_target_pairs={{0,1},{1,0},{2,3},{3,2},{4,5},{5,4},{6,7},{7,6},{8,9},{9,8},{10,11... | collective-permute-start | bytes 393224 | tf_op jit(solution)/shard_map/ppermute | solution.py:441
  51.8 2.2 %collective-permute-done.12.refs_2_ = f32[16,16,128]{2,1,0:T(8,128)S(1)} collective-permute-done((f32[16,16,128]{2,1,0:T(8,128)S(1)}, f32[16,16,128]{2,1,0:T(8,128)S(1)}, u32[]{:S(2)}, u32[]{:S(2)}) %collective-permute-start.12) | collective-permute-done | bytes 131104 | tf_op jit(solution)/shard_map/ppermute | solution.py:437
  54.1 2.6 %collective-permute-start.13 = (f32[16,16,128]{2,1,0:T(8,128)S(1)}, f32[16,16,128]{2,1,0:T(8,128)S(1)}, u32[]{:S(2)}, u32[]{:S(2)}) collective-permute-start(f32[16,16,128]{2,1,0:T(8,128)S(1)} %collective-permute-done.12.refs_2_), channel_id=1, source_target_pairs={{0,1},{1,0},{2,3},{3,2},{4,5},{5,4},{6,7},{7,6},{8,9},{9,8},{10,11... | collective-permute-start | bytes 393224 | tf_op jit(solution)/shard_map/ppermute | solution.py:441
  56.7 0.0 collective-permute-done.11.refs_1_
  56.7 1.0 %collective-permute-done.13.refs_3_ = f32[16,16,128]{2,1,0:T(8,128)S(1)} collective-permute-done((f32[16,16,128]{2,1,0:T(8,128)S(1)}, f32[16,16,128]{2,1,0:T(8,128)S(1)}, u32[]{:S(2)}, u32[]{:S(2)}) %collective-permute-start.13) | collective-permute-done | bytes 131104 | tf_op jit(solution)/shard_map/ppermute | solution.py:441
  57.7 0.9 %shard_map.71 = f32[16,4096]{1,0:T(8,128)} custom-call(s32[8]{0:T(128)S(4)} %get-tuple-element.61.facts, f32[16,16,128]{2,1,0:T(8,128)S(1)} %get-tuple-element.116.refs_0_, f32[16,16,128]{2,1,0:T(8,128)S(1)} %collective-permute-done.11.refs_1_, f32[16,16,128]{2,1,0:T(8,128)S(1)} %collective-permute-done.12.refs_2_, ...), custom_call_target="tpu_custom_call" | custom-call | tf_op jit(solution)/shard_map/pallas_call | solution.py:597
  (3 shorter events, 0.0 us)
Async XLA Ops:
  1.1 2.3 %collective-permute-start = (f32[2,16,4096]{2,1,0:T(8,128)S(1)}, f32[2,16,4096]{2,1,0:T(8,128)S(1)}, u32[]{:S(2)}, u32[]{:S(2)}) collective-permute-start(f32[2,16,4096]{2,1,0:T(8,128)S(1)} %get-tuple-element.63.first.before), channel_id=1, source_target_pairs={{0,1},{1,0},{2,3},{3,2},{4,5},{5,4},{6,7},{7,6},{8,9},{9,8},{10,11... | collective-permute-start | bytes 1572872 | tf_op jit(solution)/shard_map/ppermute | solution.py:441
  3.7 16.7 %collective-permute-start.1 = (f32[1928,128]{1,0:T(8,128)S(1)}, f32[1928,128]{1,0:T(8,128)S(1)}, u32[]{:S(2)}, u32[]{:S(2)}) collective-permute-start(f32[1928,128]{1,0:T(8,128)S(1)} %shard_map.59), channel_id=1, source_target_pairs={{3,7},{4,8},{11,15},{12,16},{19,23},{20,24},{27,31},{7,3},{8,4},{1... | collective-permute-start | bytes 2961416 | tf_op jit(solution)/shard_map/ppermute | solution.py:519
  4.4 9.3 %collective-permute-start.2 = (f32[2,16,16,128]{3,2,1,0:T(8,128)S(1)}, f32[2,16,16,128]{3,2,1,0:T(8,128)S(1)}, u32[]{:S(2)}, u32[]{:S(2)}) collective-permute-start(f32[2,16,16,128]{3,2,1,0:T(8,128)S(1)} %shard_map.56.token.refs_1_), channel_id=1, source_target_pairs={{2,0},{3,1},{0,2},{1,3},{6,4},{7,5},{4,6},{5,7},{10,8},{11,9},{8,1... | collective-permute-start | bytes 786440 | tf_op jit(solution)/shard_map/ppermute | solution.py:437
  14.1 4.3 %collective-permute-start.3 = (f32[15,16,128]{2,1,0:T(8,128)S(1)}, f32[15,16,128]{2,1,0:T(8,128)S(1)}, u32[]{:S(2)}, u32[]{:S(2)}) collective-permute-start(f32[15,16,128]{2,1,0:T(8,128)S(1)} %get-tuple-element.71), channel_id=1, source_target_pairs={{0,1},{2,3},{7,6},{5,4},{8,9},{10,11},{15,14},{13,12},{16,17},{18,... | collective-permute-start | bytes 368648 | tf_op jit(solution)/shard_map/ppermute | solution.py:565
  15.8 6.2 %collective-permute-start.4 = (f32[12,16,128]{2,1,0:T(8,128)S(1)}, f32[12,16,128]{2,1,0:T(8,128)S(1)}, u32[]{:S(2)}, u32[]{:S(2)}) collective-permute-start(f32[12,16,128]{2,1,0:T(8,128)S(1)} %get-tuple-element.79), channel_id=1, source_target_pairs={{1,2},{3,7},{6,5},{4,8},{9,10},{11,15},{14,13},{12,16},{17,18},{19... | collective-permute-start | bytes 294920 | tf_op jit(solution)/shard_map/ppermute | solution.py:564
  23.5 3.3 %collective-permute-start.5 = (f32[15,16,128]{2,1,0:T(8,128)S(1)}, f32[15,16,128]{2,1,0:T(8,128)S(1)}, u32[]{:S(2)}, u32[]{:S(2)}) collective-permute-start(f32[15,16,128]{2,1,0:T(8,128)S(1)} %get-tuple-element.85), channel_id=1, source_target_pairs={{0,1},{2,3},{7,6},{5,4},{8,9},{10,11},{15,14},{13,12},{16,17},{18,... | collective-permute-start | bytes 368648 | tf_op jit(solution)/shard_map/ppermute | solution.py:565
  24.9 6.2 %collective-permute-start.6 = (f32[12,16,128]{2,1,0:T(8,128)S(1)}, f32[12,16,128]{2,1,0:T(8,128)S(1)}, u32[]{:S(2)}, u32[]{:S(2)}) collective-permute-start(f32[12,16,128]{2,1,0:T(8,128)S(1)} %get-tuple-element.91), channel_id=1, source_target_pairs={{1,2},{3,7},{6,5},{4,8},{9,10},{11,15},{14,13},{12,16},{17,18},{19... | collective-permute-start | bytes 294920 | tf_op jit(solution)/shard_map/ppermute | solution.py:564
  32.7 3.3 %collective-permute-start.7 = (f32[15,16,128]{2,1,0:T(8,128)S(1)}, f32[15,16,128]{2,1,0:T(8,128)S(1)}, u32[]{:S(2)}, u32[]{:S(2)}) collective-permute-start(f32[15,16,128]{2,1,0:T(8,128)S(1)} %get-tuple-element.97), channel_id=1, source_target_pairs={{0,1},{2,3},{7,6},{5,4},{8,9},{10,11},{15,14},{13,12},{16,17},{18,... | collective-permute-start | bytes 368648 | tf_op jit(solution)/shard_map/ppermute | solution.py:565
  34.0 6.2 %collective-permute-start.8 = (f32[12,16,128]{2,1,0:T(8,128)S(1)}, f32[12,16,128]{2,1,0:T(8,128)S(1)}, u32[]{:S(2)}, u32[]{:S(2)}) collective-permute-start(f32[12,16,128]{2,1,0:T(8,128)S(1)} %get-tuple-element.103), channel_id=1, source_target_pairs={{1,2},{3,7},{6,5},{4,8},{9,10},{11,15},{14,13},{12,16},{17,18},{19... | collective-permute-start | bytes 294920 | tf_op jit(solution)/shard_map/ppermute | solution.py:564
  41.7 3.3 %collective-permute-start.9 = (f32[15,16,128]{2,1,0:T(8,128)S(1)}, f32[15,16,128]{2,1,0:T(8,128)S(1)}, u32[]{:S(2)}, u32[]{:S(2)}) collective-permute-start(f32[15,16,128]{2,1,0:T(8,128)S(1)} %get-tuple-element.109), channel_id=1, source_target_pairs={{0,1},{2,3},{7,6},{5,4},{8,9},{10,11},{15,14},{13,12},{16,17},{18,... | collective-permute-start | bytes 368648 | tf_op jit(solution)/shard_map/ppermute | solution.py:565
  43.1 5.7 %collective-permute-start.10 = (f32[9,16,128]{2,1,0:T(8,128)S(1)}, f32[9,16,128]{2,1,0:T(8,128)S(1)}, u32[]{:S(2)}, u32[]{:S(2)}) collective-permute-start(f32[9,16,128]{2,1,0:T(8,128)S(1)} %get-tuple-element.115), channel_id=1, source_target_pairs={{1,2},{3,7},{6,5},{4,8},{9,10},{11,15},{14,13},{12,16},{17,18},{19... | collective-permute-start | bytes 221192 | tf_op jit(solution)/shard_map/ppermute | solution.py:564
  50.2 3.9 %collective-permute-start.12 = (f32[16,16,128]{2,1,0:T(8,128)S(1)}, f32[16,16,128]{2,1,0:T(8,128)S(1)}, u32[]{:S(2)}, u32[]{:S(2)}) collective-permute-start(f32[16,16,128]{2,1,0:T(8,128)S(1)} %get-tuple-element.116.refs_0_), channel_id=1, source_target_pairs={{2,0},{3,1},{0,2},{1,3},{6,4},{7,5},{4,6},{5,7},{10,8},{11,9},{8,1... | collective-permute-start | bytes 393224 | tf_op jit(solution)/shard_map/ppermute | solution.py:437
  50.3 6.5 %collective-permute-start.11 = (f32[16,16,128]{2,1,0:T(8,128)S(1)}, f32[16,16,128]{2,1,0:T(8,128)S(1)}, u32[]{:S(2)}, u32[]{:S(2)}) collective-permute-start(f32[16,16,128]{2,1,0:T(8,128)S(1)} %get-tuple-element.116.refs_0_), channel_id=1, source_target_pairs={{0,1},{1,0},{2,3},{3,2},{4,5},{5,4},{6,7},{7,6},{8,9},{9,8},{10,11... | collective-permute-start | bytes 393224 | tf_op jit(solution)/shard_map/ppermute | solution.py:441
  54.1 3.6 %collective-permute-start.13 = (f32[16,16,128]{2,1,0:T(8,128)S(1)}, f32[16,16,128]{2,1,0:T(8,128)S(1)}, u32[]{:S(2)}, u32[]{:S(2)}) collective-permute-start(f32[16,16,128]{2,1,0:T(8,128)S(1)} %collective-permute-done.12.refs_2_), channel_id=1, source_target_pairs={{0,1},{1,0},{2,3},{3,2},{4,5},{5,4},{6,7},{7,6},{8,9},{9,8},{10,11... | collective-permute-start | bytes 393224 | tf_op jit(solution)/shard_map/ppermute | solution.py:441
